TPU v7x, 32 devices: a whole 2x2x4 slice. The times are simulated.
32 devices in a mesh: seq: 8 (over y, x, core), tp: 4 (over z).
Axes of the slice: x: 2, y: 2, z: 4, core: 2. Of those that a mesh axis runs over, the one named last changes fastest.
Arguments:
- tokens: bfloat16 [8192, 1024], P('seq'), may hold values from -6 to 6
- cotangent: bfloat16 [8192, 1024], P('seq'), may hold values from -6 to 6
- lengths: int32 [8], replicated, may hold values from 1 to 4096, 8192 in all
- retrieve: int32 [8, 8], replicated, may hold values from 0 to 63
- owners: int32 [98], replicated, may hold values from 0 to 103, as said below
- masters: float32 [4, 104, 32, 1024], P('tp', 'seq'), may hold values from -0.1875 to 0.1875
- first_moment: float32 [4, 104, 32, 1024], P('tp', 'seq')
- second_moment: float32 [4, 104, 32, 1024], P('tp', 'seq'), as said below
- averaged: float32 [4, 104, 32, 1024], P('tp', 'seq'), may hold values from -0.1875 to 0.1875
- statistics: float32 [4, 104, 32, 32], P('tp', 'seq'), as said below
- bases: float32 [4, 104, 32, 32], P('tp', 'seq'), as said below
- gains: float32 [2, 1024], replicated, may hold values from 0.5 to 1.5
- gain_first: float32 [2, 1024], replicated, may hold values from -27.1529 to 27.1529
- gain_second: float32 [2, 1024], replicated, may hold values from 106.496 to 409.6
Outputs:
- output: bfloat16 [8192, 1024], P('seq')
- grad_input: float32 [8192, 1024], P('seq')
- new_masters: float32 [4, 104, 32, 1024], P('tp', 'seq')
- new_first: float32 [4, 104, 32, 1024], P('tp', 'seq')
- new_second: float32 [4, 104, 32, 1024], P('tp', 'seq')
- new_average: float32 [4, 104, 32, 1024], P('tp', 'seq')
- new_statistics: float32 [4, 104, 32, 32], P('tp', 'seq')
- new_bases: float32 [4, 104, 32, 32], P('tp', 'seq')
- new_gains: float32 [2, 1024], replicated
- new_gain_first: float32 [2, 1024], replicated
- new_gain_second: float32 [2, 1024], replicated
Inputs may be any that keep to these rules, and one draw needn't show every extreme that they name: `owners`: the 98 panels name different slots, and slot 103 is always named. `second_moment`: positive. `statistics`: each slot's matrix is symmetric with a dominant positive diagonal. `bases`: each slot's matrix is orthogonal.
All inputs are finite; a program needn't handle non-finite values.
Results may differ from a plain program's by a relative error of at most 0.011.
Values may be sent and summed in bfloat16 or wider, within the bound.
No kernel may reach another device: no remote copies, remote signals or barrier semaphores. Data moves between devices by JAX's collectives and lax.ppermute only.
A program may use at most 256 MiB of HBM per device.

v0:
```python
import jax
import jax.numpy as jnp
from jax import lax
from jax.sharding import PartitionSpec as P

H = 8
HD = 128
FF = 2816
MEMB = 128
STEP = 10


EPSILON = 1e-06
RATE = 0.02
GAIN_RATE = 0.5
BETA_ONE = 0.9
BETA_TWO = 0.95
ADAM_EPSILON = 1e-08
WEIGHT_DECAY = 0.01
AVERAGE_DECAY = 0.8
NEGATIVE = -1e30


def document_of(positions, starts):
    return jnp.sum((positions[:, None] >= starts[None, :]).astype(jnp.int32), axis=1) - 1


def visible_mask(query_pos, key_pos, starts, recalled):
    query_doc = document_of(query_pos, starts)
    key_doc = document_of(key_pos, starts)
    member = jnp.any((key_pos // MEMB)[:, None] == recalled[None, :], axis=1)
    same_doc = (query_doc[:, None] == key_doc[None, :]) & (key_pos[None, :] <= query_pos[:, None])
    memory = (key_doc[None, :] < query_doc[:, None]) & member[None, :]
    return same_doc | memory


def orthonormal(matrix):
    columns = []
    for index in range(matrix.shape[-1]):
        vector = matrix[..., index]
        for previous in columns:
            vector = vector - jnp.sum(previous * vector, axis=-1, keepdims=True) * previous
        vector = vector * lax.rsqrt(jnp.sum(vector * vector, axis=-1, keepdims=True))
        columns.append(vector)
    return jnp.stack(columns, axis=-1)


def soap_step(gradient, weight, first_state, second, statistic, basis_old):
    high = lax.Precision.HIGHEST
    new_stat = BETA_TWO * statistic + (1.0 - BETA_TWO) * jnp.einsum(
        "spd,sqd->spq", gradient, gradient, precision=high
    )
    rotated = jnp.einsum("spq,spd->sqd", basis_old, gradient, precision=high)
    new_first = BETA_ONE * first_state + (1.0 - BETA_ONE) * rotated
    new_second = BETA_TWO * second + (1.0 - BETA_TWO) * rotated * rotated
    direction = (
        new_first
        / (1.0 - BETA_ONE**STEP)
        / (jnp.sqrt(new_second / (1.0 - BETA_TWO**STEP)) + ADAM_EPSILON)
    )
    update = jnp.einsum("spq,sqd->spd", basis_old, direction, precision=high)
    new_weight = weight - RATE * (update + WEIGHT_DECAY * weight)
    new_basis = orthonormal(jnp.einsum("spq,sqr->spr", new_stat, basis_old, precision=high))
    return (new_weight, new_first, new_second, new_stat, new_basis)


def adam_gain(gradient, weight, first_state, second):
    new_first = BETA_ONE * first_state + (1.0 - BETA_ONE) * gradient
    new_second = BETA_TWO * second + (1.0 - BETA_TWO) * gradient * gradient
    direction = (
        new_first
        / (1.0 - BETA_ONE**STEP)
        / (jnp.sqrt(new_second / (1.0 - BETA_TWO**STEP)) + ADAM_EPSILON)
    )
    return (weight - GAIN_RATE * direction, new_first, new_second)


def project(left, right):
    return lax.dot_general(
        left, right, (((1,), (1,)), ((), ())), preferred_element_type=jnp.float32
    )


def contract_rows(left, right):
    return lax.dot_general(
        left, right, (((0,), (0,)), ((), ())), preferred_element_type=jnp.float32
    )


def norm_back(grad_normed, unit_rows, inverse, gain_row):
    scaled = grad_normed * gain_row
    return inverse * (scaled - unit_rows * jnp.mean(scaled * unit_rows, axis=-1, keepdims=True))


def shards(
    tokens,
    cotangent,
    lengths,
    retrieve,
    owners,
    masters,
    first_moment,
    second_moment,
    averaged,
    statistics,
    bases,
    gains,
    gain_first,
    gain_second,
):
    tok_rows, width = tokens.shape
    seq_count = lax.axis_size("seq")
    seq_here = lax.axis_index("seq")
    tp_count = lax.axis_size("tp")
    heads_dev = H // tp_count
    ff_dev = FF // tp_count
    query_width = heads_dev * HD
    slots_dev = masters.shape[1]
    panel = masters.shape[2]
    total_keys = tok_rows * seq_count
    key_block = min(1024, total_keys)
    score_scale = HD ** (-0.5)
    starts = jnp.cumsum(lengths) - lengths
    recalled = lax.dynamic_index_in_dim(retrieve, seq_here, 0, keepdims=False)
    query_pos = seq_here * tok_rows + jnp.arange(tok_rows, dtype=jnp.int32)
    needed = (seq_here * tok_rows + tok_rows - 1) // key_block + 1
    gathered = lax.all_gather(masters[0].astype(jnp.bfloat16), "seq", axis=0, tiled=True)
    weight_rows = jnp.take(gathered, owners, axis=0).reshape(-1, width)
    w_query = weight_rows[:query_width]
    w_key = weight_rows[query_width : 2 * query_width]
    w_value = weight_rows[2 * query_width : 3 * query_width]
    w_out = weight_rows[3 * query_width : 4 * query_width]
    base_row = 4 * query_width
    w_gate = weight_rows[base_row : base_row + ff_dev]
    w_up = weight_rows[base_row + ff_dev : base_row + 2 * ff_dev]
    w_down = weight_rows[base_row + 2 * ff_dev : base_row + 3 * ff_dev]
    inputs = tokens.astype(jnp.float32)
    inverse_one = lax.rsqrt(jnp.mean(inputs * inputs, axis=-1, keepdims=True) + EPSILON)
    unit_one = inputs * inverse_one
    normed_one = (unit_one * gains[0]).astype(jnp.bfloat16)
    queries = project(normed_one, w_query).astype(jnp.bfloat16)
    key_rows = project(normed_one, w_key).astype(jnp.bfloat16)
    value_rows = project(normed_one, w_value).astype(jnp.bfloat16)
    queries_three = queries.reshape(tok_rows, heads_dev, HD)
    key_all, value_all = (
        lax.all_gather(key_rows, "seq", axis=0, tiled=True),
        lax.all_gather(value_rows, "seq", axis=0, tiled=True),
    )

    def block_of(rows_all, index):
        return lax.dynamic_slice_in_dim(rows_all, index * key_block, key_block, 0).reshape(
            key_block, heads_dev, HD
        )

    def masked_scores(key_part, start):
        visible = visible_mask(
            query_pos, start + jnp.arange(key_block, dtype=jnp.int32), starts, recalled
        )
        raw_scores = jnp.einsum(
            "qhd,khd->hqk", queries_three, key_part, preferred_element_type=jnp.float32
        )
        return (visible, jnp.where(visible[None], raw_scores * score_scale, NEGATIVE))

    def first_pass(index, carry):
        running_top, running_sum = carry
        visible, scores = masked_scores(block_of(key_all, index), index * key_block)
        new_top = jnp.maximum(running_top, jnp.max(scores, axis=-1))
        exps = jnp.where(visible[None], jnp.exp(scores - new_top[..., None]), 0.0)
        running_sum = running_sum * jnp.exp(running_top - new_top) + jnp.sum(exps, axis=-1)
        return (new_top, running_sum)

    start_top = jnp.full((heads_dev, tok_rows), NEGATIVE, jnp.float32)
    start_sum = jnp.zeros((heads_dev, tok_rows), jnp.float32)
    final_top, final_sum = lax.fori_loop(0, needed, first_pass, (start_top, start_sum))
    log_total = final_top + jnp.log(final_sum)

    def probabilities(index):
        visible, scores = masked_scores(block_of(key_all, index), index * key_block)
        return jnp.where(visible[None], jnp.exp(scores - log_total[..., None]), 0.0)

    def second_pass(index, carry):
        probs = probabilities(index)
        return carry + jnp.einsum(
            "hqk,khd->qhd",
            probs.astype(jnp.bfloat16),
            block_of(value_all, index),
            preferred_element_type=jnp.float32,
        )

    start_out = jnp.zeros((tok_rows, heads_dev, HD), jnp.float32)
    attended_f = lax.fori_loop(0, needed, second_pass, start_out)
    attended = attended_f.reshape(tok_rows, query_width).astype(jnp.bfloat16)
    branch = lax.psum(jnp.dot(attended, w_out, preferred_element_type=jnp.float32), "tp")
    mixed = inputs + branch
    inverse_two = lax.rsqrt(jnp.mean(mixed * mixed, axis=-1, keepdims=True) + EPSILON)
    unit_two = mixed * inverse_two
    normed_two = (unit_two * gains[1]).astype(jnp.bfloat16)
    gate = project(normed_two, w_gate)
    up_rows = project(normed_two, w_up)
    sigma = jax.nn.sigmoid(gate)
    silu_gate = gate * sigma
    hidden = (silu_gate * up_rows).astype(jnp.bfloat16)
    feed = lax.psum(jnp.dot(hidden, w_down, preferred_element_type=jnp.float32), "tp")
    output = (mixed + feed).astype(jnp.bfloat16)
    grad_out_rows = cotangent.astype(jnp.float32)
    d_hidden = project(cotangent, w_down)
    d_hidden = d_hidden.astype(jnp.bfloat16).astype(jnp.float32)
    grad_down = contract_rows(hidden, cotangent)
    slope = sigma * (1.0 + gate * (1.0 - sigma))
    d_gate = (d_hidden * up_rows * slope).astype(jnp.bfloat16)
    d_up = (d_hidden * silu_gate).astype(jnp.bfloat16)
    grad_gate = contract_rows(d_gate, normed_two)
    grad_up = contract_rows(d_up, normed_two)
    d_normed_two = jnp.dot(d_gate, w_gate, preferred_element_type=jnp.float32) + jnp.dot(
        d_up, w_up, preferred_element_type=jnp.float32
    )
    d_normed_two = lax.psum(d_normed_two, "tp")
    grad_gain_two = jnp.sum(d_normed_two * unit_two, axis=0)
    d_mixed = grad_out_rows + norm_back(d_normed_two, unit_two, inverse_two, gains[1])
    d_branch = d_mixed.astype(jnp.bfloat16)
    grad_wout = contract_rows(attended, d_branch)
    d_attended = project(d_branch, w_out).astype(jnp.bfloat16)
    d_attended_three = d_attended.reshape(tok_rows, heads_dev, HD)

    def delta_pass(index, carry):
        probs = probabilities(index)
        grad_probs = jnp.einsum(
            "qhd,khd->hqk",
            d_attended_three,
            block_of(value_all, index),
            preferred_element_type=jnp.float32,
        )
        return carry + jnp.sum(probs * grad_probs, axis=-1)

    start_delta = jnp.zeros((heads_dev, tok_rows), jnp.float32)
    delta = lax.fori_loop(0, needed, delta_pass, start_delta)

    def score_grads(index):
        probs = probabilities(index)
        grad_probs = jnp.einsum(
            "qhd,khd->hqk",
            d_attended_three,
            block_of(value_all, index),
            preferred_element_type=jnp.float32,
        )
        d_scores = (probs * (grad_probs - delta[..., None])).astype(jnp.bfloat16)
        return (probs, d_scores)

    start_query = jnp.zeros((tok_rows, heads_dev, HD), jnp.float32)

    def grad_pass(index, carry):
        query_sum, joined_buffer = carry
        probs, d_scores = score_grads(index)
        query_sum = query_sum + jnp.einsum(
            "hqk,khd->qhd", d_scores, block_of(key_all, index), preferred_element_type=jnp.float32
        )
        d_keys = (
            jnp.einsum("hqk,qhd->khd", d_scores, queries_three, preferred_element_type=jnp.float32)
            * score_scale
        )
        d_values = jnp.einsum(
            "hqk,qhd->khd",
            probs.astype(jnp.bfloat16),
            d_attended_three,
            preferred_element_type=jnp.float32,
        )
        joined = jnp.concatenate(
            [d_keys.reshape(key_block, query_width), d_values.reshape(key_block, query_width)],
            axis=1,
        )
        joined_buffer = lax.dynamic_update_slice_in_dim(joined_buffer, joined, index * key_block, 0)
        return (query_sum, joined_buffer)

    start_joined = jnp.zeros((total_keys, 2 * query_width), jnp.float32)
    d_query_f, joined_all = lax.fori_loop(0, needed, grad_pass, (start_query, start_joined))
    own_kv = lax.psum_scatter(joined_all, "seq", scatter_dimension=0, tiled=True)
    d_keys_own = own_kv[:, :query_width].astype(jnp.bfloat16)
    d_values_own = own_kv[:, query_width:].astype(jnp.bfloat16)
    d_queries = (d_query_f * score_scale).reshape(tok_rows, query_width).astype(jnp.bfloat16)
    grad_query = contract_rows(d_queries, normed_one)
    grad_key = contract_rows(d_keys_own, normed_one)
    grad_value = contract_rows(d_values_own, normed_one)
    d_normed_one = jnp.dot(d_queries, w_query, preferred_element_type=jnp.float32)
    d_normed_one = d_normed_one + jnp.dot(d_keys_own, w_key, preferred_element_type=jnp.float32)
    d_normed_one = d_normed_one + jnp.dot(d_values_own, w_value, preferred_element_type=jnp.float32)
    d_normed_one = lax.psum(d_normed_one, "tp")
    grad_gain_one = jnp.sum(d_normed_one * unit_one, axis=0)
    grad_input = d_mixed + norm_back(d_normed_one, unit_one, inverse_one, gains[0])
    grad_rows = jnp.concatenate(
        [grad_query, grad_key, grad_value, grad_wout, grad_gate, grad_up, grad_down], axis=0
    )
    slab = (
        jnp.zeros((slots_dev * seq_count, panel, width), jnp.float32)
        .at[owners]
        .set(grad_rows.reshape(-1, panel, width))
    )
    gain_grad = jnp.stack([grad_gain_one, grad_gain_two])
    own_grad = lax.psum_scatter(slab, "seq", scatter_dimension=0, tiled=True)
    gain_total = lax.psum(gain_grad, "seq")
    new_weight, new_first, new_second, new_stat, new_basis = soap_step(
        own_grad, masters[0], first_moment[0], second_moment[0], statistics[0], bases[0]
    )
    new_average = AVERAGE_DECAY * averaged[0] + (1.0 - AVERAGE_DECAY) * new_weight
    new_gains, new_gain_first, new_gain_second = adam_gain(
        gain_total, gains, gain_first, gain_second
    )
    return (
        output,
        grad_input,
        new_weight[None],
        new_first[None],
        new_second[None],
        new_average[None],
        new_stat[None],
        new_basis[None],
        new_gains,
        new_gain_first,
        new_gain_second,
    )


def solution(mesh):
    in_specs = (
        P("seq", None),
        P("seq", None),
        P(),
        P(),
        P(),
        P("tp", "seq", None, None),
        P("tp", "seq", None, None),
        P("tp", "seq", None, None),
        P("tp", "seq", None, None),
        P("tp", "seq", None, None),
        P("tp", "seq", None, None),
        P(),
        P(),
        P(),
    )
    out_specs = (
        P("seq", None),
        P("seq", None),
        P("tp", "seq", None, None),
        P("tp", "seq", None, None),
        P("tp", "seq", None, None),
        P("tp", "seq", None, None),
        P("tp", "seq", None, None),
        P("tp", "seq", None, None),
        P(),
        P(),
        P(),
    )
    return jax.shard_map(shards, mesh=mesh, in_specs=in_specs, out_specs=out_specs, check_vma=False)
```

profile of v0, /device:TPU:0, one launch (start us, length us, event | category | flops | bytes accessed | tf_op | source)
XLA Modules:
  0.0 1390.2 jit_solution(11115701763370091583)
XLA Ops:
  7.3 2.6 bitcast_convert_fusion
  13.7 47.3 %all-gather.4.cloned.1.call-done = bf16[104,32,1024]{2,1,0:T(8,128)(2,1)} async-done(((bf16[13,32,1024]{2,1,0:T(8,128)(2,1)}), bf16[104,32,1024]{2,1,0:T(8,128)(2,1)}) %all-gather.4.cloned.1.call-update) | async-done | bytes 6815760 | tf_op jit(solution)/shard_map/all_gather | solution.py:127
  61.0 9.0 gather_fusion
  70.0 3.5 broadcast_select_fusion
  73.4 2.7 copy-done.13
  84.1 3.2 convolution_convert_fusion.4
  87.4 29.3 %all-gather.8.cloned.1.call-done = bf16[8192,256]{1,0:T(8,128)(2,1)} async-done(((bf16[1024,256]{1,0:T(8,128)(2,1)}), bf16[8192,256]{1,0:T(8,128)(2,1)}) %all-gather.8.cloned.1.call-update) | async-done | bytes 4194320 | tf_op jit(solution)/shard_map/all_gather | solution.py:146
  116.7 6.4 copy.1991
  123.0 8.4 while.60
  126.2 3.0 fusion.682
  131.5 24.4 %all-gather.6.cloned.1.call-done = bf16[8192,256]{1,0:T(8,128)(2,1)} async-done(((bf16[1024,256]{1,0:T(8,128)(2,1)}), bf16[8192,256]{1,0:T(8,128)(2,1)}) %all-gather.6.cloned.1.call-update) | async-done | bytes 4194320 | tf_op jit(solution)/shard_map/all_gather | solution.py:147
  155.9 6.3 copy.1990
  163.3 10.9 while.61
  167.9 6.3 fusion.687
  176.3 3.8 fusion.591
  180.3 4.7 fusion.584
  186.0 2.8 convolution_convert_fusion
  188.8 254.0 %all-reduce.5.cloned.1.call-done = f32[1024,1024]{1,0:T(8,128)} async-done(((f32[1024,1024]{1,0:T(8,128)}), f32[1024,1024]{1,0:T(8,128)}) %all-reduce.5.cloned.1.call-update) | async-done | bytes 4194320 | tf_op jit(solution)/shard_map/psum | solution.py:193
  442.8 2.8 multiply_reduce_fusion.2
  450.0 3.8 fusion.67
  456.7 3.9 convolution_add_fusion
  460.8 153.9 %all-reduce.7.cloned.1.call-done = f32[1024,1024]{1,0:T(8,128)} async-done(((f32[1024,1024]{1,0:T(8,128)}), f32[1024,1024]{1,0:T(8,128)}) %all-reduce.7.cloned.1.call-update) | async-done | bytes 4194320 | tf_op jit(solution)/shard_map/psum | solution.py:217
  614.8 5.3 multiply_reduce_fusion
  625.1 8.1 while.62
  629.6 3.5 fusion.693
  633.3 7.8 broadcast_in_dim.211
  641.1 15.3 %while.63 = (s32[]{:T(128)}, f32[1024,2,128]{0,2,1:T(8,128)S(1)}, f32[8192,512]{0,1:T(8,128)}, s32[]{:T(128)}, bf16[8192,256]{0,1:T(8,128)(2,1)}, /*index=5*/s32...) while((s32[]{:T(128)}, f32[1024,2,128]{0,2,1:T(8,128)S(1)}, ...), condition=%wide.region_29.30_spmd.clone, body=%wide.region_25.29_spmd.clone.sunk | while | flops 2716942336 | bytes 55142692 | solution.py:275
  645.8 3.6 fusion.705
  650.4 3.1 fusion.707
  657.8 5.3 fusion.593
  664.0 2.7 fusion.595
  666.6 267.0 %reduce-scatter.3.cloned.1.call-done = f32[1024,512]{0,1:T(8,128)} async-done(((f32[8192,512]{0,1:T(8,128)}), f32[1024,512]{0,1:T(8,128)}) %reduce-scatter.3.cloned.1.call-update) | async-done | bytes 2097168 | tf_op jit(solution)/shard_map/reduce_scatter | solution.py:276
  937.7 2.9 add_add_fusion
  942.2 2.7 convolution_dynamic-update-slice_fusion.6
  950.0 3.2 convolution_dynamic-update-slice_fusion.2
  953.3 3.3 convolution_dynamic-update-slice_fusion.1
  956.6 3.3 convolution_dynamic-update-slice_fusion
  959.9 6.6 broadcast_in_dim.212
  966.6 27.3 %scatter_fusion = f32[104,32,1024]{2,1,0:T(8,128)} fusion(f32[104,32,1024]{2,1,0:T(8,128)} %broadcast_in_dim.212, s32[98]{0:T(128)S(1)} %copy-done.52, f32[98,32,1024]{2,1,0:T(8,128)} %bitcast.19), kind=kCustom, calls=%fused_computation.1 | custom fusion | bytes 38535560 | tf_op jit(solution)/shard_map/scatter | solution.py:295
  993.9 238.3 %all-reduce.9.cloned.1.call-done = (f32[1024,1024]{1,0:T(8,128)}, f32[1024,1024]{1,0:T(8,128)}) async-done(((f32[1024,1024]{1,0:T(8,128)}, f32[1024,1024]{1,0:T(8,128)}), (f32[1024,1024]{1,0:T(8,128)}, f32[1024,1024]{1,0:T(8,128)})) %all-reduce.9.cloned.1.call-update) | async-done | bytes 8388624 | tf_op jit(solution)/shard_map/psum | solution.py:203
  1232.3 3.3 fusion.64
  1235.7 13.9 %psum.39 = f32[2,1024]{1,0:T(2,128)S(1)} all-reduce(f32[2,1024]{1,0:T(2,128)S(1)} %pad_maximum_fusion), channel_id=1, replica_groups=mesh['seq'=8,'tp'=4] {'seq'}, use_global_device_ids=true, to_apply=%region_565.566 | all-reduce | flops 2048 | bytes 16384 | tf_op jit(solution)/shard_map/psum | solution.py:299
  1250.2 7.2 add_convert_fusion
  1258.7 2.8 fusion.63
  1261.6 71.2 %reduce-scatter.5.cloned.1.call-done = f32[13,32,1024]{2,1,0:T(8,128)} async-done(((f32[104,32,1024]{2,1,0:T(8,128)}), f32[13,32,1024]{2,1,0:T(8,128)}) %reduce-scatter.5.cloned.1.call-update) | async-done | bytes 1703952 | tf_op jit(solution)/shard_map/reduce_scatter | solution.py:298
  1332.8 3.7 fusion.83
  1374.0 6.0 fusion.73
  1380.0 3.0 fusion.96
  (400 shorter events, 103.0 us)
Async XLA Ops:
  7.2 1329.3 %copy-start = (f32[1,13,32,32]{3,2,1,0:T(8,128)S(1)}, f32[1,13,32,32]{3,2,1,0:T(8,128)}, u32[]{:S(2)}) copy-start(f32[1,13,32,32]{3,2,1,0:T(8,128)} %param.32) | copy-start | bytes 159748
  7.2 4.1 copy-start.8
  7.2 4.6 copy-start.46
  7.2 53.8 %all-gather.4.cloned.1.call-start = ((), (), s32[]{:S(2)}) async-start(), calls=%async_computation.2 | async-start | bytes 7667712 | tf_op jit(solution)/shard_map/all_gather | solution.py:127
  9.9 106.7 %all-gather.8.cloned.1.call-start = ((), (), s32[]{:S(2)}) async-start(), calls=%async_computation.4 | async-start | bytes 4718592 | tf_op jit(solution)/shard_map/all_gather | solution.py:146
  11.8 58.1 %copy-start.42 = (f32[1024]{0:T(1024)}, f32[1024]{0:T(1024)S(1)}, u32[]{:S(2)}) copy-start(f32[1024]{0:T(1024)S(1)} %add_rsqrt_fusion.1) | copy-start | bytes 12292
  11.8 58.1 %copy-start.44 = (f32[1,1024]{1,0:T(1,128)}, f32[1,1024]{1,0:T(1,128)S(1)}, u32[]{:S(2)}) copy-start(f32[1,1024]{1,0:T(1,128)S(1)} %get-tuple-element.2012) | copy-start | bytes 12292
  77.4 5.7 copy-start.26
  79.8 76.1 %all-gather.6.cloned.1.call-start = ((), (), s32[]{:S(2)}) async-start(), calls=%async_computation.3 | async-start | bytes 4718592 | tf_op jit(solution)/shard_map/all_gather | solution.py:147
  83.1 40.0 %copy-start.6 = (bf16[1024,256]{0,1:T(8,128)(2,1)}, bf16[1024,256]{0,1:T(8,128)(2,1)S(1)}, u32[]{:S(2)}) copy-start(bf16[1024,256]{0,1:T(8,128)(2,1)S(1)} %convolution_convert_fusion.2) | copy-start | bytes 1572868
  87.3 355.5 %all-reduce.5.cloned.1.call-start = ((), (), s32[]{:S(2)}) async-start(), calls=%async_computation.5 | async-start | bytes 8388608 | tf_op jit(solution)/shard_map/psum | solution.py:193
  180.2 434.6 %all-reduce.7.cloned.1.call-start = ((), (), s32[]{:S(2)}) async-start(), calls=%async_computation.6 | async-start | bytes 8388608 | tf_op jit(solution)/shard_map/psum | solution.py:217
  180.2 5.8 copy-start.28
  445.6 4.1 copy-start.1
  446.1 3.7 copy-start.22
  449.8 7.0 copy-start.54
  460.6 159.4 %copy-start.29 = (bf16[1024,1024]{1,0:T(8,128)(2,1)S(1)}, bf16[1024,1024]{1,0:T(8,128)(2,1)}, u32[]{:S(2)}) copy-start(bf16[1024,1024]{1,0:T(8,128)(2,1)} %param.23) | copy-start | bytes 6291460
  460.6 473.1 %reduce-scatter.3.cloned.1.call-start = ((), (), s32[]{:S(2)}) async-start(), calls=%async_computation.7 | async-start | bytes 18874368 | tf_op jit(solution)/shard_map/reduce_scatter | solution.py:276
  614.8 5.3 copy-start.2
  614.8 5.9 copy-start.16
  620.7 3.3 copy-start.21
  633.3 7.8 copy-start.7
  656.4 575.8 %all-reduce.9.cloned.1.call-start = ((), (), s32[]{:S(2)}) async-start(), calls=%async_computation.9 | async-start | bytes 16777216 | tf_op jit(solution)/shard_map/psum | solution.py:203
  657.8 6.2 copy-start.27
  663.9 271.5 %copy-start.25 = (bf16[8,32,1024]{2,1,0:T(8,128)(2,1)S(1)}, bf16[8,32,1024]{2,1,0:T(8,128)(2,1)}, u32[]{:S(2)}) copy-start(bf16[8,32,1024]{2,1,0:T(8,128)(2,1)} %copy-done.24) | copy-start | bytes 1572868
  940.6 392.2 %reduce-scatter.5.cloned.1.call-start = ((), (), s32[]{:S(2)}) async-start(), calls=%async_computation.8 | async-start | bytes 15335424 | tf_op jit(solution)/shard_map/reduce_scatter | solution.py:298
  944.9 3.4 copy-start.4
  944.9 3.4 copy-start.20
  946.6 3.4 copy-start.23
  946.6 3.4 copy-start.58
  953.3 3.3 copy-start.30
  953.3 3.3 copy-start.56
  959.9 6.6 copy-start.52
  993.8 238.4 %copy-start.9 = (bf16[1024,1024]{1,0:T(8,128)(2,1)S(1)}, bf16[1024,1024]{1,0:T(8,128)(2,1)}, u32[]{:S(2)}) copy-start(bf16[1024,1024]{1,0:T(8,128)(2,1)} %param.22) | copy-start | bytes 6291460
  993.8 238.4 %copy-start.43 = (f32[1024]{0:T(1024)S(1)}, f32[1024]{0:T(1024)}, u32[]{:S(2)}) copy-start(f32[1024]{0:T(1024)} %copy-done.42) | copy-start | bytes 12292
  993.9 238.4 %copy-start.45 = (f32[1,1024]{1,0:T(1,128)S(1)}, f32[1,1024]{1,0:T(1,128)}, u32[]{:S(2)}) copy-start(f32[1,1024]{1,0:T(1,128)} %copy-done.44) | copy-start | bytes 12292
  993.9 241.7 %copy-start.48 = (f32[1024]{0:T(1024)S(1)}, f32[1024]{0:T(1024)}, u32[]{:S(2)}) copy-start(f32[1024]{0:T(1024)} %get-tuple-element.1064) | copy-start | bytes 12292
  993.9 255.7 %copy-start.47 = (f32[2,1024]{1,0:T(2,128)S(1)}, f32[2,1024]{1,0:T(2,128)}, u32[]{:S(2)}) copy-start(f32[2,1024]{1,0:T(2,128)} %param.33) | copy-start | bytes 24580
  993.9 255.7 %copy-start.49 = (f32[2,1024]{1,0:T(2,128)S(1)}, f32[2,1024]{1,0:T(2,128)}, u32[]{:S(2)}) copy-start(f32[2,1024]{1,0:T(2,128)} %param.34) | copy-start | bytes 24580
  993.9 255.7 %copy-start.50 = (f32[2,1024]{1,0:T(2,128)S(1)}, f32[2,1024]{1,0:T(2,128)}, u32[]{:S(2)}) copy-start(f32[2,1024]{1,0:T(2,128)} %param.35) | copy-start | bytes 24580
  1250.2 7.2 copy-start.5
  1250.2 8.5 copy-start.15
  1258.7 74.1 %copy-start.41 = (f32[1,13,32,32]{3,2,1,0:T(8,128)S(1)}, f32[1,13,32,32]{3,2,1,0:T(8,128)}, u32[]{:S(2)}) copy-start(f32[1,13,32,32]{3,2,1,0:T(8,128)} %param.31) | copy-start | bytes 159748
  1336.5 17.9 %copy-start.40 = (f32[13,32,32]{2,1,0:T(8,128)}, f32[13,32,32]{2,1,0:T(8,128)S(1)}, u32[]{:S(2)}) copy-start(f32[13,32,32]{2,1,0:T(8,128)S(1)} %fusion.83) | copy-start | bytes 159748
  1353.7 18.6 %copy-start.17 = (f32[13,32,1024]{2,1,0:T(8,128)S(1)}, f32[13,32,1024]{2,1,0:T(8,128)}, u32[]{:S(2)}) copy-start(f32[13,32,1024]{2,1,0:T(8,128)} %reduce-scatter.5.cloned.1.call-done) | copy-start | bytes 5111812
  1373.9 6.0 copy-start.32
  1373.9 6.0 copy-start.33
  1374.0 6.0 copy-start.34
  (21 other events, 38.6 us)
Sparse Core Ops, SparseCore 0:
  10.5 50.4 all-gather.3
  79.9 36.7 all-gather.7
  119.1 36.7 all-gather.5
  180.3 262.4 all-reduce.4
  460.7 153.9 all-reduce.6
  656.6 277.0 reduce-scatter.2
  940.7 291.4 all-reduce.8
  1235.8 96.9 reduce-scatter.4
where the time goes:
time: 1410 us; the launch traced here: 1390 us
  waiting for transfers between devices  1090 us (77%)
  local copies, waits for them, and re-layouts  97.3 us (7%)
  matrix products  91.2 us (6%)
  other arithmetic  84.5 us (6%)
  between operations  15.9 us (1%)
    reduce_scatter x1, waiting for transfers between devices, shards(): lax.psum_scatter(joined_all, 'seq', scatter_dimension=0, tiled=True)  267 us
    psum x1, waiting for transfers between devices, shards(): lax.psum(jnp.dot(attended, w_out, preferred_element_type=jnp.float32), 'tp')  254 us
    psum x1, waiting for transfers between devices, shards(): lax.psum(jnp.dot(hidden, w_down, preferred_element_type=jnp.float32), 'tp')  238 us
    psum x1, waiting for transfers between devices, shards(): d_normed_two = lax.psum(d_normed_two, 'tp')  154 us
    reduce_scatter x1, waiting for transfers between devices, shards(): own_grad = lax.psum_scatter(slab, 'seq', scatter_dimension=0, tiled=True)  71.2 us
    all_gather x1, waiting for transfers between devices, shards(): lax.all_gather(masters[0].astype(jnp.bfloat16), 'seq', axis=0, tiled=True)  47.3 us
    unnamed x127, local copies, waits for them, and re-layouts  32.4 us
    all_gather x1, waiting for transfers between devices, shards(): lax.all_gather(key_rows, 'seq', axis=0, tiled=True)  29.3 us
  transfers between devices with their start and end apart: 8, of which 8 were waited for; matrix products, arithmetic and copies ran while one was open for 8% of the time, Pallas kernels for 0%

commit v1 on v0

v1 whole, which is shorter than its diff:
```python
import functools

import jax
import jax.numpy as jnp
from jax import lax
from jax.experimental import pallas as pl
from jax.experimental.pallas import tpu as pltpu
from jax.sharding import PartitionSpec as P

H = 8
HD = 128
FF = 2816
MEMB = 128
STEP = 10

EPSILON = 1e-06
RATE = 0.02
GAIN_RATE = 0.5
BETA_ONE = 0.9
BETA_TWO = 0.95
ADAM_EPSILON = 1e-08
WEIGHT_DECAY = 0.01
AVERAGE_DECAY = 0.8
NEGATIVE = -1e30
START_TOP = -1e29
LOG2E = 1.4426950408889634

BF = jnp.bfloat16
F32 = jnp.float32
I32 = jnp.int32
HIGH = lax.Precision.HIGHEST
ANY = pl.BlockSpec(memory_space=pl.ANY)
SMEM = pl.BlockSpec(memory_space=pltpu.SMEM)
VMEM = pl.BlockSpec(memory_space=pltpu.VMEM)
VMEM_BYTES = 58 * 2**20

NT = (((1,), (1,)), ((), ()))
NN = (((1,), (0,)), ((), ()))
TN = (((0,), (0,)), ((), ()))


def mm(left, right, dims):
    return lax.dot_general(left, right, dims, preferred_element_type=F32)


def params(**more):
    return pltpu.CompilerParams(vmem_limit_bytes=VMEM_BYTES, **more)


def cost(flops, moved, exps=0):
    return pl.CostEstimate(flops=int(flops), bytes_accessed=int(moved), transcendentals=int(exps))


def routes(count):
    bits = []
    bit = 2
    while bit < count:
        bits.append(bit)
        bit *= 2
    return bits, bits[::-1]


def swap(value, count, bit):
    return lax.ppermute(value, "seq", [(i, i ^ bit) for i in range(count)])


def gather_seq(own, count, order):
    pieces = {0: own}
    for bit in [*order, 1]:
        pieces.update({m | bit: swap(p, count, bit) for m, p in pieces.items()})
    return [pieces[m] for m in range(count)]


def plus(left, right):
    return (left.astype(F32) + right.astype(F32)).astype(left.dtype)


def reduce_seq(parts, count, order):
    parts = dict(enumerate(parts))
    bits = [1, *order[::-1]]
    for at, bit in enumerate(bits):
        stay = [m for m in parts if not m & bit]
        came = {m: swap(parts[m | bit], count, bit) for m in stay}
        if at == len(bits) - 1:
            return parts[0], came[0]
        parts = {m: plus(parts[m], came[m]) for m in stay}
    return None


def ring(value, count, step):
    return lax.ppermute(value, "tp", [(i, (i + step) % count) for i in range(count)])


def gather_tp(own, count):
    pieces = [own]
    for _ in range(count - 1):
        pieces.append(ring(pieces[-1], count, 1))
    return pieces


def reduce_tp(parts, count):
    total = parts[count - 1]
    for k in range(count - 2, -1, -1):
        came = ring(total, count, -1)
        if k == 0:
            return parts[0], came
        total = plus(parts[k], came)
    return None


def sum_all(value, n_seq, n_tp):
    for axis, count in (("seq", n_seq), ("tp", n_tp)):
        bit = 1
        while bit < count:
            value = value + lax.ppermute(value, axis, [(i, i ^ bit) for i in range(count)])
            bit *= 2
    return value


def panel_copies(owners_ref, me, first, amount, slots_dev, split, pieces, view, sem, back):
    def one(i, carry):
        slot = owners_ref[first + i]
        spot = lax.bitwise_xor(slot // slots_dev, me)
        row = slot % slots_dev
        for m, (low, high) in enumerate(pieces):
            for ref, base, size in ((low, 0, split), (high, split, slots_dev - split)):

                @pl.when((spot == m) & (row >= base) & (row < base + size))
                def _(ref=ref, base=base):
                    there = ref.at[row - base]
                    source, target = (view(i), there) if back else (there, view(i))
                    pltpu.make_async_copy(source, target, sem).start()

        return carry

    lax.fori_loop(0, amount, one, 0)


def norm_rows(rows, gain):
    inverse = lax.rsqrt(jnp.mean(rows * rows, axis=-1, keepdims=True) + EPSILON)
    unit = rows * inverse
    return unit, inverse, unit * gain


def project_kernel(cfg, meta, owners, x_ref, gain_ref, *refs):
    n, qw, slots_dev, split, panel = cfg
    low, high = refs[:n], refs[n : 2 * n]
    q_ref, k_ref, v_ref, normed_ref, w_ref, sem = refs[2 * n :]
    amount = 3 * qw // panel

    @pl.when(pl.program_id(0) == 0)
    def _():
        panel_copies(
            owners, meta[0], 0, amount, slots_dev, split, list(zip(low, high, strict=True)),
            lambda i: w_ref.at[i], sem, False,
        )

    _, _, normed = norm_rows(x_ref[...].astype(F32), gain_ref[0:1, :])
    normed = normed.astype(BF)
    normed_ref[...] = normed

    @pl.when(pl.program_id(0) == 0)
    def _():
        pltpu.make_async_copy(w_ref, w_ref, sem).wait()

    for at, out in enumerate((q_ref, k_ref, v_ref)):
        w = w_ref[at * qw // panel : (at + 1) * qw // panel].reshape(qw, x_ref.shape[1])
        out[...] = mm(normed, w, NT).astype(BF)


def project_in(meta, owners, x, gains, pieces, qw, slots_dev, split, panel):
    n = len(pieces)
    tok, d = x.shape
    tile = 256
    out = lambda w: pl.BlockSpec((tile, w), lambda i: (i, 0))
    return pl.pallas_call(
        functools.partial(project_kernel, (n, qw, slots_dev, split, panel)),
        grid=(tok // tile,),
        in_specs=[SMEM, SMEM, out(d), pl.BlockSpec(gains.shape, lambda i: (0, 0))] + [ANY] * (2 * n),
        out_specs=[out(qw), out(qw), out(qw), out(d)],
        out_shape=[jax.ShapeDtypeStruct((tok, qw), BF)] * 3 + [jax.ShapeDtypeStruct((tok, d), BF)],
        scratch_shapes=[pltpu.VMEM((3 * qw // panel, panel, d), BF), pltpu.SemaphoreType.DMA],
        compiler_params=params(),
        cost_estimate=cost(6 * tok * d * qw, 4 * tok * d + 6 * qw * (tok + d)),
        name="project",
    )(meta, owners, x, gains, *[p[0] for p in pieces], *[p[1] for p in pieces])


def weights_kernel(cfg, meta, owners, *refs):
    n, sizes, slots_dev, split = cfg
    pieces = list(zip(refs[:n], refs[n : 2 * n], strict=True))
    outs, sem = refs[2 * n : -1], refs[-1]
    first = 0
    for out, size in zip(outs, sizes, strict=True):
        panel_copies(
            owners, meta[0], first, size, slots_dev, split, pieces,
            lambda i, out=out: out.at[i], sem.at[0], False,
        )
        first += size
    for out in outs:
        pltpu.make_async_copy(out, out, sem.at[0]).wait()


def order_weights(meta, owners, pieces, sizes, slots_dev, split):
    n = len(pieces)
    panel, d = pieces[0][0].shape[1:]
    got = pl.pallas_call(
        functools.partial(weights_kernel, (n, sizes, slots_dev, split)),
        in_specs=[SMEM, SMEM] + [ANY] * (2 * n),
        out_specs=[VMEM] * len(sizes),
        out_shape=[jax.ShapeDtypeStruct((s, panel, d), BF) for s in sizes],
        scratch_shapes=[pltpu.SemaphoreType.DMA((1,))],
        compiler_params=params(),
        cost_estimate=cost(0, 4 * sum(sizes) * panel * d),
        name="order_weights",
    )(meta, owners, *[p[0] for p in pieces], *[p[1] for p in pieces])
    return [g.reshape(-1, d) for g in got]


def doc_start(meta, positions, docs):
    start = jnp.int32(0)
    found = jnp.zeros_like(positions)
    for at in range(docs):
        found = jnp.where(positions >= start, start, found)
        start = start + meta[1 + at]
    return found


def load_pieces(me, pieces, buffer, sem, tok):
    for m, piece in enumerate(pieces):
        owner = lax.bitwise_xor(me, m)
        at = pl.multiple_of(owner * tok, tok)
        pltpu.make_async_copy(piece, buffer.at[pl.ds(at, tok)], sem).start()


def member_table(meta, table, docs, picks, blocks):
    def clear(i, c):
        table[i] = 0
        return c

    lax.fori_loop(0, blocks, clear, 0)
    for e in range(picks):
        table[meta[1 + docs + e]] = 1


def memory_list(meta, blocks_ref, docs, picks, limit):
    count = jnp.int32(0)
    for e in range(picks):
        block = meta[1 + docs + e]
        fresh = (block + 1) * MEMB <= limit
        for other in range(e):
            fresh = fresh & (meta[1 + docs + other] != block)

        @pl.when(fresh)
        def _(count=count, block=block):
            blocks_ref[count] = block

        count = count + fresh.astype(I32)
    return count


def hide(scores, at, table, starts, queries, fill):
    rows = scores.shape[0]
    row = lax.broadcasted_iota(I32, (MEMB, scores.shape[1]), 0)
    kept = []
    for b in range(rows // MEMB):
        base = at + b * MEMB
        lowest = starts * (1 - table[base // MEMB]) - base
        seen = (row >= lowest) & (row <= queries - base)
        kept.append(jnp.where(seen, scores[b * MEMB : (b + 1) * MEMB], fill))
    return jnp.concatenate(kept, axis=0)


def attend_kernel(cfg, meta, q_ref, *refs):
    n, docs, picks, qt, kt = cfg
    keys, values = refs[:n], refs[n : 2 * n]
    out_ref, wide_ref, log_ref, kbuf, vbuf, acc, table, blocks, sems = refs[2 * n :]
    tok, width = q_ref.shape
    me = meta[0]
    factor = HD**-0.5 * LOG2E
    load_pieces(me, keys, kbuf, sems.at[0], tok)
    load_pieces(me, values, vbuf, sems.at[1], tok)
    member_table(meta, table, docs, picks, kbuf.shape[0] // MEMB)
    pltpu.make_async_copy(kbuf, kbuf, sems.at[0]).wait()
    pltpu.make_async_copy(vbuf, vbuf, sems.at[1]).wait()
    for head in range(width // HD):
        cols = slice(head * HD, (head + 1) * HD)

        def query_tile(t, carry, head=head, cols=cols):
            base = pl.multiple_of(t * qt, qt)
            first = me * tok + base
            queries = first + lax.broadcasted_iota(I32, (1, qt), 1)
            starts = doc_start(meta, queries, docs)
            low_tile = doc_start(meta, first, docs) // kt
            high_tile = (first + qt - 1) // kt
            q = q_ref[pl.ds(base, qt), cols]
            acc[...] = jnp.zeros_like(acc)

            def visit(at, rows, state, masked):
                top, total = state
                scores = mm(kbuf[pl.ds(at, rows), cols], q, NT)
                if masked:
                    scores = hide(scores, at, table, starts, queries, NEGATIVE)
                new_top = jnp.maximum(top, jnp.max(scores, axis=0, keepdims=True))
                fade = jnp.exp2((top - new_top) * factor)
                probs = jnp.exp2((scores - new_top) * factor)
                total = total * fade + jnp.sum(probs, axis=0, keepdims=True)
                acc[...] = acc[...] * fade + mm(vbuf[pl.ds(at, rows), cols], probs.astype(BF), TN)
                return new_top, total

            def dense(i, state):
                return visit(pl.multiple_of(i * kt, kt), kt, state, True)

            def memory(i, state):
                return visit(pl.multiple_of(blocks[i] * MEMB, MEMB), MEMB, state, False)

            count = memory_list(meta, blocks, docs, picks, low_tile * kt)
            state = (jnp.full((1, qt), START_TOP, F32), jnp.zeros((1, qt), F32))
            state = lax.fori_loop(low_tile, high_tile + 1, dense, state)
            top, total = lax.fori_loop(0, count, memory, state)
            rows = jnp.transpose(acc[...] * (1.0 / total))
            wide_ref[pl.ds(base, qt), cols] = rows
            out_ref[pl.ds(base, qt), cols] = rows.astype(BF)
            log_ref[head : head + 1, pl.ds(base, qt)] = top * factor + jnp.log2(total)
            return carry

        lax.fori_loop(0, tok // qt, query_tile, 0)


def attend(meta, q, keys, values, docs, picks):
    n = len(keys)
    tok, width = q.shape
    qt, kt = 512, 512
    return pl.pallas_call(
        functools.partial(attend_kernel, (n, docs, picks, qt, kt)),
        in_specs=[SMEM, VMEM] + [ANY] * (2 * n),
        out_specs=[VMEM] * 3,
        out_shape=[
            jax.ShapeDtypeStruct((tok, width), BF),
            jax.ShapeDtypeStruct((tok, width), F32),
            jax.ShapeDtypeStruct((width // HD, tok), F32),
        ],
        scratch_shapes=[
            pltpu.VMEM((n * tok, width), BF),
            pltpu.VMEM((n * tok, width), BF),
            pltpu.VMEM((HD, qt), F32),
            pltpu.SMEM((n * tok // MEMB,), I32),
            pltpu.SMEM((picks,), I32),
            pltpu.SemaphoreType.DMA((2,)),
        ],
        compiler_params=params(),
        cost_estimate=cost(4 * tok * n * tok * width // 2, 4 * n * tok * width, tok * n * tok),
        name="attend",
    )(meta, q, *keys, *values)


def attend_back_kernel(cfg, meta, q_ref, g_ref, wide_ref, log_ref, *refs):
    n, docs, picks, qt, kt = cfg
    keys, values = refs[:n], refs[n : 2 * n]
    dq_ref = refs[2 * n]
    dk_out, dv_out = refs[2 * n + 1 : 3 * n + 1], refs[3 * n + 1 : 4 * n + 1]
    kbuf, vbuf, dk_acc, dv_acc, acc, stage, table, blocks, sems = refs[4 * n + 1 :]
    tok, width = q_ref.shape
    me = meta[0]
    scale = HD**-0.5
    factor = scale * LOG2E
    load_pieces(me, keys, kbuf, sems.at[0], tok)
    load_pieces(me, values, vbuf, sems.at[1], tok)
    member_table(meta, table, docs, picks, kbuf.shape[0] // MEMB)

    def clear(i, c):
        at = pl.ds(pl.multiple_of(i * 256, 256), 256)
        dk_acc[at, :] = jnp.zeros((256, width), F32)
        dv_acc[at, :] = jnp.zeros((256, width), F32)
        return c

    lax.fori_loop(0, kbuf.shape[0] // 256, clear, 0)
    pltpu.make_async_copy(kbuf, kbuf, sems.at[0]).wait()
    pltpu.make_async_copy(vbuf, vbuf, sems.at[1]).wait()
    for head in range(width // HD):
        cols = slice(head * HD, (head + 1) * HD)

        def query_tile(t, carry, head=head, cols=cols):
            base = pl.multiple_of(t * qt, qt)
            first = me * tok + base
            queries = first + lax.broadcasted_iota(I32, (1, qt), 1)
            starts = doc_start(meta, queries, docs)
            low_tile = doc_start(meta, first, docs) // kt
            high_tile = (first + qt - 1) // kt
            q = q_ref[pl.ds(base, qt), cols]
            grad = g_ref[pl.ds(base, qt), cols]
            logs = log_ref[head : head + 1, pl.ds(base, qt)]
            product = grad.astype(F32) * wide_ref[pl.ds(base, qt), cols]
            delta = jnp.sum(jnp.transpose(product), axis=0, keepdims=True)
            acc[...] = jnp.zeros_like(acc)

            def visit(at, rows, masked):
                here = pl.ds(at, rows)
                k = kbuf[here, cols]
                probs = jnp.exp2(mm(k, q, NT) * factor - logs)
                if masked:
                    probs = hide(probs, at, table, starts, queries, 0.0)
                slopes = probs * (mm(vbuf[here, cols], grad, NT) - delta)
                slopes = slopes.astype(BF)
                dv_acc[here, cols] += mm(probs.astype(BF), grad, NN)
                dk_acc[here, cols] += mm(slopes, q, NN)
                acc[...] += mm(k, slopes, TN)

            def dense(i, c):
                visit(pl.multiple_of(i * kt, kt), kt, True)
                return c

            def memory(i, c):
                visit(pl.multiple_of(blocks[i] * MEMB, MEMB), MEMB, False)
                return c

            count = memory_list(meta, blocks, docs, picks, low_tile * kt)
            lax.fori_loop(low_tile, high_tile + 1, dense, 0)
            lax.fori_loop(0, count, memory, 0)
            dq_ref[pl.ds(base, qt), cols] = (jnp.transpose(acc[...]) * scale).astype(BF)
            return carry

        lax.fori_loop(0, tok // qt, query_tile, 0)

    def put(slot, m):
        which, out = (0, dk_out[m]) if slot == 0 else (1, dv_out[m])
        return pltpu.make_async_copy(stage.at[which], out, sems.at[2 + which])

    for m in range(n):
        at = pl.ds(pl.multiple_of(lax.bitwise_xor(me, m) * tok, tok), tok)
        for which in range(2):
            if m:
                put(which, m - 1).wait()
            rows = dk_acc[at, :] * scale if which == 0 else dv_acc[at, :]
            stage[which] = rows.astype(BF)
            put(which, m).start()
    for which in range(2):
        put(which, n - 1).wait()


def attend_back(meta, q, grad, wide, logs, keys, values, docs, picks):
    n = len(keys)
    tok, width = q.shape
    qt, kt = 512, 512
    got = pl.pallas_call(
        functools.partial(attend_back_kernel, (n, docs, picks, qt, kt)),
        in_specs=[SMEM] + [VMEM] * 4 + [ANY] * (2 * n),
        out_specs=[VMEM] + [ANY] * (2 * n),
        out_shape=[jax.ShapeDtypeStruct((tok, width), BF)] * (2 * n + 1),
        scratch_shapes=[
            pltpu.VMEM((n * tok, width), BF),
            pltpu.VMEM((n * tok, width), BF),
            pltpu.VMEM((n * tok, width), F32),
            pltpu.VMEM((n * tok, width), F32),
            pltpu.VMEM((HD, qt), F32),
            pltpu.VMEM((2, tok, width), BF),
            pltpu.SMEM((n * tok // MEMB,), I32),
            pltpu.SMEM((picks,), I32),
            pltpu.SemaphoreType.DMA((4,)),
        ],
        compiler_params=params(),
        cost_estimate=cost(10 * tok * n * tok * width // 2, 8 * n * tok * width, tok * n * tok),
        name="attend_back",
    )(meta, q, grad, wide, logs, *keys, *values)
    return got[0], got[1 : n + 1], got[n + 1 :]


def feed_kernel(cfg, meta, x_ref, g_ref, gain_ref, wg, wu, wd, *refs):
    n = cfg
    heads, wo = refs[:n], refs[n : 2 * n]
    mixed_ref, normed_ref, hidden_ref, dgate_ref, dup_ref, back_ref, feed_ref = refs[2 * n :]
    mixed = x_ref[...].astype(F32)
    for a, w in zip(heads, wo, strict=True):
        mixed = mixed + mm(a[...], w[...], NN)
    mixed_ref[...] = mixed
    _, _, normed = norm_rows(mixed, gain_ref[1:2, :])
    normed = normed.astype(BF)
    normed_ref[...] = normed
    gate = mm(normed, wg[...], NT)
    up = mm(normed, wu[...], NT)
    sigma = jax.nn.sigmoid(gate)
    silu = gate * sigma
    hidden = (silu * up).astype(BF)
    hidden_ref[...] = hidden
    grad = g_ref[...]
    d_hidden = mm(grad, wd[...], NT).astype(BF).astype(F32)
    d_gate = (d_hidden * up * (sigma * (1.0 + gate * (1.0 - sigma)))).astype(BF)
    d_up = (d_hidden * silu).astype(BF)
    dgate_ref[...] = d_gate
    dup_ref[...] = d_up
    back_ref[...] = (mm(d_gate, wg[...], NN) + mm(d_up, wu[...], NN)).astype(BF)
    feed_ref[...] = mm(hidden, wd[...], NN).astype(BF)


def feed_forward(meta, x, grad, gains, wg, wu, wd, heads, wo):
    n = len(heads)
    tok, d = x.shape
    ff, qw = wg.shape[0], wo[0].shape[0]
    tile = tok // n
    rows = lambda w: pl.BlockSpec((tile, w), lambda i, meta: (i, 0))
    turned = lambda w: pl.BlockSpec((tile, w), lambda i, meta: ((meta[0] - i + n) % n, 0))
    whole = lambda a: pl.BlockSpec(a.shape, lambda i, meta: (0, 0))
    shape = lambda w, t: jax.ShapeDtypeStruct((tok, w), t)
    return pl.pallas_call(
        functools.partial(feed_kernel, n),
        grid_spec=pltpu.PrefetchScalarGridSpec(
            num_scalar_prefetch=1,
            grid=(n,),
            in_specs=[rows(d), rows(d), whole(gains), whole(wg), whole(wu), whole(wd)]
            + [rows(qw)] * n + [whole(w) for w in wo],
            out_specs=[rows(d), rows(d), rows(ff), rows(ff), rows(ff), turned(d), turned(d)],
        ),
        out_shape=[shape(d, F32), shape(d, BF), shape(ff, BF), shape(ff, BF), shape(ff, BF), shape(d, BF), shape(d, BF)],
        compiler_params=params(),
        cost_estimate=cost(2 * tok * d * (6 * ff + n * qw), 20 * tok * d, tok * ff),
        name="feed_forward",
    )(meta, x, grad, gains, wg, wu, wd, *heads, *wo)


def place_kernel(n, meta, *refs):
    pieces, out = refs[:n], refs[n]
    rows = pieces[0].shape[0]
    for k, piece in enumerate(pieces):
        block = lax.rem(meta[0] - k + n, n)
        out[pl.ds(pl.multiple_of(block * rows, rows), rows), :] = piece[...].astype(out.dtype)


def place(meta, pieces, kind=BF):
    n = len(pieces)
    rows, d = pieces[0].shape
    return pl.pallas_call(
        functools.partial(place_kernel, n),
        in_specs=[SMEM] + [VMEM] * n,
        out_specs=VMEM,
        out_shape=jax.ShapeDtypeStruct((n * rows, d), kind),
        compiler_params=params(),
        cost_estimate=cost(0, 6 * n * rows * d),
        name="place",
    )(meta, *pieces)


def norm_back(grad_normed, unit_rows, inverse, gain_row):
    scaled = grad_normed * gain_row
    return inverse * (scaled - unit_rows * jnp.mean(scaled * unit_rows, axis=-1, keepdims=True))


def slots_kernel(cfg, meta, owners, *refs):
    n, sizes, slots_dev, split, panel = cfg
    count = len(sizes)
    lefts, rights = refs[:count], refs[count : 2 * count]
    low, high = refs[2 * count : 2 * count + n], refs[2 * count + n : 2 * count + 2 * n]
    stage, zero, named, sem, zero_sem = refs[2 * count + 2 * n :]
    pieces = list(zip(low, high, strict=True))
    me = meta[0]
    panels = sum(sizes)

    def clear(i, c):
        named[i] = 0
        return c

    lax.fori_loop(0, n * slots_dev, clear, 0)

    def mark(i, c):
        named[owners[i]] = 1
        return c

    lax.fori_loop(0, panels, mark, 0)
    zero[...] = jnp.zeros_like(zero)

    def blank(i, c):
        spot = lax.bitwise_xor(i // slots_dev, me)
        row = i % slots_dev
        for m, (a, b) in enumerate(pieces):
            for ref, base, size in ((a, 0, split), (b, split, slots_dev - split)):

                @pl.when((named[i] == 0) & (spot == m) & (row >= base) & (row < base + size))
                def _(ref=ref, base=base):
                    pltpu.make_async_copy(zero, ref.at[row - base], zero_sem).start()

        return c

    lax.fori_loop(0, n * slots_dev, blank, 0)
    first = 0
    for left, right, size in zip(lefts, rights, sizes, strict=True):
        product = mm(left[...], right[...], TN).astype(BF)
        stage[first : first + size] = product.reshape(size, panel, right.shape[1])
        panel_copies(
            owners, me, first, size, slots_dev, split, pieces,
            lambda i, first=first: stage.at[first + i], sem, True,
        )
        first += size
    pltpu.make_async_copy(stage, stage, sem).wait()

    def finish(i, c):
        @pl.when(named[i] == 0)
        def _():
            pltpu.make_async_copy(zero, zero, zero_sem).wait()

        return c

    lax.fori_loop(0, n * slots_dev, finish, 0)


def grads_to_slots(meta, owners, lefts, rights, n, slots_dev, split, panel):
    sizes = tuple(a.shape[1] // panel for a in lefts)
    tok, d = rights[0].shape
    count = len(lefts)
    shape = lambda s: jax.ShapeDtypeStruct((s, panel, d), BF)
    got = pl.pallas_call(
        functools.partial(slots_kernel, (n, sizes, slots_dev, split, panel)),
        in_specs=[SMEM, SMEM] + [VMEM] * (2 * count),
        out_specs=[ANY] * (2 * n),
        out_shape=[shape(split)] * n + [shape(slots_dev - split)] * n,
        scratch_shapes=[
            pltpu.VMEM((sum(sizes), panel, d), BF),
            pltpu.VMEM((panel, d), BF),
            pltpu.SMEM((n * slots_dev,), I32),
            pltpu.SemaphoreType.DMA,
            pltpu.SemaphoreType.DMA,
        ],
        compiler_params=params(),
        cost_estimate=cost(2 * tok * d * sum(sizes) * panel, 4 * sum(sizes) * panel * d + 4 * tok * d),
        name="grads_to_slots",
    )(meta, owners, *lefts, *rights)
    return got[:n], got[n:]


def soap_kernel(g1, g2, weight_ref, first_ref, second_ref, average_ref, stat_ref, basis_ref,
                weight_out, first_out, second_out, average_out, stat_out, turned_out):
    high = functools.partial(lax.dot_general, precision=HIGH, preferred_element_type=F32)
    grad = g1[0].astype(F32) + g2[0].astype(F32)
    basis = basis_ref[0]
    stat = BETA_TWO * stat_ref[0] + (1.0 - BETA_TWO) * high(grad, grad, NT)
    stat_out[0] = stat
    turned_out[0] = high(stat, basis, NN)
    rotated = high(basis, grad, TN)
    first = BETA_ONE * first_ref[0] + (1.0 - BETA_ONE) * rotated
    second = BETA_TWO * second_ref[0] + (1.0 - BETA_TWO) * rotated * rotated
    first_out[0] = first
    second_out[0] = second
    direction = (first / (1.0 - BETA_ONE**STEP)) / (
        jnp.sqrt(second / (1.0 - BETA_TWO**STEP)) + ADAM_EPSILON
    )
    weight = weight_ref[0]
    new_weight = weight - RATE * (high(basis, direction, NN) + WEIGHT_DECAY * weight)
    weight_out[0] = new_weight
    average_out[0] = AVERAGE_DECAY * average_ref[0] + (1.0 - AVERAGE_DECAY) * new_weight


def soap(g1, g2, weight, first, second, average, stat, basis):
    slots, panel, d = weight.shape
    big = pl.BlockSpec((1, panel, d), lambda i: (i, 0, 0))
    small = pl.BlockSpec((1, panel, panel), lambda i: (i, 0, 0))
    shape = jax.ShapeDtypeStruct
    return pl.pallas_call(
        soap_kernel,
        grid=(slots,),
        in_specs=[big] * 6 + [small] * 2,
        out_specs=[big] * 4 + [small] * 2,
        out_shape=[shape((slots, panel, d), F32)] * 4 + [shape((slots, panel, panel), F32)] * 2,
        compiler_params=params(),
        cost_estimate=cost(36 * slots * panel * panel * d, 40 * slots * panel * d),
        name="soap",
    )(g1, g2, weight, first, second, average, stat, basis)


def orthonormal_kernel(columns_ref, out_ref):
    size = columns_ref.shape[0]
    columns = columns_ref[...]
    index = lax.broadcasted_iota(I32, columns.shape, 0)
    out_ref[...] = columns

    def step(i, c):
        vector = out_ref[i]
        vector = vector * lax.rsqrt(jnp.sum(vector * vector, axis=0, keepdims=True))
        rest = out_ref[...]
        share = jnp.sum(rest * vector[None], axis=1, keepdims=True)
        rest = jnp.where(index > i, rest - share * vector[None], rest)
        out_ref[...] = rest
        out_ref[i] = vector
        return c

    lax.fori_loop(0, size, step, 0)


def orthonormal(matrix):
    columns = jnp.transpose(matrix, (2, 1, 0))
    found = pl.pallas_call(
        orthonormal_kernel,
        in_specs=[VMEM],
        out_specs=VMEM,
        out_shape=jax.ShapeDtypeStruct(columns.shape, F32),
        compiler_params=params(),
        name="orthonormal",
    )(columns)
    return jnp.transpose(found, (2, 1, 0))


def adam_gain(gradient, weight, first_state, second):
    new_first = BETA_ONE * first_state + (1.0 - BETA_ONE) * gradient
    new_second = BETA_TWO * second + (1.0 - BETA_TWO) * gradient * gradient
    direction = (
        new_first
        / (1.0 - BETA_ONE**STEP)
        / (jnp.sqrt(new_second / (1.0 - BETA_TWO**STEP)) + ADAM_EPSILON)
    )
    return (weight - GAIN_RATE * direction, new_first, new_second)


def back_kernel(cfg, meta, dq, dk, dv, wq, wk, wv, out):
    out[...] = (mm(dq[...], wq[...], NN) + mm(dk[...], wk[...], NN) + mm(dv[...], wv[...], NN)).astype(BF)


def back_in(meta, dq, dk, dv, wq, wk, wv, n):
    tok, qw = dq.shape
    d = wq.shape[1]
    tile = tok // n
    rows = pl.BlockSpec((tile, qw), lambda i, meta: (i, 0))
    whole = pl.BlockSpec((qw, d), lambda i, meta: (0, 0))
    return pl.pallas_call(
        functools.partial(back_kernel, n),
        grid_spec=pltpu.PrefetchScalarGridSpec(
            num_scalar_prefetch=1,
            grid=(n,),
            in_specs=[rows] * 3 + [whole] * 3,
            out_specs=pl.BlockSpec((tile, d), lambda i, meta: ((meta[0] - i + n) % n, 0)),
        ),
        out_shape=jax.ShapeDtypeStruct((tok, d), BF),
        compiler_params=params(),
        cost_estimate=cost(6 * tok * d * qw, 6 * qw * (tok + d) + 2 * tok * d),
        name="back_in",
    )(meta, dq, dk, dv, wq, wk, wv)


def shards(
    tokens,
    cotangent,
    lengths,
    retrieve,
    owners,
    masters,
    first_moment,
    second_moment,
    averaged,
    statistics,
    bases,
    gains,
    gain_first,
    gain_second,
):
    tok, d = tokens.shape
    n_seq, n_tp = lax.axis_size("seq"), lax.axis_size("tp")
    me, z = lax.axis_index("seq"), lax.axis_index("tp")
    qw, ff = H // n_tp * HD, FF // n_tp
    slots_dev, panel = masters.shape[1:3]
    split = (slots_dev + 1) // 2
    docs, picks = lengths.shape[0], retrieve.shape[1]
    recalled = lax.dynamic_index_in_dim(retrieve, me, 0, keepdims=False)
    meta = jnp.concatenate([me.astype(I32).reshape(1), lengths, recalled])
    place_meta = z.astype(I32).reshape(1)
    forth, back = routes(n_seq)
    block = tok // n_tp

    own = masters[0].astype(BF)
    low = gather_seq(own[:split], n_seq, forth)
    high = gather_seq(own[split:], n_seq, back)
    pieces = list(zip(low, high, strict=True))
    q, k, v, normed_one = project_in(meta, owners, tokens, gains, pieces, qw, slots_dev, split, panel)
    keys = gather_seq(k, n_seq, forth)
    values = gather_seq(v, n_seq, back)
    sizes = tuple(s // panel for s in (qw, qw, qw, qw, ff, ff, ff))
    wq, wk, wv, wo, wg, wu, wd = order_weights(meta, owners, pieces, sizes, slots_dev, split)
    wo_all = gather_tp(wo, n_tp)
    attended, wide, logs = attend(meta, q, keys, values, docs, picks)
    heads = gather_tp(attended, n_tp)
    mixed, normed_two, hidden, d_gate, d_up, back_two, feed = feed_forward(
        place_meta, tokens, cotangent, gains, wg, wu, wd, heads, wo_all
    )

    def turned(rows):
        return [rows[i * block : (i + 1) * block] for i in range(n_tp)]

    def mine(rows):
        return lax.dynamic_slice_in_dim(rows, z * block, block, 0)

    a, b = reduce_tp(turned(back_two), n_tp)
    d_normed_two = a.astype(F32) + b.astype(F32)
    mixed_here = mine(mixed)
    unit_two, inverse_two, _ = norm_rows(mixed_here, gains[1])
    grad_gain_two = jnp.sum(d_normed_two * unit_two, axis=0)
    d_mixed = mine(cotangent).astype(F32) + norm_back(d_normed_two, unit_two, inverse_two, gains[1])
    d_branch = place(place_meta, gather_tp(d_mixed.astype(BF), n_tp))
    d_attended = mm(d_branch, wo, NT).astype(BF)
    dq, dk_parts, dv_parts = attend_back(meta, q, d_attended, wide, logs, keys, values, docs, picks)

    a, b = reduce_tp(turned(feed), n_tp)
    out_here = (mixed_here + a.astype(F32) + b.astype(F32)).astype(BF)
    output = place(place_meta, gather_tp(out_here, n_tp))

    dk = plus(*reduce_seq(dk_parts, n_seq, forth))
    dv = plus(*reduce_seq(dv_parts, n_seq, back))

    low, high = grads_to_slots(
        meta,
        owners,
        [dq, dk, dv, attended, d_gate, d_up, hidden],
        [normed_one, normed_one, normed_one, d_branch, normed_two, normed_two, cotangent],
        n_seq, slots_dev, split, panel,
    )
    low_pair = reduce_seq(low, n_seq, forth)
    high_pair = reduce_seq(high, n_seq, back)

    back_one = back_in(place_meta, dq, dk, dv, wq, wk, wv, n_tp)
    a, b = reduce_tp(turned(back_one), n_tp)
    d_normed_one = a.astype(F32) + b.astype(F32)
    unit_one, inverse_one, _ = norm_rows(mine(tokens).astype(F32), gains[0])
    grad_gain_one = jnp.sum(d_normed_one * unit_one, axis=0)
    grad_here = d_mixed + norm_back(d_normed_one, unit_one, inverse_one, gains[0])
    grad_input = place(place_meta, gather_tp(grad_here.astype(BF), n_tp), F32)

    gain_total = sum_all(jnp.stack([grad_gain_one, grad_gain_two]), n_seq, n_tp)
    new_gains, new_gain_first, new_gain_second = adam_gain(gain_total, gains, gain_first, gain_second)

    g1 = jnp.concatenate([low_pair[0], high_pair[0]], axis=0)
    g2 = jnp.concatenate([low_pair[1], high_pair[1]], axis=0)
    new_weight, new_first, new_second, new_average, new_stat, turned_basis = soap(
        g1, g2, masters[0], first_moment[0], second_moment[0], averaged[0], statistics[0], bases[0]
    )
    new_basis = orthonormal(turned_basis)
    return (
        output,
        grad_input,
        new_weight[None],
        new_first[None],
        new_second[None],
        new_average[None],
        new_stat[None],
        new_basis[None],
        new_gains,
        new_gain_first,
        new_gain_second,
    )


def solution(mesh):
    by_token, by_slot = P("seq", None), P("tp", "seq", None, None)
    in_specs = (by_token, by_token, P(), P(), P()) + (by_slot,) * 6 + (P(),) * 3
    out_specs = (by_token, by_token) + (by_slot,) * 6 + (P(),) * 3
    return jax.shard_map(shards, mesh=mesh, in_specs=in_specs, out_specs=out_specs, check_vma=False)
```

time: 1410 us -> 576 us (0.41); the launches traced: 1390 us -> 580 us
  waiting for transfers between devices: 1090 us -> 299 us
  Pallas kernels: 0 us -> 136 us
  starting transfers between devices: 0.91 us -> 98.9 us
  matrix products: 91.2 us -> 3.13 us
  local copies, waits for them, and re-layouts: 97.3 us -> 13.6 us
  other arithmetic: 84.5 us -> 27.2 us
  between operations: 15.9 us -> 1.68 us
    psum x3 -> x0, waiting for transfers between devices: 646 us -> none  [the longest x1 254 us: shards(): lax.psum(jnp.dot(attended, w_out, preferred_element_type=jnp.float32), 'tp')]
    reduce_scatter x2 -> x0, waiting for transfers between devices: 338 us -> none  [the longest x1 267 us: shards(): lax.psum_scatter(joined_all, 'seq', scatter_dimension=0, tiled=True)]
    ppermute x0 -> x85, waiting for transfers between devices: none -> 299 us  [the longest x24 174 us: ring(): lax.ppermute(value, 'tp', [(i, (i + step) % count) for i in range(count)])]
    pallas_call x0 -> x12, Pallas kernels: none -> 136 us  [the longest x1 29.5 us: grads_to_slots(): pl.pallas_call(functools.partial(slots_kernel, (n, sizes, slots_dev, spli...]
    all_gather x3 -> x0, waiting for transfers between devices: 101 us -> none  [the longest x1 47.3 us: shards(): lax.all_gather(masters[0].astype(jnp.bfloat16), 'seq', axis=0, tiled=True)]
    ppermute x0 -> x85, starting transfers between devices: none -> 98.9 us  [the longest x56 72.4 us: swap(): return lax.ppermute(value, 'seq', [(i, i ^ bit) for i in range(count)])]
    dot_general x34 -> x1, matrix products: 91.2 us -> 3.13 us  [mm(): return lax.dot_general(left, right, dims, preferred_element_type=F32)]
    reduce_sum x96 -> x2, other arithmetic: 31.8 us -> 1.56 us  [norm_rows(): inverse = lax.rsqrt(jnp.mean(rows * rows, axis=-1, keepdims=True) + EPSILON)]
  transfers between devices with their start and end apart: 8 -> 85, of which waited for: 8 -> 42; matrix products, arithmetic and copies ran while one was open for 8% -> 6% of each run, Pallas kernels for 0% -> 18%
where the time goes in v1:
time: 576 us; the launch traced here: 580 us
  waiting for transfers between devices  299 us (52%)
  Pallas kernels  136 us (24%)
  starting transfers between devices  98.9 us (17%)
  other arithmetic  27.2 us (5%)
  local copies, waits for them, and re-layouts  13.6 us (2%)
    ppermute x24, waiting for transfers between devices, ring(): lax.ppermute(value, 'tp', [(i, (i + step) % count) for i in range(count)])  174 us
    ppermute x56, waiting for transfers between devices, swap(): return lax.ppermute(value, 'seq', [(i, i ^ bit) for i in range(count)])  114 us
    ppermute x56, starting transfers between devices, swap(): return lax.ppermute(value, 'seq', [(i, i ^ bit) for i in range(count)])  72.4 us
    pallas_call x1, Pallas kernels, grads_to_slots(): pl.pallas_call(functools.partial(slots_kernel, (n, sizes, slots_dev, spli...  29.5 us
    pallas_call x1, Pallas kernels, attend_back(): pl.pallas_call(functools.partial(attend_back_kernel, (n, docs, picks, qt,...  20.4 us
    pallas_call x1, Pallas kernels, feed_forward(): pl.pallas_call(functools.partial(feed_kernel, n), grid_spec=pltpu.Prefetc...  20.3 us
    ppermute x24, starting transfers between devices, ring(): lax.ppermute(value, 'tp', [(i, (i + step) % count) for i in range(count)])  19 us
    convert_element_type x22, other arithmetic, plus(): return (left.astype(F32) + right.astype(F32)).astype(left.dtype)  16 us
  transfers between devices with their start and end apart: 85, of which 42 were waited for; matrix products, arithmetic and copies ran while one was open for 6% of the time, Pallas kernels for 18%

profile of v1, /device:TPU:0, one launch (start us, length us, event | category | flops | bytes accessed | tf_op | source)
XLA Modules:
  0.0 579.6 jit_solution(17343652052997238991)
XLA Ops:
  2.3 3.0 collective-permute-start.1
  7.6 9.9 %collective-permute-done.10.refs_12_ = bf16[6,32,1024]{2,1,0:T(8,128)(2,1)S(1)} collective-permute-done((bf16[6,32,1024]{2,1,0:T(8,128)(2,1)S(1)}, bf16[6,32,1024]{2,1,0:T(8,128)(2,1)S(1)}, u32[]{:S(2)}, u32[]{:S(2)}) %collective-permute-start.10) | collective-permute-done | bytes 393248 | tf_op jit(solution)/shard_map/ppermute | solution.py:64
  19.1 5.3 collective-permute-done.8.refs_10_
  27.8 7.8 %collective-permute-done.5.refs_6_ = bf16[7,32,1024]{2,1,0:T(8,128)(2,1)S(1)} collective-permute-done((bf16[7,32,1024]{2,1,0:T(8,128)(2,1)S(1)}, bf16[7,32,1024]{2,1,0:T(8,128)(2,1)S(1)}, u32[]{:S(2)}, u32[]{:S(2)}) %collective-permute-start.5) | collective-permute-done | bytes 458784 | tf_op jit(solution)/shard_map/ppermute | solution.py:64
  39.2 7.4 %project.1 = (bf16[1024,256]{1,0:T(8,128)(2,1)}, bf16[1024,256]{1,0:T(8,128)(2,1)}, bf16[1024,256]{1,0:T(8,128)(2,1)}, bf16[1024,1024]{1,0:T(8,128)(2,1)}) custom-call(s32[17]{0:T(128)} %pad_add_fusion.meta, s32[98]{0:T(128)} %owners.5, bf16[1024,1024]{1,0:T(8,128)(2,1)} %x_ref.3, f32[2,1024]{1,0:T(2,128)} %gain_ref.3, bf16[7,32,1024]{2,1,0:T(8,128)(2,1)} %copy-done.3, ...), custom_call_target="tpu_custom_call" | custom-call | flops 1610612736 | bytes 7340032 | tf_op jit(solution)/shard_map/project/pallas_call | solution.py:176
  50.7 10.9 %collective-permute-done.15.refs_2_ = bf16[1024,256]{1,0:T(8,128)(2,1)S(1)} collective-permute-done((bf16[1024,256]{1,0:T(8,128)(2,1)}, bf16[1024,256]{1,0:T(8,128)(2,1)S(1)}, u32[]{:S(2)}, u32[]{:S(2)}) %collective-permute-start.15) | collective-permute-done | bytes 524320 | tf_op jit(solution)/shard_map/ppermute | solution.py:64
  63.7 9.5 %collective-permute-done.17.refs_4_ = bf16[1024,256]{1,0:T(8,128)(2,1)S(1)} collective-permute-done((bf16[1024,256]{1,0:T(8,128)(2,1)}, bf16[1024,256]{1,0:T(8,128)(2,1)S(1)}, u32[]{:S(2)}, u32[]{:S(2)}) %collective-permute-start.17) | collective-permute-done | bytes 524320 | tf_op jit(solution)/shard_map/ppermute | solution.py:64
  75.5 7.8 %collective-permute-done.19.refs_6_ = bf16[1024,256]{1,0:T(8,128)(2,1)S(1)} collective-permute-done((bf16[1024,256]{1,0:T(8,128)(2,1)S(1)}, bf16[1024,256]{1,0:T(8,128)(2,1)S(1)}, u32[]{:S(2)}, u32[]{:S(2)}) %collective-permute-start.19) | collective-permute-done | bytes 524320 | tf_op jit(solution)/shard_map/ppermute | solution.py:64
  85.5 9.0 %order_weights.1 = (bf16[8,32,1024]{2,1,0:T(8,128)(2,1)}, bf16[8,32,1024]{2,1,0:T(8,128)(2,1)}, bf16[8,32,1024]{2,1,0:T(8,128)(2,1)}, bf16[8,32,1024]{2,1,0:T(8,...) custom-call(s32[17]{0:T(128)} %pad_add_fusion.meta, ...), custom_call_target="tpu_custom_call" | custom-call | bytes 12845056 | tf_op jit(solution)/shard_map/order_weights/pallas_call | solution.py:207
  97.2 11.5 %attend.1 = (bf16[1024,256]{1,0:T(8,128)(2,1)}, f32[1024,256]{1,0:T(8,128)}, f32[2,1024]{1,0:T(2,128)}) custom-call(s32[17]{0:T(128)} %pad_add_fusion.meta, bf16[1024,256]{1,0:T(8,128)(2,1)} %get-tuple-element.74.q_ref, bf16[1024,256]{1,0:T(8,128)(2,1)} %get-tuple-element.75.refs_0_, bf16[1024,256]{1,0:T(8,128)(2,1)} %copy-done.47, ...), custom_call_target="tpu_custom_call" | custom-call | flops 4294967296 | bytes 8388608 | tf_op jit(solution)/shard_map/attend/pallas_call | solution.py:334
  112.0 11.4 %collective-permute-done.28.refs_1_ = bf16[1024,256]{1,0:T(8,128)(2,1)S(1)} collective-permute-done((bf16[1024,256]{1,0:T(8,128)(2,1)}, bf16[1024,256]{1,0:T(8,128)(2,1)S(1)}, u32[]{:S(2)}, u32[]{:S(2)}) %collective-permute-start.28) | collective-permute-done | bytes 524320 | tf_op jit(solution)/shard_map/ppermute | solution.py:91
  123.4 11.2 %collective-permute-done.32.refs_6_ = bf16[256,1024]{1,0:T(8,128)(2,1)S(1)} collective-permute-done((bf16[256,1024]{1,0:T(8,128)(2,1)S(1)}, bf16[256,1024]{1,0:T(8,128)(2,1)S(1)}, u32[]{:S(2)}, u32[]{:S(2)}) %collective-permute-start.32) | collective-permute-done | bytes 524320 | tf_op jit(solution)/shard_map/ppermute | solution.py:91
  134.6 11.2 %collective-permute-done.29.refs_2_ = bf16[1024,256]{1,0:T(8,128)(2,1)S(1)} collective-permute-done((bf16[1024,256]{1,0:T(8,128)(2,1)S(1)}, bf16[1024,256]{1,0:T(8,128)(2,1)S(1)}, u32[]{:S(2)}, u32[]{:S(2)}) %collective-permute-start.29) | collective-permute-done | bytes 524320 | tf_op jit(solution)/shard_map/ppermute | solution.py:91
  145.9 11.2 %collective-permute-done.33.refs_7_ = bf16[256,1024]{1,0:T(8,128)(2,1)S(1)} collective-permute-done((bf16[256,1024]{1,0:T(8,128)(2,1)S(1)}, bf16[256,1024]{1,0:T(8,128)(2,1)S(1)}, u32[]{:S(2)}, u32[]{:S(2)}) %collective-permute-start.33) | collective-permute-done | bytes 524320 | tf_op jit(solution)/shard_map/ppermute | solution.py:91
  157.1 11.3 %collective-permute-done.30.refs_3_ = bf16[1024,256]{1,0:T(8,128)(2,1)} collective-permute-done((bf16[1024,256]{1,0:T(8,128)(2,1)S(1)}, bf16[1024,256]{1,0:T(8,128)(2,1)}, u32[]{:S(2)}, u32[]{:S(2)}) %collective-permute-start.30) | collective-permute-done | bytes 524320 | tf_op jit(solution)/shard_map/ppermute | solution.py:91
  168.5 20.3 %feed_forward.1 = (f32[1024,1024]{1,0:T(8,128)}, bf16[1024,1024]{1,0:T(8,128)(2,1)}, bf16[1024,704]{1,0:T(8,128)(2,1)}, bf16[1024,704]{1,0:T(8,128)(2,1)}, bf16[...) custom-call(s32[1]{0:T(128)} %bitcast.meta, bf16[1024,1024]{1,0:T(8,128)(2,1)} %x_ref.3, ...), custom_call_target="tpu_custom_call" | custom-call | flops 11005853696 | bytes 20971520 | tf_op jit(solution)/shard_map/feed_forward/pallas_call | solution.py:504
  193.4 10.3 %collective-permute-done.40 = bf16[256,1024]{1,0:T(8,128)(2,1)S(1)} collective-permute-done((bf16[256,1024]{1,0:T(8,128)(2,1)S(1)}, bf16[256,1024]{1,0:T(8,128)(2,1)S(1)}, u32[]{:S(2)}, u32[]{:S(2)}) %collective-permute-start.40) | collective-permute-done | bytes 524320 | tf_op jit(solution)/shard_map/ppermute | solution.py:91
  205.6 9.4 %collective-permute-done.34 = bf16[256,1024]{1,0:T(8,128)(2,1)S(1)} collective-permute-done((bf16[256,1024]{1,0:T(8,128)(2,1)S(1)}, bf16[256,1024]{1,0:T(8,128)(2,1)S(1)}, u32[]{:S(2)}, u32[]{:S(2)}) %collective-permute-start.34) | collective-permute-done | bytes 524320 | tf_op jit(solution)/shard_map/ppermute | solution.py:91
  218.6 7.6 %collective-permute-done.41 = bf16[256,1024]{1,0:T(8,128)(2,1)S(1)} collective-permute-done((bf16[256,1024]{1,0:T(8,128)(2,1)S(1)}, bf16[256,1024]{1,0:T(8,128)(2,1)S(1)}, u32[]{:S(2)}, u32[]{:S(2)}) %collective-permute-start.41) | collective-permute-done | bytes 524320 | tf_op jit(solution)/shard_map/ppermute | solution.py:91
  229.5 8.1 %collective-permute-done.35 = bf16[256,1024]{1,0:T(8,128)(2,1)} collective-permute-done((bf16[256,1024]{1,0:T(8,128)(2,1)}, bf16[256,1024]{1,0:T(8,128)(2,1)}, u32[]{:S(2)}, u32[]{:S(2)}) %collective-permute-start.35) | collective-permute-done | bytes 524320 | tf_op jit(solution)/shard_map/ppermute | solution.py:91
  240.8 7.9 %collective-permute-done.42 = bf16[256,1024]{1,0:T(8,128)(2,1)S(1)} collective-permute-done((bf16[256,1024]{1,0:T(8,128)(2,1)S(1)}, bf16[256,1024]{1,0:T(8,128)(2,1)S(1)}, u32[]{:S(2)}, u32[]{:S(2)}) %collective-permute-start.42) | collective-permute-done | bytes 524320 | tf_op jit(solution)/shard_map/ppermute | solution.py:91
  250.3 9.6 %collective-permute-done.36 = bf16[256,1024]{1,0:T(8,128)(2,1)S(1)} collective-permute-done((bf16[256,1024]{1,0:T(8,128)(2,1)S(1)}, bf16[256,1024]{1,0:T(8,128)(2,1)S(1)}, u32[]{:S(2)}, u32[]{:S(2)}) %collective-permute-start.36) | collective-permute-done | bytes 524320 | tf_op jit(solution)/shard_map/ppermute | solution.py:91
  262.1 16.6 %collective-permute-done.43.refs_1_ = bf16[256,1024]{1,0:T(8,128)(2,1)S(1)} collective-permute-done((bf16[256,1024]{1,0:T(8,128)(2,1)S(1)}, bf16[256,1024]{1,0:T(8,128)(2,1)S(1)}, u32[]{:S(2)}, u32[]{:S(2)}) %collective-permute-start.43) | collective-permute-done | bytes 524320 | tf_op jit(solution)/shard_map/ppermute | solution.py:91
  278.7 15.7 %collective-permute-done.44.refs_2_ = bf16[256,1024]{1,0:T(8,128)(2,1)S(1)} collective-permute-done((bf16[256,1024]{1,0:T(8,128)(2,1)S(1)}, bf16[256,1024]{1,0:T(8,128)(2,1)S(1)}, u32[]{:S(2)}, u32[]{:S(2)}) %collective-permute-start.44) | collective-permute-done | bytes 524320 | tf_op jit(solution)/shard_map/ppermute | solution.py:91
  294.4 16.6 %collective-permute-done.45.refs_3_ = bf16[256,1024]{1,0:T(8,128)(2,1)S(1)} collective-permute-done((bf16[256,1024]{1,0:T(8,128)(2,1)S(1)}, bf16[256,1024]{1,0:T(8,128)(2,1)S(1)}, u32[]{:S(2)}, u32[]{:S(2)}) %collective-permute-start.45) | collective-permute-done | bytes 524320 | tf_op jit(solution)/shard_map/ppermute | solution.py:91
  311.9 3.0 place.4.refs_10_
  314.8 3.1 convolution_convert_fusion.g_ref
  318.0 20.4 %attend_back.1 = (bf16[1024,256]{1,0:T(8,128)(2,1)}, bf16[1024,256]{1,0:T(8,128)(2,1)}, bf16[1024,256]{1,0:T(8,128)(2,1)}, bf16[1024,256]{1,0:T(8,128)(2,1)}, bf...) custom-call(s32[17]{0:T(128)} %pad_add_fusion.meta, ...), custom_call_target="tpu_custom_call" | custom-call | flops 10737418240 | bytes 16777216 | tf_op jit(solution)/shard_map/attend_back/pallas_call | solution.py:445
  342.0 3.0 collective-permute-start.58
  347.1 10.2 %collective-permute-done.58 = bf16[1024,256]{1,0:T(8,128)(2,1)S(1)} collective-permute-done((bf16[1024,256]{1,0:T(8,128)(2,1)S(1)}, bf16[1024,256]{1,0:T(8,128)(2,1)S(1)}, u32[]{:S(2)}, u32[]{:S(2)}) %collective-permute-start.58) | collective-permute-done | bytes 524320 | tf_op jit(solution)/shard_map/ppermute | solution.py:64
  357.3 37.6 %collective-permute-start.51 = (bf16[1024,256]{1,0:T(8,128)(2,1)S(1)}, bf16[1024,256]{1,0:T(8,128)(2,1)S(1)}, u32[]{:S(2)}, u32[]{:S(2)}) collective-permute-start(bf16[1024,256]{1,0:T(8,128)(2,1)S(1)} %add_convert_fusion.11), channel_id=1, source_target_pairs={{0,16},{4,20},{8,24},{12,28},{16,0},{20,4},{24,8},{28,12},{1,17},{... | collective-permute-start | bytes 1572872 | tf_op jit(solution)/shard_map/ppermute | solution.py:64
  395.7 12.1 %collective-permute-done.51 = bf16[1024,256]{1,0:T(8,128)(2,1)S(1)} collective-permute-done((bf16[1024,256]{1,0:T(8,128)(2,1)S(1)}, bf16[1024,256]{1,0:T(8,128)(2,1)S(1)}, u32[]{:S(2)}, u32[]{:S(2)}) %collective-permute-start.51) | collective-permute-done | bytes 524320 | tf_op jit(solution)/shard_map/ppermute | solution.py:64
  410.6 8.4 %collective-permute-done.59 = bf16[1024,256]{1,0:T(8,128)(2,1)S(1)} collective-permute-done((bf16[1024,256]{1,0:T(8,128)(2,1)S(1)}, bf16[1024,256]{1,0:T(8,128)(2,1)S(1)}, u32[]{:S(2)}, u32[]{:S(2)}) %collective-permute-start.59) | collective-permute-done | bytes 524320 | tf_op jit(solution)/shard_map/ppermute | solution.py:64
  420.1 8.7 %collective-permute-done.48 = bf16[1024,256]{1,0:T(8,128)(2,1)S(1)} collective-permute-done((bf16[1024,256]{1,0:T(8,128)(2,1)S(1)}, bf16[1024,256]{1,0:T(8,128)(2,1)S(1)}, u32[]{:S(2)}, u32[]{:S(2)}) %collective-permute-start.48) | collective-permute-done | bytes 524320 | tf_op jit(solution)/shard_map/ppermute | solution.py:64
  429.9 5.4 back_in.1
  440.1 29.5 %grads_to_slots.1 = (bf16[7,32,1024]{2,1,0:T(8,128)(2,1)}, bf16[7,32,1024]{2,1,0:T(8,128)(2,1)}, bf16[7,32,1024]{2,1,0:T(8,128)(2,1)}, bf16[7,32,1024]{2,1,0:T(8...) custom-call(s32[17]{0:T(128)} %pad_add_fusion.meta, ...), custom_call_target="tpu_custom_call" | custom-call | flops 6576668672 | bytes 17039360 | tf_op jit(solution)/shard_map/grads_to_slots/pallas_call | solution.py:609
  479.5 6.9 %collective-permute-done.61 = bf16[256,1024]{1,0:T(8,128)(2,1)} collective-permute-done((bf16[256,1024]{1,0:T(8,128)(2,1)}, bf16[256,1024]{1,0:T(8,128)(2,1)}, u32[]{:S(2)}, u32[]{:S(2)}) %collective-permute-start.61) | collective-permute-done | bytes 524320 | tf_op jit(solution)/shard_map/ppermute | solution.py:91
  491.4 5.3 collective-permute-done.78
  497.5 3.6 collective-permute-done.62
  508.0 6.5 %collective-permute-done.74 = bf16[7,32,1024]{2,1,0:T(8,128)(2,1)S(1)} collective-permute-done((bf16[7,32,1024]{2,1,0:T(8,128)(2,1)S(1)}, bf16[7,32,1024]{2,1,0:T(8,128)(2,1)S(1)}, u32[]{:S(2)}, u32[]{:S(2)}) %collective-permute-start.74) | collective-permute-done | bytes 458784 | tf_op jit(solution)/shard_map/ppermute | solution.py:64
  519.8 4.6 collective-permute-done.68
  524.6 3.9 collective-permute-done.81
  530.3 3.0 collective-permute-done.64.refs_2_
  535.8 7.1 %collective-permute-done.83 = f32[2,1024]{1,0:T(2,128)S(1)} collective-permute-done((f32[2,1024]{1,0:T(2,128)S(1)}, f32[2,1024]{1,0:T(2,128)S(1)}, u32[]{:S(2)}, u32[]{:S(2)}) %collective-permute-start.83) | collective-permute-done | bytes 8224 | tf_op jit(solution)/shard_map/ppermute | solution.py:115
  542.9 4.6 collective-permute-start.84
  547.5 15.7 %soap.1 = (f32[13,32,1024]{2,1,0:T(8,128)}, f32[13,32,1024]{2,1,0:T(8,128)}, f32[13,32,1024]{2,1,0:T(8,128)}, f32[13,32,1024]{2,1,0:T(8,128)}, f32[13,32,32]{2,1,0:T(8,128)}, /*index=5*/f32[13,32,32]{2,1,0:T(8,128)}) custom-call(bf16[13,32,1024]{2,1,0:T(8,128)(2,1)} %pad_maximum_fusion.g1, bf16[13,32,1024]{2,1,0:T(8,128)(2,1)} %pad_maximum_fusion.1.g2, ...), custom_call_target="tpu_custom_call" | custom-call | flops 490733568 | bytes 17039360 | tf_op jit(solution)/shard_map/soap/pallas_call | solution.py:655
  565.4 6.8 %orthonormal.1 = f32[32,32,13]{2,1,0:T(8,128)} custom-call(f32[32,32,13]{2,1,0:T(8,128)} %bitcast.34), custom_call_target="tpu_custom_call" | custom-call | tf_op jit(solution)/shard_map/orthonormal/pallas_call | solution.py:688
  575.8 3.8 place.5
  (316 shorter events, 104.4 us)
Async XLA Ops:
  2.3 15.2 %collective-permute-start.1 = (bf16[7,32,1024]{2,1,0:T(8,128)(2,1)S(1)}, bf16[7,32,1024]{2,1,0:T(8,128)(2,1)S(1)}, u32[]{:S(2)}, u32[]{:S(2)}) collective-permute-start(bf16[7,32,1024]{2,1,0:T(8,128)(2,1)S(1)} %slice.64.refs_0_), channel_id=1, source_target_pairs={{0,8},{4,12},{8,0},{12,4},{16,24},{20,28},{24,16},{28,20},{1,9},{5... | collective-permute-start | bytes 1376264 | tf_op jit(solution)/shard_map/ppermute | solution.py:64
  6.9 17.4 %collective-permute-start.8 = (bf16[6,32,1024]{2,1,0:T(8,128)(2,1)S(1)}, bf16[6,32,1024]{2,1,0:T(8,128)(2,1)}, u32[]{:S(2)}, u32[]{:S(2)}) collective-permute-start(bf16[6,32,1024]{2,1,0:T(8,128)(2,1)S(1)} %slice.65.refs_8_), channel_id=1, source_target_pairs={{0,8},{4,12},{8,0},{12,4},{16,24},{20,28},{24,16},{28,20},{1,9},{5... | collective-permute-start | bytes 1179656 | tf_op jit(solution)/shard_map/ppermute | solution.py:64
  7.5 18.6 %collective-permute-start.7 = (bf16[6,32,1024]{2,1,0:T(8,128)(2,1)S(1)}, bf16[6,32,1024]{2,1,0:T(8,128)(2,1)S(1)}, u32[]{:S(2)}, u32[]{:S(2)}) collective-permute-start(bf16[6,32,1024]{2,1,0:T(8,128)(2,1)S(1)} %slice.65.refs_8_), channel_id=1, source_target_pairs={{0,4},{4,0},{8,12},{12,8},{16,20},{20,16},{24,28},{28,24},{1,5},{5... | collective-permute-start | bytes 1179656 | tf_op jit(solution)/shard_map/ppermute | solution.py:64
  7.5 19.8 %collective-permute-start.3 = (bf16[7,32,1024]{2,1,0:T(8,128)(2,1)S(1)}, bf16[7,32,1024]{2,1,0:T(8,128)(2,1)S(1)}, u32[]{:S(2)}, u32[]{:S(2)}) collective-permute-start(bf16[7,32,1024]{2,1,0:T(8,128)(2,1)S(1)} %slice.64.refs_0_), channel_id=1, source_target_pairs={{0,16},{4,20},{8,24},{12,28},{16,0},{20,4},{24,8},{28,12},{1,17},{... | collective-permute-start | bytes 1376264 | tf_op jit(solution)/shard_map/ppermute | solution.py:64
  17.5 18.2 %collective-permute-start.5 = (bf16[7,32,1024]{2,1,0:T(8,128)(2,1)S(1)}, bf16[7,32,1024]{2,1,0:T(8,128)(2,1)S(1)}, u32[]{:S(2)}, u32[]{:S(2)}) collective-permute-start(bf16[7,32,1024]{2,1,0:T(8,128)(2,1)S(1)} %collective-permute-done.1.refs_2_), channel_id=1, source_target_pairs={{0,16},{4,20},{8,24},{12,28},{16,0},{20,4},{24,8},{28,12},{1,17},{... | collective-permute-start | bytes 1376264 | tf_op jit(solution)/shard_map/ppermute | solution.py:64
  46.6 15.0 %collective-permute-start.15 = (bf16[1024,256]{1,0:T(8,128)(2,1)}, bf16[1024,256]{1,0:T(8,128)(2,1)S(1)}, u32[]{:S(2)}, u32[]{:S(2)}) collective-permute-start(bf16[1024,256]{1,0:T(8,128)(2,1)} %get-tuple-element.75.refs_0_), channel_id=1, source_target_pairs={{0,8},{4,12},{8,0},{12,4},{16,24},{20,28},{24,16},{28,20},{1,9},{5... | collective-permute-start | bytes 1572872 | tf_op jit(solution)/shard_map/ppermute | solution.py:64
  46.9 15.0 %collective-permute-start.24 = (bf16[1024,256]{1,0:T(8,128)(2,1)}, bf16[1024,256]{1,0:T(8,128)(2,1)S(1)}, u32[]{:S(2)}, u32[]{:S(2)}) collective-permute-start(bf16[1024,256]{1,0:T(8,128)(2,1)} %get-tuple-element.76.refs_8_), channel_id=1, source_target_pairs={{0,16},{4,20},{8,24},{12,28},{16,0},{20,4},{24,8},{28,12},{1,17},{... | collective-permute-start | bytes 1572872 | tf_op jit(solution)/shard_map/ppermute | solution.py:64
  48.7 24.5 %collective-permute-start.17 = (bf16[1024,256]{1,0:T(8,128)(2,1)}, bf16[1024,256]{1,0:T(8,128)(2,1)S(1)}, u32[]{:S(2)}, u32[]{:S(2)}) collective-permute-start(bf16[1024,256]{1,0:T(8,128)(2,1)} %get-tuple-element.75.refs_0_), channel_id=1, source_target_pairs={{0,16},{4,20},{8,24},{12,28},{16,0},{20,4},{24,8},{28,12},{1,17},{... | collective-permute-start | bytes 1572872 | tf_op jit(solution)/shard_map/ppermute | solution.py:64
  49.0 26.0 %collective-permute-start.22 = (bf16[1024,256]{1,0:T(8,128)(2,1)}, bf16[1024,256]{1,0:T(8,128)(2,1)S(1)}, u32[]{:S(2)}, u32[]{:S(2)}) collective-permute-start(bf16[1024,256]{1,0:T(8,128)(2,1)} %get-tuple-element.76.refs_8_), channel_id=1, source_target_pairs={{0,8},{4,12},{8,0},{12,4},{16,24},{20,28},{24,16},{28,20},{1,9},{5... | collective-permute-start | bytes 1572872 | tf_op jit(solution)/shard_map/ppermute | solution.py:64
  50.7 24.2 %collective-permute-start.14 = (bf16[1024,256]{1,0:T(8,128)(2,1)}, bf16[1024,256]{1,0:T(8,128)(2,1)S(1)}, u32[]{:S(2)}, u32[]{:S(2)}) collective-permute-start(bf16[1024,256]{1,0:T(8,128)(2,1)} %get-tuple-element.75.refs_0_), channel_id=1, source_target_pairs={{0,4},{4,0},{8,12},{12,8},{16,20},{20,16},{24,28},{28,24},{1,5},{5... | collective-permute-start | bytes 1572872 | tf_op jit(solution)/shard_map/ppermute | solution.py:64
  61.9 21.4 %collective-permute-start.19 = (bf16[1024,256]{1,0:T(8,128)(2,1)S(1)}, bf16[1024,256]{1,0:T(8,128)(2,1)S(1)}, u32[]{:S(2)}, u32[]{:S(2)}) collective-permute-start(bf16[1024,256]{1,0:T(8,128)(2,1)S(1)} %collective-permute-done.15.refs_2_), channel_id=1, source_target_pairs={{0,16},{4,20},{8,24},{12,28},{16,0},{20,4},{24,8},{28,12},{1,17},{... | collective-permute-start | bytes 1572872 | tf_op jit(solution)/shard_map/ppermute | solution.py:64
  74.9 19.7 %collective-permute-start.25 = (bf16[1024,256]{1,0:T(8,128)(2,1)S(1)}, bf16[1024,256]{1,0:T(8,128)(2,1)S(1)}, u32[]{:S(2)}, u32[]{:S(2)}) collective-permute-start(bf16[1024,256]{1,0:T(8,128)(2,1)S(1)} %collective-permute-done.24.refs_12_), channel_id=1, source_target_pairs={{0,4},{4,0},{8,12},{12,8},{16,20},{20,16},{24,28},{28,24},{1,5},{5... | collective-permute-start | bytes 1572872 | tf_op jit(solution)/shard_map/ppermute | solution.py:64
  75.4 21.0 %collective-permute-start.18 = (bf16[1024,256]{1,0:T(8,128)(2,1)S(1)}, bf16[1024,256]{1,0:T(8,128)(2,1)S(1)}, u32[]{:S(2)}, u32[]{:S(2)}) collective-permute-start(bf16[1024,256]{1,0:T(8,128)(2,1)S(1)} %collective-permute-done.17.refs_4_), channel_id=1, source_target_pairs={{0,4},{4,0},{8,12},{12,8},{16,20},{20,16},{24,28},{28,24},{1,5},{5... | collective-permute-start | bytes 1572872 | tf_op jit(solution)/shard_map/ppermute | solution.py:64
  94.7 16.1 %collective-permute-start.31 = (bf16[256,1024]{1,0:T(8,128)(2,1)}, bf16[256,1024]{1,0:T(8,128)(2,1)S(1)}, u32[]{:S(2)}, u32[]{:S(2)}) collective-permute-start(bf16[256,1024]{1,0:T(8,128)(2,1)} %bitcast.61), channel_id=1, source_target_pairs={{0,1},{1,2},{2,3},{3,0},{4,5},{5,6},{6,7},{7,4},{8,9},{9,10},{10,1... | collective-permute-start | bytes 1572872 | tf_op jit(solution)/shard_map/ppermute | solution.py:91
  108.8 14.6 %collective-permute-start.28 = (bf16[1024,256]{1,0:T(8,128)(2,1)}, bf16[1024,256]{1,0:T(8,128)(2,1)S(1)}, u32[]{:S(2)}, u32[]{:S(2)}) collective-permute-start(bf16[1024,256]{1,0:T(8,128)(2,1)} %get-tuple-element.77.refs_0_.refs_3_), channel_id=1, source_target_pairs={{0,1},{1,2},{2,3},{3,0},{4,5},{5,6},{6,7},{7,4},{8,9},{9,10},{10,1... | collective-permute-start | bytes 1572872 | tf_op jit(solution)/shard_map/ppermute | solution.py:91
  110.8 23.8 %collective-permute-start.32 = (bf16[256,1024]{1,0:T(8,128)(2,1)S(1)}, bf16[256,1024]{1,0:T(8,128)(2,1)S(1)}, u32[]{:S(2)}, u32[]{:S(2)}) collective-permute-start(bf16[256,1024]{1,0:T(8,128)(2,1)S(1)} %collective-permute-done.31.refs_5_), channel_id=1, source_target_pairs={{0,1},{1,2},{2,3},{3,0},{4,5},{5,6},{6,7},{7,4},{8,9},{9,10},{10,1... | collective-permute-start | bytes 1572872 | tf_op jit(solution)/shard_map/ppermute | solution.py:91
  123.4 22.5 %collective-permute-start.29 = (bf16[1024,256]{1,0:T(8,128)(2,1)S(1)}, bf16[1024,256]{1,0:T(8,128)(2,1)S(1)}, u32[]{:S(2)}, u32[]{:S(2)}) collective-permute-start(bf16[1024,256]{1,0:T(8,128)(2,1)S(1)} %collective-permute-done.28.refs_1_), channel_id=1, source_target_pairs={{0,1},{1,2},{2,3},{3,0},{4,5},{5,6},{6,7},{7,4},{8,9},{9,10},{10,1... | collective-permute-start | bytes 1572872 | tf_op jit(solution)/shard_map/ppermute | solution.py:91
  134.6 22.5 %collective-permute-start.33 = (bf16[256,1024]{1,0:T(8,128)(2,1)S(1)}, bf16[256,1024]{1,0:T(8,128)(2,1)S(1)}, u32[]{:S(2)}, u32[]{:S(2)}) collective-permute-start(bf16[256,1024]{1,0:T(8,128)(2,1)S(1)} %collective-permute-done.32.refs_6_), channel_id=1, source_target_pairs={{0,1},{1,2},{2,3},{3,0},{4,5},{5,6},{6,7},{7,4},{8,9},{9,10},{10,1... | collective-permute-start | bytes 1572872 | tf_op jit(solution)/shard_map/ppermute | solution.py:91
  145.9 22.6 %collective-permute-start.30 = (bf16[1024,256]{1,0:T(8,128)(2,1)S(1)}, bf16[1024,256]{1,0:T(8,128)(2,1)}, u32[]{:S(2)}, u32[]{:S(2)}) collective-permute-start(bf16[1024,256]{1,0:T(8,128)(2,1)S(1)} %collective-permute-done.29.refs_2_), channel_id=1, source_target_pairs={{0,1},{1,2},{2,3},{3,0},{4,5},{5,6},{6,7},{7,4},{8,9},{9,10},{10,1... | collective-permute-start | bytes 1572872 | tf_op jit(solution)/shard_map/ppermute | solution.py:91
  191.2 23.7 %collective-permute-start.34 = (bf16[256,1024]{1,0:T(8,128)(2,1)S(1)}, bf16[256,1024]{1,0:T(8,128)(2,1)S(1)}, u32[]{:S(2)}, u32[]{:S(2)}) collective-permute-start(bf16[256,1024]{1,0:T(8,128)(2,1)S(1)} %slice.53), channel_id=1, source_target_pairs={{0,3},{1,0},{2,1},{3,2},{4,7},{5,4},{6,5},{7,6},{8,11},{9,8},{10,9... | collective-permute-start | bytes 1572872 | tf_op jit(solution)/shard_map/ppermute | solution.py:91
  203.9 22.3 %collective-permute-start.41 = (bf16[256,1024]{1,0:T(8,128)(2,1)S(1)}, bf16[256,1024]{1,0:T(8,128)(2,1)S(1)}, u32[]{:S(2)}, u32[]{:S(2)}) collective-permute-start(bf16[256,1024]{1,0:T(8,128)(2,1)S(1)} %add_convert_fusion.17), channel_id=1, source_target_pairs={{0,3},{1,0},{2,1},{3,2},{4,7},{5,4},{6,5},{7,6},{8,11},{9,8},{10,9... | collective-permute-start | bytes 1572872 | tf_op jit(solution)/shard_map/ppermute | solution.py:91
  217.0 20.5 %collective-permute-start.35 = (bf16[256,1024]{1,0:T(8,128)(2,1)}, bf16[256,1024]{1,0:T(8,128)(2,1)}, u32[]{:S(2)}, u32[]{:S(2)}) collective-permute-start(bf16[256,1024]{1,0:T(8,128)(2,1)} %add_convert_fusion.20), channel_id=1, source_target_pairs={{0,3},{1,0},{2,1},{3,2},{4,7},{5,4},{6,5},{7,6},{8,11},{9,8},{10,9... | collective-permute-start | bytes 1572872 | tf_op jit(solution)/shard_map/ppermute | solution.py:91
  226.4 22.3 %collective-permute-start.42 = (bf16[256,1024]{1,0:T(8,128)(2,1)S(1)}, bf16[256,1024]{1,0:T(8,128)(2,1)S(1)}, u32[]{:S(2)}, u32[]{:S(2)}) collective-permute-start(bf16[256,1024]{1,0:T(8,128)(2,1)S(1)} %add_convert_fusion.16), channel_id=1, source_target_pairs={{0,3},{1,0},{2,1},{3,2},{4,7},{5,4},{6,5},{7,6},{8,11},{9,8},{10,9... | collective-permute-start | bytes 1572872 | tf_op jit(solution)/shard_map/ppermute | solution.py:91
  238.9 21.0 %collective-permute-start.36 = (bf16[256,1024]{1,0:T(8,128)(2,1)S(1)}, bf16[256,1024]{1,0:T(8,128)(2,1)S(1)}, u32[]{:S(2)}, u32[]{:S(2)}) collective-permute-start(bf16[256,1024]{1,0:T(8,128)(2,1)S(1)} %add_convert_fusion.19), channel_id=1, source_target_pairs={{0,3},{1,0},{2,1},{3,2},{4,7},{5,4},{6,5},{7,6},{8,11},{9,8},{10,9... | collective-permute-start | bytes 1572872 | tf_op jit(solution)/shard_map/ppermute | solution.py:91
  262.0 16.6 %collective-permute-start.43 = (bf16[256,1024]{1,0:T(8,128)(2,1)S(1)}, bf16[256,1024]{1,0:T(8,128)(2,1)S(1)}, u32[]{:S(2)}, u32[]{:S(2)}) collective-permute-start(bf16[256,1024]{1,0:T(8,128)(2,1)S(1)} %get-tuple-element.149.refs_0_), channel_id=1, source_target_pairs={{0,1},{1,2},{2,3},{3,0},{4,5},{5,6},{6,7},{7,4},{8,9},{9,10},{10,1... | collective-permute-start | bytes 1572872 | tf_op jit(solution)/shard_map/ppermute | solution.py:91
  278.7 15.7 %collective-permute-start.44 = (bf16[256,1024]{1,0:T(8,128)(2,1)S(1)}, bf16[256,1024]{1,0:T(8,128)(2,1)S(1)}, u32[]{:S(2)}, u32[]{:S(2)}) collective-permute-start(bf16[256,1024]{1,0:T(8,128)(2,1)S(1)} %collective-permute-done.43.refs_1_), channel_id=1, source_target_pairs={{0,1},{1,2},{2,3},{3,0},{4,5},{5,6},{6,7},{7,4},{8,9},{9,10},{10,1... | collective-permute-start | bytes 1572872 | tf_op jit(solution)/shard_map/ppermute | solution.py:91
  294.4 16.7 %collective-permute-start.45 = (bf16[256,1024]{1,0:T(8,128)(2,1)S(1)}, bf16[256,1024]{1,0:T(8,128)(2,1)S(1)}, u32[]{:S(2)}, u32[]{:S(2)}) collective-permute-start(bf16[256,1024]{1,0:T(8,128)(2,1)S(1)} %collective-permute-done.44.refs_2_), channel_id=1, source_target_pairs={{0,1},{1,2},{2,3},{3,0},{4,5},{5,6},{6,7},{7,4},{8,9},{9,10},{10,1... | collective-permute-start | bytes 1572872 | tf_op jit(solution)/shard_map/ppermute | solution.py:91
  294.4 44.6 %collective-permute-start.37 = (bf16[256,1024]{1,0:T(8,128)(2,1)S(1)}, bf16[256,1024]{1,0:T(8,128)(2,1)S(1)}, u32[]{:S(2)}, u32[]{:S(2)}) collective-permute-start(bf16[256,1024]{1,0:T(8,128)(2,1)S(1)} %get-tuple-element.151.refs_0_), channel_id=1, source_target_pairs={{0,1},{1,2},{2,3},{3,0},{4,5},{5,6},{6,7},{7,4},{8,9},{9,10},{10,1... | collective-permute-start | bytes 1572872 | tf_op jit(solution)/shard_map/ppermute | solution.py:91
  339.0 69.0 %collective-permute-start.38 = (bf16[256,1024]{1,0:T(8,128)(2,1)S(1)}, bf16[256,1024]{1,0:T(8,128)(2,1)}, u32[]{:S(2)}, u32[]{:S(2)}) collective-permute-start(bf16[256,1024]{1,0:T(8,128)(2,1)S(1)} %collective-permute-done.37.refs_1_), channel_id=1, source_target_pairs={{0,1},{1,2},{2,3},{3,0},{4,5},{5,6},{6,7},{7,4},{8,9},{9,10},{10,1... | collective-permute-start | bytes 1572872 | tf_op jit(solution)/shard_map/ppermute | solution.py:91
  339.2 55.9 %collective-permute-start.47 = (bf16[1024,256]{1,0:T(8,128)(2,1)}, bf16[1024,256]{1,0:T(8,128)(2,1)S(1)}, u32[]{:S(2)}, u32[]{:S(2)}) collective-permute-start(bf16[1024,256]{1,0:T(8,128)(2,1)} %get-tuple-element.88), channel_id=1, source_target_pairs={{0,4},{4,0},{8,12},{12,8},{16,20},{20,16},{24,28},{28,24},{1,5},{5... | collective-permute-start | bytes 1572872 | tf_op jit(solution)/shard_map/ppermute | solution.py:64
  342.0 15.3 %collective-permute-start.58 = (bf16[1024,256]{1,0:T(8,128)(2,1)S(1)}, bf16[1024,256]{1,0:T(8,128)(2,1)S(1)}, u32[]{:S(2)}, u32[]{:S(2)}) collective-permute-start(bf16[1024,256]{1,0:T(8,128)(2,1)S(1)} %add_convert_fusion.4), channel_id=1, source_target_pairs={{0,8},{4,12},{8,0},{12,4},{16,24},{20,28},{24,16},{28,20},{1,9},{5... | collective-permute-start | bytes 1572872 | tf_op jit(solution)/shard_map/ppermute | solution.py:64
  346.3 49.2 %collective-permute-start.49 = (bf16[1024,256]{1,0:T(8,128)(2,1)S(1)}, bf16[1024,256]{1,0:T(8,128)(2,1)S(1)}, u32[]{:S(2)}, u32[]{:S(2)}) collective-permute-start(bf16[1024,256]{1,0:T(8,128)(2,1)S(1)} %copy-done.57), channel_id=1, source_target_pairs={{0,4},{4,0},{8,12},{12,8},{16,20},{20,16},{24,28},{28,24},{1,5},{5... | collective-permute-start | bytes 1572872 | tf_op jit(solution)/shard_map/ppermute | solution.py:64
  346.6 63.5 %collective-permute-start.53 = (bf16[1024,256]{1,0:T(8,128)(2,1)S(1)}, bf16[1024,256]{1,0:T(8,128)(2,1)S(1)}, u32[]{:S(2)}, u32[]{:S(2)}) collective-permute-start(bf16[1024,256]{1,0:T(8,128)(2,1)S(1)} %copy-done.56), channel_id=1, source_target_pairs={{0,4},{4,0},{8,12},{12,8},{16,20},{20,16},{24,28},{28,24},{1,5},{5... | collective-permute-start | bytes 1572872 | tf_op jit(solution)/shard_map/ppermute | solution.py:64
  357.3 50.4 %collective-permute-start.51 = (bf16[1024,256]{1,0:T(8,128)(2,1)S(1)}, bf16[1024,256]{1,0:T(8,128)(2,1)S(1)}, u32[]{:S(2)}, u32[]{:S(2)}) collective-permute-start(bf16[1024,256]{1,0:T(8,128)(2,1)S(1)} %add_convert_fusion.11), channel_id=1, source_target_pairs={{0,16},{4,20},{8,24},{12,28},{16,0},{20,4},{24,8},{28,12},{1,17},{... | collective-permute-start | bytes 1572872 | tf_op jit(solution)/shard_map/ppermute | solution.py:64
  395.1 15.4 %collective-permute-start.55 = (bf16[1024,256]{1,0:T(8,128)(2,1)S(1)}, bf16[1024,256]{1,0:T(8,128)(2,1)S(1)}, u32[]{:S(2)}, u32[]{:S(2)}) collective-permute-start(bf16[1024,256]{1,0:T(8,128)(2,1)S(1)} %add_convert_fusion.7), channel_id=1, source_target_pairs={{0,8},{4,12},{8,0},{12,4},{16,24},{20,28},{24,16},{28,20},{1,9},{5... | collective-permute-start | bytes 1572872 | tf_op jit(solution)/shard_map/ppermute | solution.py:64
  395.5 23.5 %collective-permute-start.59 = (bf16[1024,256]{1,0:T(8,128)(2,1)S(1)}, bf16[1024,256]{1,0:T(8,128)(2,1)S(1)}, u32[]{:S(2)}, u32[]{:S(2)}) collective-permute-start(bf16[1024,256]{1,0:T(8,128)(2,1)S(1)} %add_convert_fusion.3), channel_id=1, source_target_pairs={{0,16},{4,20},{8,24},{12,28},{16,0},{20,4},{24,8},{28,12},{1,17},{... | collective-permute-start | bytes 1572872 | tf_op jit(solution)/shard_map/ppermute | solution.py:64
  408.0 20.8 %collective-permute-start.48 = (bf16[1024,256]{1,0:T(8,128)(2,1)S(1)}, bf16[1024,256]{1,0:T(8,128)(2,1)S(1)}, u32[]{:S(2)}, u32[]{:S(2)}) collective-permute-start(bf16[1024,256]{1,0:T(8,128)(2,1)S(1)} %add_convert_fusion.14), channel_id=1, source_target_pairs={{0,16},{4,20},{8,24},{12,28},{16,0},{20,4},{24,8},{28,12},{1,17},{... | collective-permute-start | bytes 1572872 | tf_op jit(solution)/shard_map/ppermute | solution.py:64
  410.1 18.7 %collective-permute-start.52 = (bf16[1024,256]{1,0:T(8,128)(2,1)S(1)}, bf16[1024,256]{1,0:T(8,128)(2,1)S(1)}, u32[]{:S(2)}, u32[]{:S(2)}) collective-permute-start(bf16[1024,256]{1,0:T(8,128)(2,1)S(1)} %add_convert_fusion.10), channel_id=1, source_target_pairs={{0,8},{4,12},{8,0},{12,4},{16,24},{20,28},{24,16},{28,20},{1,9},{5... | collective-permute-start | bytes 1572872 | tf_op jit(solution)/shard_map/ppermute | solution.py:64
  410.5 61.7 %collective-permute-start.39 = (bf16[256,1024]{1,0:T(8,128)(2,1)}, bf16[256,1024]{1,0:T(8,128)(2,1)S(1)}, u32[]{:S(2)}, u32[]{:S(2)}) collective-permute-start(bf16[256,1024]{1,0:T(8,128)(2,1)} %collective-permute-done.38.refs_2_), channel_id=1, source_target_pairs={{0,1},{1,2},{2,3},{3,0},{4,5},{5,6},{6,7},{7,4},{8,9},{9,10},{10,1... | collective-permute-start | bytes 1572872 | tf_op jit(solution)/shard_map/ppermute | solution.py:91
  437.2 33.0 %collective-permute-start.60 = (bf16[256,1024]{1,0:T(8,128)(2,1)}, bf16[256,1024]{1,0:T(8,128)(2,1)}, u32[]{:S(2)}, u32[]{:S(2)}) collective-permute-start(bf16[256,1024]{1,0:T(8,128)(2,1)} %slice.69), channel_id=1, source_target_pairs={{0,3},{1,0},{2,1},{3,2},{4,7},{5,4},{6,5},{7,6},{8,11},{9,8},{10,9... | collective-permute-start | bytes 1572872 | tf_op jit(solution)/shard_map/ppermute | solution.py:91
  476.1 30.2 %collective-permute-start.72 = (bf16[7,32,1024]{2,1,0:T(8,128)(2,1)}, bf16[7,32,1024]{2,1,0:T(8,128)(2,1)S(1)}, u32[]{:S(2)}, u32[]{:S(2)}) collective-permute-start(bf16[7,32,1024]{2,1,0:T(8,128)(2,1)} %get-tuple-element.118), channel_id=1, source_target_pairs={{0,4},{4,0},{8,12},{12,8},{16,20},{20,16},{24,28},{28,24},{1,5},{5... | collective-permute-start | bytes 1376264 | tf_op jit(solution)/shard_map/ppermute | solution.py:64
  476.5 14.3 %collective-permute-start.76 = (bf16[6,32,1024]{2,1,0:T(8,128)(2,1)}, bf16[6,32,1024]{2,1,0:T(8,128)(2,1)S(1)}, u32[]{:S(2)}, u32[]{:S(2)}) collective-permute-start(bf16[6,32,1024]{2,1,0:T(8,128)(2,1)} %get-tuple-element.122), channel_id=1, source_target_pairs={{0,4},{4,0},{8,12},{12,8},{16,20},{20,16},{24,28},{28,24},{1,5},{5... | collective-permute-start | bytes 1179656 | tf_op jit(solution)/shard_map/ppermute | solution.py:64
  490.6 28.5 %collective-permute-start.66 = (bf16[7,32,1024]{2,1,0:T(8,128)(2,1)S(1)}, bf16[7,32,1024]{2,1,0:T(8,128)(2,1)S(1)}, u32[]{:S(2)}, u32[]{:S(2)}) collective-permute-start(bf16[7,32,1024]{2,1,0:T(8,128)(2,1)S(1)} %copy-done.63), channel_id=1, source_target_pairs={{0,4},{4,0},{8,12},{12,8},{16,20},{20,16},{24,28},{28,24},{1,5},{5... | collective-permute-start | bytes 1376264 | tf_op jit(solution)/shard_map/ppermute | solution.py:64
  503.8 20.6 %collective-permute-start.68 = (bf16[7,32,1024]{2,1,0:T(8,128)(2,1)S(1)}, bf16[7,32,1024]{2,1,0:T(8,128)(2,1)S(1)}, u32[]{:S(2)}, u32[]{:S(2)}) collective-permute-start(bf16[7,32,1024]{2,1,0:T(8,128)(2,1)S(1)} %add_convert_fusion.25), channel_id=1, source_target_pairs={{0,16},{4,20},{8,24},{12,28},{16,0},{20,4},{24,8},{28,12},{1,17},{... | collective-permute-start | bytes 1376264 | tf_op jit(solution)/shard_map/ppermute | solution.py:64
  506.2 28.5 %collective-permute-start.79 = (bf16[6,32,1024]{2,1,0:T(8,128)(2,1)S(1)}, bf16[6,32,1024]{2,1,0:T(8,128)(2,1)S(1)}, u32[]{:S(2)}, u32[]{:S(2)}) collective-permute-start(bf16[6,32,1024]{2,1,0:T(8,128)(2,1)S(1)} %add_convert_fusion.27), channel_id=1, source_target_pairs={{0,16},{4,20},{8,24},{12,28},{16,0},{20,4},{24,8},{28,12},{1,17},{... | collective-permute-start | bytes 1179656 | tf_op jit(solution)/shard_map/ppermute | solution.py:64
  515.7 19.1 %collective-permute-start.75 = (bf16[7,32,1024]{2,1,0:T(8,128)(2,1)S(1)}, bf16[7,32,1024]{2,1,0:T(8,128)(2,1)S(1)}, u32[]{:S(2)}, u32[]{:S(2)}) collective-permute-start(bf16[7,32,1024]{2,1,0:T(8,128)(2,1)S(1)} %add_convert_fusion.21), channel_id=1, source_target_pairs={{0,8},{4,12},{8,0},{12,4},{16,24},{20,28},{24,16},{28,20},{1,9},{5... | collective-permute-start | bytes 1376264 | tf_op jit(solution)/shard_map/ppermute | solution.py:64
  533.3 41.7 %collective-permute-start.65 = (bf16[256,1024]{1,0:T(8,128)(2,1)S(1)}, bf16[256,1024]{1,0:T(8,128)(2,1)S(1)}, u32[]{:S(2)}, u32[]{:S(2)}) collective-permute-start(bf16[256,1024]{1,0:T(8,128)(2,1)S(1)} %collective-permute-done.64.refs_2_), channel_id=1, source_target_pairs={{0,1},{1,2},{2,3},{3,0},{4,5},{5,6},{6,7},{7,4},{8,9},{9,10},{10,1... | collective-permute-start | bytes 1572872 | tf_op jit(solution)/shard_map/ppermute | solution.py:91
  542.9 31.4 %collective-permute-start.84 = (f32[2,1024]{1,0:T(2,128)S(1)}, f32[2,1024]{1,0:T(2,128)S(1)}, u32[]{:S(2)}, u32[]{:S(2)}) collective-permute-start(f32[2,1024]{1,0:T(2,128)S(1)} %add.211), channel_id=1, source_target_pairs={{0,2},{1,3},{2,0},{3,1},{4,6},{5,7},{6,4},{7,5},{8,10},{9,11},{10,... | collective-permute-start | bytes 24584 | tf_op jit(solution)/shard_map/ppermute | solution.py:115
  (102 other events, 1695.5 us)

commit v2 on v1

v2 whole, which is shorter than its diff:
```python
import functools

import jax
import jax.numpy as jnp
from jax import lax
from jax.experimental import pallas as pl
from jax.experimental.pallas import tpu as pltpu
from jax.sharding import PartitionSpec as P

H = 8
HD = 128
FF = 2816
MEMB = 128
STEP = 10

EPSILON = 1e-06
RATE = 0.02
GAIN_RATE = 0.5
BETA_ONE = 0.9
BETA_TWO = 0.95
ADAM_EPSILON = 1e-08
WEIGHT_DECAY = 0.01
AVERAGE_DECAY = 0.8
NEGATIVE = -1e30
START_TOP = -1e29
LOG2E = 1.4426950408889634

BF = jnp.bfloat16
F32 = jnp.float32
I32 = jnp.int32
HIGH = lax.Precision.HIGHEST
ANY = pl.BlockSpec(memory_space=pl.ANY)
SMEM = pl.BlockSpec(memory_space=pltpu.SMEM)
VMEM = pl.BlockSpec(memory_space=pltpu.VMEM)
VMEM_BYTES = 58 * 2**20

NT = (((1,), (1,)), ((), ()))
NN = (((1,), (0,)), ((), ()))
TN = (((0,), (0,)), ((), ()))


def mm(left, right, dims):
    return lax.dot_general(left, right, dims, preferred_element_type=F32)


QUICK = pl.CostEstimate(flops=1000, bytes_accessed=1000, transcendentals=0)


def params(**more):
    return pltpu.CompilerParams(vmem_limit_bytes=VMEM_BYTES, **more)


def pin(*values):
    return lax.optimization_barrier(values)


def routes(count):
    bits = []
    bit = 2
    while bit < count:
        bits.append(bit)
        bit *= 2
    return bits, bits[::-1]


def swap(value, count, bit):
    return lax.ppermute(value, "seq", [(i, i ^ bit) for i in range(count)])


def gather_seq(owns, count, beside=None):
    orders = routes(count)
    held = [{0: own} for own in owns]
    hops = len(orders[0])
    for stage in range(hops + 1):
        for i, pieces in enumerate(held):
            order = orders[i % 2]
            come = {}
            for m, piece in pieces.items():
                if m & 1 or bin(m).count("1") != stage:
                    continue
                for bit in order:
                    if all(other == bit or not m & other for other in order[order.index(bit) :]) and not m & bit:
                        come[m | bit] = swap(piece, count, bit)
                come[m | 1] = swap(piece, count, 1)
            pieces.update(come)
        if stage < hops:
            held, beside = pin(held, beside)
    return [[pieces[m] for m in range(count)] for pieces in held], beside


def plus(left, right):
    return (left.astype(F32) + right.astype(F32)).astype(left.dtype)


def reduce_bits(count, route):
    return [1, *routes(count)[route][::-1]]


def reduce_place(count, route, m):
    bits = reduce_bits(count, route)
    block = 0
    for bit in bits[1:]:
        block = 2 * block + bool(m & bit)
    return int(bool(m & bits[0])), block


def reduce_level(pair, count, route, at):
    keep, send = pair
    bits = reduce_bits(count, route)
    came = swap(send, count, bits[at])
    if at == len(bits) - 1:
        return keep, came
    half = keep.shape[0] // 2
    return plus(keep[:half], came[:half]), plus(keep[half:], came[half:])


def reduce_levels(pairs, count, at):
    return [reduce_level(pair, count, i % 2, at) for i, pair in enumerate(pairs)]


def direct_reduce(rows, count, sizes):
    parts = []
    for m in range(0, count, 2):
        at = reduce_place(count, 0, m)[1]
        part = rows[at * sizes : (at + 1) * sizes]
        parts.append(swap(part, count, m) if m else part)
    return parts


def direct_gather(rows, count):
    return jnp.concatenate([swap(rows, count, m) if m else rows for m in range(0, count, 2)], axis=0)


def core_gather(rows, count):
    return jnp.concatenate([rows, swap(rows, count, 1)], axis=0)


def gather_place(count, distance):
    return distance // 2 + (count // 2) * (distance % 2)


def ring(value, count, step):
    return lax.ppermute(value, "tp", [(i, (i + step) % count) for i in range(count)])


def trade_tp(parts, count):
    return [parts[0]] + [ring(parts[k], count, k) for k in range(1, count)]


def gather_tp(own, count):
    pieces = [own]
    for _ in range(count - 1):
        pieces.append(ring(pieces[-1], count, 1))
    return pieces


def reduce_tp(parts, count):
    total = parts[count - 1]
    for k in range(count - 2, -1, -1):
        came = ring(total, count, -1)
        if k == 0:
            return parts[0], came
        total = plus(parts[k], came)
    return None


def sum_steps(n_seq, n_tp):
    steps = []
    for axis, count in (("seq", n_seq), ("tp", n_tp)):
        bit = 1
        while bit < count:
            pairs = [(i, i ^ bit) for i in range(count)]
            steps.append(lambda v, axis=axis, pairs=pairs: v + lax.ppermute(v, axis, pairs))
            bit *= 2
    return steps


def panel_copies(owners_ref, me, first, amount, slots_dev, split, pieces, view, sem, back):
    def one(i, carry):
        slot = owners_ref[first + i]
        spot = lax.bitwise_xor(slot // slots_dev, me)
        row = slot % slots_dev
        for m, (low, high) in enumerate(pieces):
            for ref, base, size in ((low, 0, split), (high, split, slots_dev - split)):

                @pl.when((spot == m) & (row >= base) & (row < base + size))
                def _(ref=ref, base=base):
                    there = ref.at[row - base]
                    source, target = (view(i), there) if back else (there, view(i))
                    pltpu.make_async_copy(source, target, sem).start()

        return carry

    lax.fori_loop(0, amount, one, 0)


def norm_rows(rows, gain):
    inverse = lax.rsqrt(jnp.mean(rows * rows, axis=-1, keepdims=True) + EPSILON)
    unit = rows * inverse
    return unit, inverse, unit * gain


def project_kernel(cfg, meta, owners, x_ref, gain_ref, *refs):
    n, pq, pf, cap, slots_dev, split = cfg
    pieces = list(zip(refs[:n], refs[n : 2 * n], strict=True))
    outs = refs[2 * n : 2 * n + 3]
    normed_ref, inner, share, sems = refs[2 * n + 3 :]
    me, panel, d = meta[0], inner.shape[1], x_ref.shape[1]
    mine = jnp.clip(pf - me * cap, 0, cap)

    @pl.when(pl.program_id(0) == 0)
    def _():
        copies = functools.partial(panel_copies, owners, me)
        copies(0, 3 * pq, slots_dev, split, pieces, lambda i: inner.at[i], sems.at[0], False)
        copies(3 * pq, pq, slots_dev, split, pieces, lambda i: share.at[3 * cap + i], sems.at[1], False)
        for kind in range(3):
            for j in range(cap):

                @pl.when(j >= mine)
                def _(at=kind * cap + j):
                    share[at] = jnp.zeros(share.shape[1:], BF)

            copies(
                4 * pq + kind * pf + me * cap, mine, slots_dev, split, pieces,
                lambda i, kind=kind: share.at[kind * cap + i], sems.at[1], False,
            )

    _, _, normed = norm_rows(x_ref[...].astype(F32), gain_ref[0:1, :])
    normed = normed.astype(BF)
    normed_ref[...] = normed

    @pl.when(pl.program_id(0) == 0)
    def _():
        pltpu.make_async_copy(inner, inner, sems.at[0]).wait()

    for at in range(3):
        w = inner[at * pq : (at + 1) * pq].reshape(pq * panel, d)
        outs[at][...] = mm(normed, w, NT).astype(BF)

    @pl.when(pl.program_id(0) == pl.num_programs(0) - 1)
    def _():
        def finish(i, c):
            pltpu.make_async_copy(share.at[0], share.at[0], sems.at[1]).wait()
            return c

        lax.fori_loop(0, 3 * mine + pq, finish, 0)


def project_in(meta, owners, x, gains, pieces, pq, pf, cap, slots_dev, split):
    n = len(pieces)
    tok, d = x.shape
    panel = pieces[0][0].shape[1]
    qw = pq * panel
    tile = 256
    out = lambda w: pl.BlockSpec((tile, w), lambda i: (i, 0))
    whole = lambda count: pl.BlockSpec((count, panel, d), lambda i: (0, 0, 0))
    shape = lambda *dims: jax.ShapeDtypeStruct(dims, BF)
    q, k, v, normed, inner, share = pl.pallas_call(
        functools.partial(project_kernel, (n, pq, pf, cap, slots_dev, split)),
        grid=(tok // tile,),
        in_specs=[SMEM, SMEM, out(d), pl.BlockSpec(gains.shape, lambda i: (0, 0))] + [ANY] * (2 * n),
        out_specs=[out(qw)] * 3 + [out(d), whole(3 * pq), whole(3 * cap + pq)],
        out_shape=[shape(tok, qw)] * 3 + [shape(tok, d), shape(3 * pq, panel, d), shape(3 * cap + pq, panel, d)],
        scratch_shapes=[pltpu.SemaphoreType.DMA((2,))],
        compiler_params=params(),
        cost_estimate=QUICK,
        name="project",
    )(meta, owners, x, gains, *[p[0] for p in pieces], *[p[1] for p in pieces])
    return q, k, v, normed, inner.reshape(3, qw, d), share.reshape(-1, d)


def doc_start(meta, positions, docs):
    start = jnp.int32(0)
    found = jnp.zeros_like(positions)
    for at in range(docs):
        found = jnp.where(positions >= start, start, found)
        start = start + meta[2 + at]
    return found


def load_pieces(me, pieces, buffer, sem, tok):
    for m, piece in enumerate(pieces):
        owner = lax.bitwise_xor(me, m)
        at = pl.multiple_of(owner * tok, tok)
        pltpu.make_async_copy(piece, buffer.at[pl.ds(at, tok)], sem).start()


def member_table(meta, table, docs, picks, blocks):
    def clear(i, c):
        table[i] = 0
        return c

    lax.fori_loop(0, blocks, clear, 0)
    for e in range(picks):
        table[meta[2 + docs + e]] = 1


def memory_list(meta, blocks_ref, docs, picks, limit):
    count = jnp.int32(0)
    for e in range(picks):
        block = meta[2 + docs + e]
        fresh = (block + 1) * MEMB <= limit
        for other in range(e):
            fresh = fresh & (meta[2 + docs + other] != block)

        @pl.when(fresh)
        def _(count=count, block=block):
            blocks_ref[count] = block

        count = count + fresh.astype(I32)
    return count


def hide(scores, at, table, starts, queries, fill):
    rows = scores.shape[0]
    row = lax.broadcasted_iota(I32, (MEMB, scores.shape[1]), 0)
    kept = []
    for b in range(rows // MEMB):
        base = at + b * MEMB
        lowest = starts * (1 - table[base // MEMB]) - base
        seen = (row >= lowest) & (row <= queries - base)
        kept.append(jnp.where(seen, scores[b * MEMB : (b + 1) * MEMB], fill))
    return jnp.concatenate(kept, axis=0)


def attend_kernel(cfg, meta, q_ref, *refs):
    n, docs, picks, qt, kt, block = cfg
    keys, values = refs[:n], refs[n : 2 * n]
    out_ref, turn_ref, wide_ref, log_ref, kbuf, vbuf, acc, table, blocks, sems = refs[2 * n :]
    tok, width = q_ref.shape
    me = meta[0]
    factor = HD**-0.5 * LOG2E
    load_pieces(me, keys, kbuf, sems.at[0], tok)
    load_pieces(me, values, vbuf, sems.at[1], tok)
    member_table(meta, table, docs, picks, kbuf.shape[0] // MEMB)
    pltpu.make_async_copy(kbuf, kbuf, sems.at[0]).wait()
    pltpu.make_async_copy(vbuf, vbuf, sems.at[1]).wait()
    for head in range(width // HD):
        cols = slice(head * HD, (head + 1) * HD)

        def query_tile(t, carry, head=head, cols=cols):
            base = pl.multiple_of(t * qt, qt)
            first = me * tok + base
            queries = first + lax.broadcasted_iota(I32, (1, qt), 1)
            starts = doc_start(meta, queries, docs)
            low_tile = doc_start(meta, first, docs) // kt
            high_tile = (first + qt - 1) // kt
            q = q_ref[pl.ds(base, qt), cols]
            acc[...] = jnp.zeros_like(acc)

            def visit(at, rows, state, masked):
                top, total = state
                scores = mm(kbuf[pl.ds(at, rows), cols], q, NT)
                if masked:
                    scores = hide(scores, at, table, starts, queries, NEGATIVE)
                new_top = jnp.maximum(top, jnp.max(scores, axis=0, keepdims=True))
                fade = jnp.exp2((top - new_top) * factor)
                probs = jnp.exp2((scores - new_top) * factor)
                total = total * fade + jnp.sum(probs, axis=0, keepdims=True)
                acc[...] = acc[...] * fade + mm(vbuf[pl.ds(at, rows), cols], probs.astype(BF), TN)
                return new_top, total

            def dense(i, state):
                return visit(pl.multiple_of(i * kt, kt), kt, state, True)

            def memory(i, state):
                return visit(pl.multiple_of(blocks[i] * MEMB, MEMB), MEMB, state, False)

            count = memory_list(meta, blocks, docs, picks, low_tile * kt)
            state = (jnp.full((1, qt), START_TOP, F32), jnp.zeros((1, qt), F32))
            state = lax.fori_loop(low_tile, high_tile + 1, dense, state)
            top, total = lax.fori_loop(0, count, memory, state)
            rows = jnp.transpose(acc[...] * (1.0 / total))
            wide_ref[pl.ds(base, qt), cols] = rows
            rows = rows.astype(BF)
            out_ref[pl.ds(base, qt), cols] = rows
            spans = tok // block
            for part in range(qt // block):
                spot = lax.rem(base // block + part - meta[1] + spans, spans)
                spot = pl.multiple_of(spot * block, block)
                turn_ref[pl.ds(spot, block), cols] = rows[part * block : (part + 1) * block]
            log_ref[head : head + 1, pl.ds(base, qt)] = top * factor + jnp.log2(total)
            return carry

        lax.fori_loop(0, tok // qt, query_tile, 0)


def attend(meta, q, keys, values, docs, picks, block):
    n = len(keys)
    tok, width = q.shape
    qt, kt = 512, 512
    return pl.pallas_call(
        functools.partial(attend_kernel, (n, docs, picks, qt, kt, block)),
        in_specs=[SMEM, VMEM] + [ANY] * (2 * n),
        out_specs=[VMEM] * 4,
        out_shape=[
            jax.ShapeDtypeStruct((tok, width), BF),
            jax.ShapeDtypeStruct((tok, width), BF),
            jax.ShapeDtypeStruct((tok, width), F32),
            jax.ShapeDtypeStruct((width // HD, tok), F32),
        ],
        scratch_shapes=[
            pltpu.VMEM((n * tok, width), BF),
            pltpu.VMEM((n * tok, width), BF),
            pltpu.VMEM((HD, qt), F32),
            pltpu.SMEM((n * tok // MEMB,), I32),
            pltpu.SMEM((picks,), I32),
            pltpu.SemaphoreType.DMA((2,)),
        ],
        compiler_params=params(),
        cost_estimate=QUICK,
        name="attend",
    )(meta, q, *keys, *values)


def attend_back_kernel(cfg, meta, q_ref, wide_ref, log_ref, *refs):
    n, docs, picks, qt, kt, spans = cfg
    parts, refs = refs[:spans], refs[spans:]
    keys, values = refs[:n], refs[n : 2 * n]
    dq_ref = refs[2 * n]
    outs = (refs[2 * n + 1 : 2 * n + 3], refs[2 * n + 3 : 2 * n + 5])
    kbuf, vbuf, dk_acc, dv_acc, g_ref, acc, stage, table, blocks, sems = refs[2 * n + 5 :]
    tok, width = q_ref.shape
    me = meta[0]
    block = tok // spans
    scale = HD**-0.5
    factor = scale * LOG2E
    load_pieces(me, keys, kbuf, sems.at[0], tok)
    load_pieces(me, values, vbuf, sems.at[1], tok)
    member_table(meta, table, docs, picks, kbuf.shape[0] // MEMB)

    def clear(i, c):
        at = pl.ds(pl.multiple_of(i * 256, 256), 256)
        dk_acc[at, :] = jnp.zeros((256, width), F32)
        dv_acc[at, :] = jnp.zeros((256, width), F32)
        return c

    lax.fori_loop(0, kbuf.shape[0] // 256, clear, 0)
    for k, part in enumerate(parts):
        spot = pl.multiple_of(lax.rem(meta[1] - k + spans, spans) * block, block)
        g_ref[pl.ds(spot, block), :] = part[...]
    pltpu.make_async_copy(kbuf, kbuf, sems.at[0]).wait()
    pltpu.make_async_copy(vbuf, vbuf, sems.at[1]).wait()
    for head in range(width // HD):
        cols = slice(head * HD, (head + 1) * HD)

        def query_tile(t, carry, head=head, cols=cols):
            base = pl.multiple_of(t * qt, qt)
            first = me * tok + base
            queries = first + lax.broadcasted_iota(I32, (1, qt), 1)
            starts = doc_start(meta, queries, docs)
            low_tile = doc_start(meta, first, docs) // kt
            high_tile = (first + qt - 1) // kt
            q = q_ref[pl.ds(base, qt), cols]
            grad = g_ref[pl.ds(base, qt), cols]
            logs = log_ref[head : head + 1, pl.ds(base, qt)]
            product = grad.astype(F32) * wide_ref[pl.ds(base, qt), cols]
            delta = jnp.sum(jnp.transpose(product), axis=0, keepdims=True)
            acc[...] = jnp.zeros_like(acc)

            def visit(at, rows, masked):
                here = pl.ds(at, rows)
                k = kbuf[here, cols]
                probs = jnp.exp2(mm(k, q, NT) * factor - logs)
                if masked:
                    probs = hide(probs, at, table, starts, queries, 0.0)
                slopes = probs * (mm(vbuf[here, cols], grad, NT) - delta)
                slopes = slopes.astype(BF)
                dv_acc[here, cols] += mm(probs.astype(BF), grad, NN)
                dk_acc[here, cols] += mm(slopes, q, NN)
                acc[...] += mm(k, slopes, TN)

            def dense(i, c):
                visit(pl.multiple_of(i * kt, kt), kt, True)
                return c

            def memory(i, c):
                visit(pl.multiple_of(blocks[i] * MEMB, MEMB), MEMB, False)
                return c

            count = memory_list(meta, blocks, docs, picks, low_tile * kt)
            lax.fori_loop(low_tile, high_tile + 1, dense, 0)
            lax.fori_loop(0, count, memory, 0)
            dq_ref[pl.ds(base, qt), cols] = (jnp.transpose(acc[...]) * scale).astype(BF)
            return carry

        lax.fori_loop(0, tok // qt, query_tile, 0)

    def put(which, m):
        side, at = reduce_place(n, which, m)
        out = outs[which][side].at[at * tok : (at + 1) * tok]
        return pltpu.make_async_copy(stage.at[which], out, sems.at[2 + which])

    for m in range(n):
        at = pl.ds(pl.multiple_of(lax.bitwise_xor(me, m) * tok, tok), tok)
        for which in range(2):
            if m:
                put(which, m - 1).wait()
            rows = dk_acc[at, :] * scale if which == 0 else dv_acc[at, :]
            stage[which] = rows.astype(BF)
            put(which, m).start()
    for which in range(2):
        put(which, n - 1).wait()


def attend_back(meta, q, grads, wide, logs, keys, values, docs, picks):
    n = len(keys)
    tok, width = q.shape
    qt, kt = 512, 512
    got = pl.pallas_call(
        functools.partial(attend_back_kernel, (n, docs, picks, qt, kt, len(grads))),
        in_specs=[SMEM] + [VMEM] * (3 + len(grads)) + [ANY] * (2 * n),
        out_specs=[VMEM] + [ANY] * 4,
        out_shape=[jax.ShapeDtypeStruct((tok, width), BF)]
        + [jax.ShapeDtypeStruct((n * tok // 2, width), BF)] * 4,
        scratch_shapes=[
            pltpu.VMEM((n * tok, width), BF),
            pltpu.VMEM((n * tok, width), BF),
            pltpu.VMEM((n * tok, width), F32),
            pltpu.VMEM((n * tok, width), F32),
            pltpu.VMEM((tok, width), BF),
            pltpu.VMEM((HD, qt), F32),
            pltpu.VMEM((2, tok, width), BF),
            pltpu.SMEM((n * tok // MEMB,), I32),
            pltpu.SMEM((picks,), I32),
            pltpu.SemaphoreType.DMA((4,)),
        ],
        compiler_params=params(),
        cost_estimate=QUICK,
        name="attend_back",
    )(meta, q, wide, logs, *grads, *keys, *values)
    return got[0], got[1:3], got[3:5]


def mix_kernel(first, meta, x_ref, gain_ref, wo_ref, *refs):
    heads, (mixed_ref, left_ref, right_ref) = refs[:-3], refs[-3:]
    spans, qw = len(heads), heads[0].shape[1]
    mixed = x_ref[...].astype(F32)
    for k, head in enumerate(heads):
        mixed = mixed + mm(head[...], wo_ref[lax.rem(meta[1] - k + spans, spans), first:], NN)
    mixed_ref[...] = mixed
    _, _, normed = norm_rows(mixed, gain_ref[1:2, :])
    normed = normed.astype(BF)
    half = normed.shape[1] // 2
    left_ref[...] = normed[:, :half]
    right_ref[...] = normed[:, half:]


def mix(meta, x, gains, weights, heads):
    block, d = heads[0].shape[0], x.shape[1]
    whole = lambda a: pl.BlockSpec(a.shape, lambda i, meta: (0, 0))
    shape = lambda w, t: jax.ShapeDtypeStruct((block, w), t)
    outs = [shape(d, F32), shape(d // 2, BF), shape(d // 2, BF)]
    return pl.pallas_call(
        functools.partial(mix_kernel, weights.shape[1] - heads[0].shape[1]),
        grid_spec=pltpu.PrefetchScalarGridSpec(
            num_scalar_prefetch=1,
            grid=(1,),
            in_specs=[pl.BlockSpec((block, d), lambda i, meta: (meta[1], 0)), whole(gains), VMEM]
            + [whole(h) for h in heads],
            out_specs=[whole(o) for o in outs],
        ),
        out_shape=outs,
        compiler_params=params(),
        cost_estimate=QUICK,
        name="mix",
    )(meta, x, gains, weights, *heads)


def feed_kernel(cfg, meta, w_ref, g_ref, *refs):
    n, spans, fs = cfg
    pieces = refs[: 2 * n]
    normed_ref, hidden_ref, dgate_ref, dup_ref = refs[2 * n : 2 * n + 4]
    backs = (refs[2 * n + 4 : 2 * n + 6], refs[2 * n + 6 : 2 * n + 8])
    feeds = refs[2 * n + 8 : 2 * n + 10]
    rows, stage, feed, wg, wu, wd, sem, out_sem = refs[2 * n + 10 :]
    at = pl.program_id(0)
    block, half = g_ref.shape[0], g_ref.shape[1] // 2

    @pl.when(at == 0)
    def _():
        for m in range(n):
            pltpu.make_async_copy(pieces[m], rows.at[m, :, :half], sem).start()
            pltpu.make_async_copy(pieces[n + m], rows.at[m, :, half:], sem).start()
        for t in range(spans):
            for kind, w in enumerate((wg, wu, wd)):
                w[t * fs : (t + 1) * fs] = w_ref[t, kind * fs : (kind + 1) * fs]
        pltpu.make_async_copy(rows, rows, sem).wait()

    normed = rows[at]
    normed_ref[...] = normed
    gate = mm(normed, wg[...], NT)
    up = mm(normed, wu[...], NT)
    sigma = jax.nn.sigmoid(gate)
    silu = gate * sigma
    hidden = (silu * up).astype(BF)
    hidden_ref[...] = hidden
    d_hidden = mm(g_ref[...], wd[...], NT).astype(BF).astype(F32)
    d_gate = (d_hidden * up * (sigma * (1.0 + gate * (1.0 - sigma)))).astype(BF)
    d_up = (d_hidden * silu).astype(BF)
    dgate_ref[...] = d_gate
    dup_ref[...] = d_up
    stage[at] = (mm(d_gate, wg[...], NN) + mm(d_up, wu[...], NN)).astype(BF)
    feed[at] = mm(hidden, wd[...], NN).astype(BF)
    for m in range(n):

        @pl.when(at == m)
        def _(m=m):
            for route, cols in enumerate((slice(0, half), slice(half, 2 * half))):
                side, spot = reduce_place(n, route, m)
                there = backs[route][side].at[spot * block : (spot + 1) * block]
                pltpu.make_async_copy(stage.at[m, :, cols], there, out_sem).start()
            side, spot = reduce_place(n, 0, m)
            there = feeds[side].at[spot * block : (spot + 1) * block]
            pltpu.make_async_copy(feed.at[m], there, out_sem).start()

    @pl.when(at == n - 1)
    def _():
        pltpu.make_async_copy(stage, stage, out_sem).wait()
        pltpu.make_async_copy(feed, feed, out_sem).wait()


def feed_forward(meta, weights, grads, pieces, fs):
    n = len(pieces) // 2
    rows, d = grads.shape
    block = rows // n
    spans = weights.shape[0]
    units = spans * fs
    turned = lambda w: pl.BlockSpec((block, w), lambda m, meta: (lax.bitwise_xor(meta[0], m), 0))
    shape = lambda w: jax.ShapeDtypeStruct((rows, w), BF)
    got = pl.pallas_call(
        functools.partial(feed_kernel, (n, spans, fs)),
        grid_spec=pltpu.PrefetchScalarGridSpec(
            num_scalar_prefetch=1,
            grid=(n,),
            in_specs=[VMEM, turned(d)] + [ANY] * (2 * n),
            out_specs=[turned(d), turned(units), turned(units), turned(units)] + [ANY] * 6,
            scratch_shapes=[
                pltpu.VMEM((n, block, d), BF),
                pltpu.VMEM((n, block, d), BF),
                pltpu.VMEM((n, block, d), BF),
                pltpu.VMEM((units, d), BF),
                pltpu.VMEM((units, d), BF),
                pltpu.VMEM((units, d), BF),
                pltpu.SemaphoreType.DMA,
                pltpu.SemaphoreType.DMA,
            ],
        ),
        out_shape=[shape(d), shape(units), shape(units), shape(units)]
        + [jax.ShapeDtypeStruct((rows // 2, d // 2), BF)] * 4
        + [jax.ShapeDtypeStruct((rows // 2, d), BF)] * 2,
        compiler_params=params(),
        cost_estimate=QUICK,
        name="feed_forward",
    )(meta, weights, grads, *pieces)
    return got[:4], (got[4:6], got[6:8]), got[8:]


def branch_kernel(cfg, meta, left_a, left_b, right_a, right_b, mixed_ref, g_ref, gain_ref, wo_ref, *refs):
    first, n, spans = cfg
    heads, (mixed_out, gain_out), parts = refs[:spans], refs[spans : spans + 2], refs[spans + 2 : 2 * spans + 2]
    sides, (outer, sem) = refs[2 * spans + 2 : 2 * spans + 4], refs[2 * spans + 4 :]
    qw, out_rows = parts[0].shape[1], outer.shape[1] // n
    total = lambda a, b: a[...].astype(F32) + b[...].astype(F32)
    grad = jnp.concatenate([total(left_a, left_b), total(right_a, right_b)], axis=1)
    gain = gain_ref[1:2, :]
    unit, inverse, _ = norm_rows(mixed_ref[...], gain)
    gain_out[...] = jnp.sum(grad * unit, axis=0, keepdims=True)
    d_mixed = g_ref[...].astype(F32) + norm_back(grad, unit, inverse, gain)
    mixed_out[...] = d_mixed
    branch = d_mixed.astype(BF)
    for k, part in enumerate(parts):
        part[...] = mm(branch, wo_ref[lax.rem(meta[1] + k, spans), first:], NT).astype(BF)
    for k in range(spans):
        if outer.shape[1] > qw:
            outer[k, qw:] = jnp.zeros((outer.shape[1] - qw, outer.shape[2]), BF)
        outer[k, :qw] = mm(heads[(spans - k) % spans][...], branch, TN).astype(BF)
        spread(meta, outer.at[k], sides, n, 0, out_rows, sem, k * out_rows, spans * out_rows)
    pltpu.make_async_copy(outer, outer, sem).wait()


def branch_back(meta, pairs, mixed, grads, gains, weights, heads, n, first):
    block, d = mixed.shape
    spans, qw = weights.shape[0], weights.shape[1] - first
    out_rows = share_rows(qw, n)
    whole = lambda a: pl.BlockSpec(a.shape, lambda i, meta: (0, 0))
    terms = [*pairs[0], *pairs[1]]
    shape = jax.ShapeDtypeStruct
    outs = [shape((block, d), F32), shape((1, d), F32)] + [shape((block, qw), BF)] * spans
    got = pl.pallas_call(
        functools.partial(branch_kernel, (first, n, spans)),
        grid_spec=pltpu.PrefetchScalarGridSpec(
            num_scalar_prefetch=1,
            grid=(1,),
            in_specs=[whole(t) for t in terms]
            + [whole(mixed), pl.BlockSpec((block, d), lambda i, meta: (meta[1], 0)), whole(gains), VMEM]
            + [whole(h) for h in heads],
            out_specs=[whole(o) for o in outs] + [ANY] * 2,
            scratch_shapes=[pltpu.VMEM((spans, n * out_rows, d), BF), pltpu.SemaphoreType.DMA],
        ),
        out_shape=outs + [shape((n // 2 * spans * out_rows, d), BF)] * 2,
        compiler_params=params(),
        cost_estimate=QUICK,
        name="branch_back",
    )(meta, *terms, mixed, grads, gains, weights, *heads)
    return got[0], got[1], got[2 : 2 + spans], got[2 + spans :]


def place_kernel(n, meta, *refs):
    pieces, out = refs[:n], refs[n]
    rows = out.shape[0] // n
    for k, piece in enumerate(pieces):
        block = lax.rem(meta[1] - k + n, n)
        out[pl.ds(pl.multiple_of(block * rows, rows), rows), :] = piece[:rows, :].astype(out.dtype)


def place(meta, pieces, rows, kind=BF):
    n, d = len(pieces), pieces[0].shape[1]
    return pl.pallas_call(
        functools.partial(place_kernel, n),
        in_specs=[SMEM] + [VMEM] * n,
        out_specs=VMEM,
        out_shape=jax.ShapeDtypeStruct((n * rows, d), kind),
        compiler_params=params(),
        cost_estimate=QUICK,
        name="place",
    )(meta, *pieces)


def norm_back(grad_normed, unit_rows, inverse, gain_row):
    scaled = grad_normed * gain_row
    return inverse * (scaled - unit_rows * jnp.mean(scaled * unit_rows, axis=-1, keepdims=True))


def feed_grads_kernel(cfg, meta, d_gate, d_up, hidden, normed, grads, out):
    spans, fs = cfg
    for kind, (left, right) in enumerate(((d_gate, normed), (d_up, normed), (hidden, grads))):
        product = mm(left[...], right[...], TN).astype(BF)
        for t in range(spans):
            out[t, kind * fs : (kind + 1) * fs] = product[t * fs : (t + 1) * fs]


def feed_grads(meta, d_gate, d_up, hidden, normed, grads, fs):
    (rows, units), d = d_gate.shape, normed.shape[1]
    return pl.pallas_call(
        functools.partial(feed_grads_kernel, (units // fs, fs)),
        in_specs=[SMEM] + [VMEM] * 5,
        out_specs=VMEM,
        out_shape=jax.ShapeDtypeStruct((units // fs, 3 * fs, d), BF),
        compiler_params=params(),
        cost_estimate=QUICK,
        name="feed_grads",
    )(meta, d_gate, d_up, hidden, normed, grads)


def share_rows(rows, n):
    return -(-rows // (16 * n)) * 16


def spread(meta, stage, sides, n, route, rows, sem, base=0, total=None):
    for m in range(n):
        at = pl.ds(pl.multiple_of(lax.bitwise_xor(meta[0], m) * rows, rows), rows)
        side, spot = reduce_place(n, route, m)
        first = spot * (total or rows) + base
        pltpu.make_async_copy(stage.at[at], sides[side].at[first : first + rows], sem).start()


def late_kernel(cfg, meta, dq, dk, dv, normed, *refs):
    n, qw = cfg
    sides, (stage, sem) = refs[:2], refs[2:]
    used = 3 * qw
    if stage.shape[0] > used:
        stage[used:] = jnp.zeros((stage.shape[0] - used, stage.shape[1]), BF)
    for at, left in enumerate((dq, dk, dv)):
        stage[at * qw : (at + 1) * qw] = mm(left[...], normed[...], TN).astype(BF)
    spread(meta, stage, sides, n, 0, stage.shape[0] // n, sem)
    pltpu.make_async_copy(stage, stage, sem).wait()


def late_grads(meta, dq, dk, dv, normed, n):
    (tok, qw), d = dq.shape, normed.shape[1]
    rows = share_rows(3 * qw, n)
    return pl.pallas_call(
        functools.partial(late_kernel, (n, qw)),
        in_specs=[SMEM] + [VMEM] * 4,
        out_specs=[ANY] * 2,
        out_shape=[jax.ShapeDtypeStruct((n * rows // 2, d), BF)] * 2,
        scratch_shapes=[pltpu.VMEM((n * rows, d), BF), pltpu.SemaphoreType.DMA],
        compiler_params=params(),
        cost_estimate=QUICK,
        name="late_grads",
    )(meta, dq, dk, dv, normed)


def soap_kernel(cfg, meta, held, early, late, weight_ref, first_ref, second_ref, average_ref, stat_ref, basis_ref,
                weight_out, first_out, second_out, average_out, stat_out, turned_out, grads, wide, sem):
    n, late_panels, out_panels, pf, cap, rows, out_rows, group = cfg
    slots, panel, width = weight_ref.shape
    me, step = meta[0], pl.program_id(0)
    inner_panels = late_panels - out_panels

    def fetch(slot, source, share, base):
        grain = min(share, panel)
        for part in range(panel // grain):
            row = source * panel + part * grain
            at = gather_place(n, lax.bitwise_xor(me, row // share)) * (rows + out_rows) + base + row % share
            there = grads.at[slot, part * grain : (part + 1) * grain]
            pltpu.make_async_copy(late.at[pl.ds(pl.multiple_of(at, grain), grain)], there, sem).start()

    @pl.when(step == 0)
    def _():
        for slot in range(slots):
            source = held[slot]

            @pl.when(source < 0)
            def _(slot=slot):
                grads[slot] = jnp.zeros((panel, grads.shape[2]), BF)

            @pl.when((source >= 0) & (source < inner_panels))
            def _(slot=slot, source=source):
                fetch(slot, source, rows, 0)

            @pl.when((source >= inner_panels) & (source < late_panels))
            def _(slot=slot, source=source):
                fetch(slot, source - inner_panels, out_rows, rows)

            @pl.when(source >= late_panels)
            def _(slot=slot, source=source):
                kind, unit = (source - late_panels) // pf, (source - late_panels) % pf
                spot = (unit // cap) * 3 * cap + kind * cap + unit % cap
                pltpu.make_async_copy(early.at[spot], grads.at[slot], sem).start()

        for slot in range(slots):

            @pl.when(held[slot] >= 0)
            def _(slot=slot):
                pltpu.make_async_copy(grads.at[slot], grads.at[slot], sem).wait()

    high = functools.partial(lax.dot_general, precision=HIGH, preferred_element_type=F32)
    cols = pl.ds(pl.multiple_of(step * width, width), width)

    def parts(value):
        top = value.astype(BF)
        return top, (value - top.astype(F32)).astype(BF)

    for low in range(0, slots, group):
        count = min(group, slots - low)
        size = count * panel
        slot_range = slice(low, low + count)
        diagonal = wide.at[low // group]

        @pl.when(step == 0)
        def _(low=low, count=count, diagonal=diagonal):
            diagonal[...] = jnp.zeros_like(diagonal)
            for j in range(count):
                at = slice(j * panel, (j + 1) * panel)
                diagonal[at, at] = basis_ref[low + j]
                stat_out[low + j] = BETA_TWO * stat_ref[low + j]

        grad = grads[slot_range, :, cols].reshape(size, width)
        square = mm(grad, grad, NT)
        for j in range(count):
            at = slice(j * panel, (j + 1) * panel)
            stat_out[low + j] += (1.0 - BETA_TWO) * square[at, at]
        top, rest = parts(diagonal[:size, :size])
        flat = lambda ref, slot_range=slot_range, size=size: ref[slot_range].reshape(size, width)
        rotated = mm(top, grad, TN) + mm(rest, grad, TN)
        first = BETA_ONE * flat(first_ref) + (1.0 - BETA_ONE) * rotated
        second = BETA_TWO * flat(second_ref) + (1.0 - BETA_TWO) * rotated * rotated
        direction = (first / (1.0 - BETA_ONE**STEP)) / (
            jnp.sqrt(second / (1.0 - BETA_TWO**STEP)) + ADAM_EPSILON
        )
        high_part, low_part = parts(direction)
        update = mm(top, high_part, NN) + (mm(top, low_part, NN) + mm(rest, high_part, NN))
        weight = flat(weight_ref)
        new_weight = weight - RATE * (update + WEIGHT_DECAY * weight)
        average = AVERAGE_DECAY * flat(average_ref) + (1.0 - AVERAGE_DECAY) * new_weight
        shape = (count, panel, width)
        first_out[slot_range] = first.reshape(shape)
        second_out[slot_range] = second.reshape(shape)
        weight_out[slot_range] = new_weight.reshape(shape)
        average_out[slot_range] = average.reshape(shape)

        @pl.when(step == pl.num_programs(0) - 1)
        def _(low=low, count=count):
            for j in range(count):
                turned_out[low + j] = high(stat_out[low + j], basis_ref[low + j], NN)


def soap(meta, held, early, late, n, weight, first, second, average, stat, basis, late_panels, out_panels, pf, cap, rows):
    slots, panel, d = weight.shape
    width, group = 256, 8
    out_rows = late.shape[0] // n - rows
    big = pl.BlockSpec((slots, panel, width), lambda i, meta, held: (0, 0, i))
    small = pl.BlockSpec((slots, panel, panel), lambda i, meta, held: (0, 0, 0))
    shape = jax.ShapeDtypeStruct
    return pl.pallas_call(
        functools.partial(soap_kernel, (n, late_panels, out_panels, pf, cap, rows, out_rows, group)),
        grid_spec=pltpu.PrefetchScalarGridSpec(
            num_scalar_prefetch=2,
            grid=(d // width,),
            in_specs=[ANY] * 2 + [big] * 4 + [small] * 2,
            out_specs=[big] * 4 + [small] * 2,
            scratch_shapes=[
                pltpu.VMEM((slots, panel, d), BF),
                pltpu.VMEM((-(-slots // group), group * panel, group * panel), F32),
                pltpu.SemaphoreType.DMA,
            ],
        ),
        out_shape=[shape((slots, panel, d), F32)] * 4 + [shape((slots, panel, panel), F32)] * 2,
        compiler_params=params(),
        cost_estimate=QUICK,
        name="soap",
    )(meta, held, early, late, weight, first, second, average, stat, basis)


def orthonormal_kernel(columns_ref, out_ref):
    size = columns_ref.shape[0]
    out_ref[...] = columns_ref[...]
    for i in range(size):
        vector = out_ref[i]
        vector = vector * lax.rsqrt(jnp.sum(vector * vector, axis=0, keepdims=True))
        out_ref[i] = vector
        if i < size - 1:
            rest = out_ref[i + 1 :]
            out_ref[i + 1 :] = rest - jnp.sum(rest * vector[None], axis=1, keepdims=True) * vector[None]


def orthonormal(matrix):
    columns = jnp.transpose(matrix, (2, 1, 0))
    found = pl.pallas_call(
        orthonormal_kernel,
        in_specs=[VMEM],
        out_specs=VMEM,
        out_shape=jax.ShapeDtypeStruct(columns.shape, F32),
        compiler_params=params(),
        name="orthonormal",
    )(columns)
    return jnp.transpose(found, (2, 1, 0))


def adam_gain(gradient, weight, first_state, second):
    new_first = BETA_ONE * first_state + (1.0 - BETA_ONE) * gradient
    new_second = BETA_TWO * second + (1.0 - BETA_TWO) * gradient * gradient
    direction = (
        new_first
        / (1.0 - BETA_ONE**STEP)
        / (jnp.sqrt(new_second / (1.0 - BETA_TWO**STEP)) + ADAM_EPSILON)
    )
    return (weight - GAIN_RATE * direction, new_first, new_second)


def back_kernel(meta, dq, dk, dv, wq, wk, wv, out):
    out[...] = (mm(dq[...], wq[...], NN) + mm(dk[...], wk[...], NN) + mm(dv[...], wv[...], NN)).astype(BF)


def back_in(meta, dq, dk, dv, wq, wk, wv, n, low, high):
    tok, (qw, d) = dq.shape[0], wq.shape
    tile = tok // n
    rows = pl.BlockSpec((tile, qw), lambda i, meta: ((meta[1] - i - low + n) % n, 0))
    whole = pl.BlockSpec((qw, d), lambda i, meta: (0, 0))
    return pl.pallas_call(
        back_kernel,
        grid_spec=pltpu.PrefetchScalarGridSpec(
            num_scalar_prefetch=1,
            grid=(high - low,),
            in_specs=[rows] * 3 + [whole] * 3,
            out_specs=pl.BlockSpec((tile, d), lambda i, meta: (i, 0)),
        ),
        out_shape=jax.ShapeDtypeStruct(((high - low) * tile, d), BF),
        compiler_params=params(),
        cost_estimate=QUICK,
        name="back_in",
    )(meta, dq, dk, dv, wq, wk, wv)


def shards(
    tokens,
    cotangent,
    lengths,
    retrieve,
    owners,
    masters,
    first_moment,
    second_moment,
    averaged,
    statistics,
    bases,
    gains,
    gain_first,
    gain_second,
):
    tok, d = tokens.shape
    n_seq, n_tp = lax.axis_size("seq"), lax.axis_size("tp")
    me, z = lax.axis_index("seq"), lax.axis_index("tp")
    qw, ff = H // n_tp * HD, FF // n_tp
    slots_dev, panel = masters.shape[1:3]
    split = (slots_dev + 1) // 2
    docs, picks = lengths.shape[0], retrieve.shape[1]
    recalled = lax.dynamic_index_in_dim(retrieve, me, 0, keepdims=False)
    meta = jnp.concatenate([jnp.stack([me, z]).astype(I32), lengths, recalled])
    block = tok // n_tp
    pq, pf = qw // panel, ff // panel
    cap = -(-pf // n_seq)
    fs = cap * panel
    slot_ids = me * slots_dev + jnp.arange(slots_dev, dtype=I32)
    panel_ids = jnp.arange(1, owners.shape[0] + 1, dtype=I32)
    held = jnp.sum(jnp.where(slot_ids[:, None] == owners[None, :], panel_ids[None, :], 0), axis=1) - 1

    def mine(rows):
        return lax.dynamic_slice_in_dim(rows, z * block, block, 0)

    def whole_tp(rows):
        return lax.all_gather(rows, "tp", axis=0, tiled=True)

    def whole_seq(rows):
        return lax.all_gather(rows, "seq", axis=0, tiled=True)

    own = masters[0].astype(BF)
    pieces, _ = gather_seq([own[:split], own[split:]], n_seq)
    pieces = list(zip(*pieces, strict=True))
    q, k, v, normed_one, inner, share = project_in(
        meta, owners, tokens, gains, pieces, pq, pf, cap, slots_dev, split
    )
    (keys, values), _ = gather_seq([k, v], n_seq)
    weights = whole_tp(share).reshape(n_tp, -1, d)
    own_grads, keys[n_seq - 2], values[n_seq - 2] = pin(mine(cotangent), keys[n_seq - 2], values[n_seq - 2])
    grads_all = whole_seq(own_grads)
    attended, turned_heads, wide, logs = attend(meta, q, keys, values, docs, picks, block)
    heads = trade_tp([turned_heads[i * block : (i + 1) * block] for i in range(n_tp)], n_tp)
    mixed, left, right = mix(meta, tokens, gains, weights, heads)
    (left, right), _ = gather_seq([left, right], n_seq)
    (normed_two, hidden, d_gate, d_up), pairs, feed = feed_forward(meta, weights, grads_all, left + right, fs)

    last = len(routes(n_seq)[0])
    inner_rows, out_rows = share_rows(3 * qw, n_seq), share_rows(qw, n_seq)
    feed_sums_in = (d_gate, d_up, hidden, normed_two, grads_all)
    for at in range(last + 1):
        pairs = reduce_levels(pairs, n_seq, at)
        if at == last - 1:
            pairs, feed, feed_sums = pin(pairs, (feed[0], swap(feed[1], n_seq, 1)), feed_sums)
            feed = plus(*feed)
        elif at == 0:
            pairs, feed, feed_sums_in = pin(pairs, feed, feed_sums_in)
            feed_sums = feed_grads(meta, *feed_sums_in, fs)
    d_mixed, grad_gain_two, d_heads, outer = branch_back(
        meta, pairs, mixed, cotangent, gains, weights, heads, n_seq, 3 * fs
    )
    d_heads = trade_tp(d_heads, n_tp)
    outer = plus(outer[0], swap(outer[1], n_seq, 1))

    size = n_tp * out_rows
    parts = {}
    for m in range(0, n_seq, 2):
        at = reduce_place(n_seq, 0, m)[1]
        parts[m] = jnp.concatenate([feed[at * block : (at + 1) * block], outer[at * size : (at + 1) * size]], axis=0)
    d_heads, parts, feed_sums = pin(d_heads, parts, feed_sums)
    parts = [swap(part, n_seq, m) if m else part for m, part in parts.items()]
    feed_sums = lax.psum_scatter(feed_sums.reshape(-1, d), "tp", scatter_dimension=0, tiled=True)
    dq, *pairs = attend_back(meta, q, d_heads, wide, logs, keys, values, docs, picks)
    parts, feed_sums, dq, pairs = pin(parts, feed_sums, dq, pairs)
    pairs = reduce_levels(pairs, n_seq, 0)
    total = sum(part.astype(F32) for part in parts)
    output = (mixed + total[:block]).astype(BF)
    outer = [total[block + k * out_rows : block + (k + 1) * out_rows].astype(BF) for k in range(n_tp)]
    outputs = [output]
    for at in range(last + 1):
        if at:
            pairs = reduce_levels(pairs, n_seq, at)
            while len(outputs) < n_tp and (at == last or len(outputs) < 1 + 2 * at):
                outputs.append(ring(outputs[-1], n_tp, 1))
        pairs, outputs, feed_sums, dq = pin(pairs, outputs, feed_sums, dq)
    dk, dv = [plus(*pair) for pair in pairs]
    early = whole_seq(feed_sums).reshape(-1, panel, d)

    inputs = (meta, dq, dk, dv, inner[0], inner[1], inner[2], n_tp)
    total = back_in(*inputs, n_tp - 1, n_tp)
    total, lefts = pin(total, (dq, dk, dv))
    back_rest = back_in(meta, *lefts, *inputs[4:], 0, n_tp - 1)
    late = late_grads(meta, *lefts, normed_one, n_seq)

    def advance(late, step):
        if step == 1:
            late = plus(late[0], swap(late[1], n_seq, 1))
        elif step == 2:
            parts = direct_reduce(late, n_seq, inner_rows)
            late = sum(part.astype(F32) for part in parts).astype(BF)
            late = jnp.concatenate([late, outer], axis=0)
        elif step == 3:
            late = direct_gather(late, n_seq)
        elif step == 4:
            late = core_gather(late, n_seq)
        return late

    steps = max(2 * (n_tp - 1), 6)
    gain_steps = sum_steps(n_seq, n_tp)
    gather = []
    for step in range(steps):
        if step < n_tp - 1:
            k = n_tp - 2 - step
            came = ring(total, n_tp, -1)
            late = advance(late, step)
            if step == 0:
                outer = trade_tp(outer, n_tp)
            came, late, back_rest, outer = pin(came, late, back_rest, outer)
            if step == 0:
                outer = sum(part.astype(F32) for part in outer).astype(BF)
            part = back_rest[k * block : (k + 1) * block]
            if k:
                total = plus(part, came)
                continue
            d_normed_one = part.astype(F32) + came.astype(F32)
            unit_one, inverse_one, _ = norm_rows(mine(tokens).astype(F32), gains[0])
            grad_gain_one = jnp.sum(d_normed_one * unit_one, axis=0)
            grad_here = d_mixed + norm_back(d_normed_one, unit_one, inverse_one, gains[0])
            gain_total = jnp.stack([grad_gain_one, grad_gain_two[0]])
            gather.append(grad_here.astype(BF))
            continue
        if len(gather) < n_tp:
            gather.append(ring(gather[-1], n_tp, 1))
        if gain_steps:
            gain_total = gain_steps.pop(0)(gain_total)
        late = advance(late, step)
        if step == steps - 2:
            new_weight, new_first, new_second, new_average, new_stat, turned_basis = soap(
                meta, held, early, late, n_seq, masters[0], first_moment[0], second_moment[0], averaged[0],
                statistics[0], bases[0], 4 * pq, pq, pf, cap, inner_rows,
            )
            gather[-1], turned_basis, gain_total = pin(gather[-1], turned_basis, gain_total)
        elif step == steps - 1:
            new_basis = orthonormal(turned_basis)
            gather, new_basis, gain_total = pin(gather, new_basis, gain_total)
        else:
            gather[-1], late, gain_total = pin(gather[-1], late, gain_total)
    for step in gain_steps:
        gain_total = step(gain_total)
    output = place(meta, outputs, block)
    grad_input = place(meta, gather, block, F32)
    new_gains, new_gain_first, new_gain_second = adam_gain(gain_total, gains, gain_first, gain_second)
    return (
        output,
        grad_input,
        new_weight[None],
        new_first[None],
        new_second[None],
        new_average[None],
        new_stat[None],
        new_basis[None],
        new_gains,
        new_gain_first,
        new_gain_second,
    )


def solution(mesh):
    by_token, by_slot = P("seq", None), P("tp", "seq", None, None)
    in_specs = (by_token, by_token, P(), P(), P()) + (by_slot,) * 6 + (P(),) * 3
    out_specs = (by_token, by_token) + (by_slot,) * 6 + (P(),) * 3
    return jax.shard_map(shards, mesh=mesh, in_specs=in_specs, out_specs=out_specs, check_vma=False)
```

time: 576 us -> 519 us (0.901); the launches traced: 580 us -> 516 us
  waiting for transfers between devices: 299 us -> 257 us
  starting transfers between devices: 98.9 us -> 82.6 us
  between operations: 1.68 us -> 15.2 us
  Pallas kernels: 136 us -> 128 us
  other arithmetic: 27.2 us -> 20.3 us
    ppermute x24 -> x18, waiting for transfers between devices: 174 us -> 70.4 us  [ring(): lax.ppermute(value, 'tp', [(i, (i + step) % count) for i in range(count)])]
    ppermute x56 -> x67, waiting for transfers between devices: 114 us -> 153 us  [swap(): return lax.ppermute(value, 'seq', [(i, i ^ bit) for i in range(count)])]
    ppermute x56 -> x67, starting transfers between devices: 72.4 us -> 46.1 us  [swap(): return lax.ppermute(value, 'seq', [(i, i ^ bit) for i in range(count)])]
    all_gather x0 -> x3, waiting for transfers between devices: none -> 15.8 us  [the longest x1 13.3 us: whole_tp(): return lax.all_gather(rows, 'tp', axis=0, tiled=True)]
    ppermute x24 -> x18, starting transfers between devices: 19 us -> 32 us  [ring(): lax.ppermute(value, 'tp', [(i, (i + step) % count) for i in range(count)])]
    reduce_scatter x0 -> x1, waiting for transfers between devices: none -> 12.2 us  [shards(): lax.psum_scatter(feed_sums.reshape(-1, d), 'tp', scatter_dimension=0, til...]
    ppermute x5, waiting for transfers between devices: 11.9 us -> 5.62 us  [sum_steps(): lax.ppermute(v, axis, pairs)]
    convert_element_type x22 -> x15, other arithmetic: 16 us -> 11.2 us  [plus(): return (left.astype(F32) + right.astype(F32)).astype(left.dtype)]
  transfers between devices with their start and end apart: 85 -> 94, of which waited for: 42 -> 53; matrix products, arithmetic and copies ran while one was open for 6% -> 5% of each run, Pallas kernels for 18% -> 17%
where the time goes in v2:
time: 519 us; the launch traced here: 516 us
  waiting for transfers between devices  257 us (50%)
  Pallas kernels  128 us (25%)
  starting transfers between devices  82.6 us (16%)
  other arithmetic  20.3 us (4%)
  between operations  15.2 us (3%)
  local copies, waits for them, and re-layouts  12.8 us (2%)
    ppermute x67, waiting for transfers between devices, swap(): return lax.ppermute(value, 'seq', [(i, i ^ bit) for i in range(count)])  153 us
    ppermute x18, waiting for transfers between devices, ring(): lax.ppermute(value, 'tp', [(i, (i + step) % count) for i in range(count)])  70.4 us
    ppermute x67, starting transfers between devices, swap(): return lax.ppermute(value, 'seq', [(i, i ^ bit) for i in range(count)])  46.1 us
    ppermute x18, starting transfers between devices, ring(): lax.ppermute(value, 'tp', [(i, (i + step) % count) for i in range(count)])  32 us
    pallas_call x1, Pallas kernels, feed_forward(): pl.pallas_call(functools.partial(feed_kernel, (n, spans, fs)), grid_spec=...  23.3 us
    pallas_call x1, Pallas kernels, attend_back(): pl.pallas_call(functools.partial(attend_back_kernel, (n, docs, picks, qt,...  20.4 us
    all_gather x1, waiting for transfers between devices, whole_tp(): return lax.all_gather(rows, 'tp', axis=0, tiled=True)  13.3 us
    pallas_call x1, Pallas kernels, soap(): pl.pallas_call(functools.partial(soap_kernel, (n, late_panels, out_panels...  12.3 us
  transfers between devices with their start and end apart: 94, of which 53 were waited for; matrix products, arithmetic and copies ran while one was open for 5% of the time, Pallas kernels for 17%

profile of v2, /device:TPU:0, one launch (start us, length us, event | category | flops | bytes accessed | tf_op | source)
XLA Modules:
  0.0 515.6 jit_solution(11062316133587710517)
XLA Ops:
  9.6 2.9 collective-permute-start.1
  14.6 17.1 %collective-permute-done.4.refs_10_ = bf16[6,32,1024]{2,1,0:T(8,128)(2,1)S(1)} collective-permute-done((bf16[6,32,1024]{2,1,0:T(8,128)(2,1)S(1)}, bf16[6,32,1024]{2,1,0:T(8,128)(2,1)S(1)}, u32[]{:S(2)}, u32[]{:S(2)}) %collective-permute-start.4) | collective-permute-done | bytes 393248 | tf_op jit(solution)/shard_map/ppermute | solution.py:67
  36.1 10.9 %collective-permute-done.11.refs_14_ = bf16[6,32,1024]{2,1,0:T(8,128)(2,1)} collective-permute-done((bf16[6,32,1024]{2,1,0:T(8,128)(2,1)S(1)}, bf16[6,32,1024]{2,1,0:T(8,128)(2,1)}, u32[]{:S(2)}, u32[]{:S(2)}) %collective-permute-start.11) | collective-permute-done | bytes 393248 | tf_op jit(solution)/shard_map/ppermute | solution.py:67
  50.6 9.2 %project.1 = (bf16[1024,256]{1,0:T(8,128)(2,1)}, bf16[1024,256]{1,0:T(8,128)(2,1)}, bf16[1024,256]{1,0:T(8,128)(2,1)}, bf16[1024,1024]{1,0:T(8,128)(2,1)}, bf16[...) custom-call(s32[18]{0:T(128)} %pad_add_fusion.meta, s32[98]{0:T(128)} %owners.1, bf16[1024,1024]{1,0:T(8,128)(2,1)} %x_ref.3, ...), custom_call_target="tpu_custom_call" | custom-call | flops 1000 | bytes 1000 | tf_op jit(solution)/shard_map/project/pallas_call | solution.py:258
  64.1 10.9 %collective-permute-done.15.refs_2_.refs_6_ = bf16[1024,256]{1,0:T(8,128)(2,1)S(1)} collective-permute-done((bf16[1024,256]{1,0:T(8,128)(2,1)}, bf16[1024,256]{1,0:T(8,128)(2,1)S(1)}, u32[]{:S(2)}, u32[]{:S(2)}) %collective-permute-start.15) | collective-permute-done | bytes 524320 | tf_op jit(solution)/shard_map/ppermute | solution.py:67
  75.5 10.1 %collective-permute-done.18.refs_10_.refs_14_ = bf16[1024,256]{1,0:T(8,128)(2,1)S(1)} collective-permute-done((bf16[1024,256]{1,0:T(8,128)(2,1)}, bf16[1024,256]{1,0:T(8,128)(2,1)S(1)}, u32[]{:S(2)}, u32[]{:S(2)}) %collective-permute-start.18) | collective-permute-done | bytes 524320 | tf_op jit(solution)/shard_map/ppermute | solution.py:67
  92.2 8.3 %collective-permute-done.22.refs_6_.refs_10_ = bf16[1024,256]{1,0:T(8,128)(2,1)} collective-permute-done((bf16[1024,256]{1,0:T(8,128)(2,1)S(1)}, bf16[1024,256]{1,0:T(8,128)(2,1)}, u32[]{:S(2)}, u32[]{:S(2)}) %collective-permute-start.22) | collective-permute-done | bytes 524320 | tf_op jit(solution)/shard_map/ppermute | solution.py:67
  100.5 2.6 collective-permute-done.25.refs_14_.refs_18_
  106.9 11.7 %attend.1 = (bf16[1024,256]{1,0:T(8,128)(2,1)}, bf16[1024,256]{1,0:T(8,128)(2,1)}, f32[1024,256]{1,0:T(8,128)}, f32[2,1024]{1,0:T(2,128)}) custom-call(s32[18]{0:T(128)} %pad_add_fusion.meta, bf16[1024,256]{1,0:T(8,128)(2,1)} %get-tuple-element.253.q_ref, bf16[1024,256]{1,0:T(8,128)(2,1)} %get-tuple-element.254.refs_0_.refs_4_, bf16[1024,256]{1,0:T(8,128)(2,1)} %copy-done.8, ...), custom_call_target="tpu_custom_call" | custom-call | flops 1000 | bytes 1000 | tf_op jit(solution)/shard_map/attend/pallas_call | solution.py:392
  121.9 2.6 collective-permute-start.29
  126.1 4.4 collective-permute-done.28.refs_1_
  130.5 11.9 %collective-permute-done.29.refs_2_ = bf16[256,256]{1,0:T(8,128)(2,1)S(1)} collective-permute-done((bf16[256,256]{1,0:T(8,128)(2,1)S(1)}, bf16[256,256]{1,0:T(8,128)(2,1)S(1)}, u32[]{:S(2)}, u32[]{:S(2)}) %collective-permute-start.29) | collective-permute-done | bytes 131104 | tf_op jit(solution)/shard_map/ppermute | solution.py:143
  142.4 13.3 %all-gather.4.cloned.1.call-done = bf16[2176,1024]{1,0:T(8,128)(2,1)} async-done(((bf16[544,1024]{1,0:T(8,128)(2,1)}), bf16[2176,1024]{1,0:T(8,128)(2,1)}) %all-gather.4.cloned.1.call-update) | async-done | bytes 4456464 | tf_op jit(solution)/shard_map/all_gather | solution.py:1014
  155.7 5.1 mix.1
  165.0 9.8 %collective-permute-done.32.refs_2_ = bf16[256,512]{1,0:T(8,128)(2,1)S(1)} collective-permute-done((bf16[256,512]{1,0:T(8,128)(2,1)}, bf16[256,512]{1,0:T(8,128)(2,1)S(1)}, u32[]{:S(2)}, u32[]{:S(2)}) %collective-permute-start.32) | collective-permute-done | bytes 262176 | tf_op jit(solution)/shard_map/ppermute | solution.py:67
  177.2 3.8 collective-permute-done.35.refs_10_
  185.3 11.5 %collective-permute-done.39.refs_6_ = bf16[256,512]{1,0:T(8,128)(2,1)S(1)} collective-permute-done((bf16[256,512]{1,0:T(8,128)(2,1)S(1)}, bf16[256,512]{1,0:T(8,128)(2,1)S(1)}, u32[]{:S(2)}, u32[]{:S(2)}) %collective-permute-start.39) | collective-permute-done | bytes 262176 | tf_op jit(solution)/shard_map/ppermute | solution.py:67
  203.5 23.3 %feed_forward.1 = (bf16[2048,1024]{1,0:T(8,128)(2,1)}, bf16[2048,384]{1,0:T(8,128)(2,1)}, bf16[2048,384]{1,0:T(8,128)(2,1)}, bf16[2048,384]{1,0:T(8,128)(2,1)}, ...) custom-call(s32[18]{0:T(128)} %pad_add_fusion.meta, ...), custom_call_target="tpu_custom_call" | custom-call | flops 1000 | bytes 1000 | tf_op jit(solution)/shard_map/feed_forward/pallas_call | solution.py:631
  234.0 11.4 %feed_grads.1 = bf16[4,288,1024]{2,1,0:T(8,128)(2,1)} custom-call(s32[18]{0:T(128)} %pad_add_fusion.meta, bf16[2048,384]{1,0:T(8,128)(2,1)} %get-tuple-element.309.d_gate, bf16[2048,384]{1,0:T(8,128)(2,1)} %get-tuple-element.310.d_up, bf16[2048,384]{1,0:T(8,128)(2,1)} %get-tuple-element.311.hidden, bf16[2048,1024]{1,0:T(8,128)(2,1)} %get-tuple-element.312.normed, ...), custom_call_target="tpu_custom_call" | custom-call | flops 1000 | bytes 1000 | tf_op jit(solution)/shard_map/feed_grads/pallas_call | solution.py:745
  249.9 5.4 %collective-permute-done.50.left_b = bf16[256,512]{1,0:T(8,128)(2,1)S(1)} collective-permute-done((bf16[256,512]{1,0:T(8,128)(2,1)S(1)}, bf16[256,512]{1,0:T(8,128)(2,1)S(1)}, u32[]{:S(2)}, u32[]{:S(2)}) %collective-permute-start.50) | collective-permute-done | bytes 262176 | tf_op jit(solution)/shard_map/ppermute | solution.py:67
  256.9 7.8 %branch_back.1 = (f32[256,1024]{1,0:T(8,128)}, f32[1,1024]{1,0:T(1,128)}, bf16[256,256]{1,0:T(8,128)(2,1)}, bf16[256,256]{1,0:T(8,128)(2,1)}, bf16[256,256]{1,0:...) custom-call(s32[18]{0:T(128)} %pad_add_fusion.meta, ...), custom_call_target="tpu_custom_call" | custom-call | flops 1000 | bytes 1000 | tf_op jit(solution)/shard_map/branch_back/pallas_call | solution.py:690
  274.9 5.3 %collective-permute-done.53.refs_2_ = bf16[256,256]{1,0:T(8,128)(2,1)S(1)} collective-permute-done((bf16[256,256]{1,0:T(8,128)(2,1)S(1)}, bf16[256,256]{1,0:T(8,128)(2,1)S(1)}, u32[]{:S(2)}, u32[]{:S(2)}) %collective-permute-start.53) | collective-permute-done | bytes 131104 | tf_op jit(solution)/shard_map/ppermute | solution.py:143
  283.8 20.4 %attend_back.1 = (bf16[1024,256]{1,0:T(8,128)(2,1)}, bf16[4096,256]{1,0:T(8,128)(2,1)}, bf16[4096,256]{1,0:T(8,128)(2,1)}, bf16[4096,256]{1,0:T(8,128)(2,1)}, bf16[4096,256]{1,0:T(8,128)(2,1)}) custom-call(s32[18]{0:T(128)} %pad_add_fusion.meta, bf16[1024,256]{1,0:T(8,128)(2,1)} %get-tuple-element.253.q_ref, f32[1024,256]{1,0:T(8,128)} %get-tuple-element.333.wide_ref, ...), custom_call_target="tpu_custom_call" | custom-call | flops 1000 | bytes 1000 | tf_op jit(solution)/shard_map/attend_back/pallas_call | solution.py:510
  304.3 12.9 %collective-permute-done.57 = bf16[384,1024]{1,0:T(8,128)(2,1)} collective-permute-done((bf16[384,1024]{1,0:T(8,128)(2,1)S(1)}, bf16[384,1024]{1,0:T(8,128)(2,1)}, u32[]{:S(2)}, u32[]{:S(2)}) %collective-permute-start.57) | collective-permute-done | bytes 786464 | tf_op jit(solution)/shard_map/ppermute | solution.py:67
  317.2 12.2 %reduce-scatter.2.cloned.1.call-done = bf16[288,1024]{1,0:T(8,128)(2,1)} async-done(((bf16[1152,1024]{1,0:T(8,128)(2,1)}), bf16[288,1024]{1,0:T(8,128)(2,1)}) %reduce-scatter.2.cloned.1.call-update) | async-done | bytes 589840 | tf_op jit(solution)/shard_map/reduce_scatter | solution.py:1059
  338.8 3.1 collective-permute-start.61
  341.9 3.8 collective-permute-start.63
  345.7 12.0 %collective-permute-done.63.refs_1_ = bf16[256,1024]{1,0:T(8,128)(2,1)S(1)} collective-permute-done((bf16[256,1024]{1,0:T(8,128)(2,1)S(1)}, bf16[256,1024]{1,0:T(8,128)(2,1)S(1)}, u32[]{:S(2)}, u32[]{:S(2)}) %collective-permute-start.63) | collective-permute-done | bytes 524320 | tf_op jit(solution)/shard_map/ppermute | solution.py:143
  359.3 3.2 collective-permute-done.62
  365.6 7.0 %collective-permute-done.64.refs_2_ = bf16[256,1024]{1,0:T(8,128)(2,1)S(1)} collective-permute-done((bf16[256,1024]{1,0:T(8,128)(2,1)S(1)}, bf16[256,1024]{1,0:T(8,128)(2,1)S(1)}, u32[]{:S(2)}, u32[]{:S(2)}) %collective-permute-start.64) | collective-permute-done | bytes 524320 | tf_op jit(solution)/shard_map/ppermute | solution.py:143
  373.9 11.0 %collective-permute-done.65 = bf16[1024,256]{1,0:T(8,128)(2,1)} collective-permute-done((bf16[1024,256]{1,0:T(8,128)(2,1)S(1)}, bf16[1024,256]{1,0:T(8,128)(2,1)}, u32[]{:S(2)}, u32[]{:S(2)}) %collective-permute-start.65) | collective-permute-done | bytes 524320 | tf_op jit(solution)/shard_map/ppermute | solution.py:67
  393.2 3.6 back_in.2
  401.3 5.5 %back_in.3 = bf16[768,1024]{1,0:T(8,128)(2,1)} custom-call(s32[18]{0:T(128)} %pad_add_fusion.meta, bf16[1024,256]{1,0:T(8,128)(2,1)} %get-tuple-element.382.dq, bf16[1024,256]{1,0:T(8,128)(2,1)} %add_convert_fusion.10.dk, bf16[1024,256]{1,0:T(8,128)(2,1)} %add_convert_fusion.9.dv, bf16[256,1024]{1,0:T(8,128)(2,1)} %bitcast.39, bf16[256,1024]{1,0:T(8,128)(2,1)} %bitcast.37, ...), custom_call_target="tpu_custom_call" | custom-call | flops 1000 | bytes 1000 | tf_op jit(solution)/shard_map/back_in/pallas_call | solution.py:962
  406.8 6.0 %late_grads.1 = (bf16[384,1024]{1,0:T(8,128)(2,1)}, bf16[384,1024]{1,0:T(8,128)(2,1)}) custom-call(s32[18]{0:T(128)} %pad_add_fusion.meta, bf16[1024,256]{1,0:T(8,128)(2,1)} %get-tuple-element.382.dq, bf16[1024,256]{1,0:T(8,128)(2,1)} %add_convert_fusion.10.dk, bf16[1024,256]{1,0:T(8,128)(2,1)} %add_convert_fusion.9.dv, ...), custom_call_target="tpu_custom_call" | custom-call | flops 1000 | bytes 1000 | tf_op jit(solution)/shard_map/late_grads/pallas_call | solution.py:783
  413.1 3.4 collective-permute-start.72
  417.1 11.3 %collective-permute-done.72 = bf16[256,1024]{1,0:T(8,128)(2,1)S(1)} collective-permute-done((bf16[256,1024]{1,0:T(8,128)(2,1)S(1)}, bf16[256,1024]{1,0:T(8,128)(2,1)S(1)}, u32[]{:S(2)}, u32[]{:S(2)}) %collective-permute-start.72) | collective-permute-done | bytes 524320 | tf_op jit(solution)/shard_map/ppermute | solution.py:143
  432.2 4.3 collective-permute-start.74
  436.5 3.1 collective-permute-done.76
  439.8 7.5 %collective-permute-done.74 = bf16[256,1024]{1,0:T(8,128)(2,1)S(1)} collective-permute-done((bf16[256,1024]{1,0:T(8,128)(2,1)S(1)}, bf16[256,1024]{1,0:T(8,128)(2,1)S(1)}, u32[]{:S(2)}, u32[]{:S(2)}) %collective-permute-start.74) | collective-permute-done | bytes 524320 | tf_op jit(solution)/shard_map/ppermute | solution.py:143
  453.2 3.6 collective-permute-done.79
  456.8 3.2 collective-permute-done.80
  467.6 12.3 %soap.1 = (f32[13,32,1024]{2,1,0:T(8,128)}, f32[13,32,1024]{2,1,0:T(8,128)}, f32[13,32,1024]{2,1,0:T(8,128)}, f32[13,32,1024]{2,1,0:T(8,128)}, f32[13,32,32]{2,1,0:T(8,128)}, /*index=5*/f32[13,32,32]{2,1,0:T(8,128)}) custom-call(s32[18]{0:T(128)} %pad_add_fusion.meta, s32[13]{0:T(128)} %broadcast_add_fusion.held, bf16[72,32,1024]{2,1,0:T(8,128)(2,1)} %bitcast.33, ...), custom_call_target="tpu_custom_call" | custom-call | flops 1000 | bytes 1000 | tf_op jit(solution)/shard_map/soap/pallas_call | solution.py:897
  479.9 3.2 collective-permute-start.86
  486.4 4.6 orthonormal.1
  491.0 4.5 collective-permute-done.86.refs_3_
  496.6 2.5 collective-permute-done.88
  500.0 3.0 place.2
  503.0 3.9 place.3
  (354 shorter events, 129.8 us)
Async XLA Ops:
  7.2 148.5 %all-gather.4.cloned.1.call-start = ((), (), s32[]{:S(2)}) async-start(), calls=%async_computation.1 | async-start | bytes 5570560 | tf_op jit(solution)/shard_map/all_gather | solution.py:1014
  9.4 23.7 %collective-permute-start = (bf16[7,32,1024]{2,1,0:T(8,128)(2,1)S(1)}, bf16[7,32,1024]{2,1,0:T(8,128)(2,1)S(1)}, u32[]{:S(2)}, u32[]{:S(2)}) collective-permute-start(bf16[7,32,1024]{2,1,0:T(8,128)(2,1)S(1)} %slice.255.refs_0_), channel_id=1, source_target_pairs={{0,4},{4,0},{8,12},{12,8},{16,20},{20,16},{24,28},{28,24},{1,5},{5... | collective-permute-start | bytes 1376264 | tf_op jit(solution)/shard_map/ppermute | solution.py:67
  9.6 23.6 %collective-permute-start.1 = (bf16[7,32,1024]{2,1,0:T(8,128)(2,1)S(1)}, bf16[7,32,1024]{2,1,0:T(8,128)(2,1)S(1)}, u32[]{:S(2)}, u32[]{:S(2)}) collective-permute-start(bf16[7,32,1024]{2,1,0:T(8,128)(2,1)S(1)} %slice.255.refs_0_), channel_id=1, source_target_pairs={{0,8},{4,12},{8,0},{12,4},{16,24},{20,28},{24,16},{28,20},{1,9},{5... | collective-permute-start | bytes 1376264 | tf_op jit(solution)/shard_map/ppermute | solution.py:67
  12.5 20.7 %collective-permute-start.2 = (bf16[7,32,1024]{2,1,0:T(8,128)(2,1)S(1)}, bf16[7,32,1024]{2,1,0:T(8,128)(2,1)S(1)}, u32[]{:S(2)}, u32[]{:S(2)}) collective-permute-start(bf16[7,32,1024]{2,1,0:T(8,128)(2,1)S(1)} %slice.255.refs_0_), channel_id=1, source_target_pairs={{0,16},{4,20},{8,24},{12,28},{16,0},{20,4},{24,8},{28,12},{1,17},{... | collective-permute-start | bytes 1376264 | tf_op jit(solution)/shard_map/ppermute | solution.py:67
  14.0 17.6 %collective-permute-start.4 = (bf16[6,32,1024]{2,1,0:T(8,128)(2,1)S(1)}, bf16[6,32,1024]{2,1,0:T(8,128)(2,1)S(1)}, u32[]{:S(2)}, u32[]{:S(2)}) collective-permute-start(bf16[6,32,1024]{2,1,0:T(8,128)(2,1)S(1)} %slice.256.refs_8_), channel_id=1, source_target_pairs={{0,8},{4,12},{8,0},{12,4},{16,24},{20,28},{24,16},{28,20},{1,9},{5... | collective-permute-start | bytes 1179656 | tf_op jit(solution)/shard_map/ppermute | solution.py:67
  14.6 18.6 %collective-permute-start.5 = (bf16[6,32,1024]{2,1,0:T(8,128)(2,1)S(1)}, bf16[6,32,1024]{2,1,0:T(8,128)(2,1)S(1)}, u32[]{:S(2)}, u32[]{:S(2)}) collective-permute-start(bf16[6,32,1024]{2,1,0:T(8,128)(2,1)S(1)} %slice.256.refs_8_), channel_id=1, source_target_pairs={{0,16},{4,20},{8,24},{12,28},{16,0},{20,4},{24,8},{28,12},{1,17},{... | collective-permute-start | bytes 1179656 | tf_op jit(solution)/shard_map/ppermute | solution.py:67
  33.3 13.7 %collective-permute-start.6 = (bf16[7,32,1024]{2,1,0:T(8,128)(2,1)S(1)}, bf16[7,32,1024]{2,1,0:T(8,128)(2,1)S(1)}, u32[]{:S(2)}, u32[]{:S(2)}) collective-permute-start(bf16[7,32,1024]{2,1,0:T(8,128)(2,1)S(1)} %collective-permute-done.1.refs_2_), channel_id=1, source_target_pairs={{0,4},{4,0},{8,12},{12,8},{16,20},{20,16},{24,28},{28,24},{1,5},{5... | collective-permute-start | bytes 1376264 | tf_op jit(solution)/shard_map/ppermute | solution.py:67
  59.8 143.6 %all-gather.6.cloned.1.call-start = ((), (), s32[]{:S(2)}) async-start(), calls=%async_computation.2 | async-start | bytes 4718592 | tf_op jit(solution)/shard_map/all_gather | solution.py:1017
  60.0 15.0 %collective-permute-start.15 = (bf16[1024,256]{1,0:T(8,128)(2,1)}, bf16[1024,256]{1,0:T(8,128)(2,1)S(1)}, u32[]{:S(2)}, u32[]{:S(2)}) collective-permute-start(bf16[1024,256]{1,0:T(8,128)(2,1)} %get-tuple-element.254.refs_0_.refs_4_), channel_id=1, source_target_pairs={{0,8},{4,12},{8,0},{12,4},{16,24},{20,28},{24,16},{28,20},{1,9},{5... | collective-permute-start | bytes 1572872 | tf_op jit(solution)/shard_map/ppermute | solution.py:67
  60.5 15.0 %collective-permute-start.16 = (bf16[1024,256]{1,0:T(8,128)(2,1)}, bf16[1024,256]{1,0:T(8,128)(2,1)S(1)}, u32[]{:S(2)}, u32[]{:S(2)}) collective-permute-start(bf16[1024,256]{1,0:T(8,128)(2,1)} %get-tuple-element.254.refs_0_.refs_4_), channel_id=1, source_target_pairs={{0,16},{4,20},{8,24},{12,28},{16,0},{20,4},{24,8},{28,12},{1,17},{... | collective-permute-start | bytes 1572872 | tf_op jit(solution)/shard_map/ppermute | solution.py:67
  61.3 14.3 %collective-permute-start.17 = (bf16[1024,256]{1,0:T(8,128)(2,1)}, bf16[1024,256]{1,0:T(8,128)(2,1)S(1)}, u32[]{:S(2)}, u32[]{:S(2)}) collective-permute-start(bf16[1024,256]{1,0:T(8,128)(2,1)} %get-tuple-element.261.refs_8_.refs_12_), channel_id=1, source_target_pairs={{0,4},{4,0},{8,12},{12,8},{16,20},{20,16},{24,28},{28,24},{1,5},{5... | collective-permute-start | bytes 1572872 | tf_op jit(solution)/shard_map/ppermute | solution.py:67
  61.3 24.4 %collective-permute-start.18 = (bf16[1024,256]{1,0:T(8,128)(2,1)}, bf16[1024,256]{1,0:T(8,128)(2,1)S(1)}, u32[]{:S(2)}, u32[]{:S(2)}) collective-permute-start(bf16[1024,256]{1,0:T(8,128)(2,1)} %get-tuple-element.261.refs_8_.refs_12_), channel_id=1, source_target_pairs={{0,8},{4,12},{8,0},{12,4},{16,24},{20,28},{24,16},{28,20},{1,9},{5... | collective-permute-start | bytes 1572872 | tf_op jit(solution)/shard_map/ppermute | solution.py:67
  62.8 23.2 %collective-permute-start.19 = (bf16[1024,256]{1,0:T(8,128)(2,1)}, bf16[1024,256]{1,0:T(8,128)(2,1)}, u32[]{:S(2)}, u32[]{:S(2)}) collective-permute-start(bf16[1024,256]{1,0:T(8,128)(2,1)} %get-tuple-element.261.refs_8_.refs_12_), channel_id=1, source_target_pairs={{0,16},{4,20},{8,24},{12,28},{16,0},{20,4},{24,8},{28,12},{1,17},{... | collective-permute-start | bytes 1572872 | tf_op jit(solution)/shard_map/ppermute | solution.py:67
  86.0 14.4 %collective-permute-start.22 = (bf16[1024,256]{1,0:T(8,128)(2,1)S(1)}, bf16[1024,256]{1,0:T(8,128)(2,1)}, u32[]{:S(2)}, u32[]{:S(2)}) collective-permute-start(bf16[1024,256]{1,0:T(8,128)(2,1)S(1)} %collective-permute-done.15.refs_2_.refs_6_), channel_id=1, source_target_pairs={{0,16},{4,20},{8,24},{12,28},{16,0},{20,4},{24,8},{28,12},{1,17},{... | collective-permute-start | bytes 1572872 | tf_op jit(solution)/shard_map/ppermute | solution.py:67
  87.0 13.4 %collective-permute-start.23 = (bf16[1024,256]{1,0:T(8,128)(2,1)S(1)}, bf16[1024,256]{1,0:T(8,128)(2,1)}, u32[]{:S(2)}, u32[]{:S(2)}) collective-permute-start(bf16[1024,256]{1,0:T(8,128)(2,1)S(1)} %collective-permute-done.18.refs_10_.refs_14_), channel_id=1, source_target_pairs={{0,4},{4,0},{8,12},{12,8},{16,20},{20,16},{24,28},{28,24},{1,5},{5... | collective-permute-start | bytes 1572872 | tf_op jit(solution)/shard_map/ppermute | solution.py:67
  88.8 14.3 %collective-permute-start.25 = (bf16[1024,256]{1,0:T(8,128)(2,1)}, bf16[1024,256]{1,0:T(8,128)(2,1)}, u32[]{:S(2)}, u32[]{:S(2)}) collective-permute-start(bf16[1024,256]{1,0:T(8,128)(2,1)} %collective-permute-done.19.refs_12_.refs_16_), channel_id=1, source_target_pairs={{0,8},{4,12},{8,0},{12,4},{16,24},{20,28},{24,16},{28,20},{1,9},{5... | collective-permute-start | bytes 1572872 | tf_op jit(solution)/shard_map/ppermute | solution.py:67
  103.1 226.3 %reduce-scatter.2.cloned.1.call-start = ((), (), s32[]{:S(2)}) async-start(), calls=%async_computation.3 | async-start | bytes 2949120 | tf_op jit(solution)/shard_map/reduce_scatter | solution.py:1059
  121.9 20.4 %collective-permute-start.29 = (bf16[256,256]{1,0:T(8,128)(2,1)S(1)}, bf16[256,256]{1,0:T(8,128)(2,1)S(1)}, u32[]{:S(2)}, u32[]{:S(2)}) collective-permute-start(bf16[256,256]{1,0:T(8,128)(2,1)S(1)} %get-tuple-element.487), channel_id=1, source_target_pairs={{0,2},{1,3},{2,0},{3,1},{4,6},{5,7},{6,4},{7,5},{8,10},{9,11},{10,... | collective-permute-start | bytes 393224 | tf_op jit(solution)/shard_map/ppermute | solution.py:143
  124.6 17.8 %collective-permute-start.30 = (bf16[256,256]{1,0:T(8,128)(2,1)S(1)}, bf16[256,256]{1,0:T(8,128)(2,1)S(1)}, u32[]{:S(2)}, u32[]{:S(2)}) collective-permute-start(bf16[256,256]{1,0:T(8,128)(2,1)S(1)} %get-tuple-element.486), channel_id=1, source_target_pairs={{0,3},{1,0},{2,1},{3,2},{4,7},{5,4},{6,5},{7,6},{8,11},{9,8},{10,9... | collective-permute-start | bytes 393224 | tf_op jit(solution)/shard_map/ppermute | solution.py:143
  160.9 13.9 %collective-permute-start.32 = (bf16[256,512]{1,0:T(8,128)(2,1)}, bf16[256,512]{1,0:T(8,128)(2,1)S(1)}, u32[]{:S(2)}, u32[]{:S(2)}) collective-permute-start(bf16[256,512]{1,0:T(8,128)(2,1)} %get-tuple-element.279.refs_0_), channel_id=1, source_target_pairs={{0,8},{4,12},{8,0},{12,4},{16,24},{20,28},{24,16},{28,20},{1,9},{5... | collective-permute-start | bytes 786440 | tf_op jit(solution)/shard_map/ppermute | solution.py:67
  162.4 14.8 %collective-permute-start.33 = (bf16[256,512]{1,0:T(8,128)(2,1)}, bf16[256,512]{1,0:T(8,128)(2,1)S(1)}, u32[]{:S(2)}, u32[]{:S(2)}) collective-permute-start(bf16[256,512]{1,0:T(8,128)(2,1)} %get-tuple-element.279.refs_0_), channel_id=1, source_target_pairs={{0,16},{4,20},{8,24},{12,28},{16,0},{20,4},{24,8},{28,12},{1,17},{... | collective-permute-start | bytes 786440 | tf_op jit(solution)/shard_map/ppermute | solution.py:67
  164.8 16.2 %collective-permute-start.35 = (bf16[256,512]{1,0:T(8,128)(2,1)}, bf16[256,512]{1,0:T(8,128)(2,1)S(1)}, u32[]{:S(2)}, u32[]{:S(2)}) collective-permute-start(bf16[256,512]{1,0:T(8,128)(2,1)} %get-tuple-element.286.refs_8_), channel_id=1, source_target_pairs={{0,8},{4,12},{8,0},{12,4},{16,24},{20,28},{24,16},{28,20},{1,9},{5... | collective-permute-start | bytes 786440 | tf_op jit(solution)/shard_map/ppermute | solution.py:67
  164.9 17.6 %collective-permute-start.36 = (bf16[256,512]{1,0:T(8,128)(2,1)}, bf16[256,512]{1,0:T(8,128)(2,1)S(1)}, u32[]{:S(2)}, u32[]{:S(2)}) collective-permute-start(bf16[256,512]{1,0:T(8,128)(2,1)} %get-tuple-element.286.refs_8_), channel_id=1, source_target_pairs={{0,16},{4,20},{8,24},{12,28},{16,0},{20,4},{24,8},{28,12},{1,17},{... | collective-permute-start | bytes 786440 | tf_op jit(solution)/shard_map/ppermute | solution.py:67
  182.5 14.3 %collective-permute-start.39 = (bf16[256,512]{1,0:T(8,128)(2,1)S(1)}, bf16[256,512]{1,0:T(8,128)(2,1)S(1)}, u32[]{:S(2)}, u32[]{:S(2)}) collective-permute-start(bf16[256,512]{1,0:T(8,128)(2,1)S(1)} %collective-permute-done.32.refs_2_), channel_id=1, source_target_pairs={{0,16},{4,20},{8,24},{12,28},{16,0},{20,4},{24,8},{28,12},{1,17},{... | collective-permute-start | bytes 786440 | tf_op jit(solution)/shard_map/ppermute | solution.py:67
  183.3 13.5 %collective-permute-start.40 = (bf16[256,512]{1,0:T(8,128)(2,1)S(1)}, bf16[256,512]{1,0:T(8,128)(2,1)S(1)}, u32[]{:S(2)}, u32[]{:S(2)}) collective-permute-start(bf16[256,512]{1,0:T(8,128)(2,1)S(1)} %collective-permute-done.35.refs_10_), channel_id=1, source_target_pairs={{0,4},{4,0},{8,12},{12,8},{16,20},{20,16},{24,28},{28,24},{1,5},{5... | collective-permute-start | bytes 786440 | tf_op jit(solution)/shard_map/ppermute | solution.py:67
  183.6 13.2 %collective-permute-start.41 = (bf16[256,512]{1,0:T(8,128)(2,1)S(1)}, bf16[256,512]{1,0:T(8,128)(2,1)S(1)}, u32[]{:S(2)}, u32[]{:S(2)}) collective-permute-start(bf16[256,512]{1,0:T(8,128)(2,1)S(1)} %collective-permute-done.36.refs_12_), channel_id=1, source_target_pairs={{0,4},{4,0},{8,12},{12,8},{16,20},{20,16},{24,28},{28,24},{1,5},{5... | collective-permute-start | bytes 786440 | tf_op jit(solution)/shard_map/ppermute | solution.py:67
  184.4 14.5 %collective-permute-start.42 = (bf16[256,512]{1,0:T(8,128)(2,1)S(1)}, bf16[256,512]{1,0:T(8,128)(2,1)S(1)}, u32[]{:S(2)}, u32[]{:S(2)}) collective-permute-start(bf16[256,512]{1,0:T(8,128)(2,1)S(1)} %collective-permute-done.36.refs_12_), channel_id=1, source_target_pairs={{0,8},{4,12},{8,0},{12,4},{16,24},{20,28},{24,16},{28,20},{1,9},{5... | collective-permute-start | bytes 786440 | tf_op jit(solution)/shard_map/ppermute | solution.py:67
  231.6 16.1 %collective-permute-start.49 = (bf16[1024,1024]{1,0:T(8,128)(2,1)}, bf16[1024,1024]{1,0:T(8,128)(2,1)S(1)}, u32[]{:S(2)}, u32[]{:S(2)}) collective-permute-start(bf16[1024,1024]{1,0:T(8,128)(2,1)} %get-tuple-element.308), channel_id=1, source_target_pairs={{0,4},{4,0},{8,12},{12,8},{16,20},{20,16},{24,28},{28,24},{1,5},{5... | collective-permute-start | bytes 6291464 | tf_op jit(solution)/shard_map/ppermute | solution.py:67
  231.9 14.1 %collective-permute-start.48 = (bf16[512,512]{1,0:T(8,128)(2,1)S(1)}, bf16[512,512]{1,0:T(8,128)(2,1)S(1)}, u32[]{:S(2)}, u32[]{:S(2)}) collective-permute-start(bf16[512,512]{1,0:T(8,128)(2,1)S(1)} %get-tuple-element.306), channel_id=1, source_target_pairs={{0,8},{4,12},{8,0},{12,4},{16,24},{20,28},{24,16},{28,20},{1,9},{5... | collective-permute-start | bytes 1572872 | tf_op jit(solution)/shard_map/ppermute | solution.py:67
  233.1 13.8 %collective-permute-start.47 = (bf16[512,512]{1,0:T(8,128)(2,1)S(1)}, bf16[512,512]{1,0:T(8,128)(2,1)S(1)}, u32[]{:S(2)}, u32[]{:S(2)}) collective-permute-start(bf16[512,512]{1,0:T(8,128)(2,1)S(1)} %get-tuple-element.304), channel_id=1, source_target_pairs={{0,16},{4,20},{8,24},{12,28},{16,0},{20,4},{24,8},{28,12},{1,17},{... | collective-permute-start | bytes 1572872 | tf_op jit(solution)/shard_map/ppermute | solution.py:67
  280.2 187.4 %all-gather.8.cloned.1.call-start = ((), (), s32[]{:S(2)}) async-start(), calls=%async_computation.4 | async-start | bytes 5308416 | tf_op jit(solution)/shard_map/all_gather | solution.py:1017
  280.2 24.0 %collective-permute-start.56 = (bf16[384,1024]{1,0:T(8,128)(2,1)S(1)}, bf16[384,1024]{1,0:T(8,128)(2,1)}, u32[]{:S(2)}, u32[]{:S(2)}) collective-permute-start(bf16[384,1024]{1,0:T(8,128)(2,1)S(1)} %get-tuple-element.329), channel_id=1, source_target_pairs={{0,8},{4,12},{8,0},{12,4},{16,24},{20,28},{24,16},{28,20},{1,9},{5... | collective-permute-start | bytes 2359304 | tf_op jit(solution)/shard_map/ppermute | solution.py:67
  281.1 36.1 %collective-permute-start.57 = (bf16[384,1024]{1,0:T(8,128)(2,1)S(1)}, bf16[384,1024]{1,0:T(8,128)(2,1)}, u32[]{:S(2)}, u32[]{:S(2)}) collective-permute-start(bf16[384,1024]{1,0:T(8,128)(2,1)S(1)} %get-tuple-element.330), channel_id=1, source_target_pairs={{0,16},{4,20},{8,24},{12,28},{16,0},{20,4},{24,8},{28,12},{1,17},{... | collective-permute-start | bytes 2359304 | tf_op jit(solution)/shard_map/ppermute | solution.py:67
  282.4 34.7 %collective-permute-start.58 = (bf16[384,1024]{1,0:T(8,128)(2,1)S(1)}, bf16[384,1024]{1,0:T(8,128)(2,1)}, u32[]{:S(2)}, u32[]{:S(2)}) collective-permute-start(bf16[384,1024]{1,0:T(8,128)(2,1)S(1)} %get-tuple-element.331), channel_id=1, source_target_pairs={{0,24},{4,28},{8,16},{12,20},{16,8},{20,12},{24,0},{28,4},{1,25},{... | collective-permute-start | bytes 2359304 | tf_op jit(solution)/shard_map/ppermute | solution.py:67
  337.3 25.3 %collective-permute-start.62 = (bf16[2048,256]{1,0:T(8,128)(2,1)S(1)}, bf16[2048,256]{1,0:T(8,128)(2,1)S(1)}, u32[]{:S(2)}, u32[]{:S(2)}) collective-permute-start(bf16[2048,256]{1,0:T(8,128)(2,1)S(1)} %get-tuple-element.357), channel_id=1, source_target_pairs={{0,8},{4,12},{8,0},{12,4},{16,24},{20,28},{24,16},{28,20},{1,9},{5... | collective-permute-start | bytes 3145736 | tf_op jit(solution)/shard_map/ppermute | solution.py:67
  338.8 26.5 %collective-permute-start.61 = (bf16[2048,256]{1,0:T(8,128)(2,1)S(1)}, bf16[2048,256]{1,0:T(8,128)(2,1)S(1)}, u32[]{:S(2)}, u32[]{:S(2)}) collective-permute-start(bf16[2048,256]{1,0:T(8,128)(2,1)S(1)} %get-tuple-element.355), channel_id=1, source_target_pairs={{0,16},{4,20},{8,24},{12,28},{16,0},{20,4},{24,8},{28,12},{1,17},{... | collective-permute-start | bytes 3145736 | tf_op jit(solution)/shard_map/ppermute | solution.py:67
  341.9 15.8 %collective-permute-start.63 = (bf16[256,1024]{1,0:T(8,128)(2,1)S(1)}, bf16[256,1024]{1,0:T(8,128)(2,1)S(1)}, u32[]{:S(2)}, u32[]{:S(2)}) collective-permute-start(bf16[256,1024]{1,0:T(8,128)(2,1)S(1)} %fusion.10.refs_0_), channel_id=1, source_target_pairs={{0,1},{1,2},{2,3},{3,0},{4,5},{5,6},{6,7},{7,4},{8,9},{9,10},{10,1... | collective-permute-start | bytes 1572872 | tf_op jit(solution)/shard_map/ppermute | solution.py:143
  357.7 14.9 %collective-permute-start.64 = (bf16[256,1024]{1,0:T(8,128)(2,1)S(1)}, bf16[256,1024]{1,0:T(8,128)(2,1)S(1)}, u32[]{:S(2)}, u32[]{:S(2)}) collective-permute-start(bf16[256,1024]{1,0:T(8,128)(2,1)S(1)} %collective-permute-done.63.refs_1_), channel_id=1, source_target_pairs={{0,1},{1,2},{2,3},{3,0},{4,5},{5,6},{6,7},{7,4},{8,9},{9,10},{10,1... | collective-permute-start | bytes 1572872 | tf_op jit(solution)/shard_map/ppermute | solution.py:143
  373.8 14.1 %collective-permute-start.67 = (bf16[256,1024]{1,0:T(8,128)(2,1)S(1)}, bf16[256,1024]{1,0:T(8,128)(2,1)}, u32[]{:S(2)}, u32[]{:S(2)}) collective-permute-start(bf16[256,1024]{1,0:T(8,128)(2,1)S(1)} %collective-permute-done.64.refs_2_), channel_id=1, source_target_pairs={{0,1},{1,2},{2,3},{3,0},{4,5},{5,6},{6,7},{7,4},{8,9},{9,10},{10,1... | collective-permute-start | bytes 1572872 | tf_op jit(solution)/shard_map/ppermute | solution.py:143
  396.8 16.0 %collective-permute-start.68 = (bf16[256,1024]{1,0:T(8,128)(2,1)}, bf16[256,1024]{1,0:T(8,128)(2,1)S(1)}, u32[]{:S(2)}, u32[]{:S(2)}) collective-permute-start(bf16[256,1024]{1,0:T(8,128)(2,1)} %back_in.2), channel_id=1, source_target_pairs={{0,3},{1,0},{2,1},{3,2},{4,7},{5,4},{6,5},{7,6},{8,11},{9,8},{10,9... | collective-permute-start | bytes 1572872 | tf_op jit(solution)/shard_map/ppermute | solution.py:143
  396.8 16.0 %collective-permute-start.69 = (bf16[32,1024]{1,0:T(8,128)(2,1)S(1)}, bf16[32,1024]{1,0:T(8,128)(2,1)S(1)}, u32[]{:S(2)}, u32[]{:S(2)}) collective-permute-start(bf16[32,1024]{1,0:T(8,128)(2,1)S(1)} %get-tuple-element.484), channel_id=1, source_target_pairs={{0,1},{1,2},{2,3},{3,0},{4,5},{5,6},{6,7},{7,4},{8,9},{9,10},{10,1... | collective-permute-start | bytes 196616 | tf_op jit(solution)/shard_map/ppermute | solution.py:143
  398.9 13.9 %collective-permute-start.70 = (bf16[32,1024]{1,0:T(8,128)(2,1)S(1)}, bf16[32,1024]{1,0:T(8,128)(2,1)S(1)}, u32[]{:S(2)}, u32[]{:S(2)}) collective-permute-start(bf16[32,1024]{1,0:T(8,128)(2,1)S(1)} %get-tuple-element.483), channel_id=1, source_target_pairs={{0,2},{1,3},{2,0},{3,1},{4,6},{5,7},{6,4},{7,5},{8,10},{9,11},{10,... | collective-permute-start | bytes 196616 | tf_op jit(solution)/shard_map/ppermute | solution.py:143
  398.9 13.9 %collective-permute-start.71 = (bf16[32,1024]{1,0:T(8,128)(2,1)S(1)}, bf16[32,1024]{1,0:T(8,128)(2,1)S(1)}, u32[]{:S(2)}, u32[]{:S(2)}) collective-permute-start(bf16[32,1024]{1,0:T(8,128)(2,1)S(1)} %get-tuple-element.482), channel_id=1, source_target_pairs={{0,3},{1,0},{2,1},{3,2},{4,7},{5,4},{6,5},{7,6},{8,11},{9,8},{10,9... | collective-permute-start | bytes 196616 | tf_op jit(solution)/shard_map/ppermute | solution.py:143
  413.1 15.3 %collective-permute-start.72 = (bf16[256,1024]{1,0:T(8,128)(2,1)S(1)}, bf16[256,1024]{1,0:T(8,128)(2,1)S(1)}, u32[]{:S(2)}, u32[]{:S(2)}) collective-permute-start(bf16[256,1024]{1,0:T(8,128)(2,1)S(1)} %add_convert_fusion.8), channel_id=1, source_target_pairs={{0,3},{1,0},{2,1},{3,2},{4,7},{5,4},{6,5},{7,6},{8,11},{9,8},{10,9... | collective-permute-start | bytes 1572872 | tf_op jit(solution)/shard_map/ppermute | solution.py:143
  432.2 15.1 %collective-permute-start.74 = (bf16[256,1024]{1,0:T(8,128)(2,1)S(1)}, bf16[256,1024]{1,0:T(8,128)(2,1)S(1)}, u32[]{:S(2)}, u32[]{:S(2)}) collective-permute-start(bf16[256,1024]{1,0:T(8,128)(2,1)S(1)} %add_convert_fusion.7), channel_id=1, source_target_pairs={{0,3},{1,0},{2,1},{3,2},{4,7},{5,4},{6,5},{7,6},{8,11},{9,8},{10,9... | collective-permute-start | bytes 1572872 | tf_op jit(solution)/shard_map/ppermute | solution.py:143
  448.3 13.8 %collective-permute-start.78 = (bf16[256,1024]{1,0:T(8,128)(2,1)S(1)}, bf16[256,1024]{1,0:T(8,128)(2,1)S(1)}, u32[]{:S(2)}, u32[]{:S(2)}) collective-permute-start(bf16[256,1024]{1,0:T(8,128)(2,1)S(1)} %fusion.7.refs_0_), channel_id=1, source_target_pairs={{0,1},{1,2},{2,3},{3,0},{4,5},{5,6},{6,7},{7,4},{8,9},{9,10},{10,1... | collective-permute-start | bytes 1572872 | tf_op jit(solution)/shard_map/ppermute | solution.py:143
  462.1 17.9 %collective-permute-start.83 = (bf16[256,1024]{1,0:T(8,128)(2,1)S(1)}, bf16[256,1024]{1,0:T(8,128)(2,1)}, u32[]{:S(2)}, u32[]{:S(2)}) collective-permute-start(bf16[256,1024]{1,0:T(8,128)(2,1)S(1)} %collective-permute-done.78.refs_1_), channel_id=1, source_target_pairs={{0,1},{1,2},{2,3},{3,0},{4,5},{5,6},{6,7},{7,4},{8,9},{9,10},{10,1... | collective-permute-start | bytes 1572872 | tf_op jit(solution)/shard_map/ppermute | solution.py:143
  479.9 15.6 %collective-permute-start.86 = (bf16[256,1024]{1,0:T(8,128)(2,1)}, bf16[256,1024]{1,0:T(8,128)(2,1)S(1)}, u32[]{:S(2)}, u32[]{:S(2)}) collective-permute-start(bf16[256,1024]{1,0:T(8,128)(2,1)} %collective-permute-done.83.refs_2_), channel_id=1, source_target_pairs={{0,1},{1,2},{2,3},{3,0},{4,5},{5,6},{6,7},{7,4},{8,9},{9,10},{10,1... | collective-permute-start | bytes 1572872 | tf_op jit(solution)/shard_map/ppermute | solution.py:143
  (117 other events, 1272.6 us)
Sparse Core Ops, SparseCore 0:
  59.9 95.7 all-gather.3
  158.2 45.1 all-gather.5
  280.3 48.9 reduce-scatter.1
  388.1 36.2 all-gather.7

commit v3 on v2

--- a/solution.py
+++ b/solution.py
@@ -127,8 +127,12 @@
     return parts
 
 
+def direct_pieces(rows, count):
+    return [swap(rows, count, m) if m else rows for m in range(0, count, 2)]
+
+
 def direct_gather(rows, count):
-    return jnp.concatenate([swap(rows, count, m) if m else rows for m in range(0, count, 2)], axis=0)
+    return jnp.concatenate(direct_pieces(rows, count), axis=0)
 
 
 def core_gather(rows, count):
@@ -311,22 +315,54 @@
     return count
 
 
-def hide(scores, at, table, starts, queries, fill):
-    rows = scores.shape[0]
-    row = lax.broadcasted_iota(I32, (MEMB, scores.shape[1]), 0)
-    kept = []
+def seen_rows(at, rows, table, starts, queries):
+    row = lax.broadcasted_iota(I32, (MEMB, queries.shape[1]), 0)
+    seen = []
     for b in range(rows // MEMB):
         base = at + b * MEMB
         lowest = starts * (1 - table[base // MEMB]) - base
-        seen = (row >= lowest) & (row <= queries - base)
-        kept.append(jnp.where(seen, scores[b * MEMB : (b + 1) * MEMB], fill))
+        seen.append((row >= lowest) & (row <= queries - base))
+    return seen
+
+
+def hide(scores, seen, fill):
+    kept = [jnp.where(mask, scores[b * MEMB : (b + 1) * MEMB], fill) for b, mask in enumerate(seen)]
     return jnp.concatenate(kept, axis=0)
+
+
+def rows_of(buffer, spots, rows, cols):
+    parts = [buffer[pl.ds(at, rows), cols] for at in spots]
+    return parts[0] if len(parts) == 1 else jnp.concatenate(parts, axis=0)
+
+
+def visit_keys(visit, state, meta, first, qt, kt, docs, picks, blocks):
+    low = doc_start(meta, first, docs) // kt
+    high = (first + qt - 1) // kt + 1
+    clear = jnp.clip((doc_start(meta, first + qt - 1, docs) + kt - 1) // kt, low, high)
+    full = jnp.clip(first // kt, clear, high)
+    count = memory_list(meta, blocks, docs, picks, low * kt)
+
+    def dense(masked):
+        return lambda i, state: visit([pl.multiple_of(i * kt, kt)], kt, state, masked)
+
+    def memory(together, base):
+        def go(i, state):
+            spots = [pl.multiple_of(blocks[base + i * together + j] * MEMB, MEMB) for j in range(together)]
+            return visit(spots, MEMB, state, False)
+
+        return go
+
+    state = lax.fori_loop(low, clear, dense(True), state)
+    state = lax.fori_loop(clear, full, dense(False), state)
+    state = lax.fori_loop(full, high, dense(True), state)
+    state = lax.fori_loop(0, count // 4, memory(4, 0), state)
+    return lax.fori_loop(0, count % 4, memory(1, count // 4 * 4), state)
 
 
 def attend_kernel(cfg, meta, q_ref, *refs):
     n, docs, picks, qt, kt, block = cfg
     keys, values = refs[:n], refs[n : 2 * n]
-    out_ref, turn_ref, wide_ref, log_ref, kbuf, vbuf, acc, table, blocks, sems = refs[2 * n :]
+    turn_ref, wide_ref, log_ref, kbuf, vbuf, acc, table, blocks, sems = refs[2 * n :]
     tok, width = q_ref.shape
     me = meta[0]
     factor = HD**-0.5 * LOG2E
@@ -335,66 +371,60 @@
     member_table(meta, table, docs, picks, kbuf.shape[0] // MEMB)
     pltpu.make_async_copy(kbuf, kbuf, sems.at[0]).wait()
     pltpu.make_async_copy(vbuf, vbuf, sems.at[1]).wait()
-    for head in range(width // HD):
-        cols = slice(head * HD, (head + 1) * HD)
-
-        def query_tile(t, carry, head=head, cols=cols):
-            base = pl.multiple_of(t * qt, qt)
-            first = me * tok + base
-            queries = first + lax.broadcasted_iota(I32, (1, qt), 1)
-            starts = doc_start(meta, queries, docs)
-            low_tile = doc_start(meta, first, docs) // kt
-            high_tile = (first + qt - 1) // kt
-            q = q_ref[pl.ds(base, qt), cols]
-            acc[...] = jnp.zeros_like(acc)
-
-            def visit(at, rows, state, masked):
-                top, total = state
-                scores = mm(kbuf[pl.ds(at, rows), cols], q, NT)
+    heads = [slice(head * HD, (head + 1) * HD) for head in range(width // HD)]
+    spans = tok // block
+
+    def query_tile(t, carry):
+        base = pl.multiple_of(t * qt, qt)
+        first = me * tok + base
+        queries = first + lax.broadcasted_iota(I32, (1, qt), 1)
+        starts = doc_start(meta, queries, docs)
+        acc[...] = jnp.zeros_like(acc)
+
+        def visit(spots, rows, state, masked):
+            seen = seen_rows(spots[0], rows, table, starts, queries) if masked else None
+            result = []
+            for head, cols in enumerate(heads):
+                top, total = state[head]
+                scores = mm(rows_of(kbuf, spots, rows, cols), q_ref[pl.ds(base, qt), cols], NT)
                 if masked:
-                    scores = hide(scores, at, table, starts, queries, NEGATIVE)
+                    scores = hide(scores, seen, NEGATIVE)
                 new_top = jnp.maximum(top, jnp.max(scores, axis=0, keepdims=True))
                 fade = jnp.exp2((top - new_top) * factor)
                 probs = jnp.exp2((scores - new_top) * factor)
                 total = total * fade + jnp.sum(probs, axis=0, keepdims=True)
-                acc[...] = acc[...] * fade + mm(vbuf[pl.ds(at, rows), cols], probs.astype(BF), TN)
-                return new_top, total
-
-            def dense(i, state):
-                return visit(pl.multiple_of(i * kt, kt), kt, state, True)
-
-            def memory(i, state):
-                return visit(pl.multiple_of(blocks[i] * MEMB, MEMB), MEMB, state, False)
-
-            count = memory_list(meta, blocks, docs, picks, low_tile * kt)
-            state = (jnp.full((1, qt), START_TOP, F32), jnp.zeros((1, qt), F32))
-            state = lax.fori_loop(low_tile, high_tile + 1, dense, state)
-            top, total = lax.fori_loop(0, count, memory, state)
-            rows = jnp.transpose(acc[...] * (1.0 / total))
+                product = mm(rows_of(vbuf, spots, rows, cols), probs.astype(BF), TN)
+                acc[head] = acc[head] * fade + product
+                result.append((new_top, total))
+            return tuple(result)
+
+        state = tuple((jnp.full((1, qt), START_TOP, F32), jnp.zeros((1, qt), F32)) for _ in heads)
+        state = visit_keys(visit, state, meta, first, qt, kt, docs, picks, blocks)
+        for head, cols in enumerate(heads):
+            top, total = state[head]
+            rows = jnp.transpose(acc[head] * (1.0 / total))
             wide_ref[pl.ds(base, qt), cols] = rows
             rows = rows.astype(BF)
-            out_ref[pl.ds(base, qt), cols] = rows
-            spans = tok // block
-            for part in range(qt // block):
-                spot = lax.rem(base // block + part - meta[1] + spans, spans)
-                spot = pl.multiple_of(spot * block, block)
-                turn_ref[pl.ds(spot, block), cols] = rows[part * block : (part + 1) * block]
+            for part in range(max(qt // block, 1)):
+                size = min(block, qt)
+                spot = lax.rem(base // block + part - meta[1] + spans, spans) * block + lax.rem(base, block)
+                spot = pl.multiple_of(spot, size)
+                turn_ref[pl.ds(spot, size), cols] = rows[part * size : (part + 1) * size]
             log_ref[head : head + 1, pl.ds(base, qt)] = top * factor + jnp.log2(total)
-            return carry
-
-        lax.fori_loop(0, tok // qt, query_tile, 0)
+        return carry
+
+    lax.fori_loop(0, tok // qt, query_tile, 0)
 
 
 def attend(meta, q, keys, values, docs, picks, block):
     n = len(keys)
     tok, width = q.shape
-    qt, kt = 512, 512
+    qt, kt = 512, 1024
     return pl.pallas_call(
         functools.partial(attend_kernel, (n, docs, picks, qt, kt, block)),
         in_specs=[SMEM, VMEM] + [ANY] * (2 * n),
-        out_specs=[VMEM] * 4,
+        out_specs=[VMEM] * 3,
         out_shape=[
-            jax.ShapeDtypeStruct((tok, width), BF),
             jax.ShapeDtypeStruct((tok, width), BF),
             jax.ShapeDtypeStruct((tok, width), F32),
             jax.ShapeDtypeStruct((width // HD, tok), F32),
@@ -402,7 +432,7 @@
         scratch_shapes=[
             pltpu.VMEM((n * tok, width), BF),
             pltpu.VMEM((n * tok, width), BF),
-            pltpu.VMEM((HD, qt), F32),
+            pltpu.VMEM((width // HD, HD, qt), F32),
             pltpu.SMEM((n * tok // MEMB,), I32),
             pltpu.SMEM((picks,), I32),
             pltpu.SemaphoreType.DMA((2,)),
@@ -441,50 +471,45 @@
         g_ref[pl.ds(spot, block), :] = part[...]
     pltpu.make_async_copy(kbuf, kbuf, sems.at[0]).wait()
     pltpu.make_async_copy(vbuf, vbuf, sems.at[1]).wait()
-    for head in range(width // HD):
-        cols = slice(head * HD, (head + 1) * HD)
-
-        def query_tile(t, carry, head=head, cols=cols):
-            base = pl.multiple_of(t * qt, qt)
-            first = me * tok + base
-            queries = first + lax.broadcasted_iota(I32, (1, qt), 1)
-            starts = doc_start(meta, queries, docs)
-            low_tile = doc_start(meta, first, docs) // kt
-            high_tile = (first + qt - 1) // kt
-            q = q_ref[pl.ds(base, qt), cols]
-            grad = g_ref[pl.ds(base, qt), cols]
-            logs = log_ref[head : head + 1, pl.ds(base, qt)]
-            product = grad.astype(F32) * wide_ref[pl.ds(base, qt), cols]
-            delta = jnp.sum(jnp.transpose(product), axis=0, keepdims=True)
-            acc[...] = jnp.zeros_like(acc)
-
-            def visit(at, rows, masked):
-                here = pl.ds(at, rows)
-                k = kbuf[here, cols]
-                probs = jnp.exp2(mm(k, q, NT) * factor - logs)
+    heads = [slice(head * HD, (head + 1) * HD) for head in range(width // HD)]
+
+    def query_tile(t, carry):
+        base = pl.multiple_of(t * qt, qt)
+        first = me * tok + base
+        queries = first + lax.broadcasted_iota(I32, (1, qt), 1)
+        starts = doc_start(meta, queries, docs)
+        here = pl.ds(base, qt)
+        deltas = []
+        for cols in heads:
+            product = g_ref[here, cols].astype(F32) * wide_ref[here, cols]
+            deltas.append(jnp.sum(jnp.transpose(product), axis=0, keepdims=True))
+        acc[...] = jnp.zeros_like(acc)
+
+        def visit(spots, rows, state, masked):
+            seen = seen_rows(spots[0], rows, table, starts, queries) if masked else None
+            for head, cols in enumerate(heads):
+                q, grad = q_ref[here, cols], g_ref[here, cols]
+                k = rows_of(kbuf, spots, rows, cols)
+                probs = jnp.exp2(mm(k, q, NT) * factor - log_ref[head : head + 1, here])
                 if masked:
-                    probs = hide(probs, at, table, starts, queries, 0.0)
-                slopes = probs * (mm(vbuf[here, cols], grad, NT) - delta)
+                    probs = hide(probs, seen, 0.0)
+                slopes = probs * (mm(rows_of(vbuf, spots, rows, cols), grad, NT) - deltas[head])
                 slopes = slopes.astype(BF)
-                dv_acc[here, cols] += mm(probs.astype(BF), grad, NN)
-                dk_acc[here, cols] += mm(slopes, q, NN)
-                acc[...] += mm(k, slopes, TN)
-
-            def dense(i, c):
-                visit(pl.multiple_of(i * kt, kt), kt, True)
-                return c
-
-            def memory(i, c):
-                visit(pl.multiple_of(blocks[i] * MEMB, MEMB), MEMB, False)
-                return c
-
-            count = memory_list(meta, blocks, docs, picks, low_tile * kt)
-            lax.fori_loop(low_tile, high_tile + 1, dense, 0)
-            lax.fori_loop(0, count, memory, 0)
-            dq_ref[pl.ds(base, qt), cols] = (jnp.transpose(acc[...]) * scale).astype(BF)
-            return carry
-
-        lax.fori_loop(0, tok // qt, query_tile, 0)
+                d_values = mm(probs.astype(BF), grad, NN)
+                d_keys = mm(slopes, q, NN)
+                for j, at in enumerate(spots):
+                    part = slice(j * rows, (j + 1) * rows)
+                    dv_acc[pl.ds(at, rows), cols] += d_values[part]
+                    dk_acc[pl.ds(at, rows), cols] += d_keys[part]
+                acc[head] += mm(k, slopes, TN)
+            return state
+
+        visit_keys(visit, jnp.int32(0), meta, first, qt, kt, docs, picks, blocks)
+        for head, cols in enumerate(heads):
+            dq_ref[here, cols] = (jnp.transpose(acc[head]) * scale).astype(BF)
+        return carry
+
+    lax.fori_loop(0, tok // qt, query_tile, 0)
 
     def put(which, m):
         side, at = reduce_place(n, which, m)
@@ -519,7 +544,7 @@
             pltpu.VMEM((n * tok, width), F32),
             pltpu.VMEM((n * tok, width), F32),
             pltpu.VMEM((tok, width), BF),
-            pltpu.VMEM((HD, qt), F32),
+            pltpu.VMEM((width // HD, HD, qt), F32),
             pltpu.VMEM((2, tok, width), BF),
             pltpu.SMEM((n * tok // MEMB,), I32),
             pltpu.SMEM((picks,), I32),
@@ -570,51 +595,56 @@
 def feed_kernel(cfg, meta, w_ref, g_ref, *refs):
     n, spans, fs = cfg
     pieces = refs[: 2 * n]
-    normed_ref, hidden_ref, dgate_ref, dup_ref = refs[2 * n : 2 * n + 4]
-    backs = (refs[2 * n + 4 : 2 * n + 6], refs[2 * n + 6 : 2 * n + 8])
-    feeds = refs[2 * n + 8 : 2 * n + 10]
-    rows, stage, feed, wg, wu, wd, sem, out_sem = refs[2 * n + 10 :]
-    at = pl.program_id(0)
-    block, half = g_ref.shape[0], g_ref.shape[1] // 2
-
-    @pl.when(at == 0)
+    normed_ref, hidden_ref, inner_ref = refs[2 * n : 2 * n + 3]
+    backs = (refs[2 * n + 3 : 2 * n + 5], refs[2 * n + 5 : 2 * n + 7])
+    feeds = refs[2 * n + 7 : 2 * n + 9]
+    rows, stage, feed, w, sem, out_sem = refs[2 * n + 9 :]
+    step, units = pl.program_id(0), spans * fs
+    block, d = rows.shape[1:]
+    tile, half = g_ref.shape[0], d // 2
+    per = tile // block
+
+    @pl.when(step == 0)
     def _():
         for m in range(n):
-            pltpu.make_async_copy(pieces[m], rows.at[m, :, :half], sem).start()
-            pltpu.make_async_copy(pieces[n + m], rows.at[m, :, half:], sem).start()
+            spot = gather_place(n, m)
+            pltpu.make_async_copy(pieces[m], rows.at[spot, :, :half], sem).start()
+            pltpu.make_async_copy(pieces[n + m], rows.at[spot, :, half:], sem).start()
         for t in range(spans):
-            for kind, w in enumerate((wg, wu, wd)):
-                w[t * fs : (t + 1) * fs] = w_ref[t, kind * fs : (kind + 1) * fs]
+            for kind, first in enumerate((0, units, 2 * units)):
+                w[first + t * fs : first + (t + 1) * fs] = w_ref[t, kind * fs : (kind + 1) * fs]
         pltpu.make_async_copy(rows, rows, sem).wait()
 
-    normed = rows[at]
+    these = pl.ds(step * per, per)
+    normed = rows[these].reshape(tile, d)
     normed_ref[...] = normed
-    gate = mm(normed, wg[...], NT)
-    up = mm(normed, wu[...], NT)
+    inner = mm(normed, w[: 2 * units], NT)
+    gate, up = inner[:, :units], inner[:, units:]
     sigma = jax.nn.sigmoid(gate)
     silu = gate * sigma
     hidden = (silu * up).astype(BF)
     hidden_ref[...] = hidden
-    d_hidden = mm(g_ref[...], wd[...], NT).astype(BF).astype(F32)
+    d_hidden = mm(g_ref[...], w[2 * units :], NT).astype(BF).astype(F32)
     d_gate = (d_hidden * up * (sigma * (1.0 + gate * (1.0 - sigma)))).astype(BF)
-    d_up = (d_hidden * silu).astype(BF)
-    dgate_ref[...] = d_gate
-    dup_ref[...] = d_up
-    stage[at] = (mm(d_gate, wg[...], NN) + mm(d_up, wu[...], NN)).astype(BF)
-    feed[at] = mm(hidden, wd[...], NN).astype(BF)
-    for m in range(n):
-
-        @pl.when(at == m)
-        def _(m=m):
-            for route, cols in enumerate((slice(0, half), slice(half, 2 * half))):
-                side, spot = reduce_place(n, route, m)
-                there = backs[route][side].at[spot * block : (spot + 1) * block]
-                pltpu.make_async_copy(stage.at[m, :, cols], there, out_sem).start()
-            side, spot = reduce_place(n, 0, m)
-            there = feeds[side].at[spot * block : (spot + 1) * block]
-            pltpu.make_async_copy(feed.at[m], there, out_sem).start()
-
-    @pl.when(at == n - 1)
+    d_inner = jnp.concatenate([d_gate, (d_hidden * silu).astype(BF)], axis=1)
+    inner_ref[...] = d_inner
+    stage[these] = mm(d_inner, w[: 2 * units], NN).astype(BF).reshape(per, block, d)
+    feed[these] = mm(hidden, w[2 * units :], NN).astype(BF).reshape(per, block, d)
+    for part in range(per):
+        at = step * per + part
+        for m in range(n):
+
+            @pl.when(at == gather_place(n, m))
+            def _(at=at, m=m):
+                for route, cols in enumerate((slice(0, half), slice(half, d))):
+                    side, spot = reduce_place(n, route, m)
+                    there = backs[route][side].at[spot * block : (spot + 1) * block]
+                    pltpu.make_async_copy(stage.at[at, :, cols], there, out_sem).start()
+                side, spot = reduce_place(n, 0, m)
+                there = feeds[side].at[spot * block : (spot + 1) * block]
+                pltpu.make_async_copy(feed.at[at], there, out_sem).start()
+
+    @pl.when(step == pl.num_programs(0) - 1)
     def _():
         pltpu.make_async_copy(stage, stage, out_sem).wait()
         pltpu.make_async_copy(feed, feed, out_sem).wait()
@@ -626,34 +656,33 @@
     block = rows // n
     spans = weights.shape[0]
     units = spans * fs
-    turned = lambda w: pl.BlockSpec((block, w), lambda m, meta: (lax.bitwise_xor(meta[0], m), 0))
+    tile = min(512, rows)
+    turned = lambda w: pl.BlockSpec((tile, w), lambda i, meta: (i, 0))
     shape = lambda w: jax.ShapeDtypeStruct((rows, w), BF)
     got = pl.pallas_call(
         functools.partial(feed_kernel, (n, spans, fs)),
         grid_spec=pltpu.PrefetchScalarGridSpec(
             num_scalar_prefetch=1,
-            grid=(n,),
+            grid=(rows // tile,),
             in_specs=[VMEM, turned(d)] + [ANY] * (2 * n),
-            out_specs=[turned(d), turned(units), turned(units), turned(units)] + [ANY] * 6,
+            out_specs=[turned(d), turned(units), turned(2 * units)] + [ANY] * 6,
             scratch_shapes=[
                 pltpu.VMEM((n, block, d), BF),
                 pltpu.VMEM((n, block, d), BF),
                 pltpu.VMEM((n, block, d), BF),
-                pltpu.VMEM((units, d), BF),
-                pltpu.VMEM((units, d), BF),
-                pltpu.VMEM((units, d), BF),
+                pltpu.VMEM((3 * units, d), BF),
                 pltpu.SemaphoreType.DMA,
                 pltpu.SemaphoreType.DMA,
             ],
         ),
-        out_shape=[shape(d), shape(units), shape(units), shape(units)]
+        out_shape=[shape(d), shape(units), shape(2 * units)]
         + [jax.ShapeDtypeStruct((rows // 2, d // 2), BF)] * 4
         + [jax.ShapeDtypeStruct((rows // 2, d), BF)] * 2,
         compiler_params=params(),
         cost_estimate=QUICK,
         name="feed_forward",
     )(meta, weights, grads, *pieces)
-    return got[:4], (got[4:6], got[6:8]), got[8:]
+    return got[:3], (got[3:5], got[5:7]), got[7:]
 
 
 def branch_kernel(cfg, meta, left_a, left_b, right_a, right_b, mixed_ref, g_ref, gain_ref, wo_ref, *refs):
@@ -732,25 +761,27 @@
     return inverse * (scaled - unit_rows * jnp.mean(scaled * unit_rows, axis=-1, keepdims=True))
 
 
-def feed_grads_kernel(cfg, meta, d_gate, d_up, hidden, normed, grads, out):
+def feed_grads_kernel(cfg, hidden, d_inner, normed, grads, out):
     spans, fs = cfg
-    for kind, (left, right) in enumerate(((d_gate, normed), (d_up, normed), (hidden, grads))):
+    units = spans * fs
+    pairs = [(d_inner.at[:, :units], normed), (d_inner.at[:, units:], normed), (hidden, grads)]
+    for kind, (left, right) in enumerate(pairs):
         product = mm(left[...], right[...], TN).astype(BF)
         for t in range(spans):
             out[t, kind * fs : (kind + 1) * fs] = product[t * fs : (t + 1) * fs]
 
 
-def feed_grads(meta, d_gate, d_up, hidden, normed, grads, fs):
-    (rows, units), d = d_gate.shape, normed.shape[1]
+def feed_grads(hidden, d_inner, normed, grads, fs):
+    (rows, units), d = hidden.shape, normed.shape[1]
     return pl.pallas_call(
         functools.partial(feed_grads_kernel, (units // fs, fs)),
-        in_specs=[SMEM] + [VMEM] * 5,
+        in_specs=[VMEM] * 4,
         out_specs=VMEM,
         out_shape=jax.ShapeDtypeStruct((units // fs, 3 * fs, d), BF),
         compiler_params=params(),
         cost_estimate=QUICK,
         name="feed_grads",
-    )(meta, d_gate, d_up, hidden, normed, grads)
+    )(hidden, d_inner, normed, grads)
 
 
 def share_rows(rows, n):
@@ -765,14 +796,18 @@
         pltpu.make_async_copy(stage.at[at], sides[side].at[first : first + rows], sem).start()
 
 
-def late_kernel(cfg, meta, dq, dk, dv, normed, *refs):
+def both(pair):
+    return (pair[0][...].astype(F32) + pair[1][...].astype(F32)).astype(BF)
+
+
+def late_kernel(cfg, meta, dq, dk_a, dk_b, dv_a, dv_b, normed, *refs):
     n, qw = cfg
     sides, (stage, sem) = refs[:2], refs[2:]
     used = 3 * qw
     if stage.shape[0] > used:
         stage[used:] = jnp.zeros((stage.shape[0] - used, stage.shape[1]), BF)
-    for at, left in enumerate((dq, dk, dv)):
-        stage[at * qw : (at + 1) * qw] = mm(left[...], normed[...], TN).astype(BF)
+    for at, left in enumerate((dq[...], both((dk_a, dk_b)), both((dv_a, dv_b)))):
+        stage[at * qw : (at + 1) * qw] = mm(left, normed[...], TN).astype(BF)
     spread(meta, stage, sides, n, 0, stage.shape[0] // n, sem)
     pltpu.make_async_copy(stage, stage, sem).wait()
 
@@ -782,14 +817,14 @@
     rows = share_rows(3 * qw, n)
     return pl.pallas_call(
         functools.partial(late_kernel, (n, qw)),
-        in_specs=[SMEM] + [VMEM] * 4,
+        in_specs=[SMEM] + [VMEM] * 6,
         out_specs=[ANY] * 2,
         out_shape=[jax.ShapeDtypeStruct((n * rows // 2, d), BF)] * 2,
         scratch_shapes=[pltpu.VMEM((n * rows, d), BF), pltpu.SemaphoreType.DMA],
         compiler_params=params(),
         cost_estimate=QUICK,
         name="late_grads",
-    )(meta, dq, dk, dv, normed)
+    )(meta, dq, *dk, *dv, normed)
 
 
 def soap_kernel(cfg, meta, held, early, late, weight_ref, first_ref, second_ref, average_ref, stat_ref, basis_ref,
@@ -950,28 +985,40 @@
     return (weight - GAIN_RATE * direction, new_first, new_second)
 
 
-def back_kernel(meta, dq, dk, dv, wq, wk, wv, out):
-    out[...] = (mm(dq[...], wq[...], NN) + mm(dk[...], wk[...], NN) + mm(dv[...], wv[...], NN)).astype(BF)
-
-
-def back_in(meta, dq, dk, dv, wq, wk, wv, n, low, high):
+def back_kernel(meta, x_ref, dq, dk_a, dk_b, dv_a, dv_b, wq, wk, wv, out, gain_out):
+    total = mm(dq[...], wq[...], NN) + mm(both((dk_a, dk_b)), wk[...], NN)
+    total = total + mm(both((dv_a, dv_b)), wv[...], NN)
+    out[...] = total.astype(BF)
+    unit, _, _ = norm_rows(x_ref[...].astype(F32), 1.0)
+    share = jnp.sum(total * unit, axis=0, keepdims=True)
+
+    @pl.when(pl.program_id(0) == 0)
+    def _():
+        gain_out[...] = share
+
+    @pl.when(pl.program_id(0) > 0)
+    def _():
+        gain_out[...] += share
+
+
+def back_in(meta, x, dq, dk, dv, wq, wk, wv, n, low, high):
     tok, (qw, d) = dq.shape[0], wq.shape
     tile = tok // n
-    rows = pl.BlockSpec((tile, qw), lambda i, meta: ((meta[1] - i - low + n) % n, 0))
+    rows = lambda w: pl.BlockSpec((tile, w), lambda i, meta: ((meta[1] - i - low + n) % n, 0))
     whole = pl.BlockSpec((qw, d), lambda i, meta: (0, 0))
     return pl.pallas_call(
         back_kernel,
         grid_spec=pltpu.PrefetchScalarGridSpec(
             num_scalar_prefetch=1,
             grid=(high - low,),
-            in_specs=[rows] * 3 + [whole] * 3,
-            out_specs=pl.BlockSpec((tile, d), lambda i, meta: (i, 0)),
+            in_specs=[rows(d)] + [rows(qw)] * 5 + [whole] * 3,
+            out_specs=[pl.BlockSpec((tile, d), lambda i, meta: (i, 0)), pl.BlockSpec((1, d), lambda i, meta: (0, 0))],
         ),
-        out_shape=jax.ShapeDtypeStruct(((high - low) * tile, d), BF),
+        out_shape=[jax.ShapeDtypeStruct(((high - low) * tile, d), BF), jax.ShapeDtypeStruct((1, d), F32)],
         compiler_params=params(),
         cost_estimate=QUICK,
         name="back_in",
-    )(meta, dq, dk, dv, wq, wk, wv)
+    )(meta, x, dq, *dk, *dv, wq, wk, wv)
 
 
 def shards(
@@ -1025,16 +1072,19 @@
     (keys, values), _ = gather_seq([k, v], n_seq)
     weights = whole_tp(share).reshape(n_tp, -1, d)
     own_grads, keys[n_seq - 2], values[n_seq - 2] = pin(mine(cotangent), keys[n_seq - 2], values[n_seq - 2])
-    grads_all = whole_seq(own_grads)
-    attended, turned_heads, wide, logs = attend(meta, q, keys, values, docs, picks, block)
+    grads_all = direct_pieces(own_grads, n_seq)
+    turned_heads, wide, logs = attend(meta, q, keys, values, docs, picks, block)
+    turned_heads, grads_all = pin(turned_heads, grads_all)
     heads = trade_tp([turned_heads[i * block : (i + 1) * block] for i in range(n_tp)], n_tp)
     mixed, left, right = mix(meta, tokens, gains, weights, heads)
+    left, grads_all = pin(left, grads_all)
+    grads_all = core_gather(jnp.concatenate(grads_all, axis=0), n_seq)
     (left, right), _ = gather_seq([left, right], n_seq)
-    (normed_two, hidden, d_gate, d_up), pairs, feed = feed_forward(meta, weights, grads_all, left + right, fs)
+    (normed_two, hidden, d_inner), pairs, feed = feed_forward(meta, weights, grads_all, left + right, fs)
 
     last = len(routes(n_seq)[0])
     inner_rows, out_rows = share_rows(3 * qw, n_seq), share_rows(qw, n_seq)
-    feed_sums_in = (d_gate, d_up, hidden, normed_two, grads_all)
+    feed_sums_in = (hidden, d_inner, normed_two, grads_all)
     for at in range(last + 1):
         pairs = reduce_levels(pairs, n_seq, at)
         if at == last - 1:
@@ -1042,7 +1092,7 @@
             feed = plus(*feed)
         elif at == 0:
             pairs, feed, feed_sums_in = pin(pairs, feed, feed_sums_in)
-            feed_sums = feed_grads(meta, *feed_sums_in, fs)
+            feed_sums = feed_grads(*feed_sums_in, fs)
     d_mixed, grad_gain_two, d_heads, outer = branch_back(
         meta, pairs, mixed, cotangent, gains, weights, heads, n_seq, 3 * fs
     )
@@ -1070,13 +1120,15 @@
             while len(outputs) < n_tp and (at == last or len(outputs) < 1 + 2 * at):
                 outputs.append(ring(outputs[-1], n_tp, 1))
         pairs, outputs, feed_sums, dq = pin(pairs, outputs, feed_sums, dq)
-    dk, dv = [plus(*pair) for pair in pairs]
+    dk, dv = pairs
+    output = place(meta, outputs, block)
     early = whole_seq(feed_sums).reshape(-1, panel, d)
 
-    inputs = (meta, dq, dk, dv, inner[0], inner[1], inner[2], n_tp)
-    total = back_in(*inputs, n_tp - 1, n_tp)
+    inputs = (meta, tokens, dq, dk, dv, inner[0], inner[1], inner[2], n_tp)
+    total, gain_a = back_in(*inputs, n_tp - 1, n_tp)
     total, lefts = pin(total, (dq, dk, dv))
-    back_rest = back_in(meta, *lefts, *inputs[4:], 0, n_tp - 1)
+    back_rest, gain_b = back_in(meta, tokens, *lefts, *inputs[5:], 0, n_tp - 1)
+    gain_total = jnp.concatenate([gain_a + gain_b, grad_gain_two], axis=0)
     late = late_grads(meta, *lefts, normed_one, n_seq)
 
     def advance(late, step):
@@ -1102,7 +1154,11 @@
             late = advance(late, step)
             if step == 0:
                 outer = trade_tp(outer, n_tp)
-            came, late, back_rest, outer = pin(came, late, back_rest, outer)
+            if step == 1:
+                came, output = pin(came, output)
+            for _ in range(min(len(gain_steps), 2 if 0 < step else 0)):
+                gain_total = gain_steps.pop(0)(gain_total)
+            came, late, back_rest, outer, held, gain_total = pin(came, late, back_rest, outer, held, gain_total)
             if step == 0:
                 outer = sum(part.astype(F32) for part in outer).astype(BF)
             part = back_rest[k * block : (k + 1) * block]
@@ -1111,14 +1167,12 @@
                 continue
             d_normed_one = part.astype(F32) + came.astype(F32)
             unit_one, inverse_one, _ = norm_rows(mine(tokens).astype(F32), gains[0])
-            grad_gain_one = jnp.sum(d_normed_one * unit_one, axis=0)
             grad_here = d_mixed + norm_back(d_normed_one, unit_one, inverse_one, gains[0])
-            gain_total = jnp.stack([grad_gain_one, grad_gain_two[0]])
             gather.append(grad_here.astype(BF))
             continue
         if len(gather) < n_tp:
             gather.append(ring(gather[-1], n_tp, 1))
-        if gain_steps:
+        for _ in range(min(len(gain_steps), 1)):
             gain_total = gain_steps.pop(0)(gain_total)
         late = advance(late, step)
         if step == steps - 2:
@@ -1134,7 +1188,6 @@
             gather[-1], late, gain_total = pin(gather[-1], late, gain_total)
     for step in gain_steps:
         gain_total = step(gain_total)
-    output = place(meta, outputs, block)
     grad_input = place(meta, gather, block, F32)
     new_gains, new_gain_first, new_gain_second = adam_gain(gain_total, gains, gain_first, gain_second)
     return (

time: 519 us -> 492 us (0.948)
  waiting for transfers between devices: 257 us -> 230 us
    ppermute x18, waiting for transfers between devices: 70.4 us -> 56.9 us  [ring(): lax.ppermute(value, 'tp', [(i, (i + step) % count) for i in range(count)])]
    ppermute x5, waiting for transfers between devices: 5.62 us -> 18.3 us  [sum_steps(): lax.ppermute(v, axis, pairs)]
    all_gather x1, waiting for transfers between devices: 13.3 us -> 1.52 us  [whole_tp(): return lax.all_gather(rows, 'tp', axis=0, tiled=True)]
    ppermute x67 -> x71, waiting for transfers between devices: 153 us -> 142 us  [swap(): return lax.ppermute(value, 'seq', [(i, i ^ bit) for i in range(count)])]
    ppermute x18, starting transfers between devices: 32 us -> 24.9 us  [ring(): lax.ppermute(value, 'tp', [(i, (i + step) % count) for i in range(count)])]
    unnamed x143 -> x177, local copies, waits for them, and re-layouts: 5.38 us -> 10.8 us
    ppermute x67 -> x71, starting transfers between devices: 46.1 us -> 51.3 us  [swap(): return lax.ppermute(value, 'seq', [(i, i ^ bit) for i in range(count)])]
    convert_element_type x15 -> x13, other arithmetic: 11.2 us -> 9.72 us  [plus(): return (left.astype(F32) + right.astype(F32)).astype(left.dtype)]
  transfers between devices with their start and end apart: 94 -> 97, of which waited for: 53 -> 48; matrix products, arithmetic and copies ran while one was open for 5% -> 5% of each run, Pallas kernels for 17% -> 16%
where the time goes in v3:
time: 492 us; the launch traced here: 488 us
  waiting for transfers between devices  230 us (47%)
  Pallas kernels  124 us (25%)
  starting transfers between devices  82.1 us (17%)
  other arithmetic  18.9 us (4%)
  local copies, waits for them, and re-layouts  17.7 us (4%)
  between operations  15.2 us (3%)
    ppermute x71, waiting for transfers between devices, swap(): return lax.ppermute(value, 'seq', [(i, i ^ bit) for i in range(count)])  142 us
    ppermute x18, waiting for transfers between devices, ring(): lax.ppermute(value, 'tp', [(i, (i + step) % count) for i in range(count)])  56.9 us
    ppermute x71, starting transfers between devices, swap(): return lax.ppermute(value, 'seq', [(i, i ^ bit) for i in range(count)])  51.3 us
    ppermute x18, starting transfers between devices, ring(): lax.ppermute(value, 'tp', [(i, (i + step) % count) for i in range(count)])  24.9 us
    pallas_call x1, Pallas kernels, feed_forward(): pl.pallas_call(functools.partial(feed_kernel, (n, spans, fs)), grid_spec=...  20.9 us
    pallas_call x1, Pallas kernels, attend_back(): pl.pallas_call(functools.partial(attend_back_kernel, (n, docs, picks, qt,...  19.5 us
    ppermute x5, waiting for transfers between devices, sum_steps(): lax.ppermute(v, axis, pairs)  18.3 us
    pallas_call x1, Pallas kernels, soap(): pl.pallas_call(functools.partial(soap_kernel, (n, late_panels, out_panels...  12.4 us
  transfers between devices with their start and end apart: 97, of which 48 were waited for; matrix products, arithmetic and copies ran while one was open for 5% of the time, Pallas kernels for 16%

profile of v3, /device:TPU:0, one launch (start us, length us, event | category | flops | bytes accessed | tf_op | source)
XLA Modules:
  0.0 488.1 jit_solution(9823087423121305987)
XLA Ops:
  9.6 2.9 collective-permute-start.1
  14.6 17.1 %collective-permute-done.4.refs_10_ = bf16[6,32,1024]{2,1,0:T(8,128)(2,1)S(1)} collective-permute-done((bf16[6,32,1024]{2,1,0:T(8,128)(2,1)S(1)}, bf16[6,32,1024]{2,1,0:T(8,128)(2,1)S(1)}, u32[]{:S(2)}, u32[]{:S(2)}) %collective-permute-start.4) | collective-permute-done | bytes 393248 | tf_op jit(solution)/shard_map/ppermute | solution.py:67
  36.1 10.9 %collective-permute-done.11.refs_14_ = bf16[6,32,1024]{2,1,0:T(8,128)(2,1)} collective-permute-done((bf16[6,32,1024]{2,1,0:T(8,128)(2,1)S(1)}, bf16[6,32,1024]{2,1,0:T(8,128)(2,1)}, u32[]{:S(2)}, u32[]{:S(2)}) %collective-permute-start.11) | collective-permute-done | bytes 393248 | tf_op jit(solution)/shard_map/ppermute | solution.py:67
  50.6 9.1 %project.1 = (bf16[1024,256]{1,0:T(8,128)(2,1)}, bf16[1024,256]{1,0:T(8,128)(2,1)}, bf16[1024,256]{1,0:T(8,128)(2,1)}, bf16[1024,1024]{1,0:T(8,128)(2,1)}, bf16[...) custom-call(s32[18]{0:T(128)} %pad_add_fusion.meta, s32[98]{0:T(128)} %owners.1, bf16[1024,1024]{1,0:T(8,128)(2,1)} %x_ref.7, ...), custom_call_target="tpu_custom_call" | custom-call | flops 1000 | bytes 1000 | tf_op jit(solution)/shard_map/project/pallas_call | solution.py:262
  64.3 10.9 %collective-permute-done.15.refs_2_.refs_6_ = bf16[1024,256]{1,0:T(8,128)(2,1)S(1)} collective-permute-done((bf16[1024,256]{1,0:T(8,128)(2,1)}, bf16[1024,256]{1,0:T(8,128)(2,1)S(1)}, u32[]{:S(2)}, u32[]{:S(2)}) %collective-permute-start.15) | collective-permute-done | bytes 524320 | tf_op jit(solution)/shard_map/ppermute | solution.py:67
  75.7 10.1 %collective-permute-done.18.refs_10_.refs_14_ = bf16[1024,256]{1,0:T(8,128)(2,1)S(1)} collective-permute-done((bf16[1024,256]{1,0:T(8,128)(2,1)}, bf16[1024,256]{1,0:T(8,128)(2,1)S(1)}, u32[]{:S(2)}, u32[]{:S(2)}) %collective-permute-start.18) | collective-permute-done | bytes 524320 | tf_op jit(solution)/shard_map/ppermute | solution.py:67
  90.4 10.2 %collective-permute-done.22.refs_6_.refs_10_ = bf16[1024,256]{1,0:T(8,128)(2,1)} collective-permute-done((bf16[1024,256]{1,0:T(8,128)(2,1)S(1)}, bf16[1024,256]{1,0:T(8,128)(2,1)}, u32[]{:S(2)}, u32[]{:S(2)}) %collective-permute-start.22) | collective-permute-done | bytes 524320 | tf_op jit(solution)/shard_map/ppermute | solution.py:67
  100.7 2.5 collective-permute-done.25.refs_14_.refs_18_
  109.4 11.5 %attend.1 = (bf16[1024,256]{1,0:T(8,128)(2,1)}, f32[1024,256]{1,0:T(8,128)}, f32[2,1024]{1,0:T(2,128)}) custom-call(s32[18]{0:T(128)} %pad_add_fusion.meta, bf16[1024,256]{1,0:T(8,128)(2,1)} %get-tuple-element.262.q_ref, bf16[1024,256]{1,0:T(8,128)(2,1)} %get-tuple-element.273.refs_0_.refs_4_, bf16[1024,256]{1,0:T(8,128)(2,1)} %copy-done.11, ...), custom_call_target="tpu_custom_call" | custom-call | flops 1000 | bytes 1000 | tf_op jit(solution)/shard_map/attend/pallas_call | solution.py:423
  120.9 10.3 %collective-permute-done.29 = bf16[256,1024]{1,0:T(8,128)(2,1)S(1)} collective-permute-done((bf16[256,1024]{1,0:T(8,128)(2,1)S(1)}, bf16[256,1024]{1,0:T(8,128)(2,1)S(1)}, u32[]{:S(2)}, u32[]{:S(2)}) %collective-permute-start.29) | collective-permute-done | bytes 524320 | tf_op jit(solution)/shard_map/ppermute | solution.py:67
  135.4 2.6 collective-permute-start.32
  139.7 5.0 %collective-permute-done.31.refs_1_ = bf16[256,256]{1,0:T(8,128)(2,1)S(1)} collective-permute-done((bf16[256,256]{1,0:T(8,128)(2,1)S(1)}, bf16[256,256]{1,0:T(8,128)(2,1)S(1)}, u32[]{:S(2)}, u32[]{:S(2)}) %collective-permute-start.31) | collective-permute-done | bytes 131104 | tf_op jit(solution)/shard_map/ppermute | solution.py:147
  144.8 7.9 %collective-permute-done.32.refs_2_ = bf16[256,256]{1,0:T(8,128)(2,1)S(1)} collective-permute-done((bf16[256,256]{1,0:T(8,128)(2,1)S(1)}, bf16[256,256]{1,0:T(8,128)(2,1)S(1)}, u32[]{:S(2)}, u32[]{:S(2)}) %collective-permute-start.32) | collective-permute-done | bytes 131104 | tf_op jit(solution)/shard_map/ppermute | solution.py:147
  154.3 5.3 %mix.1 = (f32[256,1024]{1,0:T(8,128)}, bf16[256,512]{1,0:T(8,128)(2,1)}, bf16[256,512]{1,0:T(8,128)(2,1)}) custom-call(s32[18]{0:T(128)} %pad_add_fusion.meta, bf16[1024,1024]{1,0:T(8,128)(2,1)} %x_ref.7, f32[2,1024]{1,0:T(2,128)} %gain_ref.5, bf16[4,544,1024]{2,1,0:T(8,128)(2,1)} %bitcast.27, bf16[256,256]{1,0:T(8,128)(2,1)} %get-tuple-element.531.refs_0_, ...), custom_call_target="tpu_custom_call" | custom-call | flops 1000 | bytes 1000 | tf_op jit(solution)/shard_map/mix/pallas_call | solution.py:579
  165.9 3.6 collective-permute-done.36.refs_2_
  170.9 3.9 collective-permute-done.39.refs_10_
  174.8 2.3 collective-permute-done.40.refs_12_
  182.0 3.9 collective-permute-done.43.refs_6_
  191.7 20.9 %feed_forward.1 = (bf16[2048,1024]{1,0:T(8,128)(2,1)}, bf16[2048,384]{1,0:T(8,128)(2,1)}, bf16[2048,768]{1,0:T(8,128)(2,1)}, bf16[1024,512]{1,0:T(8,128)(2,1)}, ...) custom-call(s32[18]{0:T(128)} %pad_add_fusion.meta, ...), custom_call_target="tpu_custom_call" | custom-call | flops 1000 | bytes 1000 | tf_op jit(solution)/shard_map/feed_forward/pallas_call | solution.py:662
  213.2 2.4 collective-permute-done.50
  219.8 11.2 %feed_grads.1 = bf16[4,288,1024]{2,1,0:T(8,128)(2,1)} custom-call(bf16[2048,384]{1,0:T(8,128)(2,1)} %get-tuple-element.340.hidden, bf16[2048,768]{1,0:T(8,128)(2,1)} %get-tuple-element.341.d_inner, bf16[2048,1024]{1,0:T(8,128)(2,1)} %get-tuple-element.342.normed, bf16[2048,1024]{1,0:T(8,128)(2,1)} %copy-done.3), custom_call_target="tpu_custom_call" | custom-call | flops 1000 | bytes 1000 | tf_op jit(solution)/shard_map/feed_grads/pallas_call | solution.py:776
  235.7 5.7 %collective-permute-done.54.left_b = bf16[256,512]{1,0:T(8,128)(2,1)S(1)} collective-permute-done((bf16[256,512]{1,0:T(8,128)(2,1)S(1)}, bf16[256,512]{1,0:T(8,128)(2,1)S(1)}, u32[]{:S(2)}, u32[]{:S(2)}) %collective-permute-start.54) | collective-permute-done | bytes 262176 | tf_op jit(solution)/shard_map/ppermute | solution.py:67
  243.3 7.7 %branch_back.1 = (f32[256,1024]{1,0:T(8,128)}, f32[1,1024]{1,0:T(1,128)}, bf16[256,256]{1,0:T(8,128)(2,1)}, bf16[256,256]{1,0:T(8,128)(2,1)}, bf16[256,256]{1,0:...) custom-call(s32[18]{0:T(128)} %pad_add_fusion.meta, ...), custom_call_target="tpu_custom_call" | custom-call | flops 1000 | bytes 1000 | tf_op jit(solution)/shard_map/branch_back/pallas_call | solution.py:719
  258.4 2.8 collective-permute-done.56.refs_1_
  261.2 5.2 %collective-permute-done.57.refs_2_ = bf16[256,256]{1,0:T(8,128)(2,1)S(1)} collective-permute-done((bf16[256,256]{1,0:T(8,128)(2,1)S(1)}, bf16[256,256]{1,0:T(8,128)(2,1)S(1)}, u32[]{:S(2)}, u32[]{:S(2)}) %collective-permute-start.57) | collective-permute-done | bytes 131104 | tf_op jit(solution)/shard_map/ppermute | solution.py:147
  270.2 19.5 %attend_back.1 = (bf16[1024,256]{1,0:T(8,128)(2,1)}, bf16[4096,256]{1,0:T(8,128)(2,1)}, bf16[4096,256]{1,0:T(8,128)(2,1)}, bf16[4096,256]{1,0:T(8,128)(2,1)}, bf16[4096,256]{1,0:T(8,128)(2,1)}) custom-call(s32[18]{0:T(128)} %pad_add_fusion.meta, bf16[1024,256]{1,0:T(8,128)(2,1)} %get-tuple-element.262.q_ref, f32[1024,256]{1,0:T(8,128)} %get-tuple-element.363.wide_ref, ...), custom_call_target="tpu_custom_call" | custom-call | flops 1000 | bytes 1000 | tf_op jit(solution)/shard_map/attend_back/pallas_call | solution.py:535
  289.7 13.7 %collective-permute-done.61 = bf16[384,1024]{1,0:T(8,128)(2,1)} collective-permute-done((bf16[384,1024]{1,0:T(8,128)(2,1)S(1)}, bf16[384,1024]{1,0:T(8,128)(2,1)}, u32[]{:S(2)}, u32[]{:S(2)}) %collective-permute-start.61) | collective-permute-done | bytes 786464 | tf_op jit(solution)/shard_map/ppermute | solution.py:67
  303.4 10.9 %reduce-scatter.2.cloned.1.call-done = bf16[288,1024]{1,0:T(8,128)(2,1)} async-done(((bf16[1152,1024]{1,0:T(8,128)(2,1)}), bf16[288,1024]{1,0:T(8,128)(2,1)}) %reduce-scatter.2.cloned.1.call-update) | async-done | bytes 589840 | tf_op jit(solution)/shard_map/reduce_scatter | solution.py:1109
  325.6 14.8 %collective-permute-done.67.refs_1_ = bf16[256,1024]{1,0:T(8,128)(2,1)S(1)} collective-permute-done((bf16[256,1024]{1,0:T(8,128)(2,1)S(1)}, bf16[256,1024]{1,0:T(8,128)(2,1)S(1)}, u32[]{:S(2)}, u32[]{:S(2)}) %collective-permute-start.67) | collective-permute-done | bytes 524320 | tf_op jit(solution)/shard_map/ppermute | solution.py:147
  340.5 7.0 %collective-permute-done.66 = bf16[2048,256]{1,0:T(8,128)(2,1)S(1)} collective-permute-done((bf16[2048,256]{1,0:T(8,128)(2,1)S(1)}, bf16[2048,256]{1,0:T(8,128)(2,1)S(1)}, u32[]{:S(2)}, u32[]{:S(2)}) %collective-permute-start.66) | collective-permute-done | bytes 1048608 | tf_op jit(solution)/shard_map/ppermute | solution.py:67
  349.9 4.9 %collective-permute-done.68.refs_2_ = bf16[256,1024]{1,0:T(8,128)(2,1)S(1)} collective-permute-done((bf16[256,1024]{1,0:T(8,128)(2,1)S(1)}, bf16[256,1024]{1,0:T(8,128)(2,1)S(1)}, u32[]{:S(2)}, u32[]{:S(2)}) %collective-permute-start.68) | collective-permute-done | bytes 524320 | tf_op jit(solution)/shard_map/ppermute | solution.py:147
  356.1 10.3 %collective-permute-done.69.dk_b = bf16[1024,256]{1,0:T(8,128)(2,1)S(1)} collective-permute-done((bf16[1024,256]{1,0:T(8,128)(2,1)S(1)}, bf16[1024,256]{1,0:T(8,128)(2,1)S(1)}, u32[]{:S(2)}, u32[]{:S(2)}) %collective-permute-start.69) | collective-permute-done | bytes 524320 | tf_op jit(solution)/shard_map/ppermute | solution.py:67
  366.6 2.4 collective-permute-done.71.refs_3_
  370.4 3.8 back_in.2
  376.9 2.4 collective-permute-start.75
  379.3 6.0 %back_in.3 = (bf16[768,1024]{1,0:T(8,128)(2,1)}, f32[1,1024]{1,0:T(1,128)}) custom-call(s32[18]{0:T(128)} %pad_add_fusion.meta, bf16[1024,1024]{1,0:T(8,128)(2,1)} %x_ref.7, bf16[1024,256]{1,0:T(8,128)(2,1)} %get-tuple-element.408.dq, bf16[1024,256]{1,0:T(8,128)(2,1)} %get-tuple-element.409.dk_a, bf16[1024,256]{1,0:T(8,128)(2,1)} %copy-done.4, ...), custom_call_target="tpu_custom_call" | custom-call | flops 1000 | bytes 1000 | tf_op jit(solution)/shard_map/back_in/pallas_call | solution.py:1009
  385.3 5.5 %late_grads.1 = (bf16[384,1024]{1,0:T(8,128)(2,1)}, bf16[384,1024]{1,0:T(8,128)(2,1)}) custom-call(s32[18]{0:T(128)} %pad_add_fusion.meta, bf16[1024,256]{1,0:T(8,128)(2,1)} %get-tuple-element.408.dq, bf16[1024,256]{1,0:T(8,128)(2,1)} %get-tuple-element.409.dk_a, bf16[1024,256]{1,0:T(8,128)(2,1)} %copy-done.4, bf16[1024,256]{1,0:T(8,128)(2,1)} %get-tuple-element.411.dv_a, ...), custom_call_target="tpu_custom_call" | custom-call | flops 1000 | bytes 1000 | tf_op jit(solution)/shard_map/late_grads/pallas_call | solution.py:818
  394.4 3.1 place.2
  399.0 2.3 collective-permute-done.79
  401.4 5.2 %collective-permute-done.76 = bf16[256,1024]{1,0:T(8,128)(2,1)S(1)} collective-permute-done((bf16[256,1024]{1,0:T(8,128)(2,1)}, bf16[256,1024]{1,0:T(8,128)(2,1)S(1)}, u32[]{:S(2)}, u32[]{:S(2)}) %collective-permute-start.76) | collective-permute-done | bytes 524320 | tf_op jit(solution)/shard_map/ppermute | solution.py:147
  412.2 3.8 collective-permute-start.80
  416.2 10.0 %collective-permute-done.85 = f32[2,1024]{1,0:T(2,128)S(1)} collective-permute-done((f32[2,1024]{1,0:T(2,128)S(1)}, f32[2,1024]{1,0:T(2,128)S(1)}, u32[]{:S(2)}, u32[]{:S(2)}) %collective-permute-start.85) | collective-permute-done | bytes 8224 | tf_op jit(solution)/shard_map/ppermute | solution.py:177
  427.2 2.5 collective-permute-start.86
  435.3 6.0 %collective-permute-done.90 = f32[2,1024]{1,0:T(2,128)S(1)} collective-permute-done((f32[2,1024]{1,0:T(2,128)S(1)}, f32[2,1024]{1,0:T(2,128)S(1)}, u32[]{:S(2)}, u32[]{:S(2)}) %collective-permute-start.90) | collective-permute-done | bytes 8224 | tf_op jit(solution)/shard_map/ppermute | solution.py:177
  446.1 12.4 %soap.1 = (f32[13,32,1024]{2,1,0:T(8,128)}, f32[13,32,1024]{2,1,0:T(8,128)}, f32[13,32,1024]{2,1,0:T(8,128)}, f32[13,32,1024]{2,1,0:T(8,128)}, f32[13,32,32]{2,1,0:T(8,128)}, /*index=5*/f32[13,32,32]{2,1,0:T(8,128)}) custom-call(s32[18]{0:T(128)} %pad_add_fusion.meta, s32[13]{0:T(128)} %broadcast_add_fusion.held, bf16[72,32,1024]{2,1,0:T(8,128)(2,1)} %bitcast.38, ...), custom_call_target="tpu_custom_call" | custom-call | flops 1000 | bytes 1000 | tf_op jit(solution)/shard_map/soap/pallas_call | solution.py:932
  461.4 4.6 orthonormal.1
  466.0 8.6 %collective-permute-done.93.refs_3_ = bf16[256,1024]{1,0:T(8,128)(2,1)S(1)} collective-permute-done((bf16[256,1024]{1,0:T(8,128)(2,1)S(1)}, bf16[256,1024]{1,0:T(8,128)(2,1)S(1)}, u32[]{:S(2)}, u32[]{:S(2)}) %collective-permute-start.93) | collective-permute-done | bytes 524320 | tf_op jit(solution)/shard_map/ppermute | solution.py:147
  477.5 3.8 place.3
  (395 shorter events, 123.3 us)
Async XLA Ops:
  7.2 147.0 %all-gather.3.cloned.1.call-start = ((), (), s32[]{:S(2)}) async-start(), calls=%async_computation.1 | async-start | bytes 5570560 | tf_op jit(solution)/shard_map/all_gather | solution.py:1061
  9.4 23.7 %collective-permute-start = (bf16[7,32,1024]{2,1,0:T(8,128)(2,1)S(1)}, bf16[7,32,1024]{2,1,0:T(8,128)(2,1)S(1)}, u32[]{:S(2)}, u32[]{:S(2)}) collective-permute-start(bf16[7,32,1024]{2,1,0:T(8,128)(2,1)S(1)} %slice.255.refs_0_), channel_id=1, source_target_pairs={{0,4},{4,0},{8,12},{12,8},{16,20},{20,16},{24,28},{28,24},{1,5},{5... | collective-permute-start | bytes 1376264 | tf_op jit(solution)/shard_map/ppermute | solution.py:67
  9.6 23.6 %collective-permute-start.1 = (bf16[7,32,1024]{2,1,0:T(8,128)(2,1)S(1)}, bf16[7,32,1024]{2,1,0:T(8,128)(2,1)S(1)}, u32[]{:S(2)}, u32[]{:S(2)}) collective-permute-start(bf16[7,32,1024]{2,1,0:T(8,128)(2,1)S(1)} %slice.255.refs_0_), channel_id=1, source_target_pairs={{0,8},{4,12},{8,0},{12,4},{16,24},{20,28},{24,16},{28,20},{1,9},{5... | collective-permute-start | bytes 1376264 | tf_op jit(solution)/shard_map/ppermute | solution.py:67
  12.5 20.7 %collective-permute-start.2 = (bf16[7,32,1024]{2,1,0:T(8,128)(2,1)S(1)}, bf16[7,32,1024]{2,1,0:T(8,128)(2,1)S(1)}, u32[]{:S(2)}, u32[]{:S(2)}) collective-permute-start(bf16[7,32,1024]{2,1,0:T(8,128)(2,1)S(1)} %slice.255.refs_0_), channel_id=1, source_target_pairs={{0,16},{4,20},{8,24},{12,28},{16,0},{20,4},{24,8},{28,12},{1,17},{... | collective-permute-start | bytes 1376264 | tf_op jit(solution)/shard_map/ppermute | solution.py:67
  14.0 17.6 %collective-permute-start.4 = (bf16[6,32,1024]{2,1,0:T(8,128)(2,1)S(1)}, bf16[6,32,1024]{2,1,0:T(8,128)(2,1)S(1)}, u32[]{:S(2)}, u32[]{:S(2)}) collective-permute-start(bf16[6,32,1024]{2,1,0:T(8,128)(2,1)S(1)} %slice.256.refs_8_), channel_id=1, source_target_pairs={{0,8},{4,12},{8,0},{12,4},{16,24},{20,28},{24,16},{28,20},{1,9},{5... | collective-permute-start | bytes 1179656 | tf_op jit(solution)/shard_map/ppermute | solution.py:67
  14.6 18.6 %collective-permute-start.5 = (bf16[6,32,1024]{2,1,0:T(8,128)(2,1)S(1)}, bf16[6,32,1024]{2,1,0:T(8,128)(2,1)S(1)}, u32[]{:S(2)}, u32[]{:S(2)}) collective-permute-start(bf16[6,32,1024]{2,1,0:T(8,128)(2,1)S(1)} %slice.256.refs_8_), channel_id=1, source_target_pairs={{0,16},{4,20},{8,24},{12,28},{16,0},{20,4},{24,8},{28,12},{1,17},{... | collective-permute-start | bytes 1179656 | tf_op jit(solution)/shard_map/ppermute | solution.py:67
  33.3 13.7 %collective-permute-start.6 = (bf16[7,32,1024]{2,1,0:T(8,128)(2,1)S(1)}, bf16[7,32,1024]{2,1,0:T(8,128)(2,1)S(1)}, u32[]{:S(2)}, u32[]{:S(2)}) collective-permute-start(bf16[7,32,1024]{2,1,0:T(8,128)(2,1)S(1)} %collective-permute-done.1.refs_2_), channel_id=1, source_target_pairs={{0,4},{4,0},{8,12},{12,8},{16,20},{20,16},{24,28},{28,24},{1,5},{5... | collective-permute-start | bytes 1376264 | tf_op jit(solution)/shard_map/ppermute | solution.py:67
  33.8 13.2 %collective-permute-start.8 = (bf16[7,32,1024]{2,1,0:T(8,128)(2,1)S(1)}, bf16[7,32,1024]{2,1,0:T(8,128)(2,1)S(1)}, u32[]{:S(2)}, u32[]{:S(2)}) collective-permute-start(bf16[7,32,1024]{2,1,0:T(8,128)(2,1)S(1)} %collective-permute-done.1.refs_2_), channel_id=1, source_target_pairs={{0,16},{4,20},{8,24},{12,28},{16,0},{20,4},{24,8},{28,12},{1,17},{... | collective-permute-start | bytes 1376264 | tf_op jit(solution)/shard_map/ppermute | solution.py:67
  59.8 254.6 %reduce-scatter.2.cloned.1.call-start = ((), (), s32[]{:S(2)}) async-start(), calls=%async_computation.2 | async-start | bytes 2949120 | tf_op jit(solution)/shard_map/reduce_scatter | solution.py:1109
  60.2 15.0 %collective-permute-start.15 = (bf16[1024,256]{1,0:T(8,128)(2,1)}, bf16[1024,256]{1,0:T(8,128)(2,1)S(1)}, u32[]{:S(2)}, u32[]{:S(2)}) collective-permute-start(bf16[1024,256]{1,0:T(8,128)(2,1)} %get-tuple-element.273.refs_0_.refs_4_), channel_id=1, source_target_pairs={{0,8},{4,12},{8,0},{12,4},{16,24},{20,28},{24,16},{28,20},{1,9},{5... | collective-permute-start | bytes 1572872 | tf_op jit(solution)/shard_map/ppermute | solution.py:67
  60.7 15.0 %collective-permute-start.16 = (bf16[1024,256]{1,0:T(8,128)(2,1)}, bf16[1024,256]{1,0:T(8,128)(2,1)S(1)}, u32[]{:S(2)}, u32[]{:S(2)}) collective-permute-start(bf16[1024,256]{1,0:T(8,128)(2,1)} %get-tuple-element.273.refs_0_.refs_4_), channel_id=1, source_target_pairs={{0,16},{4,20},{8,24},{12,28},{16,0},{20,4},{24,8},{28,12},{1,17},{... | collective-permute-start | bytes 1572872 | tf_op jit(solution)/shard_map/ppermute | solution.py:67
  61.5 14.3 %collective-permute-start.17 = (bf16[1024,256]{1,0:T(8,128)(2,1)}, bf16[1024,256]{1,0:T(8,128)(2,1)S(1)}, u32[]{:S(2)}, u32[]{:S(2)}) collective-permute-start(bf16[1024,256]{1,0:T(8,128)(2,1)} %get-tuple-element.282.refs_8_.refs_12_), channel_id=1, source_target_pairs={{0,4},{4,0},{8,12},{12,8},{16,20},{20,16},{24,28},{28,24},{1,5},{5... | collective-permute-start | bytes 1572872 | tf_op jit(solution)/shard_map/ppermute | solution.py:67
  61.5 24.4 %collective-permute-start.18 = (bf16[1024,256]{1,0:T(8,128)(2,1)}, bf16[1024,256]{1,0:T(8,128)(2,1)S(1)}, u32[]{:S(2)}, u32[]{:S(2)}) collective-permute-start(bf16[1024,256]{1,0:T(8,128)(2,1)} %get-tuple-element.282.refs_8_.refs_12_), channel_id=1, source_target_pairs={{0,8},{4,12},{8,0},{12,4},{16,24},{20,28},{24,16},{28,20},{1,9},{5... | collective-permute-start | bytes 1572872 | tf_op jit(solution)/shard_map/ppermute | solution.py:67
  63.0 23.2 %collective-permute-start.19 = (bf16[1024,256]{1,0:T(8,128)(2,1)}, bf16[1024,256]{1,0:T(8,128)(2,1)}, u32[]{:S(2)}, u32[]{:S(2)}) collective-permute-start(bf16[1024,256]{1,0:T(8,128)(2,1)} %get-tuple-element.282.refs_8_.refs_12_), channel_id=1, source_target_pairs={{0,16},{4,20},{8,24},{12,28},{16,0},{20,4},{24,8},{28,12},{1,17},{... | collective-permute-start | bytes 1572872 | tf_op jit(solution)/shard_map/ppermute | solution.py:67
  86.2 14.4 %collective-permute-start.22 = (bf16[1024,256]{1,0:T(8,128)(2,1)S(1)}, bf16[1024,256]{1,0:T(8,128)(2,1)}, u32[]{:S(2)}, u32[]{:S(2)}) collective-permute-start(bf16[1024,256]{1,0:T(8,128)(2,1)S(1)} %collective-permute-done.15.refs_2_.refs_6_), channel_id=1, source_target_pairs={{0,16},{4,20},{8,24},{12,28},{16,0},{20,4},{24,8},{28,12},{1,17},{... | collective-permute-start | bytes 1572872 | tf_op jit(solution)/shard_map/ppermute | solution.py:67
  87.2 13.4 %collective-permute-start.23 = (bf16[1024,256]{1,0:T(8,128)(2,1)S(1)}, bf16[1024,256]{1,0:T(8,128)(2,1)}, u32[]{:S(2)}, u32[]{:S(2)}) collective-permute-start(bf16[1024,256]{1,0:T(8,128)(2,1)S(1)} %collective-permute-done.18.refs_10_.refs_14_), channel_id=1, source_target_pairs={{0,4},{4,0},{8,12},{12,8},{16,20},{20,16},{24,28},{28,24},{1,5},{5... | collective-permute-start | bytes 1572872 | tf_op jit(solution)/shard_map/ppermute | solution.py:67
  87.5 13.1 %collective-permute-start.24 = (bf16[1024,256]{1,0:T(8,128)(2,1)}, bf16[1024,256]{1,0:T(8,128)(2,1)}, u32[]{:S(2)}, u32[]{:S(2)}) collective-permute-start(bf16[1024,256]{1,0:T(8,128)(2,1)} %collective-permute-done.19.refs_12_.refs_16_), channel_id=1, source_target_pairs={{0,4},{4,0},{8,12},{12,8},{16,20},{20,16},{24,28},{28,24},{1,5},{5... | collective-permute-start | bytes 1572872 | tf_op jit(solution)/shard_map/ppermute | solution.py:67
  88.9 14.3 %collective-permute-start.25 = (bf16[1024,256]{1,0:T(8,128)(2,1)}, bf16[1024,256]{1,0:T(8,128)(2,1)}, u32[]{:S(2)}, u32[]{:S(2)}) collective-permute-start(bf16[1024,256]{1,0:T(8,128)(2,1)} %collective-permute-done.19.refs_12_.refs_16_), channel_id=1, source_target_pairs={{0,8},{4,12},{8,0},{12,4},{16,24},{20,28},{24,16},{28,20},{1,9},{5... | collective-permute-start | bytes 1572872 | tf_op jit(solution)/shard_map/ppermute | solution.py:67
  104.8 16.1 %collective-permute-start.28 = (bf16[256,1024]{1,0:T(8,128)(2,1)S(1)}, bf16[256,1024]{1,0:T(8,128)(2,1)S(1)}, u32[]{:S(2)}, u32[]{:S(2)}) collective-permute-start(bf16[256,1024]{1,0:T(8,128)(2,1)S(1)} %constant_dynamic-slice_fusion), channel_id=1, source_target_pairs={{0,8},{4,12},{8,0},{12,4},{16,24},{20,28},{24,16},{28,20},{1,9},{5... | collective-permute-start | bytes 1572872 | tf_op jit(solution)/shard_map/ppermute | solution.py:67
  106.4 24.8 %collective-permute-start.29 = (bf16[256,1024]{1,0:T(8,128)(2,1)S(1)}, bf16[256,1024]{1,0:T(8,128)(2,1)S(1)}, u32[]{:S(2)}, u32[]{:S(2)}) collective-permute-start(bf16[256,1024]{1,0:T(8,128)(2,1)S(1)} %constant_dynamic-slice_fusion), channel_id=1, source_target_pairs={{0,16},{4,20},{8,24},{12,28},{16,0},{20,4},{24,8},{28,12},{1,17},{... | collective-permute-start | bytes 1572872 | tf_op jit(solution)/shard_map/ppermute | solution.py:67
  107.4 23.8 %collective-permute-start.30 = (bf16[256,1024]{1,0:T(8,128)(2,1)S(1)}, bf16[256,1024]{1,0:T(8,128)(2,1)S(1)}, u32[]{:S(2)}, u32[]{:S(2)}) collective-permute-start(bf16[256,1024]{1,0:T(8,128)(2,1)S(1)} %constant_dynamic-slice_fusion), channel_id=1, source_target_pairs={{0,24},{4,28},{8,16},{12,20},{16,8},{20,12},{24,0},{28,4},{1,25},{... | collective-permute-start | bytes 1572872 | tf_op jit(solution)/shard_map/ppermute | solution.py:67
  135.4 17.3 %collective-permute-start.32 = (bf16[256,256]{1,0:T(8,128)(2,1)S(1)}, bf16[256,256]{1,0:T(8,128)(2,1)S(1)}, u32[]{:S(2)}, u32[]{:S(2)}) collective-permute-start(bf16[256,256]{1,0:T(8,128)(2,1)S(1)} %get-tuple-element.529), channel_id=1, source_target_pairs={{0,2},{1,3},{2,0},{3,1},{4,6},{5,7},{6,4},{7,5},{8,10},{9,11},{10,... | collective-permute-start | bytes 393224 | tf_op jit(solution)/shard_map/ppermute | solution.py:147
  138.0 14.7 %collective-permute-start.33 = (bf16[256,256]{1,0:T(8,128)(2,1)S(1)}, bf16[256,256]{1,0:T(8,128)(2,1)S(1)}, u32[]{:S(2)}, u32[]{:S(2)}) collective-permute-start(bf16[256,256]{1,0:T(8,128)(2,1)S(1)} %get-tuple-element.528), channel_id=1, source_target_pairs={{0,3},{1,0},{2,1},{3,2},{4,7},{5,4},{6,5},{7,6},{8,11},{9,8},{10,9... | collective-permute-start | bytes 393224 | tf_op jit(solution)/shard_map/ppermute | solution.py:147
  159.7 28.9 %collective-permute-start.34 = (bf16[1024,1024]{1,0:T(8,128)(2,1)S(1)}, bf16[1024,1024]{1,0:T(8,128)(2,1)S(1)}, u32[]{:S(2)}, u32[]{:S(2)}) collective-permute-start(bf16[1024,1024]{1,0:T(8,128)(2,1)S(1)} %pad_maximum_fusion), channel_id=1, source_target_pairs={{0,4},{4,0},{8,12},{12,8},{16,20},{20,16},{24,28},{28,24},{1,5},{5... | collective-permute-start | bytes 6291464 | tf_op jit(solution)/shard_map/ppermute | solution.py:67
  217.4 16.5 %collective-permute-start.53 = (bf16[1024,1024]{1,0:T(8,128)(2,1)}, bf16[1024,1024]{1,0:T(8,128)(2,1)S(1)}, u32[]{:S(2)}, u32[]{:S(2)}) collective-permute-start(bf16[1024,1024]{1,0:T(8,128)(2,1)} %get-tuple-element.339), channel_id=1, source_target_pairs={{0,4},{4,0},{8,12},{12,8},{16,20},{20,16},{24,28},{28,24},{1,5},{5... | collective-permute-start | bytes 6291464 | tf_op jit(solution)/shard_map/ppermute | solution.py:67
  217.6 14.2 %collective-permute-start.52 = (bf16[512,512]{1,0:T(8,128)(2,1)S(1)}, bf16[512,512]{1,0:T(8,128)(2,1)S(1)}, u32[]{:S(2)}, u32[]{:S(2)}) collective-permute-start(bf16[512,512]{1,0:T(8,128)(2,1)S(1)} %get-tuple-element.337), channel_id=1, source_target_pairs={{0,8},{4,12},{8,0},{12,4},{16,24},{20,28},{24,16},{28,20},{1,9},{5... | collective-permute-start | bytes 1572872 | tf_op jit(solution)/shard_map/ppermute | solution.py:67
  219.2 13.9 %collective-permute-start.51 = (bf16[512,512]{1,0:T(8,128)(2,1)S(1)}, bf16[512,512]{1,0:T(8,128)(2,1)S(1)}, u32[]{:S(2)}, u32[]{:S(2)}) collective-permute-start(bf16[512,512]{1,0:T(8,128)(2,1)S(1)} %get-tuple-element.335), channel_id=1, source_target_pairs={{0,16},{4,20},{8,24},{12,28},{16,0},{20,4},{24,8},{28,12},{1,17},{... | collective-permute-start | bytes 1572872 | tf_op jit(solution)/shard_map/ppermute | solution.py:67
  266.4 179.7 %all-gather.5.cloned.1.call-start = ((), (), s32[]{:S(2)}) async-start(), calls=%async_computation.3 | async-start | bytes 5308416 | tf_op jit(solution)/shard_map/all_gather | solution.py:1064
  266.6 23.1 %collective-permute-start.60 = (bf16[384,1024]{1,0:T(8,128)(2,1)S(1)}, bf16[384,1024]{1,0:T(8,128)(2,1)}, u32[]{:S(2)}, u32[]{:S(2)}) collective-permute-start(bf16[384,1024]{1,0:T(8,128)(2,1)S(1)} %get-tuple-element.359), channel_id=1, source_target_pairs={{0,8},{4,12},{8,0},{12,4},{16,24},{20,28},{24,16},{28,20},{1,9},{5... | collective-permute-start | bytes 2359304 | tf_op jit(solution)/shard_map/ppermute | solution.py:67
  267.3 36.1 %collective-permute-start.61 = (bf16[384,1024]{1,0:T(8,128)(2,1)S(1)}, bf16[384,1024]{1,0:T(8,128)(2,1)}, u32[]{:S(2)}, u32[]{:S(2)}) collective-permute-start(bf16[384,1024]{1,0:T(8,128)(2,1)S(1)} %get-tuple-element.360), channel_id=1, source_target_pairs={{0,16},{4,20},{8,24},{12,28},{16,0},{20,4},{24,8},{28,12},{1,17},{... | collective-permute-start | bytes 2359304 | tf_op jit(solution)/shard_map/ppermute | solution.py:67
  268.1 35.3 %collective-permute-start.62 = (bf16[384,1024]{1,0:T(8,128)(2,1)S(1)}, bf16[384,1024]{1,0:T(8,128)(2,1)}, u32[]{:S(2)}, u32[]{:S(2)}) collective-permute-start(bf16[384,1024]{1,0:T(8,128)(2,1)S(1)} %get-tuple-element.361), channel_id=1, source_target_pairs={{0,24},{4,28},{8,16},{12,20},{16,8},{20,12},{24,0},{28,4},{1,25},{... | collective-permute-start | bytes 2359304 | tf_op jit(solution)/shard_map/ppermute | solution.py:67
  322.3 25.3 %collective-permute-start.66 = (bf16[2048,256]{1,0:T(8,128)(2,1)S(1)}, bf16[2048,256]{1,0:T(8,128)(2,1)S(1)}, u32[]{:S(2)}, u32[]{:S(2)}) collective-permute-start(bf16[2048,256]{1,0:T(8,128)(2,1)S(1)} %get-tuple-element.387), channel_id=1, source_target_pairs={{0,8},{4,12},{8,0},{12,4},{16,24},{20,28},{24,16},{28,20},{1,9},{5... | collective-permute-start | bytes 3145736 | tf_op jit(solution)/shard_map/ppermute | solution.py:67
  323.8 24.9 %collective-permute-start.65 = (bf16[2048,256]{1,0:T(8,128)(2,1)S(1)}, bf16[2048,256]{1,0:T(8,128)(2,1)S(1)}, u32[]{:S(2)}, u32[]{:S(2)}) collective-permute-start(bf16[2048,256]{1,0:T(8,128)(2,1)S(1)} %get-tuple-element.385), channel_id=1, source_target_pairs={{0,16},{4,20},{8,24},{12,28},{16,0},{20,4},{24,8},{28,12},{1,17},{... | collective-permute-start | bytes 3145736 | tf_op jit(solution)/shard_map/ppermute | solution.py:67
  325.3 15.2 %collective-permute-start.67 = (bf16[256,1024]{1,0:T(8,128)(2,1)S(1)}, bf16[256,1024]{1,0:T(8,128)(2,1)S(1)}, u32[]{:S(2)}, u32[]{:S(2)}) collective-permute-start(bf16[256,1024]{1,0:T(8,128)(2,1)S(1)} %fusion.8.refs_0_), channel_id=1, source_target_pairs={{0,1},{1,2},{2,3},{3,0},{4,5},{5,6},{6,7},{7,4},{8,9},{9,10},{10,1... | collective-permute-start | bytes 1572872 | tf_op jit(solution)/shard_map/ppermute | solution.py:147
  340.5 14.3 %collective-permute-start.68 = (bf16[256,1024]{1,0:T(8,128)(2,1)S(1)}, bf16[256,1024]{1,0:T(8,128)(2,1)S(1)}, u32[]{:S(2)}, u32[]{:S(2)}) collective-permute-start(bf16[256,1024]{1,0:T(8,128)(2,1)S(1)} %collective-permute-done.67.refs_1_), channel_id=1, source_target_pairs={{0,1},{1,2},{2,3},{3,0},{4,5},{5,6},{6,7},{7,4},{8,9},{9,10},{10,1... | collective-permute-start | bytes 1572872 | tf_op jit(solution)/shard_map/ppermute | solution.py:147
  374.2 16.8 %collective-permute-start.72 = (bf16[256,1024]{1,0:T(8,128)(2,1)}, bf16[256,1024]{1,0:T(8,128)(2,1)S(1)}, u32[]{:S(2)}, u32[]{:S(2)}) collective-permute-start(bf16[256,1024]{1,0:T(8,128)(2,1)} %get-tuple-element.407), channel_id=1, source_target_pairs={{0,3},{1,0},{2,1},{3,2},{4,7},{5,4},{6,5},{7,6},{8,11},{9,8},{10,9... | collective-permute-start | bytes 1572872 | tf_op jit(solution)/shard_map/ppermute | solution.py:147
  374.8 16.1 %collective-permute-start.73 = (bf16[32,1024]{1,0:T(8,128)(2,1)S(1)}, bf16[32,1024]{1,0:T(8,128)(2,1)S(1)}, u32[]{:S(2)}, u32[]{:S(2)}) collective-permute-start(bf16[32,1024]{1,0:T(8,128)(2,1)S(1)} %get-tuple-element.526), channel_id=1, source_target_pairs={{0,1},{1,2},{2,3},{3,0},{4,5},{5,6},{6,7},{7,4},{8,9},{9,10},{10,1... | collective-permute-start | bytes 196616 | tf_op jit(solution)/shard_map/ppermute | solution.py:147
  376.9 14.1 %collective-permute-start.74 = (bf16[32,1024]{1,0:T(8,128)(2,1)S(1)}, bf16[32,1024]{1,0:T(8,128)(2,1)S(1)}, u32[]{:S(2)}, u32[]{:S(2)}) collective-permute-start(bf16[32,1024]{1,0:T(8,128)(2,1)S(1)} %get-tuple-element.525), channel_id=1, source_target_pairs={{0,2},{1,3},{2,0},{3,1},{4,6},{5,7},{6,4},{7,5},{8,10},{9,11},{10,... | collective-permute-start | bytes 196616 | tf_op jit(solution)/shard_map/ppermute | solution.py:147
  376.9 14.1 %collective-permute-start.75 = (bf16[32,1024]{1,0:T(8,128)(2,1)S(1)}, bf16[32,1024]{1,0:T(8,128)(2,1)S(1)}, u32[]{:S(2)}, u32[]{:S(2)}) collective-permute-start(bf16[32,1024]{1,0:T(8,128)(2,1)S(1)} %get-tuple-element.524), channel_id=1, source_target_pairs={{0,3},{1,0},{2,1},{3,2},{4,7},{5,4},{6,5},{7,6},{8,11},{9,8},{10,9... | collective-permute-start | bytes 196616 | tf_op jit(solution)/shard_map/ppermute | solution.py:147
  391.0 15.6 %collective-permute-start.77 = (bf16[384,1024]{1,0:T(8,128)(2,1)}, bf16[384,1024]{1,0:T(8,128)(2,1)S(1)}, u32[]{:S(2)}, u32[]{:S(2)}) collective-permute-start(bf16[384,1024]{1,0:T(8,128)(2,1)} %get-tuple-element.430), channel_id=1, source_target_pairs={{0,4},{4,0},{8,12},{12,8},{16,20},{20,16},{24,28},{28,24},{1,5},{5... | collective-permute-start | bytes 2359304 | tf_op jit(solution)/shard_map/ppermute | solution.py:67
  392.1 14.5 %collective-permute-start.76 = (bf16[256,1024]{1,0:T(8,128)(2,1)}, bf16[256,1024]{1,0:T(8,128)(2,1)S(1)}, u32[]{:S(2)}, u32[]{:S(2)}) collective-permute-start(bf16[256,1024]{1,0:T(8,128)(2,1)} %add_convert_fusion.8), channel_id=1, source_target_pairs={{0,3},{1,0},{2,1},{3,2},{4,7},{5,4},{6,5},{7,6},{8,11},{9,8},{10,9... | collective-permute-start | bytes 1572872 | tf_op jit(solution)/shard_map/ppermute | solution.py:147
  408.5 17.7 %collective-permute-start.81 = (bf16[96,1024]{1,0:T(8,128)(2,1)S(1)}, bf16[96,1024]{1,0:T(8,128)(2,1)S(1)}, u32[]{:S(2)}, u32[]{:S(2)}) collective-permute-start(bf16[96,1024]{1,0:T(8,128)(2,1)S(1)} %get-tuple-element.521), channel_id=1, source_target_pairs={{0,8},{4,12},{8,0},{12,4},{16,24},{20,28},{24,16},{28,20},{1,9},{5... | collective-permute-start | bytes 589832 | tf_op jit(solution)/shard_map/ppermute | solution.py:67
  410.0 16.1 %collective-permute-start.82 = (bf16[96,1024]{1,0:T(8,128)(2,1)S(1)}, bf16[96,1024]{1,0:T(8,128)(2,1)S(1)}, u32[]{:S(2)}, u32[]{:S(2)}) collective-permute-start(bf16[96,1024]{1,0:T(8,128)(2,1)S(1)} %get-tuple-element.523), channel_id=1, source_target_pairs={{0,16},{4,20},{8,24},{12,28},{16,0},{20,4},{24,8},{28,12},{1,17},{... | collective-permute-start | bytes 589832 | tf_op jit(solution)/shard_map/ppermute | solution.py:67
  410.6 15.6 %collective-permute-start.83 = (bf16[96,1024]{1,0:T(8,128)(2,1)S(1)}, bf16[96,1024]{1,0:T(8,128)(2,1)S(1)}, u32[]{:S(2)}, u32[]{:S(2)}) collective-permute-start(bf16[96,1024]{1,0:T(8,128)(2,1)S(1)} %get-tuple-element.522), channel_id=1, source_target_pairs={{0,24},{4,28},{8,16},{12,20},{16,8},{20,12},{24,0},{28,4},{1,25},{... | collective-permute-start | bytes 589832 | tf_op jit(solution)/shard_map/ppermute | solution.py:67
  412.2 14.1 %collective-permute-start.80 = (bf16[256,1024]{1,0:T(8,128)(2,1)S(1)}, bf16[256,1024]{1,0:T(8,128)(2,1)S(1)}, u32[]{:S(2)}, u32[]{:S(2)}) collective-permute-start(bf16[256,1024]{1,0:T(8,128)(2,1)S(1)} %add_convert_fusion.7), channel_id=1, source_target_pairs={{0,3},{1,0},{2,1},{3,2},{4,7},{5,4},{6,5},{7,6},{8,11},{9,8},{10,9... | collective-permute-start | bytes 1572872 | tf_op jit(solution)/shard_map/ppermute | solution.py:147
  427.2 14.7 %collective-permute-start.86 = (bf16[256,1024]{1,0:T(8,128)(2,1)S(1)}, bf16[256,1024]{1,0:T(8,128)(2,1)S(1)}, u32[]{:S(2)}, u32[]{:S(2)}) collective-permute-start(bf16[256,1024]{1,0:T(8,128)(2,1)S(1)} %fusion.6.refs_0_), channel_id=1, source_target_pairs={{0,1},{1,2},{2,3},{3,0},{4,5},{5,6},{6,7},{7,4},{8,9},{9,10},{10,1... | collective-permute-start | bytes 1572872 | tf_op jit(solution)/shard_map/ppermute | solution.py:147
  442.0 16.5 %collective-permute-start.91 = (bf16[256,1024]{1,0:T(8,128)(2,1)S(1)}, bf16[256,1024]{1,0:T(8,128)(2,1)S(1)}, u32[]{:S(2)}, u32[]{:S(2)}) collective-permute-start(bf16[256,1024]{1,0:T(8,128)(2,1)S(1)} %collective-permute-done.86.refs_1_), channel_id=1, source_target_pairs={{0,1},{1,2},{2,3},{3,0},{4,5},{5,6},{6,7},{7,4},{8,9},{9,10},{10,1... | collective-permute-start | bytes 1572872 | tf_op jit(solution)/shard_map/ppermute | solution.py:147
  458.5 16.0 %collective-permute-start.93 = (bf16[256,1024]{1,0:T(8,128)(2,1)S(1)}, bf16[256,1024]{1,0:T(8,128)(2,1)S(1)}, u32[]{:S(2)}, u32[]{:S(2)}) collective-permute-start(bf16[256,1024]{1,0:T(8,128)(2,1)S(1)} %collective-permute-done.91.refs_2_), channel_id=1, source_target_pairs={{0,1},{1,2},{2,3},{3,0},{4,5},{5,6},{6,7},{7,4},{8,9},{9,10},{10,1... | collective-permute-start | bytes 1572872 | tf_op jit(solution)/shard_map/ppermute | solution.py:147
  (135 other events, 1275.8 us)
Sparse Core Ops, SparseCore 0:
  59.9 94.2 all-gather.2
  266.5 47.7 reduce-scatter.1
  369.1 37.0 all-gather.4

commit v4 on v3

--- a/solution.py
+++ b/solution.py
@@ -449,7 +449,7 @@
     keys, values = refs[:n], refs[n : 2 * n]
     dq_ref = refs[2 * n]
     outs = (refs[2 * n + 1 : 2 * n + 3], refs[2 * n + 3 : 2 * n + 5])
-    kbuf, vbuf, dk_acc, dv_acc, g_ref, acc, stage, table, blocks, sems = refs[2 * n + 5 :]
+    kbuf, vbuf, dk_acc, dv_acc, g_ref, acc, stage, table, blocks, sems, out_sems = refs[2 * n + 5 :]
     tok, width = q_ref.shape
     me = meta[0]
     block = tok // spans
@@ -511,21 +511,24 @@
 
     lax.fori_loop(0, tok // qt, query_tile, 0)
 
+    depth = stage.shape[1]
+
     def put(which, m):
         side, at = reduce_place(n, which, m)
         out = outs[which][side].at[at * tok : (at + 1) * tok]
-        return pltpu.make_async_copy(stage.at[which], out, sems.at[2 + which])
+        return pltpu.make_async_copy(stage.at[which, m % depth], out, out_sems.at[which, m % depth])
 
     for m in range(n):
         at = pl.ds(pl.multiple_of(lax.bitwise_xor(me, m) * tok, tok), tok)
         for which in range(2):
-            if m:
-                put(which, m - 1).wait()
+            if m >= depth:
+                put(which, m - depth).wait()
             rows = dk_acc[at, :] * scale if which == 0 else dv_acc[at, :]
-            stage[which] = rows.astype(BF)
+            stage[which, m % depth] = rows.astype(BF)
             put(which, m).start()
-    for which in range(2):
-        put(which, n - 1).wait()
+    for m in range(max(n - depth, 0), n):
+        for which in range(2):
+            put(which, m).wait()
 
 
 def attend_back(meta, q, grads, wide, logs, keys, values, docs, picks):
@@ -545,10 +548,11 @@
             pltpu.VMEM((n * tok, width), F32),
             pltpu.VMEM((tok, width), BF),
             pltpu.VMEM((width // HD, HD, qt), F32),
-            pltpu.VMEM((2, tok, width), BF),
+            pltpu.VMEM((2, 4, tok, width), BF),
             pltpu.SMEM((n * tok // MEMB,), I32),
             pltpu.SMEM((picks,), I32),
-            pltpu.SemaphoreType.DMA((4,)),
+            pltpu.SemaphoreType.DMA((2,)),
+            pltpu.SemaphoreType.DMA((2, 4)),
         ],
         compiler_params=params(),
         cost_estimate=QUICK,
@@ -608,14 +612,14 @@
     def _():
         for m in range(n):
             spot = gather_place(n, m)
-            pltpu.make_async_copy(pieces[m], rows.at[spot, :, :half], sem).start()
-            pltpu.make_async_copy(pieces[n + m], rows.at[spot, :, half:], sem).start()
+            pltpu.make_async_copy(pieces[m], rows.at[spot, :, :half], sem.at[spot // per]).start()
+            pltpu.make_async_copy(pieces[n + m], rows.at[spot, :, half:], sem.at[spot // per]).start()
         for t in range(spans):
             for kind, first in enumerate((0, units, 2 * units)):
                 w[first + t * fs : first + (t + 1) * fs] = w_ref[t, kind * fs : (kind + 1) * fs]
-        pltpu.make_async_copy(rows, rows, sem).wait()
 
     these = pl.ds(step * per, per)
+    pltpu.make_async_copy(rows.at[these], rows.at[these], sem.at[step]).wait()
     normed = rows[these].reshape(tile, d)
     normed_ref[...] = normed
     inner = mm(normed, w[: 2 * units], NT)
@@ -671,7 +675,7 @@
                 pltpu.VMEM((n, block, d), BF),
                 pltpu.VMEM((n, block, d), BF),
                 pltpu.VMEM((3 * units, d), BF),
-                pltpu.SemaphoreType.DMA,
+                pltpu.SemaphoreType.DMA((rows // tile,)),
                 pltpu.SemaphoreType.DMA,
             ],
         ),
@@ -1108,7 +1112,7 @@
     parts = [swap(part, n_seq, m) if m else part for m, part in parts.items()]
     feed_sums = lax.psum_scatter(feed_sums.reshape(-1, d), "tp", scatter_dimension=0, tiled=True)
     dq, *pairs = attend_back(meta, q, d_heads, wide, logs, keys, values, docs, picks)
-    parts, feed_sums, dq, pairs = pin(parts, feed_sums, dq, pairs)
+    parts, dq, pairs = pin(parts, dq, pairs)
     pairs = reduce_levels(pairs, n_seq, 0)
     total = sum(part.astype(F32) for part in parts)
     output = (mixed + total[:block]).astype(BF)
@@ -1164,6 +1168,7 @@
             part = back_rest[k * block : (k + 1) * block]
             if k:
                 total = plus(part, came)
+                total, late, gain_total = pin(total, late, gain_total)
                 continue
             d_normed_one = part.astype(F32) + came.astype(F32)
             unit_one, inverse_one, _ = norm_rows(mine(tokens).astype(F32), gains[0])

time: 492 us -> 484 us (0.984)
  waiting for transfers between devices: 230 us -> 222 us
    reduce_scatter x1, waiting for transfers between devices: 10.9 us -> 2.09 us  [shards(): lax.psum_scatter(feed_sums.reshape(-1, d), 'tp', scatter_dimension=0, til...]
  transfers between devices with their start and end apart: 97 -> 97, of which waited for: 48 -> 48; matrix products, arithmetic and copies ran while one was open for 5% -> 5% of each run, Pallas kernels for 16% -> 15%
where the time goes in v4:
time: 484 us; the launch traced here: 482 us
  waiting for transfers between devices  222 us (46%)
  Pallas kernels  120 us (25%)
  starting transfers between devices  85.7 us (18%)
  other arithmetic  19.4 us (4%)
  local copies, waits for them, and re-layouts  18.9 us (4%)
  between operations  15.3 us (3%)
    ppermute x71, waiting for transfers between devices, swap(): return lax.ppermute(value, 'seq', [(i, i ^ bit) for i in range(count)])  146 us
    ppermute x18, waiting for transfers between devices, ring(): lax.ppermute(value, 'tp', [(i, (i + step) % count) for i in range(count)])  54.4 us
    ppermute x71, starting transfers between devices, swap(): return lax.ppermute(value, 'seq', [(i, i ^ bit) for i in range(count)])  53.1 us
    ppermute x18, starting transfers between devices, ring(): lax.ppermute(value, 'tp', [(i, (i + step) % count) for i in range(count)])  27.8 us
    pallas_call x1, Pallas kernels, feed_forward(): pl.pallas_call(functools.partial(feed_kernel, (n, spans, fs)), grid_spec=...  20.2 us
    ppermute x5, waiting for transfers between devices, sum_steps(): lax.ppermute(v, axis, pairs)  18.8 us
    pallas_call x1, Pallas kernels, attend_back(): pl.pallas_call(functools.partial(attend_back_kernel, (n, docs, picks, qt,...  15.4 us
    pallas_call x1, Pallas kernels, soap(): pl.pallas_call(functools.partial(soap_kernel, (n, late_panels, out_panels...  12.4 us
  transfers between devices with their start and end apart: 97, of which 48 were waited for; matrix products, arithmetic and copies ran while one was open for 5% of the time, Pallas kernels for 15%

profile of v4, /device:TPU:0, one launch (start us, length us, event | category | flops | bytes accessed | tf_op | source)
XLA Modules:
  0.0 481.9 jit_solution(18385376917982232062)
XLA Ops:
  9.6 2.9 collective-permute-start.1
  14.6 17.1 %collective-permute-done.4.refs_10_ = bf16[6,32,1024]{2,1,0:T(8,128)(2,1)S(1)} collective-permute-done((bf16[6,32,1024]{2,1,0:T(8,128)(2,1)S(1)}, bf16[6,32,1024]{2,1,0:T(8,128)(2,1)S(1)}, u32[]{:S(2)}, u32[]{:S(2)}) %collective-permute-start.4) | collective-permute-done | bytes 393248 | tf_op jit(solution)/shard_map/ppermute | solution.py:67
  36.1 10.9 %collective-permute-done.11.refs_14_ = bf16[6,32,1024]{2,1,0:T(8,128)(2,1)} collective-permute-done((bf16[6,32,1024]{2,1,0:T(8,128)(2,1)S(1)}, bf16[6,32,1024]{2,1,0:T(8,128)(2,1)}, u32[]{:S(2)}, u32[]{:S(2)}) %collective-permute-start.11) | collective-permute-done | bytes 393248 | tf_op jit(solution)/shard_map/ppermute | solution.py:67
  50.6 9.1 %project.1 = (bf16[1024,256]{1,0:T(8,128)(2,1)}, bf16[1024,256]{1,0:T(8,128)(2,1)}, bf16[1024,256]{1,0:T(8,128)(2,1)}, bf16[1024,1024]{1,0:T(8,128)(2,1)}, bf16[...) custom-call(s32[18]{0:T(128)} %pad_add_fusion.meta, s32[98]{0:T(128)} %owners.1, bf16[1024,1024]{1,0:T(8,128)(2,1)} %x_ref.7, ...), custom_call_target="tpu_custom_call" | custom-call | flops 1000 | bytes 1000 | tf_op jit(solution)/shard_map/project/pallas_call | solution.py:262
  64.3 10.9 %collective-permute-done.15.refs_2_.refs_6_ = bf16[1024,256]{1,0:T(8,128)(2,1)S(1)} collective-permute-done((bf16[1024,256]{1,0:T(8,128)(2,1)}, bf16[1024,256]{1,0:T(8,128)(2,1)S(1)}, u32[]{:S(2)}, u32[]{:S(2)}) %collective-permute-start.15) | collective-permute-done | bytes 524320 | tf_op jit(solution)/shard_map/ppermute | solution.py:67
  75.7 10.1 %collective-permute-done.18.refs_10_.refs_14_ = bf16[1024,256]{1,0:T(8,128)(2,1)S(1)} collective-permute-done((bf16[1024,256]{1,0:T(8,128)(2,1)}, bf16[1024,256]{1,0:T(8,128)(2,1)S(1)}, u32[]{:S(2)}, u32[]{:S(2)}) %collective-permute-start.18) | collective-permute-done | bytes 524320 | tf_op jit(solution)/shard_map/ppermute | solution.py:67
  90.4 10.2 %collective-permute-done.22.refs_6_.refs_10_ = bf16[1024,256]{1,0:T(8,128)(2,1)} collective-permute-done((bf16[1024,256]{1,0:T(8,128)(2,1)S(1)}, bf16[1024,256]{1,0:T(8,128)(2,1)}, u32[]{:S(2)}, u32[]{:S(2)}) %collective-permute-start.22) | collective-permute-done | bytes 524320 | tf_op jit(solution)/shard_map/ppermute | solution.py:67
  100.7 2.5 collective-permute-done.25.refs_14_.refs_18_
  109.4 11.5 %attend.1 = (bf16[1024,256]{1,0:T(8,128)(2,1)}, f32[1024,256]{1,0:T(8,128)}, f32[2,1024]{1,0:T(2,128)}) custom-call(s32[18]{0:T(128)} %pad_add_fusion.meta, bf16[1024,256]{1,0:T(8,128)(2,1)} %get-tuple-element.268.q_ref, bf16[1024,256]{1,0:T(8,128)(2,1)} %get-tuple-element.279.refs_0_.refs_4_, bf16[1024,256]{1,0:T(8,128)(2,1)} %copy-done.11, ...), custom_call_target="tpu_custom_call" | custom-call | flops 1000 | bytes 1000 | tf_op jit(solution)/shard_map/attend/pallas_call | solution.py:423
  120.9 10.3 %collective-permute-done.29 = bf16[256,1024]{1,0:T(8,128)(2,1)S(1)} collective-permute-done((bf16[256,1024]{1,0:T(8,128)(2,1)S(1)}, bf16[256,1024]{1,0:T(8,128)(2,1)S(1)}, u32[]{:S(2)}, u32[]{:S(2)}) %collective-permute-start.29) | collective-permute-done | bytes 524320 | tf_op jit(solution)/shard_map/ppermute | solution.py:67
  135.4 2.6 collective-permute-start.32
  139.7 5.0 %collective-permute-done.31.refs_1_ = bf16[256,256]{1,0:T(8,128)(2,1)S(1)} collective-permute-done((bf16[256,256]{1,0:T(8,128)(2,1)S(1)}, bf16[256,256]{1,0:T(8,128)(2,1)S(1)}, u32[]{:S(2)}, u32[]{:S(2)}) %collective-permute-start.31) | collective-permute-done | bytes 131104 | tf_op jit(solution)/shard_map/ppermute | solution.py:147
  144.8 7.9 %collective-permute-done.32.refs_2_ = bf16[256,256]{1,0:T(8,128)(2,1)S(1)} collective-permute-done((bf16[256,256]{1,0:T(8,128)(2,1)S(1)}, bf16[256,256]{1,0:T(8,128)(2,1)S(1)}, u32[]{:S(2)}, u32[]{:S(2)}) %collective-permute-start.32) | collective-permute-done | bytes 131104 | tf_op jit(solution)/shard_map/ppermute | solution.py:147
  154.3 5.3 %mix.1 = (f32[256,1024]{1,0:T(8,128)}, bf16[256,512]{1,0:T(8,128)(2,1)}, bf16[256,512]{1,0:T(8,128)(2,1)}) custom-call(s32[18]{0:T(128)} %pad_add_fusion.meta, bf16[1024,1024]{1,0:T(8,128)(2,1)} %x_ref.7, f32[2,1024]{1,0:T(2,128)} %gain_ref.5, bf16[4,544,1024]{2,1,0:T(8,128)(2,1)} %bitcast.27, bf16[256,256]{1,0:T(8,128)(2,1)} %get-tuple-element.543.refs_0_, ...), custom_call_target="tpu_custom_call" | custom-call | flops 1000 | bytes 1000 | tf_op jit(solution)/shard_map/mix/pallas_call | solution.py:583
  165.9 3.6 collective-permute-done.36.refs_2_
  170.9 3.9 collective-permute-done.39.refs_10_
  182.0 3.9 collective-permute-done.43.refs_6_
  191.7 20.2 %feed_forward.1 = (bf16[2048,1024]{1,0:T(8,128)(2,1)}, bf16[2048,384]{1,0:T(8,128)(2,1)}, bf16[2048,768]{1,0:T(8,128)(2,1)}, bf16[1024,512]{1,0:T(8,128)(2,1)}, ...) custom-call(s32[18]{0:T(128)} %pad_add_fusion.meta, ...), custom_call_target="tpu_custom_call" | custom-call | flops 1000 | bytes 1000 | tf_op jit(solution)/shard_map/feed_forward/pallas_call | solution.py:666
  212.5 2.4 collective-permute-done.50
  219.1 11.2 %feed_grads.1 = bf16[4,288,1024]{2,1,0:T(8,128)(2,1)} custom-call(bf16[2048,384]{1,0:T(8,128)(2,1)} %get-tuple-element.346.hidden, bf16[2048,768]{1,0:T(8,128)(2,1)} %get-tuple-element.347.d_inner, bf16[2048,1024]{1,0:T(8,128)(2,1)} %get-tuple-element.348.normed, bf16[2048,1024]{1,0:T(8,128)(2,1)} %copy-done.3), custom_call_target="tpu_custom_call" | custom-call | flops 1000 | bytes 1000 | tf_op jit(solution)/shard_map/feed_grads/pallas_call | solution.py:780
  235.0 5.7 %collective-permute-done.54.left_b = bf16[256,512]{1,0:T(8,128)(2,1)S(1)} collective-permute-done((bf16[256,512]{1,0:T(8,128)(2,1)S(1)}, bf16[256,512]{1,0:T(8,128)(2,1)S(1)}, u32[]{:S(2)}, u32[]{:S(2)}) %collective-permute-start.54) | collective-permute-done | bytes 262176 | tf_op jit(solution)/shard_map/ppermute | solution.py:67
  242.5 7.7 %branch_back.1 = (f32[256,1024]{1,0:T(8,128)}, f32[1,1024]{1,0:T(1,128)}, bf16[256,256]{1,0:T(8,128)(2,1)}, bf16[256,256]{1,0:T(8,128)(2,1)}, bf16[256,256]{1,0:...) custom-call(s32[18]{0:T(128)} %pad_add_fusion.meta, ...), custom_call_target="tpu_custom_call" | custom-call | flops 1000 | bytes 1000 | tf_op jit(solution)/shard_map/branch_back/pallas_call | solution.py:723
  257.6 2.8 collective-permute-done.56.refs_1_
  260.4 5.2 %collective-permute-done.57.refs_2_ = bf16[256,256]{1,0:T(8,128)(2,1)S(1)} collective-permute-done((bf16[256,256]{1,0:T(8,128)(2,1)S(1)}, bf16[256,256]{1,0:T(8,128)(2,1)S(1)}, u32[]{:S(2)}, u32[]{:S(2)}) %collective-permute-start.57) | collective-permute-done | bytes 131104 | tf_op jit(solution)/shard_map/ppermute | solution.py:147
  269.4 15.4 %attend_back.1 = (bf16[1024,256]{1,0:T(8,128)(2,1)}, bf16[4096,256]{1,0:T(8,128)(2,1)}, bf16[4096,256]{1,0:T(8,128)(2,1)}, bf16[4096,256]{1,0:T(8,128)(2,1)}, bf16[4096,256]{1,0:T(8,128)(2,1)}) custom-call(s32[18]{0:T(128)} %pad_add_fusion.meta, bf16[1024,256]{1,0:T(8,128)(2,1)} %get-tuple-element.268.q_ref, f32[1024,256]{1,0:T(8,128)} %get-tuple-element.368.wide_ref, ...), custom_call_target="tpu_custom_call" | custom-call | flops 1000 | bytes 1000 | tf_op jit(solution)/shard_map/attend_back/pallas_call | solution.py:538
  286.3 16.2 %collective-permute-done.61 = bf16[384,1024]{1,0:T(8,128)(2,1)S(1)} collective-permute-done((bf16[384,1024]{1,0:T(8,128)(2,1)S(1)}, bf16[384,1024]{1,0:T(8,128)(2,1)S(1)}, u32[]{:S(2)}, u32[]{:S(2)}) %collective-permute-start.61) | collective-permute-done | bytes 786464 | tf_op jit(solution)/shard_map/ppermute | solution.py:67
  303.9 2.9 collective-permute-done.64
  318.8 12.5 %collective-permute-done.67.refs_1_ = bf16[256,1024]{1,0:T(8,128)(2,1)S(1)} collective-permute-done((bf16[256,1024]{1,0:T(8,128)(2,1)S(1)}, bf16[256,1024]{1,0:T(8,128)(2,1)S(1)}, u32[]{:S(2)}, u32[]{:S(2)}) %collective-permute-start.67) | collective-permute-done | bytes 524320 | tf_op jit(solution)/shard_map/ppermute | solution.py:147
  332.7 5.8 %collective-permute-done.66 = bf16[2048,256]{1,0:T(8,128)(2,1)S(1)} collective-permute-done((bf16[2048,256]{1,0:T(8,128)(2,1)}, bf16[2048,256]{1,0:T(8,128)(2,1)S(1)}, u32[]{:S(2)}, u32[]{:S(2)}) %collective-permute-start.66) | collective-permute-done | bytes 1048608 | tf_op jit(solution)/shard_map/ppermute | solution.py:67
  340.9 4.3 collective-permute-done.68.refs_2_
  345.1 2.6 collective-permute-start.69
  348.4 9.6 %collective-permute-done.69.dk_b = bf16[1024,256]{1,0:T(8,128)(2,1)S(1)} collective-permute-done((bf16[1024,256]{1,0:T(8,128)(2,1)S(1)}, bf16[1024,256]{1,0:T(8,128)(2,1)S(1)}, u32[]{:S(2)}, u32[]{:S(2)}) %collective-permute-start.69) | collective-permute-done | bytes 524320 | tf_op jit(solution)/shard_map/ppermute | solution.py:67
  362.0 2.5 fusion.14
  364.5 4.0 back_in.2
  371.3 2.4 collective-permute-start.75
  373.7 6.0 %back_in.3 = (bf16[768,1024]{1,0:T(8,128)(2,1)}, f32[1,1024]{1,0:T(1,128)}) custom-call(s32[18]{0:T(128)} %pad_add_fusion.meta, bf16[1024,1024]{1,0:T(8,128)(2,1)} %x_ref.7, bf16[1024,256]{1,0:T(8,128)(2,1)} %get-tuple-element.413.dq, bf16[1024,256]{1,0:T(8,128)(2,1)} %get-tuple-element.414.dk_a, bf16[1024,256]{1,0:T(8,128)(2,1)} %copy-done.4, ...), custom_call_target="tpu_custom_call" | custom-call | flops 1000 | bytes 1000 | tf_op jit(solution)/shard_map/back_in/pallas_call | solution.py:1013
  379.8 6.1 %late_grads.1 = (bf16[384,1024]{1,0:T(8,128)(2,1)}, bf16[384,1024]{1,0:T(8,128)(2,1)}) custom-call(s32[18]{0:T(128)} %pad_add_fusion.meta, bf16[1024,256]{1,0:T(8,128)(2,1)} %get-tuple-element.413.dq, bf16[1024,256]{1,0:T(8,128)(2,1)} %get-tuple-element.414.dk_a, bf16[1024,256]{1,0:T(8,128)(2,1)} %copy-done.4, bf16[1024,256]{1,0:T(8,128)(2,1)} %get-tuple-element.416.dv_a, ...), custom_call_target="tpu_custom_call" | custom-call | flops 1000 | bytes 1000 | tf_op jit(solution)/shard_map/late_grads/pallas_call | solution.py:822
  388.8 3.1 place.2
  392.9 2.8 collective-permute-done.79
  395.7 5.8 %collective-permute-done.76 = bf16[256,1024]{1,0:T(8,128)(2,1)S(1)} collective-permute-done((bf16[256,1024]{1,0:T(8,128)(2,1)}, bf16[256,1024]{1,0:T(8,128)(2,1)S(1)}, u32[]{:S(2)}, u32[]{:S(2)}) %collective-permute-start.76) | collective-permute-done | bytes 524320 | tf_op jit(solution)/shard_map/ppermute | solution.py:147
  406.7 3.6 collective-permute-start.80
  410.4 10.0 %collective-permute-done.85 = f32[2,1024]{1,0:T(2,128)S(1)} collective-permute-done((f32[2,1024]{1,0:T(2,128)S(1)}, f32[2,1024]{1,0:T(2,128)S(1)}, u32[]{:S(2)}, u32[]{:S(2)}) %collective-permute-start.85) | collective-permute-done | bytes 8224 | tf_op jit(solution)/shard_map/ppermute | solution.py:177
  421.4 2.5 collective-permute-start.86
  429.5 6.0 %collective-permute-done.90 = f32[2,1024]{1,0:T(2,128)S(1)} collective-permute-done((f32[2,1024]{1,0:T(2,128)S(1)}, f32[2,1024]{1,0:T(2,128)S(1)}, u32[]{:S(2)}, u32[]{:S(2)}) %collective-permute-start.90) | collective-permute-done | bytes 8224 | tf_op jit(solution)/shard_map/ppermute | solution.py:177
  439.9 12.4 %soap.1 = (f32[13,32,1024]{2,1,0:T(8,128)}, f32[13,32,1024]{2,1,0:T(8,128)}, f32[13,32,1024]{2,1,0:T(8,128)}, f32[13,32,1024]{2,1,0:T(8,128)}, f32[13,32,32]{2,1,0:T(8,128)}, /*index=5*/f32[13,32,32]{2,1,0:T(8,128)}) custom-call(s32[18]{0:T(128)} %pad_add_fusion.meta, s32[13]{0:T(128)} %broadcast_add_fusion.held, bf16[72,32,1024]{2,1,0:T(8,128)(2,1)} %bitcast.38, ...), custom_call_target="tpu_custom_call" | custom-call | flops 1000 | bytes 1000 | tf_op jit(solution)/shard_map/soap/pallas_call | solution.py:936
  455.3 4.6 orthonormal.1
  459.8 8.5 %collective-permute-done.93.refs_3_ = bf16[256,1024]{1,0:T(8,128)(2,1)S(1)} collective-permute-done((bf16[256,1024]{1,0:T(8,128)(2,1)S(1)}, bf16[256,1024]{1,0:T(8,128)(2,1)S(1)}, u32[]{:S(2)}, u32[]{:S(2)}) %collective-permute-start.93) | collective-permute-done | bytes 524320 | tf_op jit(solution)/shard_map/ppermute | solution.py:147
  471.3 3.8 place.3
  (395 shorter events, 130.2 us)
Async XLA Ops:
  7.2 147.0 %all-gather.3.cloned.1.call-start = ((), (), s32[]{:S(2)}) async-start(), calls=%async_computation.1 | async-start | bytes 5570560 | tf_op jit(solution)/shard_map/all_gather | solution.py:1065
  9.4 23.7 %collective-permute-start = (bf16[7,32,1024]{2,1,0:T(8,128)(2,1)S(1)}, bf16[7,32,1024]{2,1,0:T(8,128)(2,1)S(1)}, u32[]{:S(2)}, u32[]{:S(2)}) collective-permute-start(bf16[7,32,1024]{2,1,0:T(8,128)(2,1)S(1)} %slice.255.refs_0_), channel_id=1, source_target_pairs={{0,4},{4,0},{8,12},{12,8},{16,20},{20,16},{24,28},{28,24},{1,5},{5... | collective-permute-start | bytes 1376264 | tf_op jit(solution)/shard_map/ppermute | solution.py:67
  9.6 23.6 %collective-permute-start.1 = (bf16[7,32,1024]{2,1,0:T(8,128)(2,1)S(1)}, bf16[7,32,1024]{2,1,0:T(8,128)(2,1)S(1)}, u32[]{:S(2)}, u32[]{:S(2)}) collective-permute-start(bf16[7,32,1024]{2,1,0:T(8,128)(2,1)S(1)} %slice.255.refs_0_), channel_id=1, source_target_pairs={{0,8},{4,12},{8,0},{12,4},{16,24},{20,28},{24,16},{28,20},{1,9},{5... | collective-permute-start | bytes 1376264 | tf_op jit(solution)/shard_map/ppermute | solution.py:67
  12.5 20.7 %collective-permute-start.2 = (bf16[7,32,1024]{2,1,0:T(8,128)(2,1)S(1)}, bf16[7,32,1024]{2,1,0:T(8,128)(2,1)S(1)}, u32[]{:S(2)}, u32[]{:S(2)}) collective-permute-start(bf16[7,32,1024]{2,1,0:T(8,128)(2,1)S(1)} %slice.255.refs_0_), channel_id=1, source_target_pairs={{0,16},{4,20},{8,24},{12,28},{16,0},{20,4},{24,8},{28,12},{1,17},{... | collective-permute-start | bytes 1376264 | tf_op jit(solution)/shard_map/ppermute | solution.py:67
  14.0 17.6 %collective-permute-start.4 = (bf16[6,32,1024]{2,1,0:T(8,128)(2,1)S(1)}, bf16[6,32,1024]{2,1,0:T(8,128)(2,1)S(1)}, u32[]{:S(2)}, u32[]{:S(2)}) collective-permute-start(bf16[6,32,1024]{2,1,0:T(8,128)(2,1)S(1)} %slice.256.refs_8_), channel_id=1, source_target_pairs={{0,8},{4,12},{8,0},{12,4},{16,24},{20,28},{24,16},{28,20},{1,9},{5... | collective-permute-start | bytes 1179656 | tf_op jit(solution)/shard_map/ppermute | solution.py:67
  14.6 18.6 %collective-permute-start.5 = (bf16[6,32,1024]{2,1,0:T(8,128)(2,1)S(1)}, bf16[6,32,1024]{2,1,0:T(8,128)(2,1)S(1)}, u32[]{:S(2)}, u32[]{:S(2)}) collective-permute-start(bf16[6,32,1024]{2,1,0:T(8,128)(2,1)S(1)} %slice.256.refs_8_), channel_id=1, source_target_pairs={{0,16},{4,20},{8,24},{12,28},{16,0},{20,4},{24,8},{28,12},{1,17},{... | collective-permute-start | bytes 1179656 | tf_op jit(solution)/shard_map/ppermute | solution.py:67
  33.3 13.7 %collective-permute-start.6 = (bf16[7,32,1024]{2,1,0:T(8,128)(2,1)S(1)}, bf16[7,32,1024]{2,1,0:T(8,128)(2,1)S(1)}, u32[]{:S(2)}, u32[]{:S(2)}) collective-permute-start(bf16[7,32,1024]{2,1,0:T(8,128)(2,1)S(1)} %collective-permute-done.1.refs_2_), channel_id=1, source_target_pairs={{0,4},{4,0},{8,12},{12,8},{16,20},{20,16},{24,28},{28,24},{1,5},{5... | collective-permute-start | bytes 1376264 | tf_op jit(solution)/shard_map/ppermute | solution.py:67
  33.8 13.2 %collective-permute-start.8 = (bf16[7,32,1024]{2,1,0:T(8,128)(2,1)S(1)}, bf16[7,32,1024]{2,1,0:T(8,128)(2,1)S(1)}, u32[]{:S(2)}, u32[]{:S(2)}) collective-permute-start(bf16[7,32,1024]{2,1,0:T(8,128)(2,1)S(1)} %collective-permute-done.1.refs_2_), channel_id=1, source_target_pairs={{0,16},{4,20},{8,24},{12,28},{16,0},{20,4},{24,8},{28,12},{1,17},{... | collective-permute-start | bytes 1376264 | tf_op jit(solution)/shard_map/ppermute | solution.py:67
  59.8 253.8 %reduce-scatter.2.cloned.1.call-start = ((), (), s32[]{:S(2)}) async-start(), calls=%async_computation.2 | async-start | bytes 2949120 | tf_op jit(solution)/shard_map/reduce_scatter | solution.py:1113
  60.2 15.0 %collective-permute-start.15 = (bf16[1024,256]{1,0:T(8,128)(2,1)}, bf16[1024,256]{1,0:T(8,128)(2,1)S(1)}, u32[]{:S(2)}, u32[]{:S(2)}) collective-permute-start(bf16[1024,256]{1,0:T(8,128)(2,1)} %get-tuple-element.279.refs_0_.refs_4_), channel_id=1, source_target_pairs={{0,8},{4,12},{8,0},{12,4},{16,24},{20,28},{24,16},{28,20},{1,9},{5... | collective-permute-start | bytes 1572872 | tf_op jit(solution)/shard_map/ppermute | solution.py:67
  60.7 15.0 %collective-permute-start.16 = (bf16[1024,256]{1,0:T(8,128)(2,1)}, bf16[1024,256]{1,0:T(8,128)(2,1)S(1)}, u32[]{:S(2)}, u32[]{:S(2)}) collective-permute-start(bf16[1024,256]{1,0:T(8,128)(2,1)} %get-tuple-element.279.refs_0_.refs_4_), channel_id=1, source_target_pairs={{0,16},{4,20},{8,24},{12,28},{16,0},{20,4},{24,8},{28,12},{1,17},{... | collective-permute-start | bytes 1572872 | tf_op jit(solution)/shard_map/ppermute | solution.py:67
  61.5 14.3 %collective-permute-start.17 = (bf16[1024,256]{1,0:T(8,128)(2,1)}, bf16[1024,256]{1,0:T(8,128)(2,1)S(1)}, u32[]{:S(2)}, u32[]{:S(2)}) collective-permute-start(bf16[1024,256]{1,0:T(8,128)(2,1)} %get-tuple-element.288.refs_8_.refs_12_), channel_id=1, source_target_pairs={{0,4},{4,0},{8,12},{12,8},{16,20},{20,16},{24,28},{28,24},{1,5},{5... | collective-permute-start | bytes 1572872 | tf_op jit(solution)/shard_map/ppermute | solution.py:67
  61.5 24.4 %collective-permute-start.18 = (bf16[1024,256]{1,0:T(8,128)(2,1)}, bf16[1024,256]{1,0:T(8,128)(2,1)S(1)}, u32[]{:S(2)}, u32[]{:S(2)}) collective-permute-start(bf16[1024,256]{1,0:T(8,128)(2,1)} %get-tuple-element.288.refs_8_.refs_12_), channel_id=1, source_target_pairs={{0,8},{4,12},{8,0},{12,4},{16,24},{20,28},{24,16},{28,20},{1,9},{5... | collective-permute-start | bytes 1572872 | tf_op jit(solution)/shard_map/ppermute | solution.py:67
  63.0 23.2 %collective-permute-start.19 = (bf16[1024,256]{1,0:T(8,128)(2,1)}, bf16[1024,256]{1,0:T(8,128)(2,1)}, u32[]{:S(2)}, u32[]{:S(2)}) collective-permute-start(bf16[1024,256]{1,0:T(8,128)(2,1)} %get-tuple-element.288.refs_8_.refs_12_), channel_id=1, source_target_pairs={{0,16},{4,20},{8,24},{12,28},{16,0},{20,4},{24,8},{28,12},{1,17},{... | collective-permute-start | bytes 1572872 | tf_op jit(solution)/shard_map/ppermute | solution.py:67
  86.2 14.4 %collective-permute-start.22 = (bf16[1024,256]{1,0:T(8,128)(2,1)S(1)}, bf16[1024,256]{1,0:T(8,128)(2,1)}, u32[]{:S(2)}, u32[]{:S(2)}) collective-permute-start(bf16[1024,256]{1,0:T(8,128)(2,1)S(1)} %collective-permute-done.15.refs_2_.refs_6_), channel_id=1, source_target_pairs={{0,16},{4,20},{8,24},{12,28},{16,0},{20,4},{24,8},{28,12},{1,17},{... | collective-permute-start | bytes 1572872 | tf_op jit(solution)/shard_map/ppermute | solution.py:67
  87.2 13.4 %collective-permute-start.23 = (bf16[1024,256]{1,0:T(8,128)(2,1)S(1)}, bf16[1024,256]{1,0:T(8,128)(2,1)}, u32[]{:S(2)}, u32[]{:S(2)}) collective-permute-start(bf16[1024,256]{1,0:T(8,128)(2,1)S(1)} %collective-permute-done.18.refs_10_.refs_14_), channel_id=1, source_target_pairs={{0,4},{4,0},{8,12},{12,8},{16,20},{20,16},{24,28},{28,24},{1,5},{5... | collective-permute-start | bytes 1572872 | tf_op jit(solution)/shard_map/ppermute | solution.py:67
  88.9 14.3 %collective-permute-start.25 = (bf16[1024,256]{1,0:T(8,128)(2,1)}, bf16[1024,256]{1,0:T(8,128)(2,1)}, u32[]{:S(2)}, u32[]{:S(2)}) collective-permute-start(bf16[1024,256]{1,0:T(8,128)(2,1)} %collective-permute-done.19.refs_12_.refs_16_), channel_id=1, source_target_pairs={{0,8},{4,12},{8,0},{12,4},{16,24},{20,28},{24,16},{28,20},{1,9},{5... | collective-permute-start | bytes 1572872 | tf_op jit(solution)/shard_map/ppermute | solution.py:67
  104.8 16.0 %collective-permute-start.28 = (bf16[256,1024]{1,0:T(8,128)(2,1)S(1)}, bf16[256,1024]{1,0:T(8,128)(2,1)S(1)}, u32[]{:S(2)}, u32[]{:S(2)}) collective-permute-start(bf16[256,1024]{1,0:T(8,128)(2,1)S(1)} %constant_dynamic-slice_fusion), channel_id=1, source_target_pairs={{0,8},{4,12},{8,0},{12,4},{16,24},{20,28},{24,16},{28,20},{1,9},{5... | collective-permute-start | bytes 1572872 | tf_op jit(solution)/shard_map/ppermute | solution.py:67
  106.4 24.8 %collective-permute-start.29 = (bf16[256,1024]{1,0:T(8,128)(2,1)S(1)}, bf16[256,1024]{1,0:T(8,128)(2,1)S(1)}, u32[]{:S(2)}, u32[]{:S(2)}) collective-permute-start(bf16[256,1024]{1,0:T(8,128)(2,1)S(1)} %constant_dynamic-slice_fusion), channel_id=1, source_target_pairs={{0,16},{4,20},{8,24},{12,28},{16,0},{20,4},{24,8},{28,12},{1,17},{... | collective-permute-start | bytes 1572872 | tf_op jit(solution)/shard_map/ppermute | solution.py:67
  107.4 23.8 %collective-permute-start.30 = (bf16[256,1024]{1,0:T(8,128)(2,1)S(1)}, bf16[256,1024]{1,0:T(8,128)(2,1)S(1)}, u32[]{:S(2)}, u32[]{:S(2)}) collective-permute-start(bf16[256,1024]{1,0:T(8,128)(2,1)S(1)} %constant_dynamic-slice_fusion), channel_id=1, source_target_pairs={{0,24},{4,28},{8,16},{12,20},{16,8},{20,12},{24,0},{28,4},{1,25},{... | collective-permute-start | bytes 1572872 | tf_op jit(solution)/shard_map/ppermute | solution.py:67
  135.4 17.3 %collective-permute-start.32 = (bf16[256,256]{1,0:T(8,128)(2,1)S(1)}, bf16[256,256]{1,0:T(8,128)(2,1)S(1)}, u32[]{:S(2)}, u32[]{:S(2)}) collective-permute-start(bf16[256,256]{1,0:T(8,128)(2,1)S(1)} %get-tuple-element.541), channel_id=1, source_target_pairs={{0,2},{1,3},{2,0},{3,1},{4,6},{5,7},{6,4},{7,5},{8,10},{9,11},{10,... | collective-permute-start | bytes 393224 | tf_op jit(solution)/shard_map/ppermute | solution.py:147
  138.0 14.7 %collective-permute-start.33 = (bf16[256,256]{1,0:T(8,128)(2,1)S(1)}, bf16[256,256]{1,0:T(8,128)(2,1)S(1)}, u32[]{:S(2)}, u32[]{:S(2)}) collective-permute-start(bf16[256,256]{1,0:T(8,128)(2,1)S(1)} %get-tuple-element.540), channel_id=1, source_target_pairs={{0,3},{1,0},{2,1},{3,2},{4,7},{5,4},{6,5},{7,6},{8,11},{9,8},{10,9... | collective-permute-start | bytes 393224 | tf_op jit(solution)/shard_map/ppermute | solution.py:147
  159.7 28.9 %collective-permute-start.34 = (bf16[1024,1024]{1,0:T(8,128)(2,1)S(1)}, bf16[1024,1024]{1,0:T(8,128)(2,1)S(1)}, u32[]{:S(2)}, u32[]{:S(2)}) collective-permute-start(bf16[1024,1024]{1,0:T(8,128)(2,1)S(1)} %pad_maximum_fusion), channel_id=1, source_target_pairs={{0,4},{4,0},{8,12},{12,8},{16,20},{20,16},{24,28},{28,24},{1,5},{5... | collective-permute-start | bytes 6291464 | tf_op jit(solution)/shard_map/ppermute | solution.py:67
  216.7 16.5 %collective-permute-start.53 = (bf16[1024,1024]{1,0:T(8,128)(2,1)}, bf16[1024,1024]{1,0:T(8,128)(2,1)S(1)}, u32[]{:S(2)}, u32[]{:S(2)}) collective-permute-start(bf16[1024,1024]{1,0:T(8,128)(2,1)} %get-tuple-element.345), channel_id=1, source_target_pairs={{0,4},{4,0},{8,12},{12,8},{16,20},{20,16},{24,28},{28,24},{1,5},{5... | collective-permute-start | bytes 6291464 | tf_op jit(solution)/shard_map/ppermute | solution.py:67
  216.9 14.2 %collective-permute-start.52 = (bf16[512,512]{1,0:T(8,128)(2,1)S(1)}, bf16[512,512]{1,0:T(8,128)(2,1)S(1)}, u32[]{:S(2)}, u32[]{:S(2)}) collective-permute-start(bf16[512,512]{1,0:T(8,128)(2,1)S(1)} %get-tuple-element.343), channel_id=1, source_target_pairs={{0,8},{4,12},{8,0},{12,4},{16,24},{20,28},{24,16},{28,20},{1,9},{5... | collective-permute-start | bytes 1572872 | tf_op jit(solution)/shard_map/ppermute | solution.py:67
  218.4 13.9 %collective-permute-start.51 = (bf16[512,512]{1,0:T(8,128)(2,1)S(1)}, bf16[512,512]{1,0:T(8,128)(2,1)S(1)}, u32[]{:S(2)}, u32[]{:S(2)}) collective-permute-start(bf16[512,512]{1,0:T(8,128)(2,1)S(1)} %get-tuple-element.341), channel_id=1, source_target_pairs={{0,16},{4,20},{8,24},{12,28},{16,0},{20,4},{24,8},{28,12},{1,17},{... | collective-permute-start | bytes 1572872 | tf_op jit(solution)/shard_map/ppermute | solution.py:67
  265.6 174.2 %all-gather.5.cloned.1.call-start = ((), (), s32[]{:S(2)}) async-start(), calls=%async_computation.3 | async-start | bytes 5308416 | tf_op jit(solution)/shard_map/all_gather | solution.py:1068
  265.9 20.5 %collective-permute-start.60 = (bf16[384,1024]{1,0:T(8,128)(2,1)S(1)}, bf16[384,1024]{1,0:T(8,128)(2,1)S(1)}, u32[]{:S(2)}, u32[]{:S(2)}) collective-permute-start(bf16[384,1024]{1,0:T(8,128)(2,1)S(1)} %get-tuple-element.365), channel_id=1, source_target_pairs={{0,8},{4,12},{8,0},{12,4},{16,24},{20,28},{24,16},{28,20},{1,9},{5... | collective-permute-start | bytes 2359304 | tf_op jit(solution)/shard_map/ppermute | solution.py:67
  266.5 36.0 %collective-permute-start.61 = (bf16[384,1024]{1,0:T(8,128)(2,1)S(1)}, bf16[384,1024]{1,0:T(8,128)(2,1)S(1)}, u32[]{:S(2)}, u32[]{:S(2)}) collective-permute-start(bf16[384,1024]{1,0:T(8,128)(2,1)S(1)} %get-tuple-element.366), channel_id=1, source_target_pairs={{0,16},{4,20},{8,24},{12,28},{16,0},{20,4},{24,8},{28,12},{1,17},{... | collective-permute-start | bytes 2359304 | tf_op jit(solution)/shard_map/ppermute | solution.py:67
  267.3 35.2 %collective-permute-start.62 = (bf16[384,1024]{1,0:T(8,128)(2,1)S(1)}, bf16[384,1024]{1,0:T(8,128)(2,1)S(1)}, u32[]{:S(2)}, u32[]{:S(2)}) collective-permute-start(bf16[384,1024]{1,0:T(8,128)(2,1)S(1)} %get-tuple-element.367), channel_id=1, source_target_pairs={{0,24},{4,28},{8,16},{12,20},{16,8},{20,12},{24,0},{28,4},{1,25},{... | collective-permute-start | bytes 2359304 | tf_op jit(solution)/shard_map/ppermute | solution.py:67
  313.6 24.9 %collective-permute-start.66 = (bf16[2048,256]{1,0:T(8,128)(2,1)}, bf16[2048,256]{1,0:T(8,128)(2,1)S(1)}, u32[]{:S(2)}, u32[]{:S(2)}) collective-permute-start(bf16[2048,256]{1,0:T(8,128)(2,1)} %get-tuple-element.392), channel_id=1, source_target_pairs={{0,8},{4,12},{8,0},{12,4},{16,24},{20,28},{24,16},{28,20},{1,9},{5... | collective-permute-start | bytes 3145736 | tf_op jit(solution)/shard_map/ppermute | solution.py:67
  315.0 24.7 %collective-permute-start.65 = (bf16[2048,256]{1,0:T(8,128)(2,1)}, bf16[2048,256]{1,0:T(8,128)(2,1)S(1)}, u32[]{:S(2)}, u32[]{:S(2)}) collective-permute-start(bf16[2048,256]{1,0:T(8,128)(2,1)} %get-tuple-element.390), channel_id=1, source_target_pairs={{0,16},{4,20},{8,24},{12,28},{16,0},{20,4},{24,8},{28,12},{1,17},{... | collective-permute-start | bytes 3145736 | tf_op jit(solution)/shard_map/ppermute | solution.py:67
  316.5 14.8 %collective-permute-start.67 = (bf16[256,1024]{1,0:T(8,128)(2,1)S(1)}, bf16[256,1024]{1,0:T(8,128)(2,1)S(1)}, u32[]{:S(2)}, u32[]{:S(2)}) collective-permute-start(bf16[256,1024]{1,0:T(8,128)(2,1)S(1)} %fusion.8.refs_0_), channel_id=1, source_target_pairs={{0,1},{1,2},{2,3},{3,0},{4,5},{5,6},{6,7},{7,4},{8,9},{9,10},{10,1... | collective-permute-start | bytes 1572872 | tf_op jit(solution)/shard_map/ppermute | solution.py:147
  331.3 13.9 %collective-permute-start.68 = (bf16[256,1024]{1,0:T(8,128)(2,1)S(1)}, bf16[256,1024]{1,0:T(8,128)(2,1)S(1)}, u32[]{:S(2)}, u32[]{:S(2)}) collective-permute-start(bf16[256,1024]{1,0:T(8,128)(2,1)S(1)} %collective-permute-done.67.refs_1_), channel_id=1, source_target_pairs={{0,1},{1,2},{2,3},{3,0},{4,5},{5,6},{6,7},{7,4},{8,9},{9,10},{10,1... | collective-permute-start | bytes 1572872 | tf_op jit(solution)/shard_map/ppermute | solution.py:147
  348.2 13.6 %collective-permute-start.71 = (bf16[256,1024]{1,0:T(8,128)(2,1)S(1)}, bf16[256,1024]{1,0:T(8,128)(2,1)S(1)}, u32[]{:S(2)}, u32[]{:S(2)}) collective-permute-start(bf16[256,1024]{1,0:T(8,128)(2,1)S(1)} %collective-permute-done.68.refs_2_), channel_id=1, source_target_pairs={{0,1},{1,2},{2,3},{3,0},{4,5},{5,6},{6,7},{7,4},{8,9},{9,10},{10,1... | collective-permute-start | bytes 1572872 | tf_op jit(solution)/shard_map/ppermute | solution.py:147
  368.6 17.4 %collective-permute-start.72 = (bf16[256,1024]{1,0:T(8,128)(2,1)}, bf16[256,1024]{1,0:T(8,128)(2,1)S(1)}, u32[]{:S(2)}, u32[]{:S(2)}) collective-permute-start(bf16[256,1024]{1,0:T(8,128)(2,1)} %get-tuple-element.412), channel_id=1, source_target_pairs={{0,3},{1,0},{2,1},{3,2},{4,7},{5,4},{6,5},{7,6},{8,11},{9,8},{10,9... | collective-permute-start | bytes 1572872 | tf_op jit(solution)/shard_map/ppermute | solution.py:147
  369.2 16.7 %collective-permute-start.73 = (bf16[32,1024]{1,0:T(8,128)(2,1)S(1)}, bf16[32,1024]{1,0:T(8,128)(2,1)S(1)}, u32[]{:S(2)}, u32[]{:S(2)}) collective-permute-start(bf16[32,1024]{1,0:T(8,128)(2,1)S(1)} %get-tuple-element.538), channel_id=1, source_target_pairs={{0,1},{1,2},{2,3},{3,0},{4,5},{5,6},{6,7},{7,4},{8,9},{9,10},{10,1... | collective-permute-start | bytes 196616 | tf_op jit(solution)/shard_map/ppermute | solution.py:147
  371.3 14.7 %collective-permute-start.74 = (bf16[32,1024]{1,0:T(8,128)(2,1)S(1)}, bf16[32,1024]{1,0:T(8,128)(2,1)S(1)}, u32[]{:S(2)}, u32[]{:S(2)}) collective-permute-start(bf16[32,1024]{1,0:T(8,128)(2,1)S(1)} %get-tuple-element.537), channel_id=1, source_target_pairs={{0,2},{1,3},{2,0},{3,1},{4,6},{5,7},{6,4},{7,5},{8,10},{9,11},{10,... | collective-permute-start | bytes 196616 | tf_op jit(solution)/shard_map/ppermute | solution.py:147
  371.3 14.7 %collective-permute-start.75 = (bf16[32,1024]{1,0:T(8,128)(2,1)S(1)}, bf16[32,1024]{1,0:T(8,128)(2,1)S(1)}, u32[]{:S(2)}, u32[]{:S(2)}) collective-permute-start(bf16[32,1024]{1,0:T(8,128)(2,1)S(1)} %get-tuple-element.536), channel_id=1, source_target_pairs={{0,3},{1,0},{2,1},{3,2},{4,7},{5,4},{6,5},{7,6},{8,11},{9,8},{10,9... | collective-permute-start | bytes 196616 | tf_op jit(solution)/shard_map/ppermute | solution.py:147
  387.0 14.6 %collective-permute-start.77 = (bf16[384,1024]{1,0:T(8,128)(2,1)}, bf16[384,1024]{1,0:T(8,128)(2,1)S(1)}, u32[]{:S(2)}, u32[]{:S(2)}) collective-permute-start(bf16[384,1024]{1,0:T(8,128)(2,1)} %get-tuple-element.439), channel_id=1, source_target_pairs={{0,4},{4,0},{8,12},{12,8},{16,20},{20,16},{24,28},{28,24},{1,5},{5... | collective-permute-start | bytes 2359304 | tf_op jit(solution)/shard_map/ppermute | solution.py:67
  387.0 14.5 %collective-permute-start.76 = (bf16[256,1024]{1,0:T(8,128)(2,1)}, bf16[256,1024]{1,0:T(8,128)(2,1)S(1)}, u32[]{:S(2)}, u32[]{:S(2)}) collective-permute-start(bf16[256,1024]{1,0:T(8,128)(2,1)} %add_convert_fusion.8), channel_id=1, source_target_pairs={{0,3},{1,0},{2,1},{3,2},{4,7},{5,4},{6,5},{7,6},{8,11},{9,8},{10,9... | collective-permute-start | bytes 1572872 | tf_op jit(solution)/shard_map/ppermute | solution.py:147
  403.1 17.3 %collective-permute-start.81 = (bf16[96,1024]{1,0:T(8,128)(2,1)S(1)}, bf16[96,1024]{1,0:T(8,128)(2,1)S(1)}, u32[]{:S(2)}, u32[]{:S(2)}) collective-permute-start(bf16[96,1024]{1,0:T(8,128)(2,1)S(1)} %get-tuple-element.533), channel_id=1, source_target_pairs={{0,8},{4,12},{8,0},{12,4},{16,24},{20,28},{24,16},{28,20},{1,9},{5... | collective-permute-start | bytes 589832 | tf_op jit(solution)/shard_map/ppermute | solution.py:67
  403.2 17.2 %collective-permute-start.82 = (bf16[96,1024]{1,0:T(8,128)(2,1)S(1)}, bf16[96,1024]{1,0:T(8,128)(2,1)S(1)}, u32[]{:S(2)}, u32[]{:S(2)}) collective-permute-start(bf16[96,1024]{1,0:T(8,128)(2,1)S(1)} %get-tuple-element.535), channel_id=1, source_target_pairs={{0,16},{4,20},{8,24},{12,28},{16,0},{20,4},{24,8},{28,12},{1,17},{... | collective-permute-start | bytes 589832 | tf_op jit(solution)/shard_map/ppermute | solution.py:67
  404.3 16.1 %collective-permute-start.83 = (bf16[96,1024]{1,0:T(8,128)(2,1)S(1)}, bf16[96,1024]{1,0:T(8,128)(2,1)S(1)}, u32[]{:S(2)}, u32[]{:S(2)}) collective-permute-start(bf16[96,1024]{1,0:T(8,128)(2,1)S(1)} %get-tuple-element.534), channel_id=1, source_target_pairs={{0,24},{4,28},{8,16},{12,20},{16,8},{20,12},{24,0},{28,4},{1,25},{... | collective-permute-start | bytes 589832 | tf_op jit(solution)/shard_map/ppermute | solution.py:67
  406.7 13.9 %collective-permute-start.80 = (bf16[256,1024]{1,0:T(8,128)(2,1)S(1)}, bf16[256,1024]{1,0:T(8,128)(2,1)S(1)}, u32[]{:S(2)}, u32[]{:S(2)}) collective-permute-start(bf16[256,1024]{1,0:T(8,128)(2,1)S(1)} %add_convert_fusion.7), channel_id=1, source_target_pairs={{0,3},{1,0},{2,1},{3,2},{4,7},{5,4},{6,5},{7,6},{8,11},{9,8},{10,9... | collective-permute-start | bytes 1572872 | tf_op jit(solution)/shard_map/ppermute | solution.py:147
  421.4 14.2 %collective-permute-start.86 = (bf16[256,1024]{1,0:T(8,128)(2,1)S(1)}, bf16[256,1024]{1,0:T(8,128)(2,1)S(1)}, u32[]{:S(2)}, u32[]{:S(2)}) collective-permute-start(bf16[256,1024]{1,0:T(8,128)(2,1)S(1)} %fusion.6.refs_0_), channel_id=1, source_target_pairs={{0,1},{1,2},{2,3},{3,0},{4,5},{5,6},{6,7},{7,4},{8,9},{9,10},{10,1... | collective-permute-start | bytes 1572872 | tf_op jit(solution)/shard_map/ppermute | solution.py:147
  435.7 16.5 %collective-permute-start.91 = (bf16[256,1024]{1,0:T(8,128)(2,1)S(1)}, bf16[256,1024]{1,0:T(8,128)(2,1)S(1)}, u32[]{:S(2)}, u32[]{:S(2)}) collective-permute-start(bf16[256,1024]{1,0:T(8,128)(2,1)S(1)} %collective-permute-done.86.refs_1_), channel_id=1, source_target_pairs={{0,1},{1,2},{2,3},{3,0},{4,5},{5,6},{6,7},{7,4},{8,9},{9,10},{10,1... | collective-permute-start | bytes 1572872 | tf_op jit(solution)/shard_map/ppermute | solution.py:147
  452.3 16.1 %collective-permute-start.93 = (bf16[256,1024]{1,0:T(8,128)(2,1)S(1)}, bf16[256,1024]{1,0:T(8,128)(2,1)S(1)}, u32[]{:S(2)}, u32[]{:S(2)}) collective-permute-start(bf16[256,1024]{1,0:T(8,128)(2,1)S(1)} %collective-permute-done.91.refs_2_), channel_id=1, source_target_pairs={{0,1},{1,2},{2,3},{3,0},{4,5},{5,6},{6,7},{7,4},{8,9},{9,10},{10,1... | collective-permute-start | bytes 1572872 | tf_op jit(solution)/shard_map/ppermute | solution.py:147
  (135 other events, 1291.6 us)
Sparse Core Ops, SparseCore 0:
  59.9 94.2 all-gather.2
  265.8 47.7 reduce-scatter.1
  361.9 36.0 all-gather.4

commit v5 on v4

--- a/solution.py
+++ b/solution.py
@@ -362,7 +362,8 @@
 def attend_kernel(cfg, meta, q_ref, *refs):
     n, docs, picks, qt, kt, block = cfg
     keys, values = refs[:n], refs[n : 2 * n]
-    turn_ref, wide_ref, log_ref, kbuf, vbuf, acc, table, blocks, sems = refs[2 * n :]
+    turns, refs = refs[2 * n : 2 * n + q_ref.shape[0] // block], refs[2 * n + q_ref.shape[0] // block :]
+    wide_ref, log_ref, kbuf, vbuf, acc, table, blocks, sems = refs
     tok, width = q_ref.shape
     me = meta[0]
     factor = HD**-0.5 * LOG2E
@@ -405,11 +406,16 @@
             rows = jnp.transpose(acc[head] * (1.0 / total))
             wide_ref[pl.ds(base, qt), cols] = rows
             rows = rows.astype(BF)
+            size = min(block, qt)
+            inside = pl.ds(pl.multiple_of(lax.rem(base, block), size), size)
             for part in range(max(qt // block, 1)):
-                size = min(block, qt)
-                spot = lax.rem(base // block + part - meta[1] + spans, spans) * block + lax.rem(base, block)
-                spot = pl.multiple_of(spot, size)
-                turn_ref[pl.ds(spot, size), cols] = rows[part * size : (part + 1) * size]
+                spot = lax.rem(base // block + part - meta[1] + spans, spans)
+                for k, turn in enumerate(turns):
+
+                    @pl.when(spot == k)
+                    def _(turn=turn, part=part, rows=rows, cols=cols):
+                        turn[inside, cols] = rows[part * size : (part + 1) * size]
+
             log_ref[head : head + 1, pl.ds(base, qt)] = top * factor + jnp.log2(total)
         return carry
 
@@ -420,12 +426,12 @@
     n = len(keys)
     tok, width = q.shape
     qt, kt = 512, 1024
-    return pl.pallas_call(
+    *turns, wide, logs = pl.pallas_call(
         functools.partial(attend_kernel, (n, docs, picks, qt, kt, block)),
         in_specs=[SMEM, VMEM] + [ANY] * (2 * n),
-        out_specs=[VMEM] * 3,
-        out_shape=[
-            jax.ShapeDtypeStruct((tok, width), BF),
+        out_specs=[VMEM] * (2 + tok // block),
+        out_shape=[jax.ShapeDtypeStruct((block, width), BF)] * (tok // block)
+        + [
             jax.ShapeDtypeStruct((tok, width), F32),
             jax.ShapeDtypeStruct((width // HD, tok), F32),
         ],
@@ -441,6 +447,7 @@
         cost_estimate=QUICK,
         name="attend",
     )(meta, q, *keys, *values)
+    return turns, wide, logs
 
 
 def attend_back_kernel(cfg, meta, q_ref, wide_ref, log_ref, *refs):
@@ -1079,7 +1086,7 @@
     grads_all = direct_pieces(own_grads, n_seq)
     turned_heads, wide, logs = attend(meta, q, keys, values, docs, picks, block)
     turned_heads, grads_all = pin(turned_heads, grads_all)
-    heads = trade_tp([turned_heads[i * block : (i + 1) * block] for i in range(n_tp)], n_tp)
+    heads = trade_tp(turned_heads, n_tp)
     mixed, left, right = mix(meta, tokens, gains, weights, heads)
     left, grads_all = pin(left, grads_all)
     grads_all = core_gather(jnp.concatenate(grads_all, axis=0), n_seq)
@@ -1124,6 +1131,8 @@
             while len(outputs) < n_tp and (at == last or len(outputs) < 1 + 2 * at):
                 outputs.append(ring(outputs[-1], n_tp, 1))
         pairs, outputs, feed_sums, dq = pin(pairs, outputs, feed_sums, dq)
+        if at == min(1, last):
+            pairs, outer, held = pin(pairs, outer, held)
     dk, dv = pairs
     output = place(meta, outputs, block)
     early = whole_seq(feed_sums).reshape(-1, panel, d)

time: 484 us -> 484 us (level)
    unnamed x177 -> x181, local copies, waits for them, and re-layouts: 10.7 us -> 10.9 us
  transfers between devices with their start and end apart: 97 -> 97, of which waited for: 48 -> 47; matrix products, arithmetic and copies ran while one was open for 5% -> 5% of each run, Pallas kernels for 15% -> 16%
where the time goes in v5:
time: 484 us; the launch traced here: 480 us
  waiting for transfers between devices  221 us (46%)
  Pallas kernels  122 us (25%)
  starting transfers between devices  83.7 us (17%)
  other arithmetic  20.5 us (4%)
  local copies, waits for them, and re-layouts  18.1 us (4%)
  between operations  15.2 us (3%)
    ppermute x71, waiting for transfers between devices, swap(): return lax.ppermute(value, 'seq', [(i, i ^ bit) for i in range(count)])  143 us
    ppermute x18, waiting for transfers between devices, ring(): lax.ppermute(value, 'tp', [(i, (i + step) % count) for i in range(count)])  53.6 us
    ppermute x71, starting transfers between devices, swap(): return lax.ppermute(value, 'seq', [(i, i ^ bit) for i in range(count)])  49.9 us
    ppermute x18, starting transfers between devices, ring(): lax.ppermute(value, 'tp', [(i, (i + step) % count) for i in range(count)])  30.1 us
    pallas_call x1, Pallas kernels, feed_forward(): pl.pallas_call(functools.partial(feed_kernel, (n, spans, fs)), grid_spec=...  20.2 us
    ppermute x5, waiting for transfers between devices, sum_steps(): lax.ppermute(v, axis, pairs)  19.2 us
    pallas_call x1, Pallas kernels, attend_back(): pl.pallas_call(functools.partial(attend_back_kernel, (n, docs, picks, qt,...  15.8 us
    convert_element_type x13, other arithmetic, plus(): return (left.astype(F32) + right.astype(F32)).astype(left.dtype)  12.9 us
  transfers between devices with their start and end apart: 97, of which 47 were waited for; matrix products, arithmetic and copies ran while one was open for 5% of the time, Pallas kernels for 16%

profile of v5, /device:TPU:0, one launch (start us, length us, event | category | flops | bytes accessed | tf_op | source)
XLA Modules:
  0.0 480.4 jit_solution(5331278176068242401)
XLA Ops:
  9.6 2.9 collective-permute-start.1
  14.6 17.1 %collective-permute-done.4.refs_10_ = bf16[6,32,1024]{2,1,0:T(8,128)(2,1)S(1)} collective-permute-done((bf16[6,32,1024]{2,1,0:T(8,128)(2,1)S(1)}, bf16[6,32,1024]{2,1,0:T(8,128)(2,1)S(1)}, u32[]{:S(2)}, u32[]{:S(2)}) %collective-permute-start.4) | collective-permute-done | bytes 393248 | tf_op jit(solution)/shard_map/ppermute | solution.py:67
  36.1 10.9 %collective-permute-done.11.refs_14_ = bf16[6,32,1024]{2,1,0:T(8,128)(2,1)} collective-permute-done((bf16[6,32,1024]{2,1,0:T(8,128)(2,1)S(1)}, bf16[6,32,1024]{2,1,0:T(8,128)(2,1)}, u32[]{:S(2)}, u32[]{:S(2)}) %collective-permute-start.11) | collective-permute-done | bytes 393248 | tf_op jit(solution)/shard_map/ppermute | solution.py:67
  50.6 9.2 %project.1 = (bf16[1024,256]{1,0:T(8,128)(2,1)}, bf16[1024,256]{1,0:T(8,128)(2,1)}, bf16[1024,256]{1,0:T(8,128)(2,1)}, bf16[1024,1024]{1,0:T(8,128)(2,1)}, bf16[...) custom-call(s32[18]{0:T(128)} %pad_add_fusion.meta, s32[98]{0:T(128)} %owners.1, bf16[1024,1024]{1,0:T(8,128)(2,1)} %x_ref.7, ...), custom_call_target="tpu_custom_call" | custom-call | flops 1000 | bytes 1000 | tf_op jit(solution)/shard_map/project/pallas_call | solution.py:262
  64.3 10.9 %collective-permute-done.15.refs_2_.refs_6_ = bf16[1024,256]{1,0:T(8,128)(2,1)S(1)} collective-permute-done((bf16[1024,256]{1,0:T(8,128)(2,1)}, bf16[1024,256]{1,0:T(8,128)(2,1)S(1)}, u32[]{:S(2)}, u32[]{:S(2)}) %collective-permute-start.15) | collective-permute-done | bytes 524320 | tf_op jit(solution)/shard_map/ppermute | solution.py:67
  75.8 10.1 %collective-permute-done.18.refs_10_.refs_14_ = bf16[1024,256]{1,0:T(8,128)(2,1)S(1)} collective-permute-done((bf16[1024,256]{1,0:T(8,128)(2,1)}, bf16[1024,256]{1,0:T(8,128)(2,1)S(1)}, u32[]{:S(2)}, u32[]{:S(2)}) %collective-permute-start.18) | collective-permute-done | bytes 524320 | tf_op jit(solution)/shard_map/ppermute | solution.py:67
  90.5 10.2 %collective-permute-done.22.refs_6_.refs_10_ = bf16[1024,256]{1,0:T(8,128)(2,1)} collective-permute-done((bf16[1024,256]{1,0:T(8,128)(2,1)S(1)}, bf16[1024,256]{1,0:T(8,128)(2,1)}, u32[]{:S(2)}, u32[]{:S(2)}) %collective-permute-start.22) | collective-permute-done | bytes 524320 | tf_op jit(solution)/shard_map/ppermute | solution.py:67
  100.7 2.5 collective-permute-done.25.refs_14_.refs_18_
  109.4 11.9 %attend.1 = (bf16[256,256]{1,0:T(8,128)(2,1)}, bf16[256,256]{1,0:T(8,128)(2,1)}, bf16[256,256]{1,0:T(8,128)(2,1)}, bf16[256,256]{1,0:T(8,128)(2,1)}, f32[1024,256]{1,0:T(8,128)}, /*index=5*/f32[2,1024]{1,0:T(2,128)}) custom-call(s32[18]{0:T(128)} %pad_add_fusion.meta, bf16[1024,256]{1,0:T(8,128)(2,1)} %get-tuple-element.283.q_ref, ...), custom_call_target="tpu_custom_call" | custom-call | flops 1000 | bytes 1000 | tf_op jit(solution)/shard_map/attend/pallas_call | solution.py:429
  121.3 9.9 %collective-permute-done.29 = bf16[256,1024]{1,0:T(8,128)(2,1)S(1)} collective-permute-done((bf16[256,1024]{1,0:T(8,128)(2,1)S(1)}, bf16[256,1024]{1,0:T(8,128)(2,1)S(1)}, u32[]{:S(2)}, u32[]{:S(2)}) %collective-permute-start.29) | collective-permute-done | bytes 524320 | tf_op jit(solution)/shard_map/ppermute | solution.py:67
  133.8 2.6 collective-permute-start.32
  138.1 5.3 %collective-permute-done.31.refs_1_ = bf16[256,256]{1,0:T(8,128)(2,1)S(1)} collective-permute-done((bf16[256,256]{1,0:T(8,128)(2,1)}, bf16[256,256]{1,0:T(8,128)(2,1)S(1)}, u32[]{:S(2)}, u32[]{:S(2)}) %collective-permute-start.31) | collective-permute-done | bytes 131104 | tf_op jit(solution)/shard_map/ppermute | solution.py:147
  143.4 8.0 %collective-permute-done.32.refs_2_ = bf16[256,256]{1,0:T(8,128)(2,1)S(1)} collective-permute-done((bf16[256,256]{1,0:T(8,128)(2,1)}, bf16[256,256]{1,0:T(8,128)(2,1)S(1)}, u32[]{:S(2)}, u32[]{:S(2)}) %collective-permute-start.32) | collective-permute-done | bytes 131104 | tf_op jit(solution)/shard_map/ppermute | solution.py:147
  151.4 3.9 all-gather.3.cloned.1.call-done
  155.4 5.3 %mix.1 = (f32[256,1024]{1,0:T(8,128)}, bf16[256,512]{1,0:T(8,128)(2,1)}, bf16[256,512]{1,0:T(8,128)(2,1)}) custom-call(s32[18]{0:T(128)} %pad_add_fusion.meta, bf16[1024,1024]{1,0:T(8,128)(2,1)} %x_ref.7, f32[2,1024]{1,0:T(2,128)} %gain_ref.5, bf16[4,544,1024]{2,1,0:T(8,128)(2,1)} %bitcast.27, bf16[256,256]{1,0:T(8,128)(2,1)} %get-tuple-element.315.refs_0_, ...), custom_call_target="tpu_custom_call" | custom-call | flops 1000 | bytes 1000 | tf_op jit(solution)/shard_map/mix/pallas_call | solution.py:590
  167.3 3.5 collective-permute-done.36.refs_2_
  172.5 3.5 collective-permute-done.39.refs_10_
  182.4 4.6 collective-permute-done.43.refs_6_
  192.8 20.2 %feed_forward.1 = (bf16[2048,1024]{1,0:T(8,128)(2,1)}, bf16[2048,384]{1,0:T(8,128)(2,1)}, bf16[2048,768]{1,0:T(8,128)(2,1)}, bf16[1024,512]{1,0:T(8,128)(2,1)}, ...) custom-call(s32[18]{0:T(128)} %pad_add_fusion.meta, ...), custom_call_target="tpu_custom_call" | custom-call | flops 1000 | bytes 1000 | tf_op jit(solution)/shard_map/feed_forward/pallas_call | solution.py:673
  220.1 11.2 %feed_grads.1 = bf16[4,288,1024]{2,1,0:T(8,128)(2,1)} custom-call(bf16[2048,384]{1,0:T(8,128)(2,1)} %get-tuple-element.367.hidden, bf16[2048,768]{1,0:T(8,128)(2,1)} %get-tuple-element.368.d_inner, bf16[2048,1024]{1,0:T(8,128)(2,1)} %get-tuple-element.369.normed, bf16[2048,1024]{1,0:T(8,128)(2,1)} %copy-done.3), custom_call_target="tpu_custom_call" | custom-call | flops 1000 | bytes 1000 | tf_op jit(solution)/shard_map/feed_grads/pallas_call | solution.py:787
  236.1 5.7 %collective-permute-done.54.left_b = bf16[256,512]{1,0:T(8,128)(2,1)S(1)} collective-permute-done((bf16[256,512]{1,0:T(8,128)(2,1)S(1)}, bf16[256,512]{1,0:T(8,128)(2,1)S(1)}, u32[]{:S(2)}, u32[]{:S(2)}) %collective-permute-start.54) | collective-permute-done | bytes 262176 | tf_op jit(solution)/shard_map/ppermute | solution.py:67
  242.9 7.7 %branch_back.1 = (f32[256,1024]{1,0:T(8,128)}, f32[1,1024]{1,0:T(1,128)}, bf16[256,256]{1,0:T(8,128)(2,1)}, bf16[256,256]{1,0:T(8,128)(2,1)}, bf16[256,256]{1,0:...) custom-call(s32[18]{0:T(128)} %pad_add_fusion.meta, ...), custom_call_target="tpu_custom_call" | custom-call | flops 1000 | bytes 1000 | tf_op jit(solution)/shard_map/branch_back/pallas_call | solution.py:730
  257.3 3.5 collective-permute-done.56.refs_1_
  260.8 5.2 %collective-permute-done.57.refs_2_ = bf16[256,256]{1,0:T(8,128)(2,1)S(1)} collective-permute-done((bf16[256,256]{1,0:T(8,128)(2,1)S(1)}, bf16[256,256]{1,0:T(8,128)(2,1)S(1)}, u32[]{:S(2)}, u32[]{:S(2)}) %collective-permute-start.57) | collective-permute-done | bytes 131104 | tf_op jit(solution)/shard_map/ppermute | solution.py:147
  269.8 15.8 %attend_back.1 = (bf16[1024,256]{1,0:T(8,128)(2,1)}, bf16[4096,256]{1,0:T(8,128)(2,1)}, bf16[4096,256]{1,0:T(8,128)(2,1)}, bf16[4096,256]{1,0:T(8,128)(2,1)}, bf16[4096,256]{1,0:T(8,128)(2,1)}) custom-call(s32[18]{0:T(128)} %pad_add_fusion.meta, bf16[1024,256]{1,0:T(8,128)(2,1)} %get-tuple-element.283.q_ref, f32[1024,256]{1,0:T(8,128)} %get-tuple-element.389.wide_ref, ...), custom_call_target="tpu_custom_call" | custom-call | flops 1000 | bytes 1000 | tf_op jit(solution)/shard_map/attend_back/pallas_call | solution.py:545
  286.7 16.8 %collective-permute-done.61 = bf16[384,1024]{1,0:T(8,128)(2,1)S(1)} collective-permute-done((bf16[384,1024]{1,0:T(8,128)(2,1)S(1)}, bf16[384,1024]{1,0:T(8,128)(2,1)S(1)}, u32[]{:S(2)}, u32[]{:S(2)}) %collective-permute-start.61) | collective-permute-done | bytes 786464 | tf_op jit(solution)/shard_map/ppermute | solution.py:67
  305.0 2.9 collective-permute-done.64
  317.1 2.8 collective-permute-start.67
  321.4 10.5 %collective-permute-done.67.refs_1_ = bf16[256,1024]{1,0:T(8,128)(2,1)S(1)} collective-permute-done((bf16[256,1024]{1,0:T(8,128)(2,1)S(1)}, bf16[256,1024]{1,0:T(8,128)(2,1)S(1)}, u32[]{:S(2)}, u32[]{:S(2)}) %collective-permute-start.67) | collective-permute-done | bytes 524320 | tf_op jit(solution)/shard_map/ppermute | solution.py:147
  333.5 5.6 %collective-permute-done.66 = bf16[2048,256]{1,0:T(8,128)(2,1)} collective-permute-done((bf16[2048,256]{1,0:T(8,128)(2,1)}, bf16[2048,256]{1,0:T(8,128)(2,1)}, u32[]{:S(2)}, u32[]{:S(2)}) %collective-permute-start.66) | collective-permute-done | bytes 1048608 | tf_op jit(solution)/shard_map/ppermute | solution.py:67
  342.6 3.1 collective-permute-done.68.refs_2_
  349.2 7.5 %collective-permute-done.69.dk_b = bf16[1024,256]{1,0:T(8,128)(2,1)S(1)} collective-permute-done((bf16[1024,256]{1,0:T(8,128)(2,1)S(1)}, bf16[1024,256]{1,0:T(8,128)(2,1)S(1)}, u32[]{:S(2)}, u32[]{:S(2)}) %collective-permute-start.69) | collective-permute-done | bytes 524320 | tf_op jit(solution)/shard_map/ppermute | solution.py:67
  357.1 2.5 collective-permute-done.71.refs_3_
  359.6 2.7 fusion.14
  362.4 4.1 back_in.2
  370.6 2.8 collective-permute-start.75
  373.5 6.0 %back_in.3 = (bf16[768,1024]{1,0:T(8,128)(2,1)}, f32[1,1024]{1,0:T(1,128)}) custom-call(s32[18]{0:T(128)} %pad_add_fusion.meta, bf16[1024,1024]{1,0:T(8,128)(2,1)} %x_ref.7, bf16[1024,256]{1,0:T(8,128)(2,1)} %get-tuple-element.438.dq, bf16[1024,256]{1,0:T(8,128)(2,1)} %get-tuple-element.439.dk_a, bf16[1024,256]{1,0:T(8,128)(2,1)} %copy-done.4, ...), custom_call_target="tpu_custom_call" | custom-call | flops 1000 | bytes 1000 | tf_op jit(solution)/shard_map/back_in/pallas_call | solution.py:1020
  379.5 6.3 %late_grads.1 = (bf16[384,1024]{1,0:T(8,128)(2,1)}, bf16[384,1024]{1,0:T(8,128)(2,1)}) custom-call(s32[18]{0:T(128)} %pad_add_fusion.meta, bf16[1024,256]{1,0:T(8,128)(2,1)} %get-tuple-element.438.dq, bf16[1024,256]{1,0:T(8,128)(2,1)} %get-tuple-element.439.dk_a, bf16[1024,256]{1,0:T(8,128)(2,1)} %copy-done.4, bf16[1024,256]{1,0:T(8,128)(2,1)} %get-tuple-element.441.dv_a, ...), custom_call_target="tpu_custom_call" | custom-call | flops 1000 | bytes 1000 | tf_op jit(solution)/shard_map/late_grads/pallas_call | solution.py:829
  387.6 3.1 place.2
  391.6 3.0 collective-permute-done.79
  394.6 6.9 %collective-permute-done.76 = bf16[256,1024]{1,0:T(8,128)(2,1)S(1)} collective-permute-done((bf16[256,1024]{1,0:T(8,128)(2,1)}, bf16[256,1024]{1,0:T(8,128)(2,1)S(1)}, u32[]{:S(2)}, u32[]{:S(2)}) %collective-permute-start.76) | collective-permute-done | bytes 524320 | tf_op jit(solution)/shard_map/ppermute | solution.py:147
  405.6 2.6 collective-permute-start.80
  408.4 10.1 %collective-permute-done.85 = f32[2,1024]{1,0:T(2,128)S(1)} collective-permute-done((f32[2,1024]{1,0:T(2,128)S(1)}, f32[2,1024]{1,0:T(2,128)S(1)}, u32[]{:S(2)}, u32[]{:S(2)}) %collective-permute-start.85) | collective-permute-done | bytes 8224 | tf_op jit(solution)/shard_map/ppermute | solution.py:177
  427.5 6.0 %collective-permute-done.90 = f32[2,1024]{1,0:T(2,128)S(1)} collective-permute-done((f32[2,1024]{1,0:T(2,128)S(1)}, f32[2,1024]{1,0:T(2,128)S(1)}, u32[]{:S(2)}, u32[]{:S(2)}) %collective-permute-start.90) | collective-permute-done | bytes 8224 | tf_op jit(solution)/shard_map/ppermute | solution.py:177
  438.5 12.4 %soap.1 = (f32[13,32,1024]{2,1,0:T(8,128)}, f32[13,32,1024]{2,1,0:T(8,128)}, f32[13,32,1024]{2,1,0:T(8,128)}, f32[13,32,1024]{2,1,0:T(8,128)}, f32[13,32,32]{2,1,0:T(8,128)}, /*index=5*/f32[13,32,32]{2,1,0:T(8,128)}) custom-call(s32[18]{0:T(128)} %pad_add_fusion.meta, s32[13]{0:T(128)} %broadcast_add_fusion.held, bf16[72,32,1024]{2,1,0:T(8,128)(2,1)} %bitcast.38, ...), custom_call_target="tpu_custom_call" | custom-call | flops 1000 | bytes 1000 | tf_op jit(solution)/shard_map/soap/pallas_call | solution.py:943
  453.7 4.6 orthonormal.1
  458.3 8.6 %collective-permute-done.93.refs_3_ = bf16[256,1024]{1,0:T(8,128)(2,1)S(1)} collective-permute-done((bf16[256,1024]{1,0:T(8,128)(2,1)S(1)}, bf16[256,1024]{1,0:T(8,128)(2,1)S(1)}, u32[]{:S(2)}, u32[]{:S(2)}) %collective-permute-start.93) | collective-permute-done | bytes 524320 | tf_op jit(solution)/shard_map/ppermute | solution.py:147
  469.8 3.8 place.3
  (398 shorter events, 128.7 us)
Async XLA Ops:
  7.2 148.2 %all-gather.3.cloned.1.call-start = ((), (), s32[]{:S(2)}) async-start(), calls=%async_computation.1 | async-start | bytes 5570560 | tf_op jit(solution)/shard_map/all_gather | solution.py:1072
  9.4 23.7 %collective-permute-start = (bf16[7,32,1024]{2,1,0:T(8,128)(2,1)S(1)}, bf16[7,32,1024]{2,1,0:T(8,128)(2,1)S(1)}, u32[]{:S(2)}, u32[]{:S(2)}) collective-permute-start(bf16[7,32,1024]{2,1,0:T(8,128)(2,1)S(1)} %slice.239.refs_0_), channel_id=1, source_target_pairs={{0,4},{4,0},{8,12},{12,8},{16,20},{20,16},{24,28},{28,24},{1,5},{5... | collective-permute-start | bytes 1376264 | tf_op jit(solution)/shard_map/ppermute | solution.py:67
  9.6 23.6 %collective-permute-start.1 = (bf16[7,32,1024]{2,1,0:T(8,128)(2,1)S(1)}, bf16[7,32,1024]{2,1,0:T(8,128)(2,1)S(1)}, u32[]{:S(2)}, u32[]{:S(2)}) collective-permute-start(bf16[7,32,1024]{2,1,0:T(8,128)(2,1)S(1)} %slice.239.refs_0_), channel_id=1, source_target_pairs={{0,8},{4,12},{8,0},{12,4},{16,24},{20,28},{24,16},{28,20},{1,9},{5... | collective-permute-start | bytes 1376264 | tf_op jit(solution)/shard_map/ppermute | solution.py:67
  12.5 20.7 %collective-permute-start.2 = (bf16[7,32,1024]{2,1,0:T(8,128)(2,1)S(1)}, bf16[7,32,1024]{2,1,0:T(8,128)(2,1)S(1)}, u32[]{:S(2)}, u32[]{:S(2)}) collective-permute-start(bf16[7,32,1024]{2,1,0:T(8,128)(2,1)S(1)} %slice.239.refs_0_), channel_id=1, source_target_pairs={{0,16},{4,20},{8,24},{12,28},{16,0},{20,4},{24,8},{28,12},{1,17},{... | collective-permute-start | bytes 1376264 | tf_op jit(solution)/shard_map/ppermute | solution.py:67
  14.0 17.6 %collective-permute-start.4 = (bf16[6,32,1024]{2,1,0:T(8,128)(2,1)S(1)}, bf16[6,32,1024]{2,1,0:T(8,128)(2,1)S(1)}, u32[]{:S(2)}, u32[]{:S(2)}) collective-permute-start(bf16[6,32,1024]{2,1,0:T(8,128)(2,1)S(1)} %slice.240.refs_8_), channel_id=1, source_target_pairs={{0,8},{4,12},{8,0},{12,4},{16,24},{20,28},{24,16},{28,20},{1,9},{5... | collective-permute-start | bytes 1179656 | tf_op jit(solution)/shard_map/ppermute | solution.py:67
  14.6 18.6 %collective-permute-start.5 = (bf16[6,32,1024]{2,1,0:T(8,128)(2,1)S(1)}, bf16[6,32,1024]{2,1,0:T(8,128)(2,1)S(1)}, u32[]{:S(2)}, u32[]{:S(2)}) collective-permute-start(bf16[6,32,1024]{2,1,0:T(8,128)(2,1)S(1)} %slice.240.refs_8_), channel_id=1, source_target_pairs={{0,16},{4,20},{8,24},{12,28},{16,0},{20,4},{24,8},{28,12},{1,17},{... | collective-permute-start | bytes 1179656 | tf_op jit(solution)/shard_map/ppermute | solution.py:67
  33.3 13.7 %collective-permute-start.6 = (bf16[7,32,1024]{2,1,0:T(8,128)(2,1)S(1)}, bf16[7,32,1024]{2,1,0:T(8,128)(2,1)S(1)}, u32[]{:S(2)}, u32[]{:S(2)}) collective-permute-start(bf16[7,32,1024]{2,1,0:T(8,128)(2,1)S(1)} %collective-permute-done.1.refs_2_), channel_id=1, source_target_pairs={{0,4},{4,0},{8,12},{12,8},{16,20},{20,16},{24,28},{28,24},{1,5},{5... | collective-permute-start | bytes 1376264 | tf_op jit(solution)/shard_map/ppermute | solution.py:67
  33.8 13.2 %collective-permute-start.8 = (bf16[7,32,1024]{2,1,0:T(8,128)(2,1)S(1)}, bf16[7,32,1024]{2,1,0:T(8,128)(2,1)S(1)}, u32[]{:S(2)}, u32[]{:S(2)}) collective-permute-start(bf16[7,32,1024]{2,1,0:T(8,128)(2,1)S(1)} %collective-permute-done.1.refs_2_), channel_id=1, source_target_pairs={{0,16},{4,20},{8,24},{12,28},{16,0},{20,4},{24,8},{28,12},{1,17},{... | collective-permute-start | bytes 1376264 | tf_op jit(solution)/shard_map/ppermute | solution.py:67
  59.8 254.3 %reduce-scatter.2.cloned.1.call-start = ((), (), s32[]{:S(2)}) async-start(), calls=%async_computation.2 | async-start | bytes 2949120 | tf_op jit(solution)/shard_map/reduce_scatter | solution.py:1120
  60.2 14.9 %collective-permute-start.15 = (bf16[1024,256]{1,0:T(8,128)(2,1)}, bf16[1024,256]{1,0:T(8,128)(2,1)S(1)}, u32[]{:S(2)}, u32[]{:S(2)}) collective-permute-start(bf16[1024,256]{1,0:T(8,128)(2,1)} %get-tuple-element.294.refs_0_.refs_4_), channel_id=1, source_target_pairs={{0,8},{4,12},{8,0},{12,4},{16,24},{20,28},{24,16},{28,20},{1,9},{5... | collective-permute-start | bytes 1572872 | tf_op jit(solution)/shard_map/ppermute | solution.py:67
  60.8 15.0 %collective-permute-start.16 = (bf16[1024,256]{1,0:T(8,128)(2,1)}, bf16[1024,256]{1,0:T(8,128)(2,1)S(1)}, u32[]{:S(2)}, u32[]{:S(2)}) collective-permute-start(bf16[1024,256]{1,0:T(8,128)(2,1)} %get-tuple-element.294.refs_0_.refs_4_), channel_id=1, source_target_pairs={{0,16},{4,20},{8,24},{12,28},{16,0},{20,4},{24,8},{28,12},{1,17},{... | collective-permute-start | bytes 1572872 | tf_op jit(solution)/shard_map/ppermute | solution.py:67
  61.5 14.3 %collective-permute-start.17 = (bf16[1024,256]{1,0:T(8,128)(2,1)}, bf16[1024,256]{1,0:T(8,128)(2,1)S(1)}, u32[]{:S(2)}, u32[]{:S(2)}) collective-permute-start(bf16[1024,256]{1,0:T(8,128)(2,1)} %get-tuple-element.303.refs_8_.refs_12_), channel_id=1, source_target_pairs={{0,4},{4,0},{8,12},{12,8},{16,20},{20,16},{24,28},{28,24},{1,5},{5... | collective-permute-start | bytes 1572872 | tf_op jit(solution)/shard_map/ppermute | solution.py:67
  61.5 24.4 %collective-permute-start.18 = (bf16[1024,256]{1,0:T(8,128)(2,1)}, bf16[1024,256]{1,0:T(8,128)(2,1)S(1)}, u32[]{:S(2)}, u32[]{:S(2)}) collective-permute-start(bf16[1024,256]{1,0:T(8,128)(2,1)} %get-tuple-element.303.refs_8_.refs_12_), channel_id=1, source_target_pairs={{0,8},{4,12},{8,0},{12,4},{16,24},{20,28},{24,16},{28,20},{1,9},{5... | collective-permute-start | bytes 1572872 | tf_op jit(solution)/shard_map/ppermute | solution.py:67
  63.0 23.2 %collective-permute-start.19 = (bf16[1024,256]{1,0:T(8,128)(2,1)}, bf16[1024,256]{1,0:T(8,128)(2,1)}, u32[]{:S(2)}, u32[]{:S(2)}) collective-permute-start(bf16[1024,256]{1,0:T(8,128)(2,1)} %get-tuple-element.303.refs_8_.refs_12_), channel_id=1, source_target_pairs={{0,16},{4,20},{8,24},{12,28},{16,0},{20,4},{24,8},{28,12},{1,17},{... | collective-permute-start | bytes 1572872 | tf_op jit(solution)/shard_map/ppermute | solution.py:67
  86.2 14.4 %collective-permute-start.22 = (bf16[1024,256]{1,0:T(8,128)(2,1)S(1)}, bf16[1024,256]{1,0:T(8,128)(2,1)}, u32[]{:S(2)}, u32[]{:S(2)}) collective-permute-start(bf16[1024,256]{1,0:T(8,128)(2,1)S(1)} %collective-permute-done.15.refs_2_.refs_6_), channel_id=1, source_target_pairs={{0,16},{4,20},{8,24},{12,28},{16,0},{20,4},{24,8},{28,12},{1,17},{... | collective-permute-start | bytes 1572872 | tf_op jit(solution)/shard_map/ppermute | solution.py:67
  87.3 13.4 %collective-permute-start.23 = (bf16[1024,256]{1,0:T(8,128)(2,1)S(1)}, bf16[1024,256]{1,0:T(8,128)(2,1)}, u32[]{:S(2)}, u32[]{:S(2)}) collective-permute-start(bf16[1024,256]{1,0:T(8,128)(2,1)S(1)} %collective-permute-done.18.refs_10_.refs_14_), channel_id=1, source_target_pairs={{0,4},{4,0},{8,12},{12,8},{16,20},{20,16},{24,28},{28,24},{1,5},{5... | collective-permute-start | bytes 1572872 | tf_op jit(solution)/shard_map/ppermute | solution.py:67
  87.5 13.1 %collective-permute-start.24 = (bf16[1024,256]{1,0:T(8,128)(2,1)}, bf16[1024,256]{1,0:T(8,128)(2,1)}, u32[]{:S(2)}, u32[]{:S(2)}) collective-permute-start(bf16[1024,256]{1,0:T(8,128)(2,1)} %collective-permute-done.19.refs_12_.refs_16_), channel_id=1, source_target_pairs={{0,4},{4,0},{8,12},{12,8},{16,20},{20,16},{24,28},{28,24},{1,5},{5... | collective-permute-start | bytes 1572872 | tf_op jit(solution)/shard_map/ppermute | solution.py:67
  88.9 14.3 %collective-permute-start.25 = (bf16[1024,256]{1,0:T(8,128)(2,1)}, bf16[1024,256]{1,0:T(8,128)(2,1)}, u32[]{:S(2)}, u32[]{:S(2)}) collective-permute-start(bf16[1024,256]{1,0:T(8,128)(2,1)} %collective-permute-done.19.refs_12_.refs_16_), channel_id=1, source_target_pairs={{0,8},{4,12},{8,0},{12,4},{16,24},{20,28},{24,16},{28,20},{1,9},{5... | collective-permute-start | bytes 1572872 | tf_op jit(solution)/shard_map/ppermute | solution.py:67
  104.8 16.5 %collective-permute-start.28 = (bf16[256,1024]{1,0:T(8,128)(2,1)S(1)}, bf16[256,1024]{1,0:T(8,128)(2,1)S(1)}, u32[]{:S(2)}, u32[]{:S(2)}) collective-permute-start(bf16[256,1024]{1,0:T(8,128)(2,1)S(1)} %constant_dynamic-slice_fusion), channel_id=1, source_target_pairs={{0,8},{4,12},{8,0},{12,4},{16,24},{20,28},{24,16},{28,20},{1,9},{5... | collective-permute-start | bytes 1572872 | tf_op jit(solution)/shard_map/ppermute | solution.py:67
  106.4 24.8 %collective-permute-start.29 = (bf16[256,1024]{1,0:T(8,128)(2,1)S(1)}, bf16[256,1024]{1,0:T(8,128)(2,1)S(1)}, u32[]{:S(2)}, u32[]{:S(2)}) collective-permute-start(bf16[256,1024]{1,0:T(8,128)(2,1)S(1)} %constant_dynamic-slice_fusion), channel_id=1, source_target_pairs={{0,16},{4,20},{8,24},{12,28},{16,0},{20,4},{24,8},{28,12},{1,17},{... | collective-permute-start | bytes 1572872 | tf_op jit(solution)/shard_map/ppermute | solution.py:67
  107.4 23.8 %collective-permute-start.30 = (bf16[256,1024]{1,0:T(8,128)(2,1)S(1)}, bf16[256,1024]{1,0:T(8,128)(2,1)S(1)}, u32[]{:S(2)}, u32[]{:S(2)}) collective-permute-start(bf16[256,1024]{1,0:T(8,128)(2,1)S(1)} %constant_dynamic-slice_fusion), channel_id=1, source_target_pairs={{0,24},{4,28},{8,16},{12,20},{16,8},{20,12},{24,0},{28,4},{1,25},{... | collective-permute-start | bytes 1572872 | tf_op jit(solution)/shard_map/ppermute | solution.py:67
  133.8 17.6 %collective-permute-start.32 = (bf16[256,256]{1,0:T(8,128)(2,1)}, bf16[256,256]{1,0:T(8,128)(2,1)S(1)}, u32[]{:S(2)}, u32[]{:S(2)}) collective-permute-start(bf16[256,256]{1,0:T(8,128)(2,1)} %get-tuple-element.317), channel_id=1, source_target_pairs={{0,2},{1,3},{2,0},{3,1},{4,6},{5,7},{6,4},{7,5},{8,10},{9,11},{10,... | collective-permute-start | bytes 393224 | tf_op jit(solution)/shard_map/ppermute | solution.py:147
  136.4 15.0 %collective-permute-start.33 = (bf16[256,256]{1,0:T(8,128)(2,1)}, bf16[256,256]{1,0:T(8,128)(2,1)S(1)}, u32[]{:S(2)}, u32[]{:S(2)}) collective-permute-start(bf16[256,256]{1,0:T(8,128)(2,1)} %get-tuple-element.318), channel_id=1, source_target_pairs={{0,3},{1,0},{2,1},{3,2},{4,7},{5,4},{6,5},{7,6},{8,11},{9,8},{10,9... | collective-permute-start | bytes 393224 | tf_op jit(solution)/shard_map/ppermute | solution.py:147
  160.9 28.9 %collective-permute-start.34 = (bf16[1024,1024]{1,0:T(8,128)(2,1)S(1)}, bf16[1024,1024]{1,0:T(8,128)(2,1)S(1)}, u32[]{:S(2)}, u32[]{:S(2)}) collective-permute-start(bf16[1024,1024]{1,0:T(8,128)(2,1)S(1)} %pad_maximum_fusion), channel_id=1, source_target_pairs={{0,4},{4,0},{8,12},{12,8},{16,20},{20,16},{24,28},{28,24},{1,5},{5... | collective-permute-start | bytes 6291464 | tf_op jit(solution)/shard_map/ppermute | solution.py:67
  217.8 16.1 %collective-permute-start.53 = (bf16[1024,1024]{1,0:T(8,128)(2,1)}, bf16[1024,1024]{1,0:T(8,128)(2,1)S(1)}, u32[]{:S(2)}, u32[]{:S(2)}) collective-permute-start(bf16[1024,1024]{1,0:T(8,128)(2,1)} %get-tuple-element.366), channel_id=1, source_target_pairs={{0,4},{4,0},{8,12},{12,8},{16,20},{20,16},{24,28},{28,24},{1,5},{5... | collective-permute-start | bytes 6291464 | tf_op jit(solution)/shard_map/ppermute | solution.py:67
  218.1 14.2 %collective-permute-start.52 = (bf16[512,512]{1,0:T(8,128)(2,1)S(1)}, bf16[512,512]{1,0:T(8,128)(2,1)S(1)}, u32[]{:S(2)}, u32[]{:S(2)}) collective-permute-start(bf16[512,512]{1,0:T(8,128)(2,1)S(1)} %get-tuple-element.364), channel_id=1, source_target_pairs={{0,8},{4,12},{8,0},{12,4},{16,24},{20,28},{24,16},{28,20},{1,9},{5... | collective-permute-start | bytes 1572872 | tf_op jit(solution)/shard_map/ppermute | solution.py:67
  218.8 14.3 %collective-permute-start.51 = (bf16[512,512]{1,0:T(8,128)(2,1)S(1)}, bf16[512,512]{1,0:T(8,128)(2,1)S(1)}, u32[]{:S(2)}, u32[]{:S(2)}) collective-permute-start(bf16[512,512]{1,0:T(8,128)(2,1)S(1)} %get-tuple-element.362), channel_id=1, source_target_pairs={{0,16},{4,20},{8,24},{12,28},{16,0},{20,4},{24,8},{28,12},{1,17},{... | collective-permute-start | bytes 1572872 | tf_op jit(solution)/shard_map/ppermute | solution.py:67
  266.1 172.4 %all-gather.5.cloned.1.call-start = ((), (), s32[]{:S(2)}) async-start(), calls=%async_computation.3 | async-start | bytes 5308416 | tf_op jit(solution)/shard_map/all_gather | solution.py:1075
  266.3 20.5 %collective-permute-start.60 = (bf16[384,1024]{1,0:T(8,128)(2,1)S(1)}, bf16[384,1024]{1,0:T(8,128)(2,1)S(1)}, u32[]{:S(2)}, u32[]{:S(2)}) collective-permute-start(bf16[384,1024]{1,0:T(8,128)(2,1)S(1)} %get-tuple-element.386), channel_id=1, source_target_pairs={{0,8},{4,12},{8,0},{12,4},{16,24},{20,28},{24,16},{28,20},{1,9},{5... | collective-permute-start | bytes 2359304 | tf_op jit(solution)/shard_map/ppermute | solution.py:67
  267.7 35.8 %collective-permute-start.61 = (bf16[384,1024]{1,0:T(8,128)(2,1)S(1)}, bf16[384,1024]{1,0:T(8,128)(2,1)S(1)}, u32[]{:S(2)}, u32[]{:S(2)}) collective-permute-start(bf16[384,1024]{1,0:T(8,128)(2,1)S(1)} %get-tuple-element.387), channel_id=1, source_target_pairs={{0,16},{4,20},{8,24},{12,28},{16,0},{20,4},{24,8},{28,12},{1,17},{... | collective-permute-start | bytes 2359304 | tf_op jit(solution)/shard_map/ppermute | solution.py:67
  268.3 35.2 %collective-permute-start.62 = (bf16[384,1024]{1,0:T(8,128)(2,1)S(1)}, bf16[384,1024]{1,0:T(8,128)(2,1)S(1)}, u32[]{:S(2)}, u32[]{:S(2)}) collective-permute-start(bf16[384,1024]{1,0:T(8,128)(2,1)S(1)} %get-tuple-element.388), channel_id=1, source_target_pairs={{0,24},{4,28},{8,16},{12,20},{16,8},{20,12},{24,0},{28,4},{1,25},{... | collective-permute-start | bytes 2359304 | tf_op jit(solution)/shard_map/ppermute | solution.py:67
  314.1 25.0 %collective-permute-start.66 = (bf16[2048,256]{1,0:T(8,128)(2,1)}, bf16[2048,256]{1,0:T(8,128)(2,1)}, u32[]{:S(2)}, u32[]{:S(2)}) collective-permute-start(bf16[2048,256]{1,0:T(8,128)(2,1)} %get-tuple-element.413), channel_id=1, source_target_pairs={{0,8},{4,12},{8,0},{12,4},{16,24},{20,28},{24,16},{28,20},{1,9},{5... | collective-permute-start | bytes 3145736 | tf_op jit(solution)/shard_map/ppermute | solution.py:67
  315.6 25.9 %collective-permute-start.65 = (bf16[2048,256]{1,0:T(8,128)(2,1)}, bf16[2048,256]{1,0:T(8,128)(2,1)S(1)}, u32[]{:S(2)}, u32[]{:S(2)}) collective-permute-start(bf16[2048,256]{1,0:T(8,128)(2,1)} %get-tuple-element.411), channel_id=1, source_target_pairs={{0,16},{4,20},{8,24},{12,28},{16,0},{20,4},{24,8},{28,12},{1,17},{... | collective-permute-start | bytes 3145736 | tf_op jit(solution)/shard_map/ppermute | solution.py:67
  317.1 14.8 %collective-permute-start.67 = (bf16[256,1024]{1,0:T(8,128)(2,1)S(1)}, bf16[256,1024]{1,0:T(8,128)(2,1)S(1)}, u32[]{:S(2)}, u32[]{:S(2)}) collective-permute-start(bf16[256,1024]{1,0:T(8,128)(2,1)S(1)} %fusion.8.refs_0_), channel_id=1, source_target_pairs={{0,1},{1,2},{2,3},{3,0},{4,5},{5,6},{6,7},{7,4},{8,9},{9,10},{10,1... | collective-permute-start | bytes 1572872 | tf_op jit(solution)/shard_map/ppermute | solution.py:147
  331.9 13.8 %collective-permute-start.68 = (bf16[256,1024]{1,0:T(8,128)(2,1)S(1)}, bf16[256,1024]{1,0:T(8,128)(2,1)S(1)}, u32[]{:S(2)}, u32[]{:S(2)}) collective-permute-start(bf16[256,1024]{1,0:T(8,128)(2,1)S(1)} %collective-permute-done.67.refs_1_), channel_id=1, source_target_pairs={{0,1},{1,2},{2,3},{3,0},{4,5},{5,6},{6,7},{7,4},{8,9},{9,10},{10,1... | collective-permute-start | bytes 1572872 | tf_op jit(solution)/shard_map/ppermute | solution.py:147
  366.5 19.4 %collective-permute-start.72 = (bf16[256,1024]{1,0:T(8,128)(2,1)}, bf16[256,1024]{1,0:T(8,128)(2,1)S(1)}, u32[]{:S(2)}, u32[]{:S(2)}) collective-permute-start(bf16[256,1024]{1,0:T(8,128)(2,1)} %get-tuple-element.437), channel_id=1, source_target_pairs={{0,3},{1,0},{2,1},{3,2},{4,7},{5,4},{6,5},{7,6},{8,11},{9,8},{10,9... | collective-permute-start | bytes 1572872 | tf_op jit(solution)/shard_map/ppermute | solution.py:147
  366.9 19.0 %collective-permute-start.73 = (bf16[32,1024]{1,0:T(8,128)(2,1)S(1)}, bf16[32,1024]{1,0:T(8,128)(2,1)S(1)}, u32[]{:S(2)}, u32[]{:S(2)}) collective-permute-start(bf16[32,1024]{1,0:T(8,128)(2,1)S(1)} %copy-done.77), channel_id=1, source_target_pairs={{0,1},{1,2},{2,3},{3,0},{4,5},{5,6},{6,7},{7,4},{8,9},{9,10},{10,1... | collective-permute-start | bytes 196616 | tf_op jit(solution)/shard_map/ppermute | solution.py:147
  369.1 16.7 %collective-permute-start.74 = (bf16[32,1024]{1,0:T(8,128)(2,1)S(1)}, bf16[32,1024]{1,0:T(8,128)(2,1)S(1)}, u32[]{:S(2)}, u32[]{:S(2)}) collective-permute-start(bf16[32,1024]{1,0:T(8,128)(2,1)S(1)} %copy-done.76), channel_id=1, source_target_pairs={{0,2},{1,3},{2,0},{3,1},{4,6},{5,7},{6,4},{7,5},{8,10},{9,11},{10,... | collective-permute-start | bytes 196616 | tf_op jit(solution)/shard_map/ppermute | solution.py:147
  370.6 15.3 %collective-permute-start.75 = (bf16[32,1024]{1,0:T(8,128)(2,1)S(1)}, bf16[32,1024]{1,0:T(8,128)(2,1)S(1)}, u32[]{:S(2)}, u32[]{:S(2)}) collective-permute-start(bf16[32,1024]{1,0:T(8,128)(2,1)S(1)} %get-tuple-element.450), channel_id=1, source_target_pairs={{0,3},{1,0},{2,1},{3,2},{4,7},{5,4},{6,5},{7,6},{8,11},{9,8},{10,9... | collective-permute-start | bytes 196616 | tf_op jit(solution)/shard_map/ppermute | solution.py:147
  386.9 14.6 %collective-permute-start.77 = (bf16[384,1024]{1,0:T(8,128)(2,1)}, bf16[384,1024]{1,0:T(8,128)(2,1)S(1)}, u32[]{:S(2)}, u32[]{:S(2)}) collective-permute-start(bf16[384,1024]{1,0:T(8,128)(2,1)} %get-tuple-element.469), channel_id=1, source_target_pairs={{0,4},{4,0},{8,12},{12,8},{16,20},{20,16},{24,28},{28,24},{1,5},{5... | collective-permute-start | bytes 2359304 | tf_op jit(solution)/shard_map/ppermute | solution.py:67
  386.9 14.5 %collective-permute-start.76 = (bf16[256,1024]{1,0:T(8,128)(2,1)}, bf16[256,1024]{1,0:T(8,128)(2,1)S(1)}, u32[]{:S(2)}, u32[]{:S(2)}) collective-permute-start(bf16[256,1024]{1,0:T(8,128)(2,1)} %add_convert_fusion.8), channel_id=1, source_target_pairs={{0,3},{1,0},{2,1},{3,2},{4,7},{5,4},{6,5},{7,6},{8,11},{9,8},{10,9... | collective-permute-start | bytes 1572872 | tf_op jit(solution)/shard_map/ppermute | solution.py:147
  402.1 16.5 %collective-permute-start.81 = (bf16[96,1024]{1,0:T(8,128)(2,1)S(1)}, bf16[96,1024]{1,0:T(8,128)(2,1)S(1)}, u32[]{:S(2)}, u32[]{:S(2)}) collective-permute-start(bf16[96,1024]{1,0:T(8,128)(2,1)S(1)} %get-tuple-element.563), channel_id=1, source_target_pairs={{0,8},{4,12},{8,0},{12,4},{16,24},{20,28},{24,16},{28,20},{1,9},{5... | collective-permute-start | bytes 589832 | tf_op jit(solution)/shard_map/ppermute | solution.py:67
  402.9 15.7 %collective-permute-start.82 = (bf16[96,1024]{1,0:T(8,128)(2,1)S(1)}, bf16[96,1024]{1,0:T(8,128)(2,1)S(1)}, u32[]{:S(2)}, u32[]{:S(2)}) collective-permute-start(bf16[96,1024]{1,0:T(8,128)(2,1)S(1)} %get-tuple-element.565), channel_id=1, source_target_pairs={{0,16},{4,20},{8,24},{12,28},{16,0},{20,4},{24,8},{28,12},{1,17},{... | collective-permute-start | bytes 589832 | tf_op jit(solution)/shard_map/ppermute | solution.py:67
  404.4 14.2 %collective-permute-start.83 = (bf16[96,1024]{1,0:T(8,128)(2,1)S(1)}, bf16[96,1024]{1,0:T(8,128)(2,1)S(1)}, u32[]{:S(2)}, u32[]{:S(2)}) collective-permute-start(bf16[96,1024]{1,0:T(8,128)(2,1)S(1)} %get-tuple-element.564), channel_id=1, source_target_pairs={{0,24},{4,28},{8,16},{12,20},{16,8},{20,12},{24,0},{28,4},{1,25},{... | collective-permute-start | bytes 589832 | tf_op jit(solution)/shard_map/ppermute | solution.py:67
  405.6 13.1 %collective-permute-start.80 = (bf16[256,1024]{1,0:T(8,128)(2,1)S(1)}, bf16[256,1024]{1,0:T(8,128)(2,1)S(1)}, u32[]{:S(2)}, u32[]{:S(2)}) collective-permute-start(bf16[256,1024]{1,0:T(8,128)(2,1)S(1)} %add_convert_fusion.7), channel_id=1, source_target_pairs={{0,3},{1,0},{2,1},{3,2},{4,7},{5,4},{6,5},{7,6},{8,11},{9,8},{10,9... | collective-permute-start | bytes 1572872 | tf_op jit(solution)/shard_map/ppermute | solution.py:147
  419.6 14.7 %collective-permute-start.86 = (bf16[256,1024]{1,0:T(8,128)(2,1)S(1)}, bf16[256,1024]{1,0:T(8,128)(2,1)S(1)}, u32[]{:S(2)}, u32[]{:S(2)}) collective-permute-start(bf16[256,1024]{1,0:T(8,128)(2,1)S(1)} %fusion.6.refs_0_), channel_id=1, source_target_pairs={{0,1},{1,2},{2,3},{3,0},{4,5},{5,6},{6,7},{7,4},{8,9},{9,10},{10,1... | collective-permute-start | bytes 1572872 | tf_op jit(solution)/shard_map/ppermute | solution.py:147
  434.3 16.5 %collective-permute-start.91 = (bf16[256,1024]{1,0:T(8,128)(2,1)S(1)}, bf16[256,1024]{1,0:T(8,128)(2,1)S(1)}, u32[]{:S(2)}, u32[]{:S(2)}) collective-permute-start(bf16[256,1024]{1,0:T(8,128)(2,1)S(1)} %collective-permute-done.86.refs_1_), channel_id=1, source_target_pairs={{0,1},{1,2},{2,3},{3,0},{4,5},{5,6},{6,7},{7,4},{8,9},{9,10},{10,1... | collective-permute-start | bytes 1572872 | tf_op jit(solution)/shard_map/ppermute | solution.py:147
  450.9 16.0 %collective-permute-start.93 = (bf16[256,1024]{1,0:T(8,128)(2,1)S(1)}, bf16[256,1024]{1,0:T(8,128)(2,1)S(1)}, u32[]{:S(2)}, u32[]{:S(2)}) collective-permute-start(bf16[256,1024]{1,0:T(8,128)(2,1)S(1)} %collective-permute-done.91.refs_2_), channel_id=1, source_target_pairs={{0,1},{1,2},{2,3},{3,0},{4,5},{5,6},{6,7},{7,4},{8,9},{9,10},{10,1... | collective-permute-start | bytes 1572872 | tf_op jit(solution)/shard_map/ppermute | solution.py:147
  (137 other events, 1283.3 us)
Sparse Core Ops, SparseCore 0:
  59.9 95.4 all-gather.2
  266.2 47.8 reduce-scatter.1
  359.8 37.1 all-gather.4

commit v6 on v5

--- a/solution.py
+++ b/solution.py
@@ -996,9 +996,9 @@
     return (weight - GAIN_RATE * direction, new_first, new_second)
 
 
-def back_kernel(meta, x_ref, dq, dk_a, dk_b, dv_a, dv_b, wq, wk, wv, out, gain_out):
-    total = mm(dq[...], wq[...], NN) + mm(both((dk_a, dk_b)), wk[...], NN)
-    total = total + mm(both((dv_a, dv_b)), wv[...], NN)
+def back_kernel(meta, x_ref, dq, dk_a, dk_b, dv_a, dv_b, w_ref, out, gain_out):
+    total = mm(dq[...], w_ref[0], NN) + mm(both((dk_a, dk_b)), w_ref[1], NN)
+    total = total + mm(both((dv_a, dv_b)), w_ref[2], NN)
     out[...] = total.astype(BF)
     unit, _, _ = norm_rows(x_ref[...].astype(F32), 1.0)
     share = jnp.sum(total * unit, axis=0, keepdims=True)
@@ -1012,24 +1012,24 @@
         gain_out[...] += share
 
 
-def back_in(meta, x, dq, dk, dv, wq, wk, wv, n, low, high):
-    tok, (qw, d) = dq.shape[0], wq.shape
+def back_in(meta, x, dq, dk, dv, weights, n, low, high):
+    tok, (_, qw, d) = dq.shape[0], weights.shape
     tile = tok // n
     rows = lambda w: pl.BlockSpec((tile, w), lambda i, meta: ((meta[1] - i - low + n) % n, 0))
-    whole = pl.BlockSpec((qw, d), lambda i, meta: (0, 0))
+    whole = pl.BlockSpec((3, qw, d), lambda i, meta: (0, 0, 0))
     return pl.pallas_call(
         back_kernel,
         grid_spec=pltpu.PrefetchScalarGridSpec(
             num_scalar_prefetch=1,
             grid=(high - low,),
-            in_specs=[rows(d)] + [rows(qw)] * 5 + [whole] * 3,
+            in_specs=[rows(d)] + [rows(qw)] * 5 + [whole],
             out_specs=[pl.BlockSpec((tile, d), lambda i, meta: (i, 0)), pl.BlockSpec((1, d), lambda i, meta: (0, 0))],
         ),
         out_shape=[jax.ShapeDtypeStruct(((high - low) * tile, d), BF), jax.ShapeDtypeStruct((1, d), F32)],
         compiler_params=params(),
         cost_estimate=QUICK,
         name="back_in",
-    )(meta, x, dq, *dk, *dv, wq, wk, wv)
+    )(meta, x, dq, *dk, *dv, weights)
 
 
 def shards(
@@ -1137,7 +1137,7 @@
     output = place(meta, outputs, block)
     early = whole_seq(feed_sums).reshape(-1, panel, d)
 
-    inputs = (meta, tokens, dq, dk, dv, inner[0], inner[1], inner[2], n_tp)
+    inputs = (meta, tokens, dq, dk, dv, inner, n_tp)
     total, gain_a = back_in(*inputs, n_tp - 1, n_tp)
     total, lefts = pin(total, (dq, dk, dv))
     back_rest, gain_b = back_in(meta, tokens, *lefts, *inputs[5:], 0, n_tp - 1)

time: 484 us -> 482 us (level)
  transfers between devices with their start and end apart: 97 -> 97, of which waited for: 47 -> 49; matrix products, arithmetic and copies ran while one was open for 5% -> 5% of each run, Pallas kernels for 16% -> 16%
where the time goes in v6:
time: 482 us; the launch traced here: 477 us
  waiting for transfers between devices  224 us (46%)
  Pallas kernels  121 us (25%)
  starting transfers between devices  81.6 us (17%)
  other arithmetic  20.5 us (4%)
  local copies, waits for them, and re-layouts  15.4 us (3%)
  between operations  15.2 us (3%)
    ppermute x71, waiting for transfers between devices, swap(): return lax.ppermute(value, 'seq', [(i, i ^ bit) for i in range(count)])  145 us
    ppermute x18, waiting for transfers between devices, ring(): lax.ppermute(value, 'tp', [(i, (i + step) % count) for i in range(count)])  54.2 us
    ppermute x71, starting transfers between devices, swap(): return lax.ppermute(value, 'seq', [(i, i ^ bit) for i in range(count)])  51.5 us
    ppermute x18, starting transfers between devices, ring(): lax.ppermute(value, 'tp', [(i, (i + step) % count) for i in range(count)])  25.8 us
    pallas_call x1, Pallas kernels, feed_forward(): pl.pallas_call(functools.partial(feed_kernel, (n, spans, fs)), grid_spec=...  20.2 us
    ppermute x5, waiting for transfers between devices, sum_steps(): lax.ppermute(v, axis, pairs)  19.2 us
    pallas_call x1, Pallas kernels, attend_back(): pl.pallas_call(functools.partial(attend_back_kernel, (n, docs, picks, qt,...  15.7 us
    convert_element_type x13, other arithmetic, plus(): return (left.astype(F32) + right.astype(F32)).astype(left.dtype)  12.9 us
  transfers between devices with their start and end apart: 97, of which 49 were waited for; matrix products, arithmetic and copies ran while one was open for 5% of the time, Pallas kernels for 16%

profile of v6, /device:TPU:0, one launch (start us, length us, event | category | flops | bytes accessed | tf_op | source)
XLA Modules:
  0.0 477.4 jit_solution(8515258612742929662)
XLA Ops:
  9.6 2.9 collective-permute-start.1
  14.6 17.1 %collective-permute-done.4.refs_10_ = bf16[6,32,1024]{2,1,0:T(8,128)(2,1)S(1)} collective-permute-done((bf16[6,32,1024]{2,1,0:T(8,128)(2,1)S(1)}, bf16[6,32,1024]{2,1,0:T(8,128)(2,1)S(1)}, u32[]{:S(2)}, u32[]{:S(2)}) %collective-permute-start.4) | collective-permute-done | bytes 393248 | tf_op jit(solution)/shard_map/ppermute | solution.py:67
  36.1 10.9 %collective-permute-done.11.refs_14_ = bf16[6,32,1024]{2,1,0:T(8,128)(2,1)} collective-permute-done((bf16[6,32,1024]{2,1,0:T(8,128)(2,1)S(1)}, bf16[6,32,1024]{2,1,0:T(8,128)(2,1)}, u32[]{:S(2)}, u32[]{:S(2)}) %collective-permute-start.11) | collective-permute-done | bytes 393248 | tf_op jit(solution)/shard_map/ppermute | solution.py:67
  50.6 9.1 %project.1 = (bf16[1024,256]{1,0:T(8,128)(2,1)}, bf16[1024,256]{1,0:T(8,128)(2,1)}, bf16[1024,256]{1,0:T(8,128)(2,1)}, bf16[1024,1024]{1,0:T(8,128)(2,1)}, bf16[...) custom-call(s32[18]{0:T(128)} %pad_add_fusion.meta, s32[98]{0:T(128)} %owners.1, bf16[1024,1024]{1,0:T(8,128)(2,1)} %x_ref.7, ...), custom_call_target="tpu_custom_call" | custom-call | flops 1000 | bytes 1000 | tf_op jit(solution)/shard_map/project/pallas_call | solution.py:262
  64.3 10.9 %collective-permute-done.15.refs_2_.refs_6_ = bf16[1024,256]{1,0:T(8,128)(2,1)S(1)} collective-permute-done((bf16[1024,256]{1,0:T(8,128)(2,1)}, bf16[1024,256]{1,0:T(8,128)(2,1)S(1)}, u32[]{:S(2)}, u32[]{:S(2)}) %collective-permute-start.15) | collective-permute-done | bytes 524320 | tf_op jit(solution)/shard_map/ppermute | solution.py:67
  75.7 10.1 %collective-permute-done.18.refs_10_.refs_14_ = bf16[1024,256]{1,0:T(8,128)(2,1)S(1)} collective-permute-done((bf16[1024,256]{1,0:T(8,128)(2,1)}, bf16[1024,256]{1,0:T(8,128)(2,1)S(1)}, u32[]{:S(2)}, u32[]{:S(2)}) %collective-permute-start.18) | collective-permute-done | bytes 524320 | tf_op jit(solution)/shard_map/ppermute | solution.py:67
  90.4 10.2 %collective-permute-done.22.refs_6_.refs_10_ = bf16[1024,256]{1,0:T(8,128)(2,1)} collective-permute-done((bf16[1024,256]{1,0:T(8,128)(2,1)S(1)}, bf16[1024,256]{1,0:T(8,128)(2,1)}, u32[]{:S(2)}, u32[]{:S(2)}) %collective-permute-start.22) | collective-permute-done | bytes 524320 | tf_op jit(solution)/shard_map/ppermute | solution.py:67
  100.7 2.5 collective-permute-done.25.refs_14_.refs_18_
  109.4 11.9 %attend.1 = (bf16[256,256]{1,0:T(8,128)(2,1)}, bf16[256,256]{1,0:T(8,128)(2,1)}, bf16[256,256]{1,0:T(8,128)(2,1)}, bf16[256,256]{1,0:T(8,128)(2,1)}, f32[1024,256]{1,0:T(8,128)}, /*index=5*/f32[2,1024]{1,0:T(2,128)}) custom-call(s32[18]{0:T(128)} %pad_add_fusion.meta, bf16[1024,256]{1,0:T(8,128)(2,1)} %get-tuple-element.283.q_ref, ...), custom_call_target="tpu_custom_call" | custom-call | flops 1000 | bytes 1000 | tf_op jit(solution)/shard_map/attend/pallas_call | solution.py:429
  121.3 9.9 %collective-permute-done.29 = bf16[256,1024]{1,0:T(8,128)(2,1)S(1)} collective-permute-done((bf16[256,1024]{1,0:T(8,128)(2,1)S(1)}, bf16[256,1024]{1,0:T(8,128)(2,1)S(1)}, u32[]{:S(2)}, u32[]{:S(2)}) %collective-permute-start.29) | collective-permute-done | bytes 524320 | tf_op jit(solution)/shard_map/ppermute | solution.py:67
  133.8 2.6 collective-permute-start.32
  138.1 5.3 %collective-permute-done.31.refs_1_ = bf16[256,256]{1,0:T(8,128)(2,1)S(1)} collective-permute-done((bf16[256,256]{1,0:T(8,128)(2,1)}, bf16[256,256]{1,0:T(8,128)(2,1)S(1)}, u32[]{:S(2)}, u32[]{:S(2)}) %collective-permute-start.31) | collective-permute-done | bytes 131104 | tf_op jit(solution)/shard_map/ppermute | solution.py:147
  143.4 8.1 %collective-permute-done.32.refs_2_ = bf16[256,256]{1,0:T(8,128)(2,1)S(1)} collective-permute-done((bf16[256,256]{1,0:T(8,128)(2,1)}, bf16[256,256]{1,0:T(8,128)(2,1)S(1)}, u32[]{:S(2)}, u32[]{:S(2)}) %collective-permute-start.32) | collective-permute-done | bytes 131104 | tf_op jit(solution)/shard_map/ppermute | solution.py:147
  151.4 3.9 all-gather.3.cloned.1.call-done
  155.4 5.3 %mix.1 = (f32[256,1024]{1,0:T(8,128)}, bf16[256,512]{1,0:T(8,128)(2,1)}, bf16[256,512]{1,0:T(8,128)(2,1)}) custom-call(s32[18]{0:T(128)} %pad_add_fusion.meta, bf16[1024,1024]{1,0:T(8,128)(2,1)} %x_ref.7, f32[2,1024]{1,0:T(2,128)} %gain_ref.5, bf16[4,544,1024]{2,1,0:T(8,128)(2,1)} %bitcast.25, bf16[256,256]{1,0:T(8,128)(2,1)} %get-tuple-element.315.refs_0_, ...), custom_call_target="tpu_custom_call" | custom-call | flops 1000 | bytes 1000 | tf_op jit(solution)/shard_map/mix/pallas_call | solution.py:590
  167.2 3.5 collective-permute-done.36.refs_2_
  172.1 3.8 collective-permute-done.39.refs_10_
  176.0 2.4 collective-permute-done.40.refs_12_
  183.2 3.8 collective-permute-done.43.refs_6_
  192.9 20.2 %feed_forward.1 = (bf16[2048,1024]{1,0:T(8,128)(2,1)}, bf16[2048,384]{1,0:T(8,128)(2,1)}, bf16[2048,768]{1,0:T(8,128)(2,1)}, bf16[1024,512]{1,0:T(8,128)(2,1)}, ...) custom-call(s32[18]{0:T(128)} %pad_add_fusion.meta, ...), custom_call_target="tpu_custom_call" | custom-call | flops 1000 | bytes 1000 | tf_op jit(solution)/shard_map/feed_forward/pallas_call | solution.py:673
  220.3 11.2 %feed_grads.1 = bf16[4,288,1024]{2,1,0:T(8,128)(2,1)} custom-call(bf16[2048,384]{1,0:T(8,128)(2,1)} %get-tuple-element.367.hidden, bf16[2048,768]{1,0:T(8,128)(2,1)} %get-tuple-element.368.d_inner, bf16[2048,1024]{1,0:T(8,128)(2,1)} %get-tuple-element.369.normed, bf16[2048,1024]{1,0:T(8,128)(2,1)} %copy-done.3), custom_call_target="tpu_custom_call" | custom-call | flops 1000 | bytes 1000 | tf_op jit(solution)/shard_map/feed_grads/pallas_call | solution.py:787
  236.2 5.7 %collective-permute-done.54.left_b = bf16[256,512]{1,0:T(8,128)(2,1)S(1)} collective-permute-done((bf16[256,512]{1,0:T(8,128)(2,1)S(1)}, bf16[256,512]{1,0:T(8,128)(2,1)S(1)}, u32[]{:S(2)}, u32[]{:S(2)}) %collective-permute-start.54) | collective-permute-done | bytes 262176 | tf_op jit(solution)/shard_map/ppermute | solution.py:67
  243.7 7.7 %branch_back.1 = (f32[256,1024]{1,0:T(8,128)}, f32[1,1024]{1,0:T(1,128)}, bf16[256,256]{1,0:T(8,128)(2,1)}, bf16[256,256]{1,0:T(8,128)(2,1)}, bf16[256,256]{1,0:...) custom-call(s32[18]{0:T(128)} %pad_add_fusion.meta, ...), custom_call_target="tpu_custom_call" | custom-call | flops 1000 | bytes 1000 | tf_op jit(solution)/shard_map/branch_back/pallas_call | solution.py:730
  258.1 3.6 collective-permute-done.56.refs_1_
  261.7 5.2 %collective-permute-done.57.refs_2_ = bf16[256,256]{1,0:T(8,128)(2,1)S(1)} collective-permute-done((bf16[256,256]{1,0:T(8,128)(2,1)S(1)}, bf16[256,256]{1,0:T(8,128)(2,1)S(1)}, u32[]{:S(2)}, u32[]{:S(2)}) %collective-permute-start.57) | collective-permute-done | bytes 131104 | tf_op jit(solution)/shard_map/ppermute | solution.py:147
  270.7 15.7 %attend_back.1 = (bf16[1024,256]{1,0:T(8,128)(2,1)}, bf16[4096,256]{1,0:T(8,128)(2,1)}, bf16[4096,256]{1,0:T(8,128)(2,1)}, bf16[4096,256]{1,0:T(8,128)(2,1)}, bf16[4096,256]{1,0:T(8,128)(2,1)}) custom-call(s32[18]{0:T(128)} %pad_add_fusion.meta, bf16[1024,256]{1,0:T(8,128)(2,1)} %get-tuple-element.283.q_ref, f32[1024,256]{1,0:T(8,128)} %get-tuple-element.389.wide_ref, ...), custom_call_target="tpu_custom_call" | custom-call | flops 1000 | bytes 1000 | tf_op jit(solution)/shard_map/attend_back/pallas_call | solution.py:545
  287.7 15.5 %collective-permute-done.61 = bf16[384,1024]{1,0:T(8,128)(2,1)S(1)} collective-permute-done((bf16[384,1024]{1,0:T(8,128)(2,1)S(1)}, bf16[384,1024]{1,0:T(8,128)(2,1)S(1)}, u32[]{:S(2)}, u32[]{:S(2)}) %collective-permute-start.61) | collective-permute-done | bytes 786464 | tf_op jit(solution)/shard_map/ppermute | solution.py:67
  304.6 2.9 collective-permute-done.64
  319.1 12.7 %collective-permute-done.67.refs_1_ = bf16[256,1024]{1,0:T(8,128)(2,1)S(1)} collective-permute-done((bf16[256,1024]{1,0:T(8,128)(2,1)S(1)}, bf16[256,1024]{1,0:T(8,128)(2,1)S(1)}, u32[]{:S(2)}, u32[]{:S(2)}) %collective-permute-start.67) | collective-permute-done | bytes 524320 | tf_op jit(solution)/shard_map/ppermute | solution.py:147
  331.8 7.3 %collective-permute-done.66 = bf16[2048,256]{1,0:T(8,128)(2,1)} collective-permute-done((bf16[2048,256]{1,0:T(8,128)(2,1)}, bf16[2048,256]{1,0:T(8,128)(2,1)}, u32[]{:S(2)}, u32[]{:S(2)}) %collective-permute-start.66) | collective-permute-done | bytes 1048608 | tf_op jit(solution)/shard_map/ppermute | solution.py:67
  342.5 3.1 collective-permute-done.68.refs_2_
  346.9 9.8 %collective-permute-done.69.dk_b = bf16[1024,256]{1,0:T(8,128)(2,1)S(1)} collective-permute-done((bf16[1024,256]{1,0:T(8,128)(2,1)S(1)}, bf16[1024,256]{1,0:T(8,128)(2,1)S(1)}, u32[]{:S(2)}, u32[]{:S(2)}) %collective-permute-start.69) | collective-permute-done | bytes 524320 | tf_op jit(solution)/shard_map/ppermute | solution.py:67
  357.1 2.5 collective-permute-done.71.refs_3_
  359.7 4.0 back_in.2
  368.2 6.0 %back_in.3 = (bf16[768,1024]{1,0:T(8,128)(2,1)}, f32[1,1024]{1,0:T(1,128)}) custom-call(s32[18]{0:T(128)} %pad_add_fusion.meta, bf16[1024,1024]{1,0:T(8,128)(2,1)} %x_ref.7, bf16[1024,256]{1,0:T(8,128)(2,1)} %get-tuple-element.438.dq, bf16[1024,256]{1,0:T(8,128)(2,1)} %get-tuple-element.439.dk_a, bf16[1024,256]{1,0:T(8,128)(2,1)} %copy-done.4, ...), custom_call_target="tpu_custom_call" | custom-call | flops 1000 | bytes 1000 | tf_op jit(solution)/shard_map/back_in/pallas_call | solution.py:1020
  374.3 5.5 %late_grads.1 = (bf16[384,1024]{1,0:T(8,128)(2,1)}, bf16[384,1024]{1,0:T(8,128)(2,1)}) custom-call(s32[18]{0:T(128)} %pad_add_fusion.meta, bf16[1024,256]{1,0:T(8,128)(2,1)} %get-tuple-element.438.dq, bf16[1024,256]{1,0:T(8,128)(2,1)} %get-tuple-element.439.dk_a, bf16[1024,256]{1,0:T(8,128)(2,1)} %copy-done.4, bf16[1024,256]{1,0:T(8,128)(2,1)} %get-tuple-element.441.dv_a, ...), custom_call_target="tpu_custom_call" | custom-call | flops 1000 | bytes 1000 | tf_op jit(solution)/shard_map/late_grads/pallas_call | solution.py:829
  381.2 3.1 collective-permute-start.76
  384.7 3.1 place.2
  388.4 3.2 collective-permute-done.79
  391.6 4.8 %collective-permute-done.76 = bf16[256,1024]{1,0:T(8,128)(2,1)S(1)} collective-permute-done((bf16[256,1024]{1,0:T(8,128)(2,1)}, bf16[256,1024]{1,0:T(8,128)(2,1)S(1)}, u32[]{:S(2)}, u32[]{:S(2)}) %collective-permute-start.76) | collective-permute-done | bytes 524320 | tf_op jit(solution)/shard_map/ppermute | solution.py:147
  401.3 4.2 collective-permute-start.80
  405.6 10.0 %collective-permute-done.85 = f32[2,1024]{1,0:T(2,128)S(1)} collective-permute-done((f32[2,1024]{1,0:T(2,128)S(1)}, f32[2,1024]{1,0:T(2,128)S(1)}, u32[]{:S(2)}, u32[]{:S(2)}) %collective-permute-start.85) | collective-permute-done | bytes 8224 | tf_op jit(solution)/shard_map/ppermute | solution.py:177
  416.7 2.5 collective-permute-start.86
  424.8 6.0 %collective-permute-done.90 = f32[2,1024]{1,0:T(2,128)S(1)} collective-permute-done((f32[2,1024]{1,0:T(2,128)S(1)}, f32[2,1024]{1,0:T(2,128)S(1)}, u32[]{:S(2)}, u32[]{:S(2)}) %collective-permute-start.90) | collective-permute-done | bytes 8224 | tf_op jit(solution)/shard_map/ppermute | solution.py:177
  435.4 12.4 %soap.1 = (f32[13,32,1024]{2,1,0:T(8,128)}, f32[13,32,1024]{2,1,0:T(8,128)}, f32[13,32,1024]{2,1,0:T(8,128)}, f32[13,32,1024]{2,1,0:T(8,128)}, f32[13,32,32]{2,1,0:T(8,128)}, /*index=5*/f32[13,32,32]{2,1,0:T(8,128)}) custom-call(s32[18]{0:T(128)} %pad_add_fusion.meta, s32[13]{0:T(128)} %broadcast_add_fusion.held, bf16[72,32,1024]{2,1,0:T(8,128)(2,1)} %bitcast.32, ...), custom_call_target="tpu_custom_call" | custom-call | flops 1000 | bytes 1000 | tf_op jit(solution)/shard_map/soap/pallas_call | solution.py:943
  450.6 4.6 orthonormal.1
  455.2 8.6 %collective-permute-done.93.refs_3_ = bf16[256,1024]{1,0:T(8,128)(2,1)S(1)} collective-permute-done((bf16[256,1024]{1,0:T(8,128)(2,1)S(1)}, bf16[256,1024]{1,0:T(8,128)(2,1)S(1)}, u32[]{:S(2)}, u32[]{:S(2)}) %collective-permute-start.93) | collective-permute-done | bytes 524320 | tf_op jit(solution)/shard_map/ppermute | solution.py:147
  466.8 3.8 place.3
  (397 shorter events, 122.9 us)
Async XLA Ops:
  7.2 148.1 %all-gather.3.cloned.1.call-start = ((), (), s32[]{:S(2)}) async-start(), calls=%async_computation.1 | async-start | bytes 5570560 | tf_op jit(solution)/shard_map/all_gather | solution.py:1072
  9.4 23.7 %collective-permute-start = (bf16[7,32,1024]{2,1,0:T(8,128)(2,1)S(1)}, bf16[7,32,1024]{2,1,0:T(8,128)(2,1)S(1)}, u32[]{:S(2)}, u32[]{:S(2)}) collective-permute-start(bf16[7,32,1024]{2,1,0:T(8,128)(2,1)S(1)} %slice.224.refs_0_), channel_id=1, source_target_pairs={{0,4},{4,0},{8,12},{12,8},{16,20},{20,16},{24,28},{28,24},{1,5},{5... | collective-permute-start | bytes 1376264 | tf_op jit(solution)/shard_map/ppermute | solution.py:67
  9.6 23.6 %collective-permute-start.1 = (bf16[7,32,1024]{2,1,0:T(8,128)(2,1)S(1)}, bf16[7,32,1024]{2,1,0:T(8,128)(2,1)S(1)}, u32[]{:S(2)}, u32[]{:S(2)}) collective-permute-start(bf16[7,32,1024]{2,1,0:T(8,128)(2,1)S(1)} %slice.224.refs_0_), channel_id=1, source_target_pairs={{0,8},{4,12},{8,0},{12,4},{16,24},{20,28},{24,16},{28,20},{1,9},{5... | collective-permute-start | bytes 1376264 | tf_op jit(solution)/shard_map/ppermute | solution.py:67
  12.5 20.7 %collective-permute-start.2 = (bf16[7,32,1024]{2,1,0:T(8,128)(2,1)S(1)}, bf16[7,32,1024]{2,1,0:T(8,128)(2,1)S(1)}, u32[]{:S(2)}, u32[]{:S(2)}) collective-permute-start(bf16[7,32,1024]{2,1,0:T(8,128)(2,1)S(1)} %slice.224.refs_0_), channel_id=1, source_target_pairs={{0,16},{4,20},{8,24},{12,28},{16,0},{20,4},{24,8},{28,12},{1,17},{... | collective-permute-start | bytes 1376264 | tf_op jit(solution)/shard_map/ppermute | solution.py:67
  14.0 17.6 %collective-permute-start.4 = (bf16[6,32,1024]{2,1,0:T(8,128)(2,1)S(1)}, bf16[6,32,1024]{2,1,0:T(8,128)(2,1)S(1)}, u32[]{:S(2)}, u32[]{:S(2)}) collective-permute-start(bf16[6,32,1024]{2,1,0:T(8,128)(2,1)S(1)} %slice.225.refs_8_), channel_id=1, source_target_pairs={{0,8},{4,12},{8,0},{12,4},{16,24},{20,28},{24,16},{28,20},{1,9},{5... | collective-permute-start | bytes 1179656 | tf_op jit(solution)/shard_map/ppermute | solution.py:67
  14.6 18.6 %collective-permute-start.5 = (bf16[6,32,1024]{2,1,0:T(8,128)(2,1)S(1)}, bf16[6,32,1024]{2,1,0:T(8,128)(2,1)S(1)}, u32[]{:S(2)}, u32[]{:S(2)}) collective-permute-start(bf16[6,32,1024]{2,1,0:T(8,128)(2,1)S(1)} %slice.225.refs_8_), channel_id=1, source_target_pairs={{0,16},{4,20},{8,24},{12,28},{16,0},{20,4},{24,8},{28,12},{1,17},{... | collective-permute-start | bytes 1179656 | tf_op jit(solution)/shard_map/ppermute | solution.py:67
  33.3 13.7 %collective-permute-start.6 = (bf16[7,32,1024]{2,1,0:T(8,128)(2,1)S(1)}, bf16[7,32,1024]{2,1,0:T(8,128)(2,1)S(1)}, u32[]{:S(2)}, u32[]{:S(2)}) collective-permute-start(bf16[7,32,1024]{2,1,0:T(8,128)(2,1)S(1)} %collective-permute-done.1.refs_2_), channel_id=1, source_target_pairs={{0,4},{4,0},{8,12},{12,8},{16,20},{20,16},{24,28},{28,24},{1,5},{5... | collective-permute-start | bytes 1376264 | tf_op jit(solution)/shard_map/ppermute | solution.py:67
  33.8 13.2 %collective-permute-start.8 = (bf16[7,32,1024]{2,1,0:T(8,128)(2,1)S(1)}, bf16[7,32,1024]{2,1,0:T(8,128)(2,1)S(1)}, u32[]{:S(2)}, u32[]{:S(2)}) collective-permute-start(bf16[7,32,1024]{2,1,0:T(8,128)(2,1)S(1)} %collective-permute-done.1.refs_2_), channel_id=1, source_target_pairs={{0,16},{4,20},{8,24},{12,28},{16,0},{20,4},{24,8},{28,12},{1,17},{... | collective-permute-start | bytes 1376264 | tf_op jit(solution)/shard_map/ppermute | solution.py:67
  59.8 254.3 %reduce-scatter.2.cloned.1.call-start = ((), (), s32[]{:S(2)}) async-start(), calls=%async_computation.2 | async-start | bytes 2949120 | tf_op jit(solution)/shard_map/reduce_scatter | solution.py:1120
  60.2 15.0 %collective-permute-start.15 = (bf16[1024,256]{1,0:T(8,128)(2,1)}, bf16[1024,256]{1,0:T(8,128)(2,1)S(1)}, u32[]{:S(2)}, u32[]{:S(2)}) collective-permute-start(bf16[1024,256]{1,0:T(8,128)(2,1)} %get-tuple-element.294.refs_0_.refs_4_), channel_id=1, source_target_pairs={{0,8},{4,12},{8,0},{12,4},{16,24},{20,28},{24,16},{28,20},{1,9},{5... | collective-permute-start | bytes 1572872 | tf_op jit(solution)/shard_map/ppermute | solution.py:67
  60.7 15.0 %collective-permute-start.16 = (bf16[1024,256]{1,0:T(8,128)(2,1)}, bf16[1024,256]{1,0:T(8,128)(2,1)S(1)}, u32[]{:S(2)}, u32[]{:S(2)}) collective-permute-start(bf16[1024,256]{1,0:T(8,128)(2,1)} %get-tuple-element.294.refs_0_.refs_4_), channel_id=1, source_target_pairs={{0,16},{4,20},{8,24},{12,28},{16,0},{20,4},{24,8},{28,12},{1,17},{... | collective-permute-start | bytes 1572872 | tf_op jit(solution)/shard_map/ppermute | solution.py:67
  61.5 14.3 %collective-permute-start.17 = (bf16[1024,256]{1,0:T(8,128)(2,1)}, bf16[1024,256]{1,0:T(8,128)(2,1)S(1)}, u32[]{:S(2)}, u32[]{:S(2)}) collective-permute-start(bf16[1024,256]{1,0:T(8,128)(2,1)} %get-tuple-element.303.refs_8_.refs_12_), channel_id=1, source_target_pairs={{0,4},{4,0},{8,12},{12,8},{16,20},{20,16},{24,28},{28,24},{1,5},{5... | collective-permute-start | bytes 1572872 | tf_op jit(solution)/shard_map/ppermute | solution.py:67
  61.5 24.4 %collective-permute-start.18 = (bf16[1024,256]{1,0:T(8,128)(2,1)}, bf16[1024,256]{1,0:T(8,128)(2,1)S(1)}, u32[]{:S(2)}, u32[]{:S(2)}) collective-permute-start(bf16[1024,256]{1,0:T(8,128)(2,1)} %get-tuple-element.303.refs_8_.refs_12_), channel_id=1, source_target_pairs={{0,8},{4,12},{8,0},{12,4},{16,24},{20,28},{24,16},{28,20},{1,9},{5... | collective-permute-start | bytes 1572872 | tf_op jit(solution)/shard_map/ppermute | solution.py:67
  63.0 23.2 %collective-permute-start.19 = (bf16[1024,256]{1,0:T(8,128)(2,1)}, bf16[1024,256]{1,0:T(8,128)(2,1)}, u32[]{:S(2)}, u32[]{:S(2)}) collective-permute-start(bf16[1024,256]{1,0:T(8,128)(2,1)} %get-tuple-element.303.refs_8_.refs_12_), channel_id=1, source_target_pairs={{0,16},{4,20},{8,24},{12,28},{16,0},{20,4},{24,8},{28,12},{1,17},{... | collective-permute-start | bytes 1572872 | tf_op jit(solution)/shard_map/ppermute | solution.py:67
  86.2 14.4 %collective-permute-start.22 = (bf16[1024,256]{1,0:T(8,128)(2,1)S(1)}, bf16[1024,256]{1,0:T(8,128)(2,1)}, u32[]{:S(2)}, u32[]{:S(2)}) collective-permute-start(bf16[1024,256]{1,0:T(8,128)(2,1)S(1)} %collective-permute-done.15.refs_2_.refs_6_), channel_id=1, source_target_pairs={{0,16},{4,20},{8,24},{12,28},{16,0},{20,4},{24,8},{28,12},{1,17},{... | collective-permute-start | bytes 1572872 | tf_op jit(solution)/shard_map/ppermute | solution.py:67
  87.2 13.4 %collective-permute-start.23 = (bf16[1024,256]{1,0:T(8,128)(2,1)S(1)}, bf16[1024,256]{1,0:T(8,128)(2,1)}, u32[]{:S(2)}, u32[]{:S(2)}) collective-permute-start(bf16[1024,256]{1,0:T(8,128)(2,1)S(1)} %collective-permute-done.18.refs_10_.refs_14_), channel_id=1, source_target_pairs={{0,4},{4,0},{8,12},{12,8},{16,20},{20,16},{24,28},{28,24},{1,5},{5... | collective-permute-start | bytes 1572872 | tf_op jit(solution)/shard_map/ppermute | solution.py:67
  87.5 13.1 %collective-permute-start.24 = (bf16[1024,256]{1,0:T(8,128)(2,1)}, bf16[1024,256]{1,0:T(8,128)(2,1)}, u32[]{:S(2)}, u32[]{:S(2)}) collective-permute-start(bf16[1024,256]{1,0:T(8,128)(2,1)} %collective-permute-done.19.refs_12_.refs_16_), channel_id=1, source_target_pairs={{0,4},{4,0},{8,12},{12,8},{16,20},{20,16},{24,28},{28,24},{1,5},{5... | collective-permute-start | bytes 1572872 | tf_op jit(solution)/shard_map/ppermute | solution.py:67
  88.9 14.3 %collective-permute-start.25 = (bf16[1024,256]{1,0:T(8,128)(2,1)}, bf16[1024,256]{1,0:T(8,128)(2,1)}, u32[]{:S(2)}, u32[]{:S(2)}) collective-permute-start(bf16[1024,256]{1,0:T(8,128)(2,1)} %collective-permute-done.19.refs_12_.refs_16_), channel_id=1, source_target_pairs={{0,8},{4,12},{8,0},{12,4},{16,24},{20,28},{24,16},{28,20},{1,9},{5... | collective-permute-start | bytes 1572872 | tf_op jit(solution)/shard_map/ppermute | solution.py:67
  104.8 16.5 %collective-permute-start.28 = (bf16[256,1024]{1,0:T(8,128)(2,1)S(1)}, bf16[256,1024]{1,0:T(8,128)(2,1)S(1)}, u32[]{:S(2)}, u32[]{:S(2)}) collective-permute-start(bf16[256,1024]{1,0:T(8,128)(2,1)S(1)} %constant_dynamic-slice_fusion), channel_id=1, source_target_pairs={{0,8},{4,12},{8,0},{12,4},{16,24},{20,28},{24,16},{28,20},{1,9},{5... | collective-permute-start | bytes 1572872 | tf_op jit(solution)/shard_map/ppermute | solution.py:67
  106.4 24.8 %collective-permute-start.29 = (bf16[256,1024]{1,0:T(8,128)(2,1)S(1)}, bf16[256,1024]{1,0:T(8,128)(2,1)S(1)}, u32[]{:S(2)}, u32[]{:S(2)}) collective-permute-start(bf16[256,1024]{1,0:T(8,128)(2,1)S(1)} %constant_dynamic-slice_fusion), channel_id=1, source_target_pairs={{0,16},{4,20},{8,24},{12,28},{16,0},{20,4},{24,8},{28,12},{1,17},{... | collective-permute-start | bytes 1572872 | tf_op jit(solution)/shard_map/ppermute | solution.py:67
  107.4 23.8 %collective-permute-start.30 = (bf16[256,1024]{1,0:T(8,128)(2,1)S(1)}, bf16[256,1024]{1,0:T(8,128)(2,1)S(1)}, u32[]{:S(2)}, u32[]{:S(2)}) collective-permute-start(bf16[256,1024]{1,0:T(8,128)(2,1)S(1)} %constant_dynamic-slice_fusion), channel_id=1, source_target_pairs={{0,24},{4,28},{8,16},{12,20},{16,8},{20,12},{24,0},{28,4},{1,25},{... | collective-permute-start | bytes 1572872 | tf_op jit(solution)/shard_map/ppermute | solution.py:67
  133.8 17.6 %collective-permute-start.32 = (bf16[256,256]{1,0:T(8,128)(2,1)}, bf16[256,256]{1,0:T(8,128)(2,1)S(1)}, u32[]{:S(2)}, u32[]{:S(2)}) collective-permute-start(bf16[256,256]{1,0:T(8,128)(2,1)} %get-tuple-element.317), channel_id=1, source_target_pairs={{0,2},{1,3},{2,0},{3,1},{4,6},{5,7},{6,4},{7,5},{8,10},{9,11},{10,... | collective-permute-start | bytes 393224 | tf_op jit(solution)/shard_map/ppermute | solution.py:147
  136.4 15.0 %collective-permute-start.33 = (bf16[256,256]{1,0:T(8,128)(2,1)}, bf16[256,256]{1,0:T(8,128)(2,1)S(1)}, u32[]{:S(2)}, u32[]{:S(2)}) collective-permute-start(bf16[256,256]{1,0:T(8,128)(2,1)} %get-tuple-element.318), channel_id=1, source_target_pairs={{0,3},{1,0},{2,1},{3,2},{4,7},{5,4},{6,5},{7,6},{8,11},{9,8},{10,9... | collective-permute-start | bytes 393224 | tf_op jit(solution)/shard_map/ppermute | solution.py:147
  160.9 29.0 %collective-permute-start.34 = (bf16[1024,1024]{1,0:T(8,128)(2,1)S(1)}, bf16[1024,1024]{1,0:T(8,128)(2,1)S(1)}, u32[]{:S(2)}, u32[]{:S(2)}) collective-permute-start(bf16[1024,1024]{1,0:T(8,128)(2,1)S(1)} %pad_maximum_fusion), channel_id=1, source_target_pairs={{0,4},{4,0},{8,12},{12,8},{16,20},{20,16},{24,28},{28,24},{1,5},{5... | collective-permute-start | bytes 6291464 | tf_op jit(solution)/shard_map/ppermute | solution.py:67
  217.9 16.5 %collective-permute-start.53 = (bf16[1024,1024]{1,0:T(8,128)(2,1)}, bf16[1024,1024]{1,0:T(8,128)(2,1)S(1)}, u32[]{:S(2)}, u32[]{:S(2)}) collective-permute-start(bf16[1024,1024]{1,0:T(8,128)(2,1)} %get-tuple-element.366), channel_id=1, source_target_pairs={{0,4},{4,0},{8,12},{12,8},{16,20},{20,16},{24,28},{28,24},{1,5},{5... | collective-permute-start | bytes 6291464 | tf_op jit(solution)/shard_map/ppermute | solution.py:67
  218.1 14.2 %collective-permute-start.52 = (bf16[512,512]{1,0:T(8,128)(2,1)S(1)}, bf16[512,512]{1,0:T(8,128)(2,1)S(1)}, u32[]{:S(2)}, u32[]{:S(2)}) collective-permute-start(bf16[512,512]{1,0:T(8,128)(2,1)S(1)} %get-tuple-element.364), channel_id=1, source_target_pairs={{0,8},{4,12},{8,0},{12,4},{16,24},{20,28},{24,16},{28,20},{1,9},{5... | collective-permute-start | bytes 1572872 | tf_op jit(solution)/shard_map/ppermute | solution.py:67
  219.7 13.9 %collective-permute-start.51 = (bf16[512,512]{1,0:T(8,128)(2,1)S(1)}, bf16[512,512]{1,0:T(8,128)(2,1)S(1)}, u32[]{:S(2)}, u32[]{:S(2)}) collective-permute-start(bf16[512,512]{1,0:T(8,128)(2,1)S(1)} %get-tuple-element.362), channel_id=1, source_target_pairs={{0,16},{4,20},{8,24},{12,28},{16,0},{20,4},{24,8},{28,12},{1,17},{... | collective-permute-start | bytes 1572872 | tf_op jit(solution)/shard_map/ppermute | solution.py:67
  266.9 168.5 %all-gather.5.cloned.1.call-start = ((), (), s32[]{:S(2)}) async-start(), calls=%async_computation.3 | async-start | bytes 5308416 | tf_op jit(solution)/shard_map/all_gather | solution.py:1075
  267.1 20.5 %collective-permute-start.60 = (bf16[384,1024]{1,0:T(8,128)(2,1)S(1)}, bf16[384,1024]{1,0:T(8,128)(2,1)S(1)}, u32[]{:S(2)}, u32[]{:S(2)}) collective-permute-start(bf16[384,1024]{1,0:T(8,128)(2,1)S(1)} %get-tuple-element.386), channel_id=1, source_target_pairs={{0,8},{4,12},{8,0},{12,4},{16,24},{20,28},{24,16},{28,20},{1,9},{5... | collective-permute-start | bytes 2359304 | tf_op jit(solution)/shard_map/ppermute | solution.py:67
  267.8 35.4 %collective-permute-start.61 = (bf16[384,1024]{1,0:T(8,128)(2,1)S(1)}, bf16[384,1024]{1,0:T(8,128)(2,1)S(1)}, u32[]{:S(2)}, u32[]{:S(2)}) collective-permute-start(bf16[384,1024]{1,0:T(8,128)(2,1)S(1)} %get-tuple-element.387), channel_id=1, source_target_pairs={{0,16},{4,20},{8,24},{12,28},{16,0},{20,4},{24,8},{28,12},{1,17},{... | collective-permute-start | bytes 2359304 | tf_op jit(solution)/shard_map/ppermute | solution.py:67
  268.5 34.6 %collective-permute-start.62 = (bf16[384,1024]{1,0:T(8,128)(2,1)S(1)}, bf16[384,1024]{1,0:T(8,128)(2,1)S(1)}, u32[]{:S(2)}, u32[]{:S(2)}) collective-permute-start(bf16[384,1024]{1,0:T(8,128)(2,1)S(1)} %get-tuple-element.388), channel_id=1, source_target_pairs={{0,24},{4,28},{8,16},{12,20},{16,8},{20,12},{24,0},{28,4},{1,25},{... | collective-permute-start | bytes 2359304 | tf_op jit(solution)/shard_map/ppermute | solution.py:67
  314.1 25.0 %collective-permute-start.66 = (bf16[2048,256]{1,0:T(8,128)(2,1)}, bf16[2048,256]{1,0:T(8,128)(2,1)}, u32[]{:S(2)}, u32[]{:S(2)}) collective-permute-start(bf16[2048,256]{1,0:T(8,128)(2,1)} %get-tuple-element.413), channel_id=1, source_target_pairs={{0,8},{4,12},{8,0},{12,4},{16,24},{20,28},{24,16},{28,20},{1,9},{5... | collective-permute-start | bytes 3145736 | tf_op jit(solution)/shard_map/ppermute | solution.py:67
  315.6 25.9 %collective-permute-start.65 = (bf16[2048,256]{1,0:T(8,128)(2,1)}, bf16[2048,256]{1,0:T(8,128)(2,1)S(1)}, u32[]{:S(2)}, u32[]{:S(2)}) collective-permute-start(bf16[2048,256]{1,0:T(8,128)(2,1)} %get-tuple-element.411), channel_id=1, source_target_pairs={{0,16},{4,20},{8,24},{12,28},{16,0},{20,4},{24,8},{28,12},{1,17},{... | collective-permute-start | bytes 3145736 | tf_op jit(solution)/shard_map/ppermute | solution.py:67
  317.0 14.8 %collective-permute-start.67 = (bf16[256,1024]{1,0:T(8,128)(2,1)S(1)}, bf16[256,1024]{1,0:T(8,128)(2,1)S(1)}, u32[]{:S(2)}, u32[]{:S(2)}) collective-permute-start(bf16[256,1024]{1,0:T(8,128)(2,1)S(1)} %fusion.8.refs_0_), channel_id=1, source_target_pairs={{0,1},{1,2},{2,3},{3,0},{4,5},{5,6},{6,7},{7,4},{8,9},{9,10},{10,1... | collective-permute-start | bytes 1572872 | tf_op jit(solution)/shard_map/ppermute | solution.py:147
  331.8 13.8 %collective-permute-start.68 = (bf16[256,1024]{1,0:T(8,128)(2,1)S(1)}, bf16[256,1024]{1,0:T(8,128)(2,1)S(1)}, u32[]{:S(2)}, u32[]{:S(2)}) collective-permute-start(bf16[256,1024]{1,0:T(8,128)(2,1)S(1)} %collective-permute-done.67.refs_1_), channel_id=1, source_target_pairs={{0,1},{1,2},{2,3},{3,0},{4,5},{5,6},{6,7},{7,4},{8,9},{9,10},{10,1... | collective-permute-start | bytes 1572872 | tf_op jit(solution)/shard_map/ppermute | solution.py:147
  363.7 16.5 %collective-permute-start.72 = (bf16[256,1024]{1,0:T(8,128)(2,1)}, bf16[256,1024]{1,0:T(8,128)(2,1)S(1)}, u32[]{:S(2)}, u32[]{:S(2)}) collective-permute-start(bf16[256,1024]{1,0:T(8,128)(2,1)} %get-tuple-element.437), channel_id=1, source_target_pairs={{0,3},{1,0},{2,1},{3,2},{4,7},{5,4},{6,5},{7,6},{8,11},{9,8},{10,9... | collective-permute-start | bytes 1572872 | tf_op jit(solution)/shard_map/ppermute | solution.py:147
  364.2 15.6 %collective-permute-start.73 = (bf16[32,1024]{1,0:T(8,128)(2,1)S(1)}, bf16[32,1024]{1,0:T(8,128)(2,1)S(1)}, u32[]{:S(2)}, u32[]{:S(2)}) collective-permute-start(bf16[32,1024]{1,0:T(8,128)(2,1)S(1)} %copy-done.77), channel_id=1, source_target_pairs={{0,1},{1,2},{2,3},{3,0},{4,5},{5,6},{6,7},{7,4},{8,9},{9,10},{10,1... | collective-permute-start | bytes 196616 | tf_op jit(solution)/shard_map/ppermute | solution.py:147
  365.7 14.4 %collective-permute-start.74 = (bf16[32,1024]{1,0:T(8,128)(2,1)S(1)}, bf16[32,1024]{1,0:T(8,128)(2,1)S(1)}, u32[]{:S(2)}, u32[]{:S(2)}) collective-permute-start(bf16[32,1024]{1,0:T(8,128)(2,1)S(1)} %copy-done.76), channel_id=1, source_target_pairs={{0,2},{1,3},{2,0},{3,1},{4,6},{5,7},{6,4},{7,5},{8,10},{9,11},{10,... | collective-permute-start | bytes 196616 | tf_op jit(solution)/shard_map/ppermute | solution.py:147
  366.3 13.8 %collective-permute-start.75 = (bf16[32,1024]{1,0:T(8,128)(2,1)S(1)}, bf16[32,1024]{1,0:T(8,128)(2,1)S(1)}, u32[]{:S(2)}, u32[]{:S(2)}) collective-permute-start(bf16[32,1024]{1,0:T(8,128)(2,1)S(1)} %get-tuple-element.450), channel_id=1, source_target_pairs={{0,3},{1,0},{2,1},{3,2},{4,7},{5,4},{6,5},{7,6},{8,11},{9,8},{10,9... | collective-permute-start | bytes 196616 | tf_op jit(solution)/shard_map/ppermute | solution.py:147
  381.2 15.2 %collective-permute-start.77 = (bf16[384,1024]{1,0:T(8,128)(2,1)}, bf16[384,1024]{1,0:T(8,128)(2,1)S(1)}, u32[]{:S(2)}, u32[]{:S(2)}) collective-permute-start(bf16[384,1024]{1,0:T(8,128)(2,1)} %get-tuple-element.469), channel_id=1, source_target_pairs={{0,4},{4,0},{8,12},{12,8},{16,20},{20,16},{24,28},{28,24},{1,5},{5... | collective-permute-start | bytes 2359304 | tf_op jit(solution)/shard_map/ppermute | solution.py:67
  381.2 15.2 %collective-permute-start.76 = (bf16[256,1024]{1,0:T(8,128)(2,1)}, bf16[256,1024]{1,0:T(8,128)(2,1)S(1)}, u32[]{:S(2)}, u32[]{:S(2)}) collective-permute-start(bf16[256,1024]{1,0:T(8,128)(2,1)} %add_convert_fusion.8), channel_id=1, source_target_pairs={{0,3},{1,0},{2,1},{3,2},{4,7},{5,4},{6,5},{7,6},{8,11},{9,8},{10,9... | collective-permute-start | bytes 1572872 | tf_op jit(solution)/shard_map/ppermute | solution.py:147
  397.8 17.9 %collective-permute-start.81 = (bf16[96,1024]{1,0:T(8,128)(2,1)S(1)}, bf16[96,1024]{1,0:T(8,128)(2,1)S(1)}, u32[]{:S(2)}, u32[]{:S(2)}) collective-permute-start(bf16[96,1024]{1,0:T(8,128)(2,1)S(1)} %get-tuple-element.560), channel_id=1, source_target_pairs={{0,8},{4,12},{8,0},{12,4},{16,24},{20,28},{24,16},{28,20},{1,9},{5... | collective-permute-start | bytes 589832 | tf_op jit(solution)/shard_map/ppermute | solution.py:67
  399.0 16.7 %collective-permute-start.82 = (bf16[96,1024]{1,0:T(8,128)(2,1)S(1)}, bf16[96,1024]{1,0:T(8,128)(2,1)S(1)}, u32[]{:S(2)}, u32[]{:S(2)}) collective-permute-start(bf16[96,1024]{1,0:T(8,128)(2,1)S(1)} %get-tuple-element.562), channel_id=1, source_target_pairs={{0,16},{4,20},{8,24},{12,28},{16,0},{20,4},{24,8},{28,12},{1,17},{... | collective-permute-start | bytes 589832 | tf_op jit(solution)/shard_map/ppermute | solution.py:67
  399.7 16.0 %collective-permute-start.83 = (bf16[96,1024]{1,0:T(8,128)(2,1)S(1)}, bf16[96,1024]{1,0:T(8,128)(2,1)S(1)}, u32[]{:S(2)}, u32[]{:S(2)}) collective-permute-start(bf16[96,1024]{1,0:T(8,128)(2,1)S(1)} %get-tuple-element.561), channel_id=1, source_target_pairs={{0,24},{4,28},{8,16},{12,20},{16,8},{20,12},{24,0},{28,4},{1,25},{... | collective-permute-start | bytes 589832 | tf_op jit(solution)/shard_map/ppermute | solution.py:67
  401.3 14.5 %collective-permute-start.80 = (bf16[256,1024]{1,0:T(8,128)(2,1)S(1)}, bf16[256,1024]{1,0:T(8,128)(2,1)S(1)}, u32[]{:S(2)}, u32[]{:S(2)}) collective-permute-start(bf16[256,1024]{1,0:T(8,128)(2,1)S(1)} %add_convert_fusion.7), channel_id=1, source_target_pairs={{0,3},{1,0},{2,1},{3,2},{4,7},{5,4},{6,5},{7,6},{8,11},{9,8},{10,9... | collective-permute-start | bytes 1572872 | tf_op jit(solution)/shard_map/ppermute | solution.py:147
  416.7 14.5 %collective-permute-start.86 = (bf16[256,1024]{1,0:T(8,128)(2,1)S(1)}, bf16[256,1024]{1,0:T(8,128)(2,1)S(1)}, u32[]{:S(2)}, u32[]{:S(2)}) collective-permute-start(bf16[256,1024]{1,0:T(8,128)(2,1)S(1)} %fusion.6.refs_0_), channel_id=1, source_target_pairs={{0,1},{1,2},{2,3},{3,0},{4,5},{5,6},{6,7},{7,4},{8,9},{9,10},{10,1... | collective-permute-start | bytes 1572872 | tf_op jit(solution)/shard_map/ppermute | solution.py:147
  431.2 16.5 %collective-permute-start.91 = (bf16[256,1024]{1,0:T(8,128)(2,1)S(1)}, bf16[256,1024]{1,0:T(8,128)(2,1)S(1)}, u32[]{:S(2)}, u32[]{:S(2)}) collective-permute-start(bf16[256,1024]{1,0:T(8,128)(2,1)S(1)} %collective-permute-done.86.refs_1_), channel_id=1, source_target_pairs={{0,1},{1,2},{2,3},{3,0},{4,5},{5,6},{6,7},{7,4},{8,9},{9,10},{10,1... | collective-permute-start | bytes 1572872 | tf_op jit(solution)/shard_map/ppermute | solution.py:147
  447.8 16.0 %collective-permute-start.93 = (bf16[256,1024]{1,0:T(8,128)(2,1)S(1)}, bf16[256,1024]{1,0:T(8,128)(2,1)S(1)}, u32[]{:S(2)}, u32[]{:S(2)}) collective-permute-start(bf16[256,1024]{1,0:T(8,128)(2,1)S(1)} %collective-permute-done.91.refs_2_), channel_id=1, source_target_pairs={{0,1},{1,2},{2,3},{3,0},{4,5},{5,6},{6,7},{7,4},{8,9},{9,10},{10,1... | collective-permute-start | bytes 1572872 | tf_op jit(solution)/shard_map/ppermute | solution.py:147
  (137 other events, 1286.0 us)
Sparse Core Ops, SparseCore 0:
  59.9 95.4 all-gather.2
  267.0 47.0 reduce-scatter.1
  359.7 36.7 all-gather.4
